TPU v7x, 32 devices: a whole 2x2x4 slice. The times are simulated.
32 devices in a mesh: panel: 4 (over y, x), front: 8 (over z, core).
Axes of the slice: x: 2, y: 2, z: 4, core: 2. Of those that a mesh axis runs over, the one named last changes fastest.
Arguments:
- top_source: bfloat16 [4, 128, 4096], P('panel', None, 'front'), may hold values from -6 to 6
- leaf_source: bfloat16 [4, 128, 73728], P('panel', None, 'front'), may hold values from -6 to 6
- top_inverse: bfloat16 [4, 4096, 4096], P('panel', 'front'), may hold values from -1 to 4
- leaf_inverse: bfloat16 [4, 288, 256, 256], P('panel', 'front'), may hold values from -1 to 4
- boundary: bfloat16 [4, 288, 128, 256], P('panel', 'front'), may hold values from -0.09375 to 0.09375
- touch_rows: int32 [4, 288, 128], P('panel', 'front'), may hold values from 0 to 4095, as said below
- coupling: float32 [4, 4096], P('panel', 'front'), may hold values from 0.3 to 1
Outputs:
- top_field: bfloat16 [4, 128, 4096], P('panel', None, 'front')
- leaf_field: bfloat16 [4, 128, 73728], P('panel', None, 'front')
Inputs may be any that keep to these rules, and one draw needn't show every extreme that they name: `touch_rows`: front index d owns top front rows d * 512 to (d + 1) * 512 - 1; leaf j of a panel touches only rows owned by front indices j // 36 - 1, j // 36 and j // 36 + 1.
All inputs are finite; a program needn't handle non-finite values.
Results may differ from a plain program's by a relative error of at most 0.02.
Values may be sent and summed in bfloat16 or wider, within the bound.
No kernel may reach another device: no remote copies, remote signals or barrier semaphores. Data moves between devices by JAX's collectives and lax.ppermute only.
A program may use at most 64 MiB of HBM per device.

v0:
```python
import jax
import jax.numpy as jnp
from jax import lax
from jax.sharding import PartitionSpec as P


def extended(value, sides, width):
    for axis, dim in sides:
        devices, length = (lax.axis_size(axis), value.shape[dim])
        up = [(i, (i + 1) % devices) for i in range(devices - 1)]
        down = [(j, i) for i, j in up]
        last = lax.slice_in_dim(value, length - width, length, axis=dim)
        leading = lax.slice_in_dim(value, 0, width, axis=dim)
        before = lax.ppermute(last, axis, up)
        after = lax.ppermute(leading, axis, down)
        value = jnp.concatenate([before, value, after], axis=dim)
    return value


def passed_along(block, axis, distance):
    devices = range(lax.axis_size(axis))
    route = [(i - distance, i) for i in devices if i - distance in devices]
    return lax.ppermute(block, axis, route)


def leaf_apply(inverse_blocks, vectors):
    return jnp.einsum("jab,sjb->sja", inverse_blocks, vectors, preferred_element_type=jnp.float32)


def top_fold(vectors, inverse_rows):
    return lax.dot_general(
        lax.all_gather(vectors, "front", axis=1, tiled=True),
        inverse_rows,
        (((1,), (1,)), ((), ())),
        preferred_element_type=jnp.float32,
    )


def lift_through(values, local_rows, boundary, leaf_inverse):
    rows_here = values.shape[2]
    window = extended(values, (("front", 2),), rows_here)
    flat_rows = local_rows[0].reshape(-1)
    picked = jnp.take(window[0], flat_rows, axis=1).reshape(
        values.shape[1], local_rows.shape[1], local_rows.shape[2]
    )
    lifted = jnp.einsum(
        "jkb,sjk->sjb", boundary[0], picked, preferred_element_type=jnp.float32
    ).astype(jnp.bfloat16)
    results = [leaf_apply(leaf_inverse[0], lifted)]
    return jnp.stack(results)


def place_wave(finished, fresh, first_row, in_range):
    older = lax.dynamic_slice_in_dim(finished, first_row, fresh.shape[1], 1)
    return lax.dynamic_update_slice_in_dim(
        finished, jnp.where(in_range, fresh, older), first_row, 1
    )


def body(top_source, leaf_source, top_inverse, leaf_inverse, boundary, touch_rows, coupling):
    panels_here = top_source.shape[0]
    sources_all = top_source.shape[1]
    rows_here = top_source.shape[2]
    leaf_count = leaf_inverse.shape[1]
    leaf_size = leaf_inverse.shape[2]
    group_count = lax.axis_size("panel")
    group_rank = lax.axis_index("panel")
    row_offset = lax.axis_index("front") * rows_here
    local_rows = touch_rows - (row_offset - rows_here)
    vectors = leaf_source.reshape(panels_here, sources_all, leaf_count, leaf_size)
    panel_index = 0
    interior_one = leaf_apply(leaf_inverse[panel_index], vectors[panel_index]).astype(jnp.bfloat16)
    pushed = jnp.einsum(
        "jkb,sjb->sjk", boundary[panel_index], interior_one, preferred_element_type=jnp.float32
    )
    window_one = jnp.zeros((sources_all, 3 * rows_here), jnp.float32)
    window_one = window_one.at[:, local_rows[panel_index].reshape(-1)].add(
        pushed.reshape(sources_all, -1)
    )
    interior_list = [interior_one]
    window_list = [window_one]
    interior = jnp.stack(interior_list)
    windows = jnp.stack(window_list)
    from_below = passed_along(
        windows[:, :, 2 * rows_here :].astype(jnp.bfloat16), "front", 1
    ).astype(jnp.float32)
    from_above = passed_along(windows[:, :, :rows_here].astype(jnp.bfloat16), "front", -1).astype(
        jnp.float32
    )
    known_part = windows[:, :, rows_here : 2 * rows_here] + from_below + from_above
    wave_count = 2
    wave_rows = sources_all // wave_count
    turn_count = group_count + wave_count - 1

    def forward_turn(turn_index, carry):
        incoming, top_done = carry
        wave_index = turn_index - group_rank
        in_range = (wave_index >= 0) & (wave_index < wave_count)
        first_row = jnp.clip(wave_index, 0, wave_count - 1) * wave_rows
        top_block = lax.dynamic_slice_in_dim(top_source, first_row, wave_rows, 1)
        known_block = lax.dynamic_slice_in_dim(known_part, first_row, wave_rows, 1)
        previous = incoming
        own_terms = top_block[0].astype(jnp.float32) + coupling[0] * previous.astype(jnp.float32)
        solved = top_fold((own_terms - known_block[0]).astype(jnp.bfloat16), top_inverse[0])
        previous = solved.astype(jnp.bfloat16)
        top_parts = [previous]
        top_done = place_wave(top_done, jnp.stack(top_parts), first_row, in_range)
        outgoing = passed_along(previous, "panel", 1)
        return (outgoing, top_done)

    start_edge = jnp.zeros((wave_rows, rows_here), jnp.bfloat16)
    unused_edge, forward_tops = lax.fori_loop(
        0, turn_count, forward_turn, (start_edge, jnp.zeros_like(top_source))
    )

    def backward_turn(turn_index, carry):
        incoming, top_done, fixes_done = carry
        wave_index = turn_index - (group_count - 1 - group_rank)
        in_range = (wave_index >= 0) & (wave_index < wave_count)
        first_row = jnp.clip(wave_index, 0, wave_count - 1) * wave_rows
        top_block = lax.dynamic_slice_in_dim(forward_tops, first_row, wave_rows, 1)
        arriving = incoming
        top_parts = [None] * panels_here
        fix_parts = [None] * panels_here
        for panel_index in reversed(range(panels_here)):
            correction = top_fold(arriving, top_inverse[panel_index]).astype(jnp.bfloat16)
            top_new = (
                top_block[panel_index].astype(jnp.float32) + correction.astype(jnp.float32)
            ).astype(jnp.bfloat16)
            top_parts[panel_index] = top_new
            fix_parts[panel_index] = correction
            arriving = (coupling[panel_index] * top_new.astype(jnp.float32)).astype(jnp.bfloat16)
        top_done = place_wave(top_done, jnp.stack(top_parts), first_row, in_range)
        fixes_done = place_wave(fixes_done, jnp.stack(fix_parts), first_row, in_range)
        outgoing = passed_along(arriving, "panel", -1)
        return (outgoing, top_done, fixes_done)

    backward_state = (start_edge, jnp.zeros_like(top_source), jnp.zeros_like(top_source))
    final_edge, top_field, corrections = lax.fori_loop(0, turn_count, backward_turn, backward_state)
    forward_leaf = (
        interior.astype(jnp.float32)
        - lift_through(forward_tops, local_rows, boundary, leaf_inverse)
    ).astype(jnp.bfloat16)
    leaf_field = (
        forward_leaf.astype(jnp.float32)
        - lift_through(corrections, local_rows, boundary, leaf_inverse)
    ).astype(jnp.bfloat16)
    return (top_field, leaf_field.reshape(panels_here, sources_all, -1))


def solution(mesh):
    placed = (
        P("panel", None, "front"),
        P("panel", None, "front"),
        P("panel", "front", None),
        P("panel", "front", None, None),
        P("panel", "front", None, None),
        P("panel", "front", None),
        P("panel", "front"),
    )
    return jax.shard_map(
        body,
        mesh=mesh,
        in_specs=placed,
        out_specs=(P("panel", None, "front"), P("panel", None, "front")),
        check_vma=False,
    )
```

profile of v0, /device:TPU:1, one launch (start us, length us, event | category | flops | bytes accessed | tf_op | source)
XLA Modules:
  0.0 370.5 jit_solution(14029887423466391918)
XLA Ops:
  0.7 4.4 %copy.17 = bf16[1,128,9216]{1,2,0:T(8,128)(2,1)} copy(bf16[1,128,9216]{2,1,0:T(8,128)(2,1)} %param.14) | data formatting | bytes 4718592 | tf_op args[1]
  5.1 4.7 %fusion.43 = bf16[36,128,256]{2,1,0:T(8,128)(2,1)S(1)} fusion(bf16[128,36,256]{0,2,1:T(8,128)(2,1)} %bitcast.143, bf16[1,36,256,256]{3,2,1,0:T(8,128)(2,1)} %param.16), kind=kOutput, calls=%fused_computation.42 | convolution fusion | flops 605159424 | bytes 9437184 | tf_op jit(solution)/shard_map/jab,sjb->sja/dot_general | solution.py:27
  12.1 25.6 %scatter_custom_fusion = f32[128,1536]{0,1:T(8,128)S(1)} fusion(s32[4608]{0:T(1024)S(1)} %fusion.55, f32[4608,128]{1,0:T(8,128)} %bitcast.147, f32[]{:T(128)} %constant.115.clone.1), kind=kCustom, calls=%fused_computation.47 | custom fusion | flops 589824 | bytes 786944 | tf_op jit(solution)/shard_map/scatter-add | solution.py:77
  38.4 4.6 %collective-permute-start.2 = (bf16[1,128,512]{1,2,0:T(8,128)(2,1)}, bf16[1,128,512]{1,2,0:T(8,128)(2,1)S(1)}, u32[]{:S(2)}, u32[]{:S(2)}) collective-permute-start(bf16[1,128,512]{1,2,0:T(8,128)(2,1)} %get-tuple-element.393), channel_id=1, source_target_pairs={{0,1},{1,2},{2,3},{3,4},{4,5},{5,6},{6,7},{8,9},{9,10},{10,11},{11... | collective-permute-start | bytes 393224 | tf_op jit(solution)/shard_map/ppermute | solution.py:23
  50.6 126.9 %while.34 = (s32[]{:T(128)}, bf16[64,512]{1,0:T(8,128)(2,1)S(1)}, bf16[1,128,512]{2,1,0:T(8,128)(2,1)S(1)}, s32[]{:T(128)}, bf16[1,128,512]{2,1,0:T(8,128)(2,1)}...) while((s32[]{:T(128)}, bf16[64,512]{1,0:T(8,128)(2,1)S(1)}, ...), condition=%wide.region_2.3_spmd, body=%wide.region_1.2_spmd.sunk | while | flops 268697600 | bytes 6097173 | solution.py:112
  51.5 14.1 %all_gather.18 = bf16[64,4096]{1,0:T(8,128)(2,1)S(1)} all-gather(bf16[64,512]{1,0:T(8,128)(2,1)S(1)} %fusion.68), channel_id=1, replica_groups=mesh['panel'=4,'front'=8] {'front'}, dimensions={1}, use_global_device_ids=true | all-gather | bytes 589824 | tf_op jit(solution)/shard_map/while/body/eval_jaxpr/all_gather | solution.py:32
  74.4 15.6 %all_gather.18 = bf16[64,4096]{1,0:T(8,128)(2,1)S(1)} all-gather(bf16[64,512]{1,0:T(8,128)(2,1)S(1)} %fusion.68), channel_id=1, replica_groups=mesh['panel'=4,'front'=8] {'front'}, dimensions={1}, use_global_device_ids=true | all-gather | bytes 589824 | tf_op jit(solution)/shard_map/while/body/eval_jaxpr/all_gather | solution.py:32
  93.6 4.1 %collective-permute-start = (bf16[64,512]{1,0:T(8,128)(2,1)S(1)}, bf16[64,512]{1,0:T(8,128)(2,1)S(1)}, u32[]{:S(2)}, u32[]{:S(2)}) collective-permute-start(bf16[64,512]{1,0:T(8,128)(2,1)S(1)} %get-tuple-element.493), channel_id=1, source_target_pairs={{0,8},{8,16},{16,24},{1,9},{9,17},{17,25},{2,10},{10,18},{18,26},{... | collective-permute-start | bytes 196616 | tf_op jit(solution)/shard_map/while/body/eval_jaxpr/ppermute | solution.py:23
  99.9 15.6 %all_gather.18 = bf16[64,4096]{1,0:T(8,128)(2,1)S(1)} all-gather(bf16[64,512]{1,0:T(8,128)(2,1)S(1)} %fusion.68), channel_id=1, replica_groups=mesh['panel'=4,'front'=8] {'front'}, dimensions={1}, use_global_device_ids=true | all-gather | bytes 589824 | tf_op jit(solution)/shard_map/while/body/eval_jaxpr/all_gather | solution.py:32
  119.1 4.2 %collective-permute-start = (bf16[64,512]{1,0:T(8,128)(2,1)S(1)}, bf16[64,512]{1,0:T(8,128)(2,1)S(1)}, u32[]{:S(2)}, u32[]{:S(2)}) collective-permute-start(bf16[64,512]{1,0:T(8,128)(2,1)S(1)} %get-tuple-element.493), channel_id=1, source_target_pairs={{0,8},{8,16},{16,24},{1,9},{9,17},{17,25},{2,10},{10,18},{18,26},{... | collective-permute-start | bytes 196616 | tf_op jit(solution)/shard_map/while/body/eval_jaxpr/ppermute | solution.py:23
  125.4 15.6 %all_gather.18 = bf16[64,4096]{1,0:T(8,128)(2,1)S(1)} all-gather(bf16[64,512]{1,0:T(8,128)(2,1)S(1)} %fusion.68), channel_id=1, replica_groups=mesh['panel'=4,'front'=8] {'front'}, dimensions={1}, use_global_device_ids=true | all-gather | bytes 589824 | tf_op jit(solution)/shard_map/while/body/eval_jaxpr/all_gather | solution.py:32
  144.5 5.1 %collective-permute-start = (bf16[64,512]{1,0:T(8,128)(2,1)S(1)}, bf16[64,512]{1,0:T(8,128)(2,1)S(1)}, u32[]{:S(2)}, u32[]{:S(2)}) collective-permute-start(bf16[64,512]{1,0:T(8,128)(2,1)S(1)} %get-tuple-element.493), channel_id=1, source_target_pairs={{0,8},{8,16},{16,24},{1,9},{9,17},{17,25},{2,10},{10,18},{18,26},{... | collective-permute-start | bytes 196616 | tf_op jit(solution)/shard_map/while/body/eval_jaxpr/ppermute | solution.py:23
  151.8 15.8 %all_gather.18 = bf16[64,4096]{1,0:T(8,128)(2,1)S(1)} all-gather(bf16[64,512]{1,0:T(8,128)(2,1)S(1)} %fusion.68), channel_id=1, replica_groups=mesh['panel'=4,'front'=8] {'front'}, dimensions={1}, use_global_device_ids=true | all-gather | bytes 589824 | tf_op jit(solution)/shard_map/while/body/eval_jaxpr/all_gather | solution.py:32
  171.2 4.9 %collective-permute-start = (bf16[64,512]{1,0:T(8,128)(2,1)S(1)}, bf16[64,512]{1,0:T(8,128)(2,1)S(1)}, u32[]{:S(2)}, u32[]{:S(2)}) collective-permute-start(bf16[64,512]{1,0:T(8,128)(2,1)S(1)} %get-tuple-element.493), channel_id=1, source_target_pairs={{0,8},{8,16},{16,24},{1,9},{9,17},{17,25},{2,10},{10,18},{18,26},{... | collective-permute-start | bytes 196616 | tf_op jit(solution)/shard_map/while/body/eval_jaxpr/ppermute | solution.py:23
  177.5 130.2 %while.35 = (s32[]{:T(128)}, bf16[64,512]{1,0:T(8,128)(2,1)S(1)}, bf16[1,128,512]{2,1,0:T(8,128)(2,1)S(1)}, bf16[1,128,512]{2,1,0:T(8,128)(2,1)S(1)}, f32[1,512]...) while((s32[]{:T(128)}, bf16[64,512]{1,0:T(8,128)(2,1)S(1)}, ...), condition=%wide.region_4.5_spmd, body=%wide.region_3.4_spmd.sunk | while | flops 268894208 | bytes 6162709 | solution.py:139
  177.5 15.8 %all_gather.19 = bf16[64,4096]{1,0:T(8,128)(2,1)S(1)} all-gather(bf16[64,512]{1,0:T(8,128)(2,1)S(1)} %get-tuple-element.560), channel_id=1, replica_groups=mesh['panel'=4,'front'=8] {'front'}, dimensions={1}, use_global_device_ids=true | all-gather | bytes 589824 | tf_op jit(solution)/shard_map/while/body/eval_jaxpr/all_gather | solution.py:32
  198.3 5.9 %collective-permute-done.1 = bf16[64,512]{1,0:T(8,128)(2,1)S(1)} collective-permute-done((bf16[64,512]{1,0:T(8,128)(2,1)S(1)}, bf16[64,512]{1,0:T(8,128)(2,1)S(1)}, u32[]{:S(2)}, u32[]{:S(2)}) %collective-permute-start.1) | collective-permute-done | bytes 65568 | tf_op jit(solution)/shard_map/while/body/eval_jaxpr/ppermute | solution.py:23
  204.2 15.6 %all_gather.19 = bf16[64,4096]{1,0:T(8,128)(2,1)S(1)} all-gather(bf16[64,512]{1,0:T(8,128)(2,1)S(1)} %get-tuple-element.560), channel_id=1, replica_groups=mesh['panel'=4,'front'=8] {'front'}, dimensions={1}, use_global_device_ids=true | all-gather | bytes 589824 | tf_op jit(solution)/shard_map/while/body/eval_jaxpr/all_gather | solution.py:32
  224.7 5.9 %collective-permute-done.1 = bf16[64,512]{1,0:T(8,128)(2,1)S(1)} collective-permute-done((bf16[64,512]{1,0:T(8,128)(2,1)S(1)}, bf16[64,512]{1,0:T(8,128)(2,1)S(1)}, u32[]{:S(2)}, u32[]{:S(2)}) %collective-permute-start.1) | collective-permute-done | bytes 65568 | tf_op jit(solution)/shard_map/while/body/eval_jaxpr/ppermute | solution.py:23
  230.6 15.6 %all_gather.19 = bf16[64,4096]{1,0:T(8,128)(2,1)S(1)} all-gather(bf16[64,512]{1,0:T(8,128)(2,1)S(1)} %get-tuple-element.560), channel_id=1, replica_groups=mesh['panel'=4,'front'=8] {'front'}, dimensions={1}, use_global_device_ids=true | all-gather | bytes 589824 | tf_op jit(solution)/shard_map/while/body/eval_jaxpr/all_gather | solution.py:32
  251.1 5.2 %collective-permute-done.1 = bf16[64,512]{1,0:T(8,128)(2,1)S(1)} collective-permute-done((bf16[64,512]{1,0:T(8,128)(2,1)S(1)}, bf16[64,512]{1,0:T(8,128)(2,1)S(1)}, u32[]{:S(2)}, u32[]{:S(2)}) %collective-permute-start.1) | collective-permute-done | bytes 65568 | tf_op jit(solution)/shard_map/while/body/eval_jaxpr/ppermute | solution.py:23
  256.3 15.6 %all_gather.19 = bf16[64,4096]{1,0:T(8,128)(2,1)S(1)} all-gather(bf16[64,512]{1,0:T(8,128)(2,1)S(1)} %get-tuple-element.560), channel_id=1, replica_groups=mesh['panel'=4,'front'=8] {'front'}, dimensions={1}, use_global_device_ids=true | all-gather | bytes 589824 | tf_op jit(solution)/shard_map/while/body/eval_jaxpr/all_gather | solution.py:32
  276.8 5.2 %collective-permute-done.1 = bf16[64,512]{1,0:T(8,128)(2,1)S(1)} collective-permute-done((bf16[64,512]{1,0:T(8,128)(2,1)S(1)}, bf16[64,512]{1,0:T(8,128)(2,1)S(1)}, u32[]{:S(2)}, u32[]{:S(2)}) %collective-permute-start.1) | collective-permute-done | bytes 65568 | tf_op jit(solution)/shard_map/while/body/eval_jaxpr/ppermute | solution.py:23
  282.0 15.6 %all_gather.19 = bf16[64,4096]{1,0:T(8,128)(2,1)S(1)} all-gather(bf16[64,512]{1,0:T(8,128)(2,1)S(1)} %get-tuple-element.560), channel_id=1, replica_groups=mesh['panel'=4,'front'=8] {'front'}, dimensions={1}, use_global_device_ids=true | all-gather | bytes 589824 | tf_op jit(solution)/shard_map/while/body/eval_jaxpr/all_gather | solution.py:32
  302.5 5.2 %collective-permute-done.1 = bf16[64,512]{1,0:T(8,128)(2,1)S(1)} collective-permute-done((bf16[64,512]{1,0:T(8,128)(2,1)S(1)}, bf16[64,512]{1,0:T(8,128)(2,1)S(1)}, u32[]{:S(2)}, u32[]{:S(2)}) %collective-permute-start.1) | collective-permute-done | bytes 65568 | tf_op jit(solution)/shard_map/while/body/eval_jaxpr/ppermute | solution.py:23
  320.7 10.1 %gather_fusion.1 = bf16[4608,128]{1,0:T(8,128)(2,1)} fusion(bf16[128,1536]{0,1:T(8,128)(2,1)S(1)} %maximum_bitcast_fusion.1, s32[5120]{0:T(1024)S(1)} %pad_clamp_fusion), kind=kCustom, calls=%fused_computation.1.clone | custom fusion | bytes 2377728 | tf_op jit(solution)/shard_map/jit(_take)/gather | solution.py:43
  331.7 10.2 %gather_fusion = bf16[4608,128]{1,0:T(8,128)(2,1)} fusion(bf16[128,1536]{0,1:T(8,128)(2,1)S(1)} %maximum_bitcast_fusion, s32[5120]{0:T(1024)S(1)} %pad_clamp_fusion), kind=kCustom, calls=%fused_computation.clone | custom fusion | bytes 2377728 | tf_op jit(solution)/shard_map/jit(_take)/gather | solution.py:43
  341.9 4.7 %broadcast_select_fusion.1 = (bf16[4608,128]{1,0:T(8,128)(2,1)S(1)}, bf16[4608,128]{1,0:T(8,128)(2,1)}) fusion(bf16[4608,128]{1,0:T(8,128)(2,1)} %gather_fusion, pred[4608]{0:T(1024)(128)(4,1)S(1)} %compare_and_fusion, bf16[4608,128]{1,0:T(8,128)(2,1)} %gather_fusion.1), kind=kLoop, calls=%fused_computation.44 | loop fusion | flops 1179648 | bytes 4723200 | tf_op jit(solution)/shard_map/jit(_take)/select_n | solution.py:43
  346.6 7.2 %fusion.18 = f32[36,128,256]{2,1,0:T(8,128)} fusion(bf16[1,36,256,256]{3,2,1,0:T(8,128)(2,1)} %param.16, bf16[128,36,128]{0,2,1:T(8,128)(2,1)} %bitcast.145, bf16[1,36,128,256]{3,2,1,0:T(8,128)(2,1)S(1)} %copy-done), kind=kOutput, calls=%fused_computation.25 | convolution fusion | flops 907149312 | bytes 12976128 | tf_op jit(solution)/shard_map/jab,sjb->sja/dot_general | solution.py:27
  353.8 8.2 %fusion.16 = bf16[128,36,256]{2,0,1:T(8,128)(2,1)} fusion(f32[36,128,256]{2,1,0:T(8,128)} %fusion.18, bf16[36,128,256]{2,1,0:T(8,128)(2,1)} %copy-done.1, bf16[1,36,256,256]{3,2,1,0:T(8,128)(2,1)} %param.16, bf16[128,36,128]{0,2,1:T(8,128)(2,1)S(1)} %bitcast.144, bf16[1,36,128,256]{3,2,1,0:T(8,128)(2,1)S(1)} %copy-done), kind=kOutput, calls=%fused_computation.22 | convolution fusion | flops 914227200 | bytes 17694720 | tf_op jit(solution)/shard_map/jab,sjb->sja/dot_general | solution.py:27
  362.0 4.3 %copy.26 = bf16[128,36,256]{0,2,1:T(8,128)(2,1)} copy(bf16[128,36,256]{2,0,1:T(8,128)(2,1)} %fusion.16) | data formatting | bytes 4718592 | tf_op jit(solution)/shard_map/convert_element_type | solution.py:147
  366.2 4.3 %copy.27 = bf16[1,128,9216]{2,1,0:T(8,128)(2,1)} copy(bf16[1,128,9216]{1,2,0:T(8,128)(2,1)} %bitcast.142) | data formatting | bytes 4718592
  (79 shorter events, 80.9 us)
Async XLA Ops:
  0.6 9.3 %copy-start = (bf16[1,36,128,256]{3,2,1,0:T(8,128)(2,1)S(1)}, bf16[1,36,128,256]{3,2,1,0:T(8,128)(2,1)}, u32[]{:S(2)}) copy-start(bf16[1,36,128,256]{3,2,1,0:T(8,128)(2,1)} %param.17) | copy-start | bytes 7077892
  0.6 4.4 %copy-start.8 = (s32[1,36,128]{2,0,1:T(1,128)S(1)}, s32[1,36,128]{2,0,1:T(1,128)}, u32[]{:S(2)}) copy-start(s32[1,36,128]{2,0,1:T(1,128)} %param.18) | copy-start | bytes 55300
  9.9 2.2 copy-start.1
  12.1 38.5 %copy-start.3 = (f32[1,512]{1,0:T(1,128)S(1)}, f32[1,512]{1,0:T(1,128)}, u32[]{:S(2)}) copy-start(f32[1,512]{1,0:T(1,128)} %param.19) | copy-start | bytes 6148
  38.4 7.2 %collective-permute-start.2 = (bf16[1,128,512]{1,2,0:T(8,128)(2,1)}, bf16[1,128,512]{1,2,0:T(8,128)(2,1)S(1)}, u32[]{:S(2)}, u32[]{:S(2)}) collective-permute-start(bf16[1,128,512]{1,2,0:T(8,128)(2,1)} %get-tuple-element.393), channel_id=1, source_target_pairs={{0,1},{1,2},{2,3},{3,4},{4,5},{5,6},{6,7},{8,9},{9,10},{10,11},{11... | collective-permute-start | bytes 393224 | tf_op jit(solution)/shard_map/ppermute | solution.py:23
  43.0 6.4 %collective-permute-start.3 = (bf16[1,128,512]{1,2,0:T(8,128)(2,1)S(1)}, bf16[1,128,512]{1,2,0:T(8,128)(2,1)}, u32[]{:S(2)}, u32[]{:S(2)}) collective-permute-start(bf16[1,128,512]{1,2,0:T(8,128)(2,1)S(1)} %get-tuple-element.394), channel_id=1, source_target_pairs={{1,0},{2,1},{3,2},{4,3},{5,4},{6,5},{7,6},{9,8},{10,9},{11,10},{12... | collective-permute-start | bytes 393224 | tf_op jit(solution)/shard_map/ppermute | solution.py:23
  45.0 4.4 %copy-start.4 = (s32[36,128]{1,0:T(8,128)}, s32[36,128]{1,0:T(8,128)S(1)}, u32[]{:S(2)}) copy-start(s32[36,128]{1,0:T(8,128)S(1)} %subtract_reduce_fusion) | copy-start | bytes 55300
  45.6 3.8 %copy-start.6 = (bf16[1,128,512]{1,2,0:T(8,128)(2,1)}, bf16[1,128,512]{1,2,0:T(8,128)(2,1)S(1)}, u32[]{:S(2)}) copy-start(bf16[1,128,512]{1,2,0:T(8,128)(2,1)S(1)} %collective-permute-done.2) | copy-start | bytes 393220
  69.1 4.4 %collective-permute-start = (bf16[64,512]{1,0:T(8,128)(2,1)S(1)}, bf16[64,512]{1,0:T(8,128)(2,1)S(1)}, u32[]{:S(2)}, u32[]{:S(2)}) collective-permute-start(bf16[64,512]{1,0:T(8,128)(2,1)S(1)} %get-tuple-element.493), channel_id=1, source_target_pairs={{0,8},{8,16},{16,24},{1,9},{9,17},{17,25},{2,10},{10,18},{18,26},{... | collective-permute-start | bytes 196616 | tf_op jit(solution)/shard_map/while/body/eval_jaxpr/ppermute | solution.py:23
  93.6 5.4 %collective-permute-start = (bf16[64,512]{1,0:T(8,128)(2,1)S(1)}, bf16[64,512]{1,0:T(8,128)(2,1)S(1)}, u32[]{:S(2)}, u32[]{:S(2)}) collective-permute-start(bf16[64,512]{1,0:T(8,128)(2,1)S(1)} %get-tuple-element.493), channel_id=1, source_target_pairs={{0,8},{8,16},{16,24},{1,9},{9,17},{17,25},{2,10},{10,18},{18,26},{... | collective-permute-start | bytes 196616 | tf_op jit(solution)/shard_map/while/body/eval_jaxpr/ppermute | solution.py:23
  119.1 5.5 %collective-permute-start = (bf16[64,512]{1,0:T(8,128)(2,1)S(1)}, bf16[64,512]{1,0:T(8,128)(2,1)S(1)}, u32[]{:S(2)}, u32[]{:S(2)}) collective-permute-start(bf16[64,512]{1,0:T(8,128)(2,1)S(1)} %get-tuple-element.493), channel_id=1, source_target_pairs={{0,8},{8,16},{16,24},{1,9},{9,17},{17,25},{2,10},{10,18},{18,26},{... | collective-permute-start | bytes 196616 | tf_op jit(solution)/shard_map/while/body/eval_jaxpr/ppermute | solution.py:23
  144.5 6.4 %collective-permute-start = (bf16[64,512]{1,0:T(8,128)(2,1)S(1)}, bf16[64,512]{1,0:T(8,128)(2,1)S(1)}, u32[]{:S(2)}, u32[]{:S(2)}) collective-permute-start(bf16[64,512]{1,0:T(8,128)(2,1)S(1)} %get-tuple-element.493), channel_id=1, source_target_pairs={{0,8},{8,16},{16,24},{1,9},{9,17},{17,25},{2,10},{10,18},{18,26},{... | collective-permute-start | bytes 196616 | tf_op jit(solution)/shard_map/while/body/eval_jaxpr/ppermute | solution.py:23
  171.2 6.3 %collective-permute-start = (bf16[64,512]{1,0:T(8,128)(2,1)S(1)}, bf16[64,512]{1,0:T(8,128)(2,1)S(1)}, u32[]{:S(2)}, u32[]{:S(2)}) collective-permute-start(bf16[64,512]{1,0:T(8,128)(2,1)S(1)} %get-tuple-element.493), channel_id=1, source_target_pairs={{0,8},{8,16},{16,24},{1,9},{9,17},{17,25},{2,10},{10,18},{18,26},{... | collective-permute-start | bytes 196616 | tf_op jit(solution)/shard_map/while/body/eval_jaxpr/ppermute | solution.py:23
  177.5 136.3 %copy-start.5 = (s32[36,128]{1,0:T(8,128)S(1)}, s32[36,128]{1,0:T(8,128)}, u32[]{:S(2)}) copy-start(s32[36,128]{1,0:T(8,128)} %copy-done.4) | copy-start | bytes 55300
  177.5 136.3 %copy-start.7 = (s32[4608]{0:T(1024)S(1)}, s32[4608]{0:T(1024)}, u32[]{:S(2)}) copy-start(s32[4608]{0:T(1024)} %compare_select_fusion.1) | copy-start | bytes 55300
  196.9 7.3 %collective-permute-start.1 = (bf16[64,512]{1,0:T(8,128)(2,1)S(1)}, bf16[64,512]{1,0:T(8,128)(2,1)S(1)}, u32[]{:S(2)}, u32[]{:S(2)}) collective-permute-start(bf16[64,512]{1,0:T(8,128)(2,1)S(1)} %get-tuple-element.503), channel_id=1, source_target_pairs={{8,0},{16,8},{24,16},{9,1},{17,9},{25,17},{10,2},{18,10},{26,18},{... | collective-permute-start | bytes 196616 | tf_op jit(solution)/shard_map/while/body/eval_jaxpr/ppermute | solution.py:23
  223.3 7.3 %collective-permute-start.1 = (bf16[64,512]{1,0:T(8,128)(2,1)S(1)}, bf16[64,512]{1,0:T(8,128)(2,1)S(1)}, u32[]{:S(2)}, u32[]{:S(2)}) collective-permute-start(bf16[64,512]{1,0:T(8,128)(2,1)S(1)} %get-tuple-element.503), channel_id=1, source_target_pairs={{8,0},{16,8},{24,16},{9,1},{17,9},{25,17},{10,2},{18,10},{26,18},{... | collective-permute-start | bytes 196616 | tf_op jit(solution)/shard_map/while/body/eval_jaxpr/ppermute | solution.py:23
  249.7 6.5 %collective-permute-start.1 = (bf16[64,512]{1,0:T(8,128)(2,1)S(1)}, bf16[64,512]{1,0:T(8,128)(2,1)S(1)}, u32[]{:S(2)}, u32[]{:S(2)}) collective-permute-start(bf16[64,512]{1,0:T(8,128)(2,1)S(1)} %get-tuple-element.503), channel_id=1, source_target_pairs={{8,0},{16,8},{24,16},{9,1},{17,9},{25,17},{10,2},{18,10},{26,18},{... | collective-permute-start | bytes 196616 | tf_op jit(solution)/shard_map/while/body/eval_jaxpr/ppermute | solution.py:23
  275.5 6.5 %collective-permute-start.1 = (bf16[64,512]{1,0:T(8,128)(2,1)S(1)}, bf16[64,512]{1,0:T(8,128)(2,1)S(1)}, u32[]{:S(2)}, u32[]{:S(2)}) collective-permute-start(bf16[64,512]{1,0:T(8,128)(2,1)S(1)} %get-tuple-element.503), channel_id=1, source_target_pairs={{8,0},{16,8},{24,16},{9,1},{17,9},{25,17},{10,2},{18,10},{26,18},{... | collective-permute-start | bytes 196616 | tf_op jit(solution)/shard_map/while/body/eval_jaxpr/ppermute | solution.py:23
  301.1 6.5 %collective-permute-start.1 = (bf16[64,512]{1,0:T(8,128)(2,1)S(1)}, bf16[64,512]{1,0:T(8,128)(2,1)S(1)}, u32[]{:S(2)}, u32[]{:S(2)}) collective-permute-start(bf16[64,512]{1,0:T(8,128)(2,1)S(1)} %get-tuple-element.503), channel_id=1, source_target_pairs={{8,0},{16,8},{24,16},{9,1},{17,9},{25,17},{10,2},{18,10},{26,18},{... | collective-permute-start | bytes 196616 | tf_op jit(solution)/shard_map/while/body/eval_jaxpr/ppermute | solution.py:23
  307.7 23.1 %copy-start.2 = (bf16[1,128,512]{2,1,0:T(8,128)(2,1)}, bf16[1,128,512]{2,1,0:T(8,128)(2,1)S(1)}, u32[]{:S(2)}) copy-start(bf16[1,128,512]{2,1,0:T(8,128)(2,1)S(1)} %get-tuple-element.353) | copy-start | bytes 393220
  307.8 11.9 %collective-permute-start.7 = (bf16[1,128,512]{1,2,0:T(8,128)(2,1)S(1)}, bf16[1,128,512]{1,2,0:T(8,128)(2,1)S(1)}, u32[]{:S(2)}, u32[]{:S(2)}) collective-permute-start(bf16[1,128,512]{1,2,0:T(8,128)(2,1)S(1)} %copy.23), channel_id=1, source_target_pairs={{1,0},{2,1},{3,2},{4,3},{5,4},{6,5},{7,6},{9,8},{10,9},{11,10},{12... | collective-permute-start | bytes 393224 | tf_op jit(solution)/shard_map/ppermute | solution.py:15
  310.5 9.2 %collective-permute-start.6 = (bf16[1,128,512]{1,2,0:T(8,128)(2,1)S(1)}, bf16[1,128,512]{1,2,0:T(8,128)(2,1)}, u32[]{:S(2)}, u32[]{:S(2)}) collective-permute-start(bf16[1,128,512]{1,2,0:T(8,128)(2,1)S(1)} %copy.23), channel_id=1, source_target_pairs={{0,1},{1,2},{2,3},{3,4},{4,5},{5,6},{6,7},{8,9},{9,10},{10,11},{11... | collective-permute-start | bytes 393224 | tf_op jit(solution)/shard_map/ppermute | solution.py:14
  313.9 16.9 %collective-permute-start.5 = (bf16[1,128,512]{1,2,0:T(8,128)(2,1)S(1)}, bf16[1,128,512]{1,2,0:T(8,128)(2,1)S(1)}, u32[]{:S(2)}, u32[]{:S(2)}) collective-permute-start(bf16[1,128,512]{1,2,0:T(8,128)(2,1)S(1)} %copy.20), channel_id=1, source_target_pairs={{1,0},{2,1},{3,2},{4,3},{5,4},{6,5},{7,6},{9,8},{10,9},{11,10},{12... | collective-permute-start | bytes 393224 | tf_op jit(solution)/shard_map/ppermute | solution.py:15
  315.9 14.9 %collective-permute-start.4 = (bf16[1,128,512]{1,2,0:T(8,128)(2,1)S(1)}, bf16[1,128,512]{1,2,0:T(8,128)(2,1)}, u32[]{:S(2)}, u32[]{:S(2)}) collective-permute-start(bf16[1,128,512]{1,2,0:T(8,128)(2,1)S(1)} %copy.20), channel_id=1, source_target_pairs={{0,1},{1,2},{2,3},{3,4},{4,5},{5,6},{6,7},{8,9},{9,10},{10,11},{11... | collective-permute-start | bytes 393224 | tf_op jit(solution)/shard_map/ppermute | solution.py:14
where the time goes:
time: 372 us; the launch traced here: 371 us
  blocking collectives  155 us (42%)
  matrix products  58.1 us (16%)
  starting transfers between devices  46 us (12%)
  other arithmetic  38.5 us (10%)
  waiting for transfers between devices  37.7 us (10%)
  local copies, waits for them, and re-layouts  34.4 us (9%)
    all_gather x10, blocking collectives, top_fold(): lax.all_gather(vectors, 'front', axis=1, tiled=True)  155 us
    ppermute x12, waiting for transfers between devices, passed_along(): return lax.ppermute(block, axis, route)  37.6 us
    dot_general x10, matrix products, top_fold(): lax.dot_general(lax.all_gather(vectors, 'front', axis=1, tiled=True), inv...  35.8 us
    ppermute x12, starting transfers between devices, passed_along(): return lax.ppermute(block, axis, route)  34.3 us
    scatter-add x1, other arithmetic, body(): window_one.at[:, local_rows[panel_index].reshape(-1)]  25.6 us
    gather x2, local copies, waits for them, and re-layouts, lift_through(): jnp.take(window[0], flat_rows, axis=1)  20.3 us
    dot_general x3, matrix products, leaf_apply(): jnp.einsum('jab,sjb->sja', inverse_blocks, vectors, preferred_element_typ...  20.1 us
    unnamed x20, local copies, waits for them, and re-layouts  8.73 us
  transfers between devices with their start and end apart: 16, of which 11 were waited for; matrix products, arithmetic and copies ran while one was open for 3% of the time, Pallas kernels for 0%

commit v1 on v0

v1 whole, which is shorter than its diff:
```python
import functools

import jax
import jax.numpy as jnp
from jax import lax
from jax.experimental import pallas as pl
from jax.experimental.pallas import tpu as pltpu
from jax.sharding import PartitionSpec as P

WAVES = 2
F32 = jnp.float32
BF16 = jnp.bfloat16
VMEM = pl.BlockSpec(memory_space=pltpu.VMEM)
SMEM = pl.BlockSpec(memory_space=pltpu.SMEM)


def params(mib):
    return pltpu.CompilerParams(vmem_limit_bytes=mib * 1024 * 1024)


def rows_dot(left, right):
    return lax.dot_general(left, right, (((1,), (1,)), ((), ())), preferred_element_type=F32)


def group_of(leaf_count):
    return max(g for g in (4, 3, 2, 1) if leaf_count % g == 0)


def push_kernel(group, source_ref, inverse_ref, boundary_ref, rows_ref, out_ref):
    leaf_size = inverse_ref.shape[2]
    edge = boundary_ref.shape[1]
    window = out_ref.shape[1]

    @pl.when(pl.program_id(0) == 0)
    def _():
        out_ref[...] = jnp.zeros_like(out_ref)

    columns = jnp.transpose(rows_ref[0])
    places = lax.broadcasted_iota(jnp.int32, (edge, window), 1)
    pushed, picks = [], []
    for g in range(group):
        vectors = source_ref[:, g * leaf_size : (g + 1) * leaf_size]
        interior = rows_dot(vectors, inverse_ref[g]).astype(BF16)
        pushed.append(rows_dot(interior, boundary_ref[g]).astype(BF16))
        picks.append(jnp.where(columns[:, g : g + 1] == places, 1.0, 0.0).astype(BF16))
    out_ref[...] += jnp.dot(
        jnp.concatenate(pushed, axis=1), jnp.concatenate(picks, axis=0), preferred_element_type=F32
    )


def lift_kernel(group, window_ref, source_ref, inverse_ref, boundary_ref, rows_ref, out_ref):
    leaf_size = inverse_ref.shape[2]
    edge = boundary_ref.shape[1]
    window = window_ref.shape[1]
    places = lax.broadcasted_iota(jnp.int32, (window, edge), 0)
    picks = [
        jnp.where(rows_ref[0][g : g + 1, :] == places, 1.0, 0.0).astype(BF16) for g in range(group)
    ]
    picked = jnp.dot(
        window_ref[...], jnp.concatenate(picks, axis=1), preferred_element_type=F32
    ).astype(BF16)
    for g in range(group):
        lifted = jnp.dot(
            picked[:, g * edge : (g + 1) * edge], boundary_ref[g], preferred_element_type=F32
        )
        here = slice(g * leaf_size, (g + 1) * leaf_size)
        vectors = (source_ref[:, here].astype(F32) - lifted).astype(BF16)
        out_ref[:, here] = rows_dot(vectors, inverse_ref[g]).astype(BF16)


def fold_kernel(blocks, first, meta_ref, inverse_ref, *refs):
    base_refs = refs[:blocks]
    in_refs = () if first else refs[blocks : 2 * blocks]
    out_ref = refs[-1]
    wave_rows, rows = out_ref.shape
    here = pl.ds(pl.multiple_of(meta_ref[1] * wave_rows, wave_rows), wave_rows)
    forward = meta_ref[0] == 1
    fed = meta_ref[2] == 1
    total = jnp.zeros((wave_rows, rows), F32)
    for i in range(blocks):
        if first:
            vectors = base_refs[i][here, :]
        else:
            base = jnp.where(forward, base_refs[i][here, :].astype(F32), 0.0)
            vectors = (jnp.where(fed, in_refs[i][...].astype(F32), 0.0) + base).astype(BF16)
        place = pl.ds(pl.multiple_of(meta_ref[3 + i] * rows, rows), rows)
        total += jnp.dot(vectors, inverse_ref[place, :], preferred_element_type=F32)
    out_ref[...] = total.astype(BF16)


def join_kernel(meta_ref, mine_ref, other_ref, state_ref, scale_ref, next_ref, out_ref):
    wave_rows = mine_ref.shape[0]
    here = pl.ds(pl.multiple_of(meta_ref[1] * wave_rows, wave_rows), wave_rows)
    mode = meta_ref[0]
    solved = (mine_ref[...].astype(F32) + other_ref[...].astype(F32)).astype(BF16).astype(F32)
    older = state_ref[here, :].astype(F32)
    field = (solved + jnp.where(mode == 2, older, 0.0)).astype(BF16)
    scale = scale_ref[pl.ds(jnp.where(mode == 2, 1, 0), 1), :]
    out_ref[...] = (scale * field.astype(F32)).astype(BF16)
    next_ref[...] = state_ref[...]

    @pl.when(mode > 0)
    def _():
        next_ref[here, :] = field


def turn_routes(turn, panels, waves):
    at = [s if s < panels else 2 * (panels - 1) - s for s in range(2 * panels - 1)]
    pairs = []
    for wave in range(waves):
        step = turn - wave
        if 0 <= step < 2 * (panels - 1):
            pairs.append((at[step], at[step + 1]))
    sources = [a for a, _ in pairs]
    targets = [b for _, b in pairs]
    for panel in range(panels):
        if panel not in sources and panel not in targets:
            pairs.append((panel, panel))
    spare = [p for p in targets if p not in sources]
    unfed = [p for p in sources if p not in targets]
    return pairs + list(zip(spare, unfed))


def spread(values, panel_pairs, chips):
    half = chips // 2
    received = []
    for i in range(half):
        route = []
        for start, end in panel_pairs:
            for chip in range(chips):
                for core in range(2):
                    there = chip ^ (core * half + i)
                    route.append(
                        (2 * (start * chips + chip) + core, 2 * (end * chips + there) + core)
                    )
        received.append(lax.ppermute(values, ("panel", "front"), route))
    return received


def body(top_source, leaf_source, top_inverse, leaf_inverse, boundary, touch_rows, coupling):
    sources = top_source.shape[1]
    rows = top_source.shape[2]
    width = top_inverse.shape[2]
    leaf_count, leaf_size = leaf_inverse.shape[1:3]
    edge = boundary.shape[2]
    panels = lax.axis_size("panel")
    front = lax.axis_size("front")
    chips, half = front // 2, front // 4
    chip_rows = 2 * rows
    panel = lax.axis_index("panel")
    place = lax.axis_index("front")
    chip, core = place // 2, place % 2
    wave_rows = sources // WAVES
    group = group_of(leaf_count)
    steps = leaf_count // group

    swap_core = [(i, i ^ 1) for i in range(front)]
    swap_chip = [(i, i + 1) for i in range(1, front - 1, 2)]
    swap_chip = swap_chip + [(j, i) for i, j in swap_chip]

    own_half = (chip // half) ^ core
    kept = lax.dynamic_slice_in_dim(top_inverse[0], own_half * (width // 2), width // 2, 1)
    given = lax.dynamic_slice_in_dim(top_inverse[0], (1 - own_half) * (width // 2), width // 2, 1)
    taken = lax.ppermute(given, "front", swap_core)
    low = jnp.where(core == 0, kept, taken)
    high = jnp.where(core == 0, taken, kept)
    inverse = jnp.concatenate([low.T, high.T], axis=1)

    local_rows = touch_rows[0] - (place - 1) * rows
    grouped = local_rows.reshape(steps, group, edge)
    padded = jnp.concatenate([grouped, jnp.zeros((steps, 8 - group, edge), jnp.int32)], axis=1)
    leaf_specs = [
        pl.BlockSpec((sources, group * leaf_size), lambda i: (0, i)),
        pl.BlockSpec((group, leaf_size, leaf_size), lambda i: (i, 0, 0)),
        pl.BlockSpec((group, edge, leaf_size), lambda i: (i, 0, 0)),
        pl.BlockSpec((1, 8, edge), lambda i: (i, 0, 0)),
    ]
    leaf_args = (leaf_source[0], leaf_inverse[0], boundary[0], padded)
    windows = pl.pallas_call(
        functools.partial(push_kernel, group),
        grid=(steps,),
        out_shape=jax.ShapeDtypeStruct((sources, 3 * rows), F32),
        in_specs=leaf_specs,
        out_specs=pl.BlockSpec((sources, 3 * rows), lambda i: (0, 0)),
        compiler_params=params(40),
    )(*leaf_args)
    outward = jnp.where(core == 0, windows[:, :rows], windows[:, 2 * rows :]).astype(BF16)
    inward = lax.ppermute(outward, "front", swap_chip)
    chip_part = jnp.where(core == 0, windows[:, rows:], windows[:, :chip_rows])
    own_part = top_source[0].astype(F32) - inward.astype(F32)
    blank = jnp.zeros_like(own_part)
    own_part = jnp.where(
        core == 0,
        jnp.concatenate([own_part, blank], axis=1),
        jnp.concatenate([blank, own_part], axis=1),
    )
    partial = (own_part - chip_part).astype(BF16)
    partner = lax.ppermute(partial, "front", swap_core)
    known = (partial.astype(F32) + partner.astype(F32)).astype(BF16)
    base = spread(known, [(p, p) for p in range(panels)], chips)

    mine = coupling
    later = lax.ppermute(mine, "panel", [((p + 1) % panels, p) for p in range(panels)])
    forward_scale = jnp.where(panel == panels - 1, mine, later)
    scales = jnp.concatenate([forward_scale, mine], axis=0)
    partner_scales = lax.ppermute(scales, "front", swap_core)
    scales = jnp.where(
        core == 0,
        jnp.concatenate([scales, partner_scales], axis=1),
        jnp.concatenate([partner_scales, scales], axis=1),
    )
    offsets = [(chip % half) ^ i for i in range(half)]
    state = jnp.zeros((sources, chip_rows), BF16)
    turns = 2 * (panels - 1) + WAVES
    arrived = []
    for turn in range(turns):
        up_wave = turn - panel
        down_wave = turn - (2 * (panels - 1) - panel)
        up = (up_wave >= 0) & (up_wave < WAVES)
        down = (down_wave >= 0) & (down_wave < WAVES) & (panel < panels - 1)
        mode = jnp.where(up, 1, jnp.where(down, 2, 0))
        wave = jnp.where(up, up_wave, jnp.where(down, down_wave, 0))
        fed = jnp.where((panel == 0) & up, 0, 1)
        meta = jnp.stack([mode, wave, fed] + offsets).astype(jnp.int32)
        first = turn == 0
        share = pl.pallas_call(
            functools.partial(fold_kernel, half, first),
            out_shape=jax.ShapeDtypeStruct((wave_rows, chip_rows), BF16),
            in_specs=[SMEM] + [VMEM] * (1 + half + len(arrived)),
            out_specs=VMEM,
            compiler_params=params(32),
        )(meta, inverse, *base, *arrived)
        other = lax.ppermute(share, "front", swap_core)
        state, outgoing = pl.pallas_call(
            join_kernel,
            out_shape=(
                jax.ShapeDtypeStruct((sources, chip_rows), BF16),
                jax.ShapeDtypeStruct((wave_rows, chip_rows), BF16),
            ),
            in_specs=[SMEM] + [VMEM] * 4,
            out_specs=(VMEM, VMEM),
            compiler_params=params(32),
        )(meta, share, other, state, scales)
        if turn < turns - 1:
            arrived = spread(outgoing, turn_routes(turn, panels, WAVES), chips)

    top_field = jnp.where(core == 0, state[:, :rows], state[:, rows:])
    beside = lax.ppermute(top_field, "front", swap_chip)
    window = jnp.where(
        core == 0,
        jnp.concatenate([beside, state], axis=1),
        jnp.concatenate([state, beside], axis=1),
    )
    leaf_field = pl.pallas_call(
        functools.partial(lift_kernel, group),
        grid=(steps,),
        out_shape=jax.ShapeDtypeStruct((sources, leaf_count * leaf_size), BF16),
        in_specs=[pl.BlockSpec((sources, 3 * rows), lambda i: (0, 0))] + leaf_specs,
        out_specs=pl.BlockSpec((sources, group * leaf_size), lambda i: (0, i)),
        compiler_params=params(40),
    )(window, *leaf_args)
    return (top_field[None], leaf_field[None])


def solution(mesh):
    placed = (
        P("panel", None, "front"),
        P("panel", None, "front"),
        P("panel", "front", None),
        P("panel", "front", None, None),
        P("panel", "front", None, None),
        P("panel", "front", None),
        P("panel", "front"),
    )
    return jax.shard_map(
        body,
        mesh=mesh,
        in_specs=placed,
        out_specs=(P("panel", None, "front"), P("panel", None, "front")),
        check_vma=False,
    )
```

time: 372 us -> 201 us (0.54)
  blocking collectives: 155 us -> 0 us
  matrix products: 58.1 us -> 0 us
  Pallas kernels: 0 us -> 40.7 us
  other arithmetic: 38.5 us -> 4.23 us
  waiting for transfers between devices: 37.7 us -> 60.6 us
  starting transfers between devices: 46 us -> 60.5 us
    all_gather x10 -> x0, blocking collectives: 155 us -> none  [top_fold(): lax.all_gather(vectors, 'front', axis=1, tiled=True)]
    dot_general x14 -> x0, matrix products: 58.1 us -> none  [the longest x10 35.8 us: top_fold(): lax.dot_general(lax.all_gather(vectors, 'front', axis=1, tiled=True), inv...]
    pallas_call x0 -> x18, Pallas kernels: none -> 40.7 us  [the longest x1 11.2 us: body(): pl.pallas_call(functools.partial(push_kernel, group), grid=(steps,), out_...]
    scatter-add x1 -> x0, other arithmetic: 25.6 us -> none  [body(): window_one.at[:, local_rows[panel_index].reshape(-1)]]
    ppermute x16 -> x30, waiting for transfers between devices: 37.7 us -> 60.6 us  [the longest x16 44.8 us: spread(): received.append(lax.ppermute(values, ('panel', 'front'), route))]
    gather x2 -> x0, local copies, waits for them, and re-layouts: 20.3 us -> none  [lift_through(): jnp.take(window[0], flat_rows, axis=1)]
    ppermute x16 -> x30, starting transfers between devices: 46 us -> 60.5 us  [the longest x16 48.1 us: spread(): received.append(lax.ppermute(values, ('panel', 'front'), route))]
    dynamic_slice x0 -> x3, local copies, waits for them, and re-layouts: none -> 12.8 us  [the longest x2 8.78 us: body(): lax.dynamic_slice_in_dim(top_inverse[0], own_half * (width // 2), width /...]
  transfers between devices with their start and end apart: 16 -> 30, of which waited for: 11 -> 26; matrix products, arithmetic and copies ran while one was open for 3% -> 4% of each run, Pallas kernels for 0% -> 6%
where the time goes in v1:
time: 201 us; the launch traced here: 200 us
  waiting for transfers between devices  60.6 us (30%)
  starting transfers between devices  60.5 us (30%)
  Pallas kernels  40.7 us (20%)
  local copies, waits for them, and re-layouts  32.9 us (16%)
  other arithmetic  4.23 us (2%)
    ppermute x16, starting transfers between devices, spread(): received.append(lax.ppermute(values, ('panel', 'front'), route))  48.1 us
    ppermute x16, waiting for transfers between devices, spread(): received.append(lax.ppermute(values, ('panel', 'front'), route))  44.8 us
    unnamed x32, local copies, waits for them, and re-layouts  19.3 us
    pallas_call x1, Pallas kernels, body(): pl.pallas_call(functools.partial(push_kernel, group), grid=(steps,), out_...  11.2 us
    pallas_call x8, Pallas kernels, body(): pl.pallas_call(functools.partial(fold_kernel, half, first), out_shape=jax...  11.1 us
    pallas_call x8, Pallas kernels, body(): pl.pallas_call(join_kernel, out_shape=(jax.ShapeDtypeStruct((sources, chi...  10.4 us
    dynamic_slice x2, local copies, waits for them, and re-layouts, body(): lax.dynamic_slice_in_dim(top_inverse[0], own_half * (width // 2), width /...  8.78 us
    ppermute x8, waiting for transfers between devices, body(): other = lax.ppermute(share, 'front', swap_core)  8.65 us
  transfers between devices with their start and end apart: 30, of which 26 were waited for; matrix products, arithmetic and copies ran while one was open for 4% of the time, Pallas kernels for 6%

profile of v1, /device:TPU:1, one launch (start us, length us, event | category | flops | bytes accessed | tf_op | source)
XLA Modules:
  0.0 200.1 jit_solution(8572095191089100699)
XLA Ops:
  0.7 4.9 %constant_dynamic-slice_fusion.1 = (bf16[1,512,2048]{2,1,0:T(8,128)(2,1)}, bf16[1,512,2048]{2,1,0:T(8,128)(2,1)}) fusion(bf16[1,512,4096]{2,1,0:T(8,128)(2,1)} %param.9, s32[]{:T(128)S(6)} %select_n.222, s32[]{:T(128)S(6)} %select_n.223), kind=kLoop, calls=%fused_computation.19 | loop fusion | bytes 8388616 | tf_op jit(solution)/shard_map/dynamic_slice | solution.py:162
  5.6 4.1 %copy.10 = bf16[1,512,2048]{1,2,0:T(8,128)(2,1)} copy(bf16[1,512,2048]{2,1,0:T(8,128)(2,1)} %get-tuple-element.35) | data formatting | bytes 4194304 | tf_op jit(solution)/shard_map/dynamic_slice | solution.py:163
  9.7 2.3 %copy-done.8 = bf16[1,36,256,256]{3,2,1,0:T(8,128)(2,1)S(1)} copy-done((bf16[1,36,256,256]{3,2,1,0:T(8,128)(2,1)S(1)}, bf16[1,36,256,256]{3,2,1,0:T(8,128)(2,1)}, u32[]{:S(2)}) %copy-start.8) | copy-done | bytes 4718616
  13.7 11.2 %shard_map.86 = f32[128,1536]{1,0:T(8,128)S(1)} custom-call(bf16[128,9216]{1,0:T(8,128)(2,1)S(1)} %bitcast.50, bf16[36,256,256]{2,1,0:T(8,128)(2,1)S(1)} %bitcast.48, bf16[36,128,256]{2,1,0:T(8,128)(2,1)S(1)} %bitcast.52, s32[9,8,128]{2,1,0:T(8,128)S(1)} %concatenate.28.rows_ref), custom_call_target="tpu_custom_call" | custom-call | tf_op jit(solution)/shard_map/pallas_call | solution.py:179
  25.0 4.5 %collective-permute-start.1 = (bf16[128,512]{1,0:T(8,128)(2,1)S(1)}, bf16[128,512]{1,0:T(8,128)(2,1)S(1)}, u32[]{:S(2)}, u32[]{:S(2)}) collective-permute-start(bf16[128,512]{1,0:T(8,128)(2,1)S(1)} %fusion.4), channel_id=1, source_target_pairs={{1,2},{3,4},{5,6},{2,1},{4,3},{6,5},{9,10},{11,12},{13,14},{10,9},... | collective-permute-start | bytes 393224 | tf_op jit(solution)/shard_map/ppermute | solution.py:188
  29.5 2.6 %collective-permute-done.1 = bf16[128,512]{1,0:T(8,128)(2,1)S(1)} collective-permute-done((bf16[128,512]{1,0:T(8,128)(2,1)S(1)}, bf16[128,512]{1,0:T(8,128)(2,1)S(1)}, u32[]{:S(2)}, u32[]{:S(2)}) %collective-permute-start.1) | collective-permute-done | bytes 131104 | tf_op jit(solution)/shard_map/ppermute | solution.py:188
  32.4 2.8 %collective-permute-start.6 = (f32[1,512]{1,0:T(1,128)S(1)}, f32[1,512]{1,0:T(1,128)S(1)}, u32[]{:S(2)}, u32[]{:S(2)}) collective-permute-start(f32[1,512]{1,0:T(1,128)S(1)} %copy-done.15), channel_id=1, source_target_pairs={{8,0},{16,8},{24,16},{0,24},{9,1},{17,9},{25,17},{1,25},{10,2},{18... | collective-permute-start | bytes 6152 | tf_op jit(solution)/shard_map/ppermute | solution.py:203
  35.2 3.9 %copy.9 = bf16[1,512,2048]{1,2,0:T(8,128)(2,1)} copy(bf16[1,512,2048]{2,1,0:T(8,128)(2,1)} %get-tuple-element.34) | data formatting | bytes 4194304 | tf_op jit(solution)/shard_map/dynamic_slice | solution.py:162
  39.3 4.2 %collective-permute-start.3 = (bf16[128,1024]{1,0:T(8,128)(2,1)S(1)}, bf16[128,1024]{1,0:T(8,128)(2,1)S(1)}, u32[]{:S(2)}, u32[]{:S(2)}) collective-permute-start(bf16[128,1024]{1,0:T(8,128)(2,1)S(1)} %add_convert_fusion), channel_id=1, source_target_pairs={{0,0},{1,5},{2,2},{3,7},{4,4},{5,1},{6,6},{7,3},{8,8},{9,13},{10,1... | collective-permute-start | bytes 786440 | tf_op jit(solution)/shard_map/ppermute | solution.py:136
  44.6 2.5 %fusion = (bf16[2048,512]{1,0:T(8,128)(2,1)S(1)}, bf16[2048,512]{1,0:T(8,128)(2,1)S(1)}) fusion(bf16[512,2048]{0,1:T(8,128)(2,1)} %collective-permute-done, bf16[1,512,2048]{1,2,0:T(8,128)(2,1)} %copy.9, pred[]{:T(512)S(6)} %eq.10), kind=kLoop, calls=%fused_computation.3 | loop fusion | flops 2097152 | bytes 8388609 | tf_op jit(solution)/shard_map/transpose | solution.py:167
  49.3 4.6 %collective-permute-done.4.refs_1_ = bf16[128,1024]{1,0:T(8,128)(2,1)S(1)} collective-permute-done((bf16[128,1024]{1,0:T(8,128)(2,1)S(1)}, bf16[128,1024]{1,0:T(8,128)(2,1)S(1)}, u32[]{:S(2)}, u32[]{:S(2)}) %collective-permute-start.4) | collective-permute-done | bytes 262176 | tf_op jit(solution)/shard_map/ppermute | solution.py:136
  58.2 5.0 %collective-permute-start.8 = (bf16[64,1024]{1,0:T(8,128)(2,1)}, bf16[64,1024]{1,0:T(8,128)(2,1)S(1)}, u32[]{:S(2)}, u32[]{:S(2)}) collective-permute-start(bf16[64,1024]{1,0:T(8,128)(2,1)} %get-tuple-element.17), channel_id=1, source_target_pairs={{0,8},{1,13},{2,10},{3,15},{4,12},{5,9},{6,14},{7,11},{16,16},{17,... | collective-permute-start | bytes 393224 | tf_op jit(solution)/shard_map/ppermute | solution.py:136
  63.2 2.4 %collective-permute-start.9 = (bf16[64,1024]{1,0:T(8,128)(2,1)}, bf16[64,1024]{1,0:T(8,128)(2,1)S(1)}, u32[]{:S(2)}, u32[]{:S(2)}) collective-permute-start(bf16[64,1024]{1,0:T(8,128)(2,1)} %get-tuple-element.17), channel_id=1, source_target_pairs={{0,10},{1,15},{2,8},{3,13},{4,14},{5,11},{6,12},{7,9},{16,18},{17,... | collective-permute-start | bytes 393224 | tf_op jit(solution)/shard_map/ppermute | solution.py:136
  66.0 5.1 %collective-permute-done.9.refs_3_ = bf16[64,1024]{1,0:T(8,128)(2,1)S(1)} collective-permute-done((bf16[64,1024]{1,0:T(8,128)(2,1)}, bf16[64,1024]{1,0:T(8,128)(2,1)S(1)}, u32[]{:S(2)}, u32[]{:S(2)}) %collective-permute-start.9) | collective-permute-done | bytes 131104 | tf_op jit(solution)/shard_map/ppermute | solution.py:136
  77.4 3.8 %collective-permute-start.11 = (bf16[64,1024]{1,0:T(8,128)(2,1)}, bf16[64,1024]{1,0:T(8,128)(2,1)S(1)}, u32[]{:S(2)}, u32[]{:S(2)}) collective-permute-start(bf16[64,1024]{1,0:T(8,128)(2,1)} %get-tuple-element.19), channel_id=1, source_target_pairs={{8,16},{9,21},{10,18},{11,23},{12,20},{13,17},{14,22},{15,19},{0,8... | collective-permute-start | bytes 393224 | tf_op jit(solution)/shard_map/ppermute | solution.py:136
  82.5 4.1 %collective-permute-done.11.refs_2_ = bf16[64,1024]{1,0:T(8,128)(2,1)S(1)} collective-permute-done((bf16[64,1024]{1,0:T(8,128)(2,1)}, bf16[64,1024]{1,0:T(8,128)(2,1)S(1)}, u32[]{:S(2)}, u32[]{:S(2)}) %collective-permute-start.11) | collective-permute-done | bytes 131104 | tf_op jit(solution)/shard_map/ppermute | solution.py:136
  95.7 3.8 %collective-permute-start.14 = (bf16[64,1024]{1,0:T(8,128)(2,1)}, bf16[64,1024]{1,0:T(8,128)(2,1)S(1)}, u32[]{:S(2)}, u32[]{:S(2)}) collective-permute-start(bf16[64,1024]{1,0:T(8,128)(2,1)} %get-tuple-element.21), channel_id=1, source_target_pairs={{16,24},{17,29},{18,26},{19,31},{20,28},{21,25},{22,30},{23,27},{8... | collective-permute-start | bytes 393224 | tf_op jit(solution)/shard_map/ppermute | solution.py:136
  100.0 3.8 %collective-permute-done.14.refs_2_ = bf16[64,1024]{1,0:T(8,128)(2,1)S(1)} collective-permute-done((bf16[64,1024]{1,0:T(8,128)(2,1)}, bf16[64,1024]{1,0:T(8,128)(2,1)S(1)}, u32[]{:S(2)}, u32[]{:S(2)}) %collective-permute-start.14) | collective-permute-done | bytes 131104 | tf_op jit(solution)/shard_map/ppermute | solution.py:136
  105.5 2.2 %copy-done.3 = bf16[2048,1024]{1,0:T(8,128)(2,1)S(1)} copy-done((bf16[2048,1024]{1,0:T(8,128)(2,1)S(1)}, bf16[2048,1024]{1,0:T(8,128)(2,1)}, u32[]{:S(2)}) %copy-start.3) | copy-done | bytes 4194328
  111.8 4.0 %collective-permute-start.17 = (bf16[64,1024]{1,0:T(8,128)(2,1)}, bf16[64,1024]{1,0:T(8,128)(2,1)S(1)}, u32[]{:S(2)}, u32[]{:S(2)}) collective-permute-start(bf16[64,1024]{1,0:T(8,128)(2,1)} %get-tuple-element.23), channel_id=1, source_target_pairs={{24,16},{25,21},{26,18},{27,23},{28,20},{29,17},{30,22},{31,19},{1... | collective-permute-start | bytes 393224 | tf_op jit(solution)/shard_map/ppermute | solution.py:136
  119.0 3.6 %collective-permute-done.18.refs_3_ = bf16[64,1024]{1,0:T(8,128)(2,1)S(1)} collective-permute-done((bf16[64,1024]{1,0:T(8,128)(2,1)}, bf16[64,1024]{1,0:T(8,128)(2,1)S(1)}, u32[]{:S(2)}, u32[]{:S(2)}) %collective-permute-start.18) | collective-permute-done | bytes 131104 | tf_op jit(solution)/shard_map/ppermute | solution.py:136
  122.6 2.2 %copy-done.4 = bf16[2048,1024]{1,0:T(8,128)(2,1)S(1)} copy-done((bf16[2048,1024]{1,0:T(8,128)(2,1)S(1)}, bf16[2048,1024]{1,0:T(8,128)(2,1)}, u32[]{:S(2)}) %copy-start.4) | copy-done | bytes 4194328
  128.9 2.9 %collective-permute-start.20 = (bf16[64,1024]{1,0:T(8,128)(2,1)}, bf16[64,1024]{1,0:T(8,128)(2,1)S(1)}, u32[]{:S(2)}, u32[]{:S(2)}) collective-permute-start(bf16[64,1024]{1,0:T(8,128)(2,1)} %get-tuple-element.25), channel_id=1, source_target_pairs={{16,8},{17,13},{18,10},{19,15},{20,12},{21,9},{22,14},{23,11},{24,... | collective-permute-start | bytes 393224 | tf_op jit(solution)/shard_map/ppermute | solution.py:136
  133.5 3.3 %collective-permute-done.20.refs_2_ = bf16[64,1024]{1,0:T(8,128)(2,1)S(1)} collective-permute-done((bf16[64,1024]{1,0:T(8,128)(2,1)}, bf16[64,1024]{1,0:T(8,128)(2,1)S(1)}, u32[]{:S(2)}, u32[]{:S(2)}) %collective-permute-start.20) | collective-permute-done | bytes 131104 | tf_op jit(solution)/shard_map/ppermute | solution.py:136
  145.0 8.0 %collective-permute-start.23 = (bf16[64,1024]{1,0:T(8,128)(2,1)}, bf16[64,1024]{1,0:T(8,128)(2,1)S(1)}, u32[]{:S(2)}, u32[]{:S(2)}) collective-permute-start(bf16[64,1024]{1,0:T(8,128)(2,1)} %get-tuple-element.27), channel_id=1, source_target_pairs={{8,0},{9,5},{10,2},{11,7},{12,4},{13,1},{14,6},{15,3},{16,8},{17,1... | collective-permute-start | bytes 393224 | tf_op jit(solution)/shard_map/ppermute | solution.py:136
  152.9 2.7 %collective-permute-start.24 = (bf16[64,1024]{1,0:T(8,128)(2,1)}, bf16[64,1024]{1,0:T(8,128)(2,1)S(1)}, u32[]{:S(2)}, u32[]{:S(2)}) collective-permute-start(bf16[64,1024]{1,0:T(8,128)(2,1)} %get-tuple-element.27), channel_id=1, source_target_pairs={{8,2},{9,7},{10,0},{11,5},{12,6},{13,3},{14,4},{15,1},{16,10},{17,... | collective-permute-start | bytes 393224 | tf_op jit(solution)/shard_map/ppermute | solution.py:136
  156.8 3.4 %collective-permute-done.24.refs_3_ = bf16[64,1024]{1,0:T(8,128)(2,1)S(1)} collective-permute-done((bf16[64,1024]{1,0:T(8,128)(2,1)}, bf16[64,1024]{1,0:T(8,128)(2,1)S(1)}, u32[]{:S(2)}, u32[]{:S(2)}) %collective-permute-start.24) | collective-permute-done | bytes 131104 | tf_op jit(solution)/shard_map/ppermute | solution.py:136
  167.0 5.0 %collective-permute-start.26 = (bf16[64,1024]{1,0:T(8,128)(2,1)}, bf16[64,1024]{1,0:T(8,128)(2,1)S(1)}, u32[]{:S(2)}, u32[]{:S(2)}) collective-permute-start(bf16[64,1024]{1,0:T(8,128)(2,1)} %get-tuple-element.29), channel_id=1, source_target_pairs={{8,0},{9,5},{10,2},{11,7},{12,4},{13,1},{14,6},{15,3},{16,16},{17,... | collective-permute-start | bytes 393224 | tf_op jit(solution)/shard_map/ppermute | solution.py:136
  172.6 3.7 %collective-permute-done.26.refs_2_ = bf16[64,1024]{1,0:T(8,128)(2,1)S(1)} collective-permute-done((bf16[64,1024]{1,0:T(8,128)(2,1)}, bf16[64,1024]{1,0:T(8,128)(2,1)S(1)}, u32[]{:S(2)}, u32[]{:S(2)}) %collective-permute-start.26) | collective-permute-done | bytes 131104 | tf_op jit(solution)/shard_map/ppermute | solution.py:136
  176.2 3.0 %collective-permute-done.27.refs_3_ = bf16[64,1024]{1,0:T(8,128)(2,1)S(1)} collective-permute-done((bf16[64,1024]{1,0:T(8,128)(2,1)}, bf16[64,1024]{1,0:T(8,128)(2,1)S(1)}, u32[]{:S(2)}, u32[]{:S(2)}) %collective-permute-start.27) | collective-permute-done | bytes 131104 | tf_op jit(solution)/shard_map/ppermute | solution.py:136
  188.2 3.7 %collective-permute-done.29 = bf16[128,512]{1,0:T(8,128)(2,1)S(1)} collective-permute-done((bf16[128,512]{1,0:T(8,128)(2,1)S(1)}, bf16[128,512]{1,0:T(8,128)(2,1)S(1)}, u32[]{:S(2)}, u32[]{:S(2)}) %collective-permute-start.29) | collective-permute-done | bytes 131104 | tf_op jit(solution)/shard_map/ppermute | solution.py:248
  192.0 8.1 %shard_map.103 = bf16[128,9216]{1,0:T(8,128)(2,1)} custom-call(bf16[128,1536]{1,0:T(8,128)(2,1)S(1)} %maximum_select_fusion.window_ref, bf16[128,9216]{1,0:T(8,128)(2,1)S(1)} %bitcast.51, bf16[36,256,256]{2,1,0:T(8,128)(2,1)S(1)} %bitcast.49, bf16[36,128,256]{2,1,0:T(8,128)(2,1)S(1)} %bitcast.53, s32[9,8,128]{2,1,0:T(8,128)S(1)} %concatenate.28.rows_ref), custom_call_target="tpu_custom_call" | custom-call | tf_op jit(solution)/shard_map/pallas_call | solution.py:254
  (104 shorter events, 67.7 us)
Async XLA Ops:
  9.6 35.0 %collective-permute-start = (bf16[512,2048]{0,1:T(8,128)(2,1)}, bf16[512,2048]{0,1:T(8,128)(2,1)}, u32[]{:S(2)}, u32[]{:S(2)}) collective-permute-start(bf16[512,2048]{0,1:T(8,128)(2,1)} %bitcast.55), channel_id=1, source_target_pairs={{0,1},{1,0},{2,3},{3,2},{4,5},{5,4},{6,7},{7,6},{8,9},{9,8},{10,11... | collective-permute-start | bytes 6291464 | tf_op jit(solution)/shard_map/ppermute | solution.py:164
  13.7 18.4 %copy-start.13 = (bf16[1,128,512]{2,1,0:T(8,128)(2,1)S(1)}, bf16[1,128,512]{2,1,0:T(8,128)(2,1)}, u32[]{:S(2)}) copy-start(bf16[1,128,512]{2,1,0:T(8,128)(2,1)} %param.7) | copy-start | bytes 393220
  25.0 7.2 %collective-permute-start.1 = (bf16[128,512]{1,0:T(8,128)(2,1)S(1)}, bf16[128,512]{1,0:T(8,128)(2,1)S(1)}, u32[]{:S(2)}, u32[]{:S(2)}) collective-permute-start(bf16[128,512]{1,0:T(8,128)(2,1)S(1)} %fusion.4), channel_id=1, source_target_pairs={{1,2},{3,4},{5,6},{2,1},{4,3},{6,5},{9,10},{11,12},{13,14},{10,9},... | collective-permute-start | bytes 393224 | tf_op jit(solution)/shard_map/ppermute | solution.py:188
  32.3 6.9 %collective-permute-start.2 = (bf16[128,1024]{1,0:T(8,128)(2,1)S(1)}, bf16[128,1024]{1,0:T(8,128)(2,1)S(1)}, u32[]{:S(2)}, u32[]{:S(2)}) collective-permute-start(bf16[128,1024]{1,0:T(8,128)(2,1)S(1)} %fusion.3), channel_id=1, source_target_pairs={{0,1},{1,0},{2,3},{3,2},{4,5},{5,4},{6,7},{7,6},{8,9},{9,8},{10,11... | collective-permute-start | bytes 786440 | tf_op jit(solution)/shard_map/ppermute | solution.py:198
  32.4 6.8 %collective-permute-start.6 = (f32[1,512]{1,0:T(1,128)S(1)}, f32[1,512]{1,0:T(1,128)S(1)}, u32[]{:S(2)}, u32[]{:S(2)}) collective-permute-start(f32[1,512]{1,0:T(1,128)S(1)} %copy-done.15), channel_id=1, source_target_pairs={{8,0},{16,8},{24,16},{0,24},{9,1},{17,9},{25,17},{1,25},{10,2},{18... | collective-permute-start | bytes 6152 | tf_op jit(solution)/shard_map/ppermute | solution.py:203
  39.3 10.1 %collective-permute-start.3 = (bf16[128,1024]{1,0:T(8,128)(2,1)S(1)}, bf16[128,1024]{1,0:T(8,128)(2,1)S(1)}, u32[]{:S(2)}, u32[]{:S(2)}) collective-permute-start(bf16[128,1024]{1,0:T(8,128)(2,1)S(1)} %add_convert_fusion), channel_id=1, source_target_pairs={{0,0},{1,5},{2,2},{3,7},{4,4},{5,1},{6,6},{7,3},{8,8},{9,13},{10,1... | collective-permute-start | bytes 786440 | tf_op jit(solution)/shard_map/ppermute | solution.py:136
  43.5 10.5 %collective-permute-start.4 = (bf16[128,1024]{1,0:T(8,128)(2,1)S(1)}, bf16[128,1024]{1,0:T(8,128)(2,1)S(1)}, u32[]{:S(2)}, u32[]{:S(2)}) collective-permute-start(bf16[128,1024]{1,0:T(8,128)(2,1)S(1)} %add_convert_fusion), channel_id=1, source_target_pairs={{0,2},{1,7},{2,0},{3,5},{4,6},{5,3},{6,4},{7,1},{8,10},{9,15},{10,... | collective-permute-start | bytes 786440 | tf_op jit(solution)/shard_map/ppermute | solution.py:136
  55.4 1.5 collective-permute-start.5
  55.5 1.4 collective-permute-start.7
  58.2 7.8 %collective-permute-start.8 = (bf16[64,1024]{1,0:T(8,128)(2,1)}, bf16[64,1024]{1,0:T(8,128)(2,1)S(1)}, u32[]{:S(2)}, u32[]{:S(2)}) collective-permute-start(bf16[64,1024]{1,0:T(8,128)(2,1)} %get-tuple-element.17), channel_id=1, source_target_pairs={{0,8},{1,13},{2,10},{3,15},{4,12},{5,9},{6,14},{7,11},{16,16},{17,... | collective-permute-start | bytes 393224 | tf_op jit(solution)/shard_map/ppermute | solution.py:136
  63.2 7.9 %collective-permute-start.9 = (bf16[64,1024]{1,0:T(8,128)(2,1)}, bf16[64,1024]{1,0:T(8,128)(2,1)S(1)}, u32[]{:S(2)}, u32[]{:S(2)}) collective-permute-start(bf16[64,1024]{1,0:T(8,128)(2,1)} %get-tuple-element.17), channel_id=1, source_target_pairs={{0,10},{1,15},{2,8},{3,13},{4,14},{5,11},{6,12},{7,9},{16,18},{17,... | collective-permute-start | bytes 393224 | tf_op jit(solution)/shard_map/ppermute | solution.py:136
  74.7 1.4 collective-permute-start.10
  77.4 9.2 %collective-permute-start.11 = (bf16[64,1024]{1,0:T(8,128)(2,1)}, bf16[64,1024]{1,0:T(8,128)(2,1)S(1)}, u32[]{:S(2)}, u32[]{:S(2)}) collective-permute-start(bf16[64,1024]{1,0:T(8,128)(2,1)} %get-tuple-element.19), channel_id=1, source_target_pairs={{8,16},{9,21},{10,18},{11,23},{12,20},{13,17},{14,22},{15,19},{0,8... | collective-permute-start | bytes 393224 | tf_op jit(solution)/shard_map/ppermute | solution.py:136
  81.2 7.5 %collective-permute-start.12 = (bf16[64,1024]{1,0:T(8,128)(2,1)}, bf16[64,1024]{1,0:T(8,128)(2,1)S(1)}, u32[]{:S(2)}, u32[]{:S(2)}) collective-permute-start(bf16[64,1024]{1,0:T(8,128)(2,1)} %get-tuple-element.19), channel_id=1, source_target_pairs={{8,18},{9,23},{10,16},{11,21},{12,22},{13,19},{14,20},{15,17},{0,1... | collective-permute-start | bytes 393224 | tf_op jit(solution)/shard_map/ppermute | solution.py:136
  92.2 2.1 %collective-permute-start.13 = (bf16[64,1024]{1,0:T(8,128)(2,1)S(1)}, bf16[64,1024]{1,0:T(8,128)(2,1)S(1)}, u32[]{:S(2)}, u32[]{:S(2)}) collective-permute-start(bf16[64,1024]{1,0:T(8,128)(2,1)S(1)} %shard_map.91.mine_ref), channel_id=1, source_target_pairs={{0,1},{1,0},{2,3},{3,2},{4,5},{5,4},{6,7},{7,6},{8,9},{9,8},{10,11... | collective-permute-start | bytes 393224 | tf_op jit(solution)/shard_map/ppermute | solution.py:233
  95.7 8.1 %collective-permute-start.14 = (bf16[64,1024]{1,0:T(8,128)(2,1)}, bf16[64,1024]{1,0:T(8,128)(2,1)S(1)}, u32[]{:S(2)}, u32[]{:S(2)}) collective-permute-start(bf16[64,1024]{1,0:T(8,128)(2,1)} %get-tuple-element.21), channel_id=1, source_target_pairs={{16,24},{17,29},{18,26},{19,31},{20,28},{21,25},{22,30},{23,27},{8... | collective-permute-start | bytes 393224 | tf_op jit(solution)/shard_map/ppermute | solution.py:136
  99.5 6.0 %collective-permute-start.15 = (bf16[64,1024]{1,0:T(8,128)(2,1)}, bf16[64,1024]{1,0:T(8,128)(2,1)S(1)}, u32[]{:S(2)}, u32[]{:S(2)}) collective-permute-start(bf16[64,1024]{1,0:T(8,128)(2,1)} %get-tuple-element.21), channel_id=1, source_target_pairs={{16,26},{17,31},{18,24},{19,29},{20,30},{21,27},{22,28},{23,25},{8... | collective-permute-start | bytes 393224 | tf_op jit(solution)/shard_map/ppermute | solution.py:136
  109.1 1.4 collective-permute-start.16
  111.8 7.2 %collective-permute-start.17 = (bf16[64,1024]{1,0:T(8,128)(2,1)}, bf16[64,1024]{1,0:T(8,128)(2,1)S(1)}, u32[]{:S(2)}, u32[]{:S(2)}) collective-permute-start(bf16[64,1024]{1,0:T(8,128)(2,1)} %get-tuple-element.23), channel_id=1, source_target_pairs={{24,16},{25,21},{26,18},{27,23},{28,20},{29,17},{30,22},{31,19},{1... | collective-permute-start | bytes 393224 | tf_op jit(solution)/shard_map/ppermute | solution.py:136
  115.8 6.8 %collective-permute-start.18 = (bf16[64,1024]{1,0:T(8,128)(2,1)}, bf16[64,1024]{1,0:T(8,128)(2,1)S(1)}, u32[]{:S(2)}, u32[]{:S(2)}) collective-permute-start(bf16[64,1024]{1,0:T(8,128)(2,1)} %get-tuple-element.23), channel_id=1, source_target_pairs={{24,18},{25,23},{26,16},{27,21},{28,22},{29,19},{30,20},{31,17},{1... | collective-permute-start | bytes 393224 | tf_op jit(solution)/shard_map/ppermute | solution.py:136
  126.2 1.4 collective-permute-start.19
  128.9 8.0 %collective-permute-start.20 = (bf16[64,1024]{1,0:T(8,128)(2,1)}, bf16[64,1024]{1,0:T(8,128)(2,1)S(1)}, u32[]{:S(2)}, u32[]{:S(2)}) collective-permute-start(bf16[64,1024]{1,0:T(8,128)(2,1)} %get-tuple-element.25), channel_id=1, source_target_pairs={{16,8},{17,13},{18,10},{19,15},{20,12},{21,9},{22,14},{23,11},{24,... | collective-permute-start | bytes 393224 | tf_op jit(solution)/shard_map/ppermute | solution.py:136
  131.8 6.9 %collective-permute-start.21 = (bf16[64,1024]{1,0:T(8,128)(2,1)}, bf16[64,1024]{1,0:T(8,128)(2,1)S(1)}, u32[]{:S(2)}, u32[]{:S(2)}) collective-permute-start(bf16[64,1024]{1,0:T(8,128)(2,1)} %get-tuple-element.25), channel_id=1, source_target_pairs={{16,10},{17,15},{18,8},{19,13},{20,14},{21,11},{22,12},{23,9},{24,... | collective-permute-start | bytes 393224 | tf_op jit(solution)/shard_map/ppermute | solution.py:136
  142.3 1.4 collective-permute-start.22
  145.0 11.9 %collective-permute-start.23 = (bf16[64,1024]{1,0:T(8,128)(2,1)}, bf16[64,1024]{1,0:T(8,128)(2,1)S(1)}, u32[]{:S(2)}, u32[]{:S(2)}) collective-permute-start(bf16[64,1024]{1,0:T(8,128)(2,1)} %get-tuple-element.27), channel_id=1, source_target_pairs={{8,0},{9,5},{10,2},{11,7},{12,4},{13,1},{14,6},{15,3},{16,8},{17,1... | collective-permute-start | bytes 393224 | tf_op jit(solution)/shard_map/ppermute | solution.py:136
  152.9 7.3 %collective-permute-start.24 = (bf16[64,1024]{1,0:T(8,128)(2,1)}, bf16[64,1024]{1,0:T(8,128)(2,1)S(1)}, u32[]{:S(2)}, u32[]{:S(2)}) collective-permute-start(bf16[64,1024]{1,0:T(8,128)(2,1)} %get-tuple-element.27), channel_id=1, source_target_pairs={{8,2},{9,7},{10,0},{11,5},{12,6},{13,3},{14,4},{15,1},{16,10},{17,... | collective-permute-start | bytes 393224 | tf_op jit(solution)/shard_map/ppermute | solution.py:136
  163.8 1.9 collective-permute-start.25
  167.0 9.2 %collective-permute-start.26 = (bf16[64,1024]{1,0:T(8,128)(2,1)}, bf16[64,1024]{1,0:T(8,128)(2,1)S(1)}, u32[]{:S(2)}, u32[]{:S(2)}) collective-permute-start(bf16[64,1024]{1,0:T(8,128)(2,1)} %get-tuple-element.29), channel_id=1, source_target_pairs={{8,0},{9,5},{10,2},{11,7},{12,4},{13,1},{14,6},{15,3},{16,16},{17,... | collective-permute-start | bytes 393224 | tf_op jit(solution)/shard_map/ppermute | solution.py:136
  172.0 7.3 %collective-permute-start.27 = (bf16[64,1024]{1,0:T(8,128)(2,1)}, bf16[64,1024]{1,0:T(8,128)(2,1)S(1)}, u32[]{:S(2)}, u32[]{:S(2)}) collective-permute-start(bf16[64,1024]{1,0:T(8,128)(2,1)} %get-tuple-element.29), channel_id=1, source_target_pairs={{8,2},{9,7},{10,0},{11,5},{12,6},{13,3},{14,4},{15,1},{16,18},{17,... | collective-permute-start | bytes 393224 | tf_op jit(solution)/shard_map/ppermute | solution.py:136
  181.5 10.6 %copy-start.12 = (bf16[1,36,128,256]{3,2,1,0:T(8,128)(2,1)S(1)}, bf16[1,36,128,256]{3,2,1,0:T(8,128)(2,1)}, u32[]{:S(2)}) copy-start(bf16[1,36,128,256]{3,2,1,0:T(8,128)(2,1)} %param.11) | copy-start | bytes 7077892
  182.9 1.4 collective-permute-start.28
  185.6 6.3 %collective-permute-start.29 = (bf16[128,512]{1,0:T(8,128)(2,1)S(1)}, bf16[128,512]{1,0:T(8,128)(2,1)S(1)}, u32[]{:S(2)}, u32[]{:S(2)}) collective-permute-start(bf16[128,512]{1,0:T(8,128)(2,1)S(1)} %slice_select_fusion.2), channel_id=1, source_target_pairs={{1,2},{3,4},{5,6},{2,1},{4,3},{6,5},{9,10},{11,12},{13,14},{10,9},... | collective-permute-start | bytes 393224 | tf_op jit(solution)/shard_map/ppermute | solution.py:248
  (14 other events, 53.2 us)

commit v2 on v1

v2 whole, which is shorter than its diff:
```python
import functools

import jax
import jax.numpy as jnp
from jax import lax
from jax.experimental import pallas as pl
from jax.experimental.pallas import tpu as pltpu
from jax.sharding import PartitionSpec as P

WAVES = 2
F32 = jnp.float32
BF16 = jnp.bfloat16
VMEM = pl.BlockSpec(memory_space=pltpu.VMEM)
SMEM = pl.BlockSpec(memory_space=pltpu.SMEM)
ANY = pl.BlockSpec(memory_space=pl.ANY)


def params(mib):
    return pltpu.CompilerParams(vmem_limit_bytes=mib * 1024 * 1024)


def in_vmem(value):
    return pltpu.with_memory_space_constraint(value, pltpu.VMEM)


def in_hbm(value):
    return pltpu.with_memory_space_constraint(value, pltpu.HBM)


def rows_dot(left, right):
    return lax.dot_general(left, right, (((1,), (1,)), ((), ())), preferred_element_type=F32)


def group_of(leaf_count, most):
    return max(g for g in range(1, most + 1) if leaf_count % g == 0)


def push_kernel(
    group,
    meta_ref,
    rows_ref,
    source_hbm,
    inverse_hbm,
    boundary_hbm,
    out_ref,
    interior_ref,
    inverse_ref,
    boundary_ref,
    source_ref,
    pick_ref,
    sems,
):
    leaf_count, leaf_size = inverse_ref.shape[:2]
    edge = boundary_ref.shape[1]
    window = out_ref.shape[1]
    copies = []
    for step in range(leaf_count // group):
        leaves = pl.ds(step * group, group)
        lanes = pl.ds(step * group * leaf_size, group * leaf_size)
        parts = (
            (source_hbm.at[:, lanes], source_ref.at[:, lanes]),
            (inverse_hbm.at[leaves], inverse_ref.at[leaves]),
            (boundary_hbm.at[leaves], boundary_ref.at[leaves]),
        )
        copies.append(
            [pltpu.make_async_copy(a, b, sems.at[step, i]) for i, (a, b) in enumerate(parts)]
        )
        for copy in copies[-1]:
            copy.start()
    local = rows_ref[...] - meta_ref[0, 0]
    spare = -leaf_count % 8
    if spare:
        local = jnp.concatenate([local, jnp.zeros((spare, edge), jnp.int32)], axis=0)
    columns = jnp.transpose(local).astype(jnp.int16)
    places = lax.broadcasted_iota(jnp.int16, (edge, window), 1)
    for step in range(leaf_count // group):
        for copy in copies[step]:
            copy.wait()
        first = step * group
        for g in range(group):
            pick_ref[step % 2, g * edge : (g + 1) * edge, :] = jnp.where(
                columns[:, first + g : first + g + 1] == places, jnp.bfloat16(1), jnp.bfloat16(0)
            )
        interior = []
        for j in range(first, first + group):
            lanes = slice(j * leaf_size, (j + 1) * leaf_size)
            interior.append(rows_dot(source_ref[:, lanes], inverse_ref[j]).astype(BF16))
            interior_ref[:, lanes] = interior[-1]
        pushed = [
            rows_dot(interior[g], boundary_ref[first + g]).astype(BF16) for g in range(group)
        ]
        total = jnp.dot(
            jnp.concatenate(pushed, axis=1), pick_ref[step % 2], preferred_element_type=F32
        )
        if step == 0:
            out_ref[...] = total
        else:
            out_ref[...] += total


def pick_kernel(meta_ref, rows_ref, out_ref):
    leaf_count, edge = rows_ref.shape
    window = out_ref.shape[0]
    local = (rows_ref[...] - meta_ref[0, 0]).astype(jnp.int16)
    places = lax.broadcasted_iota(jnp.int16, (window, edge), 0)
    for j in range(leaf_count):
        out_ref[:, j * edge : (j + 1) * edge] = jnp.where(
            local[j : j + 1, :] == places, jnp.bfloat16(1), jnp.bfloat16(0)
        )


def lift_matrix_kernel(inverse_ref, boundary_ref, out_ref):
    leaf_count, edge, leaf_size = boundary_ref.shape
    for j in range(leaf_count):
        out_ref[j] = rows_dot(boundary_ref[j], inverse_ref[j]).astype(BF16)


def leaf_kernel(group, window_ref, pick_ref, matrix_ref, interior_ref, out_hbm, out_ref, sems):
    leaf_count, edge, leaf_size = matrix_ref.shape
    window = window_ref[...]
    copies = []
    for step in range(leaf_count // group):
        first = step * group
        picked = jnp.dot(
            window,
            pick_ref[:, first * edge : (first + group) * edge],
            preferred_element_type=F32,
        ).astype(BF16)
        for g in range(group):
            lanes = slice((first + g) * leaf_size, (first + g + 1) * leaf_size)
            lifted = jnp.dot(
                picked[:, g * edge : (g + 1) * edge],
                matrix_ref[first + g],
                preferred_element_type=F32,
            )
            out_ref[:, lanes] = (interior_ref[:, lanes].astype(F32) - lifted).astype(BF16)
        lanes = pl.ds(first * leaf_size, group * leaf_size)
        copies.append(
            pltpu.make_async_copy(out_ref.at[:, lanes], out_hbm.at[:, lanes], sems.at[step])
        )
        copies[-1].start()
    for copy in copies:
        copy.wait()


def half_kernel(meta_ref, inverse_hbm, out_ref, sem):
    columns = out_ref.shape[1]
    start = pl.multiple_of((1 - meta_ref[0, 1]) * columns, columns)
    copy = pltpu.make_async_copy(inverse_hbm.at[:, pl.ds(start, columns)], out_ref, sem)
    copy.start()
    copy.wait()


def turn_kernel(meta_ref, inverse_hbm, taken_ref, out_ref, kept_ref, sem):
    columns, rows = out_ref.shape[0], taken_ref.shape[0]
    start = pl.multiple_of(meta_ref[0, 1] * columns, columns)
    copy = pltpu.make_async_copy(inverse_hbm.at[:, pl.ds(start, columns)], kept_ref, sem)
    copy.start()
    copy.wait()
    piece = min(columns, 256)
    for k in range(0, columns, piece):
        kept = jnp.transpose(kept_ref[:, k : k + piece])
        taken = jnp.transpose(taken_ref[:, k : k + piece])

        @pl.when(meta_ref[0, 2] == 0)
        def _():
            out_ref[k : k + piece, :rows] = kept
            out_ref[k : k + piece, rows:] = taken

        @pl.when(meta_ref[0, 2] != 0)
        def _():
            out_ref[k : k + piece, :rows] = taken
            out_ref[k : k + piece, rows:] = kept


def fold_kernel(turn, blocks, meta_ref, inverse_ref, *refs):
    base_refs = refs[:blocks]
    in_refs = refs[blocks : 2 * blocks] if turn else ()
    out_ref = refs[-1]
    wave_rows, rows = out_ref.shape
    here = pl.ds(pl.multiple_of(meta_ref[turn + 1, 1] * wave_rows, wave_rows), wave_rows)
    forward = meta_ref[turn + 1, 0] == 1
    fed = meta_ref[turn + 1, 2] == 1
    total = jnp.zeros((wave_rows, rows), F32)
    for i in range(blocks):
        if turn:
            base = jnp.where(forward, base_refs[i][here, :].astype(F32), 0.0)
            vectors = (jnp.where(fed, in_refs[i][...].astype(F32), 0.0) + base).astype(BF16)
        else:
            vectors = base_refs[i][here, :]
        place = pl.ds(pl.multiple_of(meta_ref[0, 3 + i] * rows, rows), rows)
        total += jnp.dot(vectors, inverse_ref[place, :], preferred_element_type=F32)
    out_ref[...] = total.astype(BF16)


def join_kernel(turn, meta_ref, mine_ref, other_ref, state_ref, scale_ref, next_ref, out_ref):
    wave_rows = mine_ref.shape[0]
    here = pl.ds(pl.multiple_of(meta_ref[turn + 1, 1] * wave_rows, wave_rows), wave_rows)
    mode = meta_ref[turn + 1, 0]
    solved = (mine_ref[...].astype(F32) + other_ref[...].astype(F32)).astype(BF16).astype(F32)
    older = state_ref[here, :].astype(F32)
    field = (solved + jnp.where(mode == 2, older, 0.0)).astype(BF16)
    scale = scale_ref[pl.ds(jnp.where(mode == 2, 1, 0), 1), :]
    out_ref[...] = (scale * field.astype(F32)).astype(BF16)

    @pl.when(mode > 0)
    def _():
        next_ref[here, :] = field


def turn_routes(turn, panels, waves):
    at = [s if s < panels else 2 * (panels - 1) - s for s in range(2 * panels - 1)]
    pairs = []
    for wave in range(waves):
        step = turn - wave
        if 0 <= step < 2 * (panels - 1):
            pairs.append((at[step], at[step + 1]))
    sources = [a for a, _ in pairs]
    targets = [b for _, b in pairs]
    for panel in range(panels):
        if panel not in sources and panel not in targets:
            pairs.append((panel, panel))
    spare = [p for p in targets if p not in sources]
    unfed = [p for p in sources if p not in targets]
    return pairs + list(zip(spare, unfed))


def spread(values, panel_pairs, chips):
    half = chips // 2
    received = []
    for i in range(half):
        route = []
        for start, end in panel_pairs:
            for chip in range(chips):
                for core in range(2):
                    there = chip ^ (core * half + i)
                    route.append(
                        (2 * (start * chips + chip) + core, 2 * (end * chips + there) + core)
                    )
        received.append(lax.ppermute(values, ("panel", "front"), route))
    return received


def schedule(panels, half, panel, place, rows):
    chip, core = place // 2, place % 2
    table = [[(place - 1) * rows, (chip // half) ^ core, core] + [(chip % half) ^ i for i in range(half)]]
    for turn in range(2 * (panels - 1) + WAVES):
        up_wave = turn - panel
        down_wave = turn - (2 * (panels - 1) - panel)
        up = (up_wave >= 0) & (up_wave < WAVES)
        down = (down_wave >= 0) & (down_wave < WAVES) & (panel < panels - 1)
        table.append(
            [
                jnp.where(up, 1, jnp.where(down, 2, 0)),
                jnp.where(up, up_wave, jnp.where(down, down_wave, 0)),
                jnp.where((panel == 0) & up, 0, 1),
            ]
            + [0] * half
        )
    return jnp.stack([jnp.stack([jnp.asarray(v, jnp.int32) for v in row]) for row in table])


def body(top_source, leaf_source, top_inverse, leaf_inverse, boundary, touch_rows, coupling):
    sources = top_source.shape[1]
    rows = top_source.shape[2]
    width = top_inverse.shape[2]
    leaf_count, leaf_size = leaf_inverse.shape[1:3]
    edge = boundary.shape[2]
    panels = lax.axis_size("panel")
    front = lax.axis_size("front")
    chips, half = front // 2, front // 4
    chip_rows = 2 * rows
    panel = lax.axis_index("panel")
    place = lax.axis_index("front")
    core = place % 2
    wave_rows = sources // WAVES
    group = group_of(leaf_count, 6)
    steps = leaf_count // group
    all_lanes = leaf_count * leaf_size
    meta = schedule(panels, half, panel, place, rows)

    swap_core = [(i, i ^ 1) for i in range(front)]
    swap_chip = [(i, i + 1) for i in range(1, front - 1, 2)]
    swap_chip = swap_chip + [(j, i) for i, j in swap_chip]

    windows, interior, inverse_here, boundary_here = pl.pallas_call(
        functools.partial(push_kernel, group),
        out_shape=(
            pltpu.VMEM((sources, 3 * rows), F32),
            pltpu.VMEM((sources, all_lanes), BF16),
            pltpu.VMEM((leaf_count, leaf_size, leaf_size), BF16),
            pltpu.VMEM((leaf_count, edge, leaf_size), BF16),
        ),
        in_specs=[SMEM, VMEM, ANY, ANY, ANY],
        out_specs=(VMEM, VMEM, VMEM, VMEM),
        scratch_shapes=[
            pltpu.VMEM((sources, all_lanes), BF16),
            pltpu.VMEM((2, group * edge, 3 * rows), BF16),
            pltpu.SemaphoreType.DMA((steps, 3)),
        ],
        compiler_params=params(20),
    )(meta, touch_rows[0], in_hbm(leaf_source[0]), in_hbm(leaf_inverse[0]), in_hbm(boundary[0]))
    outward = jnp.where(core == 0, windows[:, :rows], windows[:, 2 * rows :]).astype(BF16)
    inward = lax.ppermute(outward, "front", swap_chip)
    chip_part = jnp.where(core == 0, windows[:, rows:], windows[:, :chip_rows])
    own_part = top_source[0].astype(F32) - inward.astype(F32)
    blank = jnp.zeros_like(own_part)
    own_part = jnp.where(
        core == 0,
        jnp.concatenate([own_part, blank], axis=1),
        jnp.concatenate([blank, own_part], axis=1),
    )
    partial = (own_part - chip_part).astype(BF16)
    partner = lax.ppermute(partial, "front", swap_core)
    known = (partial.astype(F32) + partner.astype(F32)).astype(BF16)
    base = [in_vmem(b) for b in spread(known, [(p, p) for p in range(panels)], chips)]

    given = pl.pallas_call(
        half_kernel,
        out_shape=pltpu.VMEM((rows, width // 2), BF16),
        in_specs=[SMEM, ANY],
        out_specs=VMEM,
        scratch_shapes=[pltpu.SemaphoreType.DMA],
        compiler_params=params(4),
    )(meta, in_hbm(top_inverse[0]))
    taken = lax.ppermute(given, "front", swap_core)
    inverse = pl.pallas_call(
        turn_kernel,
        out_shape=pltpu.VMEM((width // 2, chip_rows), BF16),
        in_specs=[SMEM, ANY, VMEM],
        out_specs=VMEM,
        scratch_shapes=[pltpu.VMEM((rows, width // 2), BF16), pltpu.SemaphoreType.DMA],
        compiler_params=params(8),
    )(meta, in_hbm(top_inverse[0]), in_vmem(taken))
    inverse = in_vmem(inverse)

    later = lax.ppermute(coupling, "panel", [((p + 1) % panels, p) for p in range(panels)])
    forward_scale = jnp.where(panel == panels - 1, coupling, later)
    scales = jnp.concatenate([forward_scale, coupling], axis=0)
    partner_scales = lax.ppermute(scales, "front", swap_core)
    scales = jnp.where(
        core == 0,
        jnp.concatenate([scales, partner_scales], axis=1),
        jnp.concatenate([partner_scales, scales], axis=1),
    )
    scales = in_vmem(scales)
    state = jnp.zeros((sources, chip_rows), BF16)
    turns = 2 * (panels - 1) + WAVES
    arrived = []
    for turn in range(turns):
        share = pl.pallas_call(
            functools.partial(fold_kernel, turn, half),
            out_shape=pltpu.VMEM((wave_rows, chip_rows), BF16),
            in_specs=[SMEM] + [VMEM] * (1 + half + len(arrived)),
            out_specs=VMEM,
            compiler_params=params(4),
        )(meta, inverse, *base, *arrived)
        other = lax.ppermute(share, "front", swap_core)
        state, outgoing = pl.pallas_call(
            functools.partial(join_kernel, turn),
            out_shape=(
                pltpu.VMEM((sources, chip_rows), BF16),
                pltpu.VMEM((wave_rows, chip_rows), BF16),
            ),
            in_specs=[SMEM] + [VMEM] * 4,
            out_specs=(VMEM, VMEM),
            input_output_aliases={3: 0},
            compiler_params=params(4),
        )(meta, in_vmem(share), in_vmem(other), in_vmem(state), scales)
        if turn < turns - 1:
            routes = turn_routes(turn, panels, WAVES)
            arrived = [in_vmem(a) for a in spread(outgoing, routes, chips)]

    picks = pl.pallas_call(
        pick_kernel,
        out_shape=pltpu.VMEM((3 * rows, leaf_count * edge), BF16),
        in_specs=[SMEM, VMEM],
        out_specs=VMEM,
        compiler_params=params(4),
    )(meta, touch_rows[0])
    matrices = pl.pallas_call(
        lift_matrix_kernel,
        out_shape=pltpu.VMEM((leaf_count, edge, leaf_size), BF16),
        in_specs=[VMEM, VMEM],
        out_specs=VMEM,
        compiler_params=params(4),
    )(in_vmem(inverse_here), in_vmem(boundary_here))
    top_field = jnp.where(core == 0, state[:, :rows], state[:, rows:])
    beside = lax.ppermute(top_field, "front", swap_chip)
    window = jnp.where(
        core == 0,
        jnp.concatenate([beside, state], axis=1),
        jnp.concatenate([state, beside], axis=1),
    )
    leaf_field = pl.pallas_call(
        functools.partial(leaf_kernel, group),
        out_shape=jax.ShapeDtypeStruct((sources, all_lanes), BF16),
        in_specs=[VMEM] * 4,
        out_specs=ANY,
        scratch_shapes=[
            pltpu.VMEM((sources, all_lanes), BF16),
            pltpu.SemaphoreType.DMA((steps,)),
        ],
        compiler_params=params(8),
    )(in_vmem(window), in_vmem(picks), in_vmem(matrices), in_vmem(interior))
    return (top_field[None], leaf_field[None])


def solution(mesh):
    placed = (
        P("panel", None, "front"),
        P("panel", None, "front"),
        P("panel", "front", None),
        P("panel", "front", None, None),
        P("panel", "front", None, None),
        P("panel", "front", None),
        P("panel", "front"),
    )
    return jax.shard_map(
        body,
        mesh=mesh,
        in_specs=placed,
        out_specs=(P("panel", None, "front"), P("panel", None, "front")),
        check_vma=False,
    )
```

time: 201 us -> 156 us (0.78)
  local copies, waits for them, and re-layouts: 32.9 us -> 2.33 us
  starting transfers between devices: 60.5 us -> 51.9 us
  waiting for transfers between devices: 60.6 us -> 56.4 us
  other arithmetic: 4.23 us -> 1.25 us
    unnamed x32 -> x17, local copies, waits for them, and re-layouts: 19.3 us -> 2.18 us
    dynamic_slice x3 -> x0, local copies, waits for them, and re-layouts: 12.8 us -> none  [the longest x2 8.78 us: body(): lax.dynamic_slice_in_dim(top_inverse[0], own_half * (width // 2), width /...]
    ppermute x16, starting transfers between devices: 48.1 us -> 41.1 us  [spread(): received.append(lax.ppermute(values, ('panel', 'front'), route))]
    ppermute x16, waiting for transfers between devices: 44.8 us -> 39.8 us  [spread(): received.append(lax.ppermute(values, ('panel', 'front'), route))]
    transpose x1 -> x0, other arithmetic: 2.5 us -> none  [body(): inverse = jnp.concatenate([low.T, high.T], axis=1)]
    pallas_call x18 -> x22, Pallas kernels: 40.7 us -> 42.3 us  [the longest x8 12.2 us: body(): pl.pallas_call(functools.partial(fold_kernel, turn, half), out_shape=pltp...]
  transfers between devices with their start and end apart: 30 -> 30, of which waited for: 26 -> 26; matrix products, arithmetic and copies ran while one was open for 4% -> 1% of each run, Pallas kernels for 6% -> 10%
where the time goes in v2:
time: 156 us
  waiting for transfers between devices  56.4 us (36%)
  starting transfers between devices  51.9 us (33%)
  Pallas kernels  42.3 us (27%)
  local copies, waits for them, and re-layouts  2.33 us (1%)
    ppermute x16, starting transfers between devices, spread(): received.append(lax.ppermute(values, ('panel', 'front'), route))  41.1 us
    ppermute x16, waiting for transfers between devices, spread(): received.append(lax.ppermute(values, ('panel', 'front'), route))  39.8 us
    pallas_call x8, Pallas kernels, body(): pl.pallas_call(functools.partial(fold_kernel, turn, half), out_shape=pltp...  12.2 us
    ppermute x8, waiting for transfers between devices, body(): other = lax.ppermute(share, 'front', swap_core)  8.01 us
    pallas_call x8, Pallas kernels, body(): pl.pallas_call(functools.partial(join_kernel, turn), out_shape=(pltpu.VME...  6.76 us
    pallas_call x1, Pallas kernels, body(): pl.pallas_call(functools.partial(push_kernel, group), out_shape=(pltpu.VM...  6.71 us
    pallas_call x1, Pallas kernels, body(): pl.pallas_call(turn_kernel, out_shape=pltpu.VMEM((width // 2, chip_rows),...  5.01 us
    ppermute x1, starting transfers between devices, body(): inward = lax.ppermute(outward, 'front', swap_chip)  4.58 us
  transfers between devices with their start and end apart: 30, of which 26 were waited for; matrix products, arithmetic and copies ran while one was open for 1% of the time, Pallas kernels for 10%

profile of v2, /device:TPU:1, one launch (start us, length us, event | category | flops | bytes accessed | tf_op | source)
XLA Modules:
  0.0 155.6 jit_solution(10644781244956203103)
XLA Ops:
  1.1 3.6 %shard_map.86 = bf16[512,2048]{1,0:T(8,128)(2,1)} custom-call(s32[9,5]{1,0:T(8,128)S(1)} %stack.191.meta_ref, bf16[512,4096]{1,0:T(8,128)(2,1)} %bitcast.63), custom_call_target="tpu_custom_call" | custom-call | tf_op jit(solution)/shard_map/pallas_call | solution.py:318
  4.9 6.7 %shard_map.88 = (f32[128,1536]{1,0:T(8,128)S(1)}, bf16[128,9216]{1,0:T(8,128)(2,1)S(1)}, bf16[36,256,256]{2,1,0:T(8,128)(2,1)S(1)}, bf16[36,128,256]{2,1,0:T(8,128)(2,1)S(1)}) custom-call(s32[9,5]{1,0:T(8,128)S(1)} %stack.191.meta_ref, s32[36,128]{1,0:T(8,128)S(1)} %bitcast.61, bf16[128,9216]{1,0:T(8,128)(2,1)} %bitcast.66, bf16[36,256,256]{2,1,0:T(8,128)(2,1)} %bitcast.65, ...), custom_call_target="tpu_custom_call" | custom-call | tf_op jit(solution)/shard_map/pallas_call | solution.py:286
  11.6 2.1 %copy-done = bf16[36,256,256]{2,1,0:T(8,128)(2,1)} copy-done((bf16[36,256,256]{2,1,0:T(8,128)(2,1)}, bf16[36,256,256]{2,1,0:T(8,128)(2,1)S(1)}, u32[]{:S(2)}) %copy-start) | copy-done | bytes 4718616
  13.8 4.6 %collective-permute-start.1 = (bf16[128,512]{1,0:T(8,128)(2,1)S(1)}, bf16[128,512]{1,0:T(8,128)(2,1)S(1)}, u32[]{:S(2)}, u32[]{:S(2)}) collective-permute-start(bf16[128,512]{1,0:T(8,128)(2,1)S(1)} %select_convert_fusion), channel_id=1, source_target_pairs={{1,2},{3,4},{5,6},{2,1},{4,3},{6,5},{9,10},{11,12},{13,14},{10,9},... | collective-permute-start | bytes 393224 | tf_op jit(solution)/shard_map/ppermute | solution.py:304
  18.4 2.6 %collective-permute-done.1 = bf16[128,512]{1,0:T(8,128)(2,1)S(1)} collective-permute-done((bf16[128,512]{1,0:T(8,128)(2,1)S(1)}, bf16[128,512]{1,0:T(8,128)(2,1)S(1)}, u32[]{:S(2)}, u32[]{:S(2)}) %collective-permute-start.1) | collective-permute-done | bytes 131104 | tf_op jit(solution)/shard_map/ppermute | solution.py:304
  22.9 3.6 %collective-permute-start.4 = (bf16[128,1024]{1,0:T(8,128)(2,1)S(1)}, bf16[128,1024]{1,0:T(8,128)(2,1)S(1)}, u32[]{:S(2)}, u32[]{:S(2)}) collective-permute-start(bf16[128,1024]{1,0:T(8,128)(2,1)S(1)} %add_convert_fusion), channel_id=1, source_target_pairs={{0,2},{1,7},{2,0},{3,5},{4,6},{5,3},{6,4},{7,1},{8,10},{9,15},{10,... | collective-permute-start | bytes 786440 | tf_op jit(solution)/shard_map/ppermute | solution.py:240
  26.4 1.9 %collective-permute-start.3 = (bf16[128,1024]{1,0:T(8,128)(2,1)S(1)}, bf16[128,1024]{1,0:T(8,128)(2,1)S(1)}, u32[]{:S(2)}, u32[]{:S(2)}) collective-permute-start(bf16[128,1024]{1,0:T(8,128)(2,1)S(1)} %add_convert_fusion), channel_id=1, source_target_pairs={{0,0},{1,5},{2,2},{3,7},{4,4},{5,1},{6,6},{7,3},{8,8},{9,13},{10,1... | collective-permute-start | bytes 786440 | tf_op jit(solution)/shard_map/ppermute | solution.py:240
  28.3 2.2 %collective-permute-start.6 = (f32[1,512]{1,0:T(1,128)S(1)}, f32[1,512]{1,0:T(1,128)S(1)}, u32[]{:S(2)}, u32[]{:S(2)}) collective-permute-start(f32[1,512]{1,0:T(1,128)S(1)} %copy-done.5), channel_id=1, source_target_pairs={{8,0},{16,8},{24,16},{0,24},{9,1},{17,9},{25,17},{1,25},{10,2},{18... | collective-permute-start | bytes 6152 | tf_op jit(solution)/shard_map/ppermute | solution.py:337
  31.2 5.0 %shard_map.87.inverse_ref = bf16[2048,1024]{1,0:T(8,128)(2,1)S(1)} custom-call(s32[9,5]{1,0:T(8,128)S(1)} %stack.191.meta_ref, bf16[512,4096]{1,0:T(8,128)(2,1)} %bitcast.64, bf16[512,2048]{1,0:T(8,128)(2,1)} %collective-permute-done.taken_ref), custom_call_target="tpu_custom_call" | custom-call | tf_op jit(solution)/shard_map/pallas_call | solution.py:327
  41.9 3.2 %collective-permute-start.9 = (bf16[64,1024]{1,0:T(8,128)(2,1)S(1)}, bf16[64,1024]{1,0:T(8,128)(2,1)S(1)}, u32[]{:S(2)}, u32[]{:S(2)}) collective-permute-start(bf16[64,1024]{1,0:T(8,128)(2,1)S(1)} %get-tuple-element.22), channel_id=1, source_target_pairs={{0,10},{1,15},{2,8},{3,13},{4,14},{5,11},{6,12},{7,9},{16,18},{17,... | collective-permute-start | bytes 393224 | tf_op jit(solution)/shard_map/ppermute | solution.py:240
  45.1 1.9 %collective-permute-start.8 = (bf16[64,1024]{1,0:T(8,128)(2,1)S(1)}, bf16[64,1024]{1,0:T(8,128)(2,1)S(1)}, u32[]{:S(2)}, u32[]{:S(2)}) collective-permute-start(bf16[64,1024]{1,0:T(8,128)(2,1)S(1)} %get-tuple-element.22), channel_id=1, source_target_pairs={{0,8},{1,13},{2,10},{3,15},{4,12},{5,9},{6,14},{7,11},{16,16},{17,... | collective-permute-start | bytes 393224 | tf_op jit(solution)/shard_map/ppermute | solution.py:240
  47.1 2.5 %collective-permute-done.9.refs_3_ = bf16[64,1024]{1,0:T(8,128)(2,1)S(1)} collective-permute-done((bf16[64,1024]{1,0:T(8,128)(2,1)S(1)}, bf16[64,1024]{1,0:T(8,128)(2,1)S(1)}, u32[]{:S(2)}, u32[]{:S(2)}) %collective-permute-start.9) | collective-permute-done | bytes 131104 | tf_op jit(solution)/shard_map/ppermute | solution.py:240
  49.5 3.4 %collective-permute-done.8.refs_2_ = bf16[64,1024]{1,0:T(8,128)(2,1)S(1)} collective-permute-done((bf16[64,1024]{1,0:T(8,128)(2,1)S(1)}, bf16[64,1024]{1,0:T(8,128)(2,1)S(1)}, u32[]{:S(2)}, u32[]{:S(2)}) %collective-permute-start.8) | collective-permute-done | bytes 131104 | tf_op jit(solution)/shard_map/ppermute | solution.py:240
  56.6 2.1 %collective-permute-start.12 = (bf16[64,1024]{1,0:T(8,128)(2,1)S(1)}, bf16[64,1024]{1,0:T(8,128)(2,1)S(1)}, u32[]{:S(2)}, u32[]{:S(2)}) collective-permute-start(bf16[64,1024]{1,0:T(8,128)(2,1)S(1)} %get-tuple-element.24), channel_id=1, source_target_pairs={{8,18},{9,23},{10,16},{11,21},{12,22},{13,19},{14,20},{15,17},{0,1... | collective-permute-start | bytes 393224 | tf_op jit(solution)/shard_map/ppermute | solution.py:240
  60.6 3.3 %collective-permute-done.12.refs_3_ = bf16[64,1024]{1,0:T(8,128)(2,1)S(1)} collective-permute-done((bf16[64,1024]{1,0:T(8,128)(2,1)S(1)}, bf16[64,1024]{1,0:T(8,128)(2,1)S(1)}, u32[]{:S(2)}, u32[]{:S(2)}) %collective-permute-start.12) | collective-permute-done | bytes 131104 | tf_op jit(solution)/shard_map/ppermute | solution.py:240
  63.9 2.7 %collective-permute-done.11.refs_2_ = bf16[64,1024]{1,0:T(8,128)(2,1)S(1)} collective-permute-done((bf16[64,1024]{1,0:T(8,128)(2,1)S(1)}, bf16[64,1024]{1,0:T(8,128)(2,1)S(1)}, u32[]{:S(2)}, u32[]{:S(2)}) %collective-permute-start.11) | collective-permute-done | bytes 131104 | tf_op jit(solution)/shard_map/ppermute | solution.py:240
  73.9 2.9 %collective-permute-done.15.refs_3_ = bf16[64,1024]{1,0:T(8,128)(2,1)S(1)} collective-permute-done((bf16[64,1024]{1,0:T(8,128)(2,1)S(1)}, bf16[64,1024]{1,0:T(8,128)(2,1)S(1)}, u32[]{:S(2)}, u32[]{:S(2)}) %collective-permute-start.15) | collective-permute-done | bytes 131104 | tf_op jit(solution)/shard_map/ppermute | solution.py:240
  76.8 2.8 %collective-permute-done.14.refs_2_ = bf16[64,1024]{1,0:T(8,128)(2,1)S(1)} collective-permute-done((bf16[64,1024]{1,0:T(8,128)(2,1)S(1)}, bf16[64,1024]{1,0:T(8,128)(2,1)S(1)}, u32[]{:S(2)}, u32[]{:S(2)}) %collective-permute-start.14) | collective-permute-done | bytes 131104 | tf_op jit(solution)/shard_map/ppermute | solution.py:240
  87.1 2.2 %collective-permute-done.18.refs_3_ = bf16[64,1024]{1,0:T(8,128)(2,1)S(1)} collective-permute-done((bf16[64,1024]{1,0:T(8,128)(2,1)S(1)}, bf16[64,1024]{1,0:T(8,128)(2,1)S(1)}, u32[]{:S(2)}, u32[]{:S(2)}) %collective-permute-start.18) | collective-permute-done | bytes 131104 | tf_op jit(solution)/shard_map/ppermute | solution.py:240
  89.3 3.1 %collective-permute-done.17.refs_2_ = bf16[64,1024]{1,0:T(8,128)(2,1)S(1)} collective-permute-done((bf16[64,1024]{1,0:T(8,128)(2,1)S(1)}, bf16[64,1024]{1,0:T(8,128)(2,1)S(1)}, u32[]{:S(2)}, u32[]{:S(2)}) %collective-permute-start.17) | collective-permute-done | bytes 131104 | tf_op jit(solution)/shard_map/ppermute | solution.py:240
  99.7 2.2 %collective-permute-done.21.refs_3_ = bf16[64,1024]{1,0:T(8,128)(2,1)S(1)} collective-permute-done((bf16[64,1024]{1,0:T(8,128)(2,1)S(1)}, bf16[64,1024]{1,0:T(8,128)(2,1)S(1)}, u32[]{:S(2)}, u32[]{:S(2)}) %collective-permute-start.21) | collective-permute-done | bytes 131104 | tf_op jit(solution)/shard_map/ppermute | solution.py:240
  101.9 3.1 %collective-permute-done.20.refs_2_ = bf16[64,1024]{1,0:T(8,128)(2,1)S(1)} collective-permute-done((bf16[64,1024]{1,0:T(8,128)(2,1)S(1)}, bf16[64,1024]{1,0:T(8,128)(2,1)S(1)}, u32[]{:S(2)}, u32[]{:S(2)}) %collective-permute-start.20) | collective-permute-done | bytes 131104 | tf_op jit(solution)/shard_map/ppermute | solution.py:240
  108.7 6.2 %collective-permute-start.24 = (bf16[64,1024]{1,0:T(8,128)(2,1)S(1)}, bf16[64,1024]{1,0:T(8,128)(2,1)S(1)}, u32[]{:S(2)}, u32[]{:S(2)}) collective-permute-start(bf16[64,1024]{1,0:T(8,128)(2,1)S(1)} %get-tuple-element.32), channel_id=1, source_target_pairs={{8,2},{9,7},{10,0},{11,5},{12,6},{13,3},{14,4},{15,1},{16,10},{17,... | collective-permute-start | bytes 393224 | tf_op jit(solution)/shard_map/ppermute | solution.py:240
  114.9 3.5 %collective-permute-start.23 = (bf16[64,1024]{1,0:T(8,128)(2,1)S(1)}, bf16[64,1024]{1,0:T(8,128)(2,1)S(1)}, u32[]{:S(2)}, u32[]{:S(2)}) collective-permute-start(bf16[64,1024]{1,0:T(8,128)(2,1)S(1)} %get-tuple-element.32), channel_id=1, source_target_pairs={{8,0},{9,5},{10,2},{11,7},{12,4},{13,1},{14,6},{15,3},{16,8},{17,1... | collective-permute-start | bytes 393224 | tf_op jit(solution)/shard_map/ppermute | solution.py:240
  119.3 3.4 %collective-permute-done.23.refs_2_ = bf16[64,1024]{1,0:T(8,128)(2,1)S(1)} collective-permute-done((bf16[64,1024]{1,0:T(8,128)(2,1)S(1)}, bf16[64,1024]{1,0:T(8,128)(2,1)S(1)}, u32[]{:S(2)}, u32[]{:S(2)}) %collective-permute-start.23) | collective-permute-done | bytes 131104 | tf_op jit(solution)/shard_map/ppermute | solution.py:240
  126.5 3.9 %collective-permute-start.27 = (bf16[64,1024]{1,0:T(8,128)(2,1)S(1)}, bf16[64,1024]{1,0:T(8,128)(2,1)S(1)}, u32[]{:S(2)}, u32[]{:S(2)}) collective-permute-start(bf16[64,1024]{1,0:T(8,128)(2,1)S(1)} %get-tuple-element.34), channel_id=1, source_target_pairs={{8,2},{9,7},{10,0},{11,5},{12,6},{13,3},{14,4},{15,1},{16,18},{17,... | collective-permute-start | bytes 393224 | tf_op jit(solution)/shard_map/ppermute | solution.py:240
  132.3 2.1 %collective-permute-done.27.refs_3_ = bf16[64,1024]{1,0:T(8,128)(2,1)S(1)} collective-permute-done((bf16[64,1024]{1,0:T(8,128)(2,1)S(1)}, bf16[64,1024]{1,0:T(8,128)(2,1)S(1)}, u32[]{:S(2)}, u32[]{:S(2)}) %collective-permute-start.27) | collective-permute-done | bytes 131104 | tf_op jit(solution)/shard_map/ppermute | solution.py:240
  134.4 3.4 %collective-permute-done.26.refs_2_ = bf16[64,1024]{1,0:T(8,128)(2,1)S(1)} collective-permute-done((bf16[64,1024]{1,0:T(8,128)(2,1)S(1)}, bf16[64,1024]{1,0:T(8,128)(2,1)S(1)}, u32[]{:S(2)}, u32[]{:S(2)}) %collective-permute-start.26) | collective-permute-done | bytes 131104 | tf_op jit(solution)/shard_map/ppermute | solution.py:240
  139.5 2.7 %shard_map.105.pick_ref = bf16[1536,4608]{1,0:T(8,128)(2,1)S(1)} custom-call(s32[9,5]{1,0:T(8,128)S(1)} %stack.191.meta_ref, s32[36,128]{1,0:T(8,128)S(1)} %bitcast.62), custom_call_target="tpu_custom_call" | custom-call | tf_op jit(solution)/shard_map/pallas_call | solution.py:374
  145.4 2.7 %collective-permute-start.29 = (bf16[128,512]{1,0:T(8,128)(2,1)S(1)}, bf16[128,512]{1,0:T(8,128)(2,1)S(1)}, u32[]{:S(2)}, u32[]{:S(2)}) collective-permute-start(bf16[128,512]{1,0:T(8,128)(2,1)S(1)} %slice_select_fusion), channel_id=1, source_target_pairs={{1,2},{3,4},{5,6},{2,1},{4,3},{6,5},{9,10},{11,12},{13,14},{10,9},... | collective-permute-start | bytes 393224 | tf_op jit(solution)/shard_map/ppermute | solution.py:389
  148.8 2.9 %collective-permute-done.29 = bf16[128,512]{1,0:T(8,128)(2,1)S(1)} collective-permute-done((bf16[128,512]{1,0:T(8,128)(2,1)S(1)}, bf16[128,512]{1,0:T(8,128)(2,1)S(1)}, u32[]{:S(2)}, u32[]{:S(2)}) %collective-permute-start.29) | collective-permute-done | bytes 131104 | tf_op jit(solution)/shard_map/ppermute | solution.py:389
  151.8 3.7 %shard_map.107 = bf16[128,9216]{1,0:T(8,128)(2,1)} custom-call(bf16[128,1536]{1,0:T(8,128)(2,1)S(1)} %maximum_select_fusion.window_ref, bf16[1536,4608]{1,0:T(8,128)(2,1)S(1)} %shard_map.105.pick_ref, bf16[36,128,256]{2,1,0:T(8,128)(2,1)S(1)} %shard_map.106.matrix_ref, bf16[128,9216]{1,0:T(8,128)(2,1)S(1)} %get-tuple-element.39.interior_ref), custom_call_target="tpu_custom_call" | custom-call | tf_op jit(solution)/shard_map/pallas_call | solution.py:395
  (84 shorter events, 51.7 us)
Async XLA Ops:
  4.7 26.5 %collective-permute-start = (bf16[512,2048]{1,0:T(8,128)(2,1)}, bf16[512,2048]{1,0:T(8,128)(2,1)}, u32[]{:S(2)}, u32[]{:S(2)}) collective-permute-start(bf16[512,2048]{1,0:T(8,128)(2,1)} %shard_map.86), channel_id=1, source_target_pairs={{0,1},{1,0},{2,3},{3,2},{4,5},{5,4},{6,7},{7,6},{8,9},{9,8},{10,11... | collective-permute-start | bytes 6291464 | tf_op jit(solution)/shard_map/ppermute | solution.py:326
  4.9 16.1 %copy-start.3 = (bf16[1,128,512]{2,1,0:T(8,128)(2,1)S(1)}, bf16[1,128,512]{2,1,0:T(8,128)(2,1)}, u32[]{:S(2)}) copy-start(bf16[1,128,512]{2,1,0:T(8,128)(2,1)} %param.7) | copy-start | bytes 393220
  13.7 14.6 %copy-start.5 = (f32[1,512]{1,0:T(1,128)S(1)}, f32[1,512]{1,0:T(1,128)}, u32[]{:S(2)}) copy-start(f32[1,512]{1,0:T(1,128)} %param.13) | copy-start | bytes 6148
  13.8 7.2 %collective-permute-start.1 = (bf16[128,512]{1,0:T(8,128)(2,1)S(1)}, bf16[128,512]{1,0:T(8,128)(2,1)S(1)}, u32[]{:S(2)}, u32[]{:S(2)}) collective-permute-start(bf16[128,512]{1,0:T(8,128)(2,1)S(1)} %select_convert_fusion), channel_id=1, source_target_pairs={{1,2},{3,4},{5,6},{2,1},{4,3},{6,5},{9,10},{11,12},{13,14},{10,9},... | collective-permute-start | bytes 393224 | tf_op jit(solution)/shard_map/ppermute | solution.py:304
  21.2 1.6 %collective-permute-start.2 = (bf16[128,1024]{1,0:T(8,128)(2,1)S(1)}, bf16[128,1024]{1,0:T(8,128)(2,1)S(1)}, u32[]{:S(2)}, u32[]{:S(2)}) collective-permute-start(bf16[128,1024]{1,0:T(8,128)(2,1)S(1)} %subtract_convert_fusion), channel_id=1, source_target_pairs={{0,1},{1,0},{2,3},{3,2},{4,5},{5,4},{6,7},{7,6},{8,9},{9,8},{10,11... | collective-permute-start | bytes 786440 | tf_op jit(solution)/shard_map/ppermute | solution.py:314
  22.9 13.4 %collective-permute-start.4 = (bf16[128,1024]{1,0:T(8,128)(2,1)S(1)}, bf16[128,1024]{1,0:T(8,128)(2,1)S(1)}, u32[]{:S(2)}, u32[]{:S(2)}) collective-permute-start(bf16[128,1024]{1,0:T(8,128)(2,1)S(1)} %add_convert_fusion), channel_id=1, source_target_pairs={{0,2},{1,7},{2,0},{3,5},{4,6},{5,3},{6,4},{7,1},{8,10},{9,15},{10,... | collective-permute-start | bytes 786440 | tf_op jit(solution)/shard_map/ppermute | solution.py:240
  26.4 11.7 %collective-permute-start.3 = (bf16[128,1024]{1,0:T(8,128)(2,1)S(1)}, bf16[128,1024]{1,0:T(8,128)(2,1)S(1)}, u32[]{:S(2)}, u32[]{:S(2)}) collective-permute-start(bf16[128,1024]{1,0:T(8,128)(2,1)S(1)} %add_convert_fusion), channel_id=1, source_target_pairs={{0,0},{1,5},{2,2},{3,7},{4,4},{5,1},{6,6},{7,3},{8,8},{9,13},{10,1... | collective-permute-start | bytes 786440 | tf_op jit(solution)/shard_map/ppermute | solution.py:240
  28.3 2.9 %collective-permute-start.6 = (f32[1,512]{1,0:T(1,128)S(1)}, f32[1,512]{1,0:T(1,128)S(1)}, u32[]{:S(2)}, u32[]{:S(2)}) collective-permute-start(f32[1,512]{1,0:T(1,128)S(1)} %copy-done.5), channel_id=1, source_target_pairs={{8,0},{16,8},{24,16},{0,24},{9,1},{17,9},{25,17},{1,25},{10,2},{18... | collective-permute-start | bytes 6152 | tf_op jit(solution)/shard_map/ppermute | solution.py:337
  39.6 1.5 collective-permute-start.5
  39.7 1.4 collective-permute-start.7
  41.9 7.6 %collective-permute-start.9 = (bf16[64,1024]{1,0:T(8,128)(2,1)S(1)}, bf16[64,1024]{1,0:T(8,128)(2,1)S(1)}, u32[]{:S(2)}, u32[]{:S(2)}) collective-permute-start(bf16[64,1024]{1,0:T(8,128)(2,1)S(1)} %get-tuple-element.22), channel_id=1, source_target_pairs={{0,10},{1,15},{2,8},{3,13},{4,14},{5,11},{6,12},{7,9},{16,18},{17,... | collective-permute-start | bytes 393224 | tf_op jit(solution)/shard_map/ppermute | solution.py:240
  45.1 7.8 %collective-permute-start.8 = (bf16[64,1024]{1,0:T(8,128)(2,1)S(1)}, bf16[64,1024]{1,0:T(8,128)(2,1)S(1)}, u32[]{:S(2)}, u32[]{:S(2)}) collective-permute-start(bf16[64,1024]{1,0:T(8,128)(2,1)S(1)} %get-tuple-element.22), channel_id=1, source_target_pairs={{0,8},{1,13},{2,10},{3,15},{4,12},{5,9},{6,14},{7,11},{16,16},{17,... | collective-permute-start | bytes 393224 | tf_op jit(solution)/shard_map/ppermute | solution.py:240
  54.4 1.4 collective-permute-start.10
  56.6 7.3 %collective-permute-start.12 = (bf16[64,1024]{1,0:T(8,128)(2,1)S(1)}, bf16[64,1024]{1,0:T(8,128)(2,1)S(1)}, u32[]{:S(2)}, u32[]{:S(2)}) collective-permute-start(bf16[64,1024]{1,0:T(8,128)(2,1)S(1)} %get-tuple-element.24), channel_id=1, source_target_pairs={{8,18},{9,23},{10,16},{11,21},{12,22},{13,19},{14,20},{15,17},{0,1... | collective-permute-start | bytes 393224 | tf_op jit(solution)/shard_map/ppermute | solution.py:240
  58.7 8.0 %collective-permute-start.11 = (bf16[64,1024]{1,0:T(8,128)(2,1)S(1)}, bf16[64,1024]{1,0:T(8,128)(2,1)S(1)}, u32[]{:S(2)}, u32[]{:S(2)}) collective-permute-start(bf16[64,1024]{1,0:T(8,128)(2,1)S(1)} %get-tuple-element.24), channel_id=1, source_target_pairs={{8,16},{9,21},{10,18},{11,23},{12,20},{13,17},{14,22},{15,19},{0,8... | collective-permute-start | bytes 393224 | tf_op jit(solution)/shard_map/ppermute | solution.py:240
  68.2 1.4 collective-permute-start.13
  70.4 6.4 %collective-permute-start.15 = (bf16[64,1024]{1,0:T(8,128)(2,1)S(1)}, bf16[64,1024]{1,0:T(8,128)(2,1)S(1)}, u32[]{:S(2)}, u32[]{:S(2)}) collective-permute-start(bf16[64,1024]{1,0:T(8,128)(2,1)S(1)} %get-tuple-element.26), channel_id=1, source_target_pairs={{16,26},{17,31},{18,24},{19,29},{20,30},{21,27},{22,28},{23,25},{8... | collective-permute-start | bytes 393224 | tf_op jit(solution)/shard_map/ppermute | solution.py:240
  72.0 7.6 %collective-permute-start.14 = (bf16[64,1024]{1,0:T(8,128)(2,1)S(1)}, bf16[64,1024]{1,0:T(8,128)(2,1)S(1)}, u32[]{:S(2)}, u32[]{:S(2)}) collective-permute-start(bf16[64,1024]{1,0:T(8,128)(2,1)S(1)} %get-tuple-element.26), channel_id=1, source_target_pairs={{16,24},{17,29},{18,26},{19,31},{20,28},{21,25},{22,30},{23,27},{8... | collective-permute-start | bytes 393224 | tf_op jit(solution)/shard_map/ppermute | solution.py:240
  81.2 1.4 collective-permute-start.16
  83.4 5.9 %collective-permute-start.18 = (bf16[64,1024]{1,0:T(8,128)(2,1)S(1)}, bf16[64,1024]{1,0:T(8,128)(2,1)S(1)}, u32[]{:S(2)}, u32[]{:S(2)}) collective-permute-start(bf16[64,1024]{1,0:T(8,128)(2,1)S(1)} %get-tuple-element.28), channel_id=1, source_target_pairs={{24,18},{25,23},{26,16},{27,21},{28,22},{29,19},{30,20},{31,17},{1... | collective-permute-start | bytes 393224 | tf_op jit(solution)/shard_map/ppermute | solution.py:240
  85.1 7.2 %collective-permute-start.17 = (bf16[64,1024]{1,0:T(8,128)(2,1)S(1)}, bf16[64,1024]{1,0:T(8,128)(2,1)S(1)}, u32[]{:S(2)}, u32[]{:S(2)}) collective-permute-start(bf16[64,1024]{1,0:T(8,128)(2,1)S(1)} %get-tuple-element.28), channel_id=1, source_target_pairs={{24,16},{25,21},{26,18},{27,23},{28,20},{29,17},{30,22},{31,19},{1... | collective-permute-start | bytes 393224 | tf_op jit(solution)/shard_map/ppermute | solution.py:240
  93.9 1.4 collective-permute-start.19
  96.1 5.9 %collective-permute-start.21 = (bf16[64,1024]{1,0:T(8,128)(2,1)S(1)}, bf16[64,1024]{1,0:T(8,128)(2,1)S(1)}, u32[]{:S(2)}, u32[]{:S(2)}) collective-permute-start(bf16[64,1024]{1,0:T(8,128)(2,1)S(1)} %get-tuple-element.30), channel_id=1, source_target_pairs={{16,10},{17,15},{18,8},{19,13},{20,14},{21,11},{22,12},{23,9},{24,... | collective-permute-start | bytes 393224 | tf_op jit(solution)/shard_map/ppermute | solution.py:240
  97.8 7.2 %collective-permute-start.20 = (bf16[64,1024]{1,0:T(8,128)(2,1)S(1)}, bf16[64,1024]{1,0:T(8,128)(2,1)S(1)}, u32[]{:S(2)}, u32[]{:S(2)}) collective-permute-start(bf16[64,1024]{1,0:T(8,128)(2,1)S(1)} %get-tuple-element.30), channel_id=1, source_target_pairs={{16,8},{17,13},{18,10},{19,15},{20,12},{21,9},{22,14},{23,11},{24,... | collective-permute-start | bytes 393224 | tf_op jit(solution)/shard_map/ppermute | solution.py:240
  106.5 1.4 collective-permute-start.22
  108.7 10.6 %collective-permute-start.24 = (bf16[64,1024]{1,0:T(8,128)(2,1)S(1)}, bf16[64,1024]{1,0:T(8,128)(2,1)S(1)}, u32[]{:S(2)}, u32[]{:S(2)}) collective-permute-start(bf16[64,1024]{1,0:T(8,128)(2,1)S(1)} %get-tuple-element.32), channel_id=1, source_target_pairs={{8,2},{9,7},{10,0},{11,5},{12,6},{13,3},{14,4},{15,1},{16,10},{17,... | collective-permute-start | bytes 393224 | tf_op jit(solution)/shard_map/ppermute | solution.py:240
  114.9 7.8 %collective-permute-start.23 = (bf16[64,1024]{1,0:T(8,128)(2,1)S(1)}, bf16[64,1024]{1,0:T(8,128)(2,1)S(1)}, u32[]{:S(2)}, u32[]{:S(2)}) collective-permute-start(bf16[64,1024]{1,0:T(8,128)(2,1)S(1)} %get-tuple-element.32), channel_id=1, source_target_pairs={{8,0},{9,5},{10,2},{11,7},{12,4},{13,1},{14,6},{15,3},{16,8},{17,1... | collective-permute-start | bytes 393224 | tf_op jit(solution)/shard_map/ppermute | solution.py:240
  124.3 1.4 collective-permute-start.25
  126.5 8.0 %collective-permute-start.27 = (bf16[64,1024]{1,0:T(8,128)(2,1)S(1)}, bf16[64,1024]{1,0:T(8,128)(2,1)S(1)}, u32[]{:S(2)}, u32[]{:S(2)}) collective-permute-start(bf16[64,1024]{1,0:T(8,128)(2,1)S(1)} %get-tuple-element.34), channel_id=1, source_target_pairs={{8,2},{9,7},{10,0},{11,5},{12,6},{13,3},{14,4},{15,1},{16,18},{17,... | collective-permute-start | bytes 393224 | tf_op jit(solution)/shard_map/ppermute | solution.py:240
  130.4 7.5 %collective-permute-start.26 = (bf16[64,1024]{1,0:T(8,128)(2,1)S(1)}, bf16[64,1024]{1,0:T(8,128)(2,1)S(1)}, u32[]{:S(2)}, u32[]{:S(2)}) collective-permute-start(bf16[64,1024]{1,0:T(8,128)(2,1)S(1)} %get-tuple-element.34), channel_id=1, source_target_pairs={{8,0},{9,5},{10,2},{11,7},{12,4},{13,1},{14,6},{15,3},{16,16},{17,... | collective-permute-start | bytes 393224 | tf_op jit(solution)/shard_map/ppermute | solution.py:240
  139.4 4.5 %collective-permute-start.28 = (bf16[64,1024]{1,0:T(8,128)(2,1)S(1)}, bf16[64,1024]{1,0:T(8,128)(2,1)S(1)}, u32[]{:S(2)}, u32[]{:S(2)}) collective-permute-start(bf16[64,1024]{1,0:T(8,128)(2,1)S(1)} %shard_map.103.mine_ref), channel_id=1, source_target_pairs={{0,1},{1,0},{2,3},{3,2},{4,5},{5,4},{6,7},{7,6},{8,9},{9,8},{10,11... | collective-permute-start | bytes 393224 | tf_op jit(solution)/shard_map/ppermute | solution.py:358
  145.4 6.3 %collective-permute-start.29 = (bf16[128,512]{1,0:T(8,128)(2,1)S(1)}, bf16[128,512]{1,0:T(8,128)(2,1)S(1)}, u32[]{:S(2)}, u32[]{:S(2)}) collective-permute-start(bf16[128,512]{1,0:T(8,128)(2,1)S(1)} %slice_select_fusion), channel_id=1, source_target_pairs={{1,2},{3,4},{5,6},{2,1},{4,3},{6,5},{9,10},{11,12},{13,14},{10,9},... | collective-permute-start | bytes 393224 | tf_op jit(solution)/shard_map/ppermute | solution.py:389
  (6 other events, 25.1 us)

commit v3 on v2

v3 whole, which is shorter than its diff:
```python
import functools

import jax
import jax.numpy as jnp
from jax import lax
from jax.experimental import pallas as pl
from jax.experimental.pallas import tpu as pltpu
from jax.sharding import PartitionSpec as P

WAVES = 2
F32 = jnp.float32
BF16 = jnp.bfloat16
VMEM = pl.BlockSpec(memory_space=pltpu.VMEM)
ANY = pl.BlockSpec(memory_space=pl.ANY)


def params(mib):
    return pltpu.CompilerParams(vmem_limit_bytes=mib * 1024 * 1024)


def in_vmem(value):
    return pltpu.with_memory_space_constraint(value, pltpu.VMEM)


def in_hbm(value):
    return pltpu.with_memory_space_constraint(value, pltpu.HBM)


def rows_dot(left, right):
    return lax.dot_general(left, right, (((1,), (1,)), ((), ())), preferred_element_type=F32)


def group_of(leaf_count, most):
    return max(g for g in range(1, most + 1) if leaf_count % g == 0)


def own_place():
    place = lax.axis_index("front")
    return place // 2, place % 2


def own_turn(turn):
    panel = lax.axis_index("panel")
    panels = lax.axis_size("panel")
    up_wave = turn - panel
    down_wave = turn - (2 * (panels - 1) - panel)
    up = (up_wave >= 0) & (up_wave < WAVES)
    down = (down_wave >= 0) & (down_wave < WAVES) & (panel < panels - 1)
    wave = jnp.where(up, up_wave, jnp.where(down, down_wave, 0))
    return up, down, wave, (panel > 0) | down


def push_kernel(
    group,
    rows_ref,
    top_ref,
    source_hbm,
    inverse_hbm,
    boundary_hbm,
    outward_ref,
    partial_ref,
    interior_ref,
    source_ref,
    inverse_ref,
    boundary_ref,
    pick_ref,
    total_ref,
    sems,
):
    leaf_count, leaf_size = inverse_ref.shape[:2]
    edge = boundary_ref.shape[1]
    rows = top_ref.shape[1]
    window = 3 * rows
    copies = []
    for step in range(leaf_count // group):
        leaves = pl.ds(step * group, group)
        lanes = pl.ds(step * group * leaf_size, group * leaf_size)
        parts = (
            (source_hbm.at[:, lanes], source_ref.at[:, lanes]),
            (inverse_hbm.at[leaves], inverse_ref.at[leaves]),
            (boundary_hbm.at[leaves], boundary_ref.at[leaves]),
        )
        copies.append(
            [pltpu.make_async_copy(a, b, sems.at[step, i]) for i, (a, b) in enumerate(parts)]
        )
        for copy in copies[-1]:
            copy.start()
    local = rows_ref[...] - (lax.axis_index("front") - 1) * rows
    spare = -leaf_count % 8
    if spare:
        local = jnp.concatenate([local, jnp.zeros((spare, edge), jnp.int32)], axis=0)
    columns = jnp.transpose(local).astype(jnp.int16)
    places = lax.broadcasted_iota(jnp.int16, (edge, window), 1)
    for step in range(leaf_count // group):
        for copy in copies[step]:
            copy.wait()
        first = step * group
        for g in range(group):
            pick_ref[step % 2, g * edge : (g + 1) * edge, :] = jnp.where(
                columns[:, first + g : first + g + 1] == places, jnp.bfloat16(1), jnp.bfloat16(0)
            )
        interior = []
        for j in range(first, first + group):
            lanes = slice(j * leaf_size, (j + 1) * leaf_size)
            interior.append(rows_dot(source_ref[:, lanes], inverse_ref[j]).astype(BF16))
            interior_ref[:, lanes] = interior[-1]
        pushed = [
            rows_dot(interior[g], boundary_ref[first + g]).astype(BF16) for g in range(group)
        ]
        total = jnp.dot(
            jnp.concatenate(pushed, axis=1), pick_ref[step % 2], preferred_element_type=F32
        )
        if step == 0:
            total_ref[...] = total
        else:
            total_ref[...] += total
    core = own_place()[1]
    top = top_ref[...].astype(F32)

    @pl.when(core == 0)
    def _():
        outward_ref[...] = total_ref[:, :rows].astype(BF16)
        partial_ref[:, :rows] = top - total_ref[:, rows : 2 * rows]
        partial_ref[:, rows:] = -total_ref[:, 2 * rows :]

    @pl.when(core != 0)
    def _():
        outward_ref[...] = total_ref[:, 2 * rows :].astype(BF16)
        partial_ref[:, :rows] = -total_ref[:, :rows]
        partial_ref[:, rows:] = top - total_ref[:, rows : 2 * rows]


def pick_kernel(rows_ref, after_ref, out_ref):
    leaf_count, edge = rows_ref.shape
    window = out_ref.shape[0]
    rows = window // 3
    place = lax.axis_index("front")
    local = rows_ref[...] - (place - 1) * rows
    shifted = jnp.where(local < rows, local + 2 * rows, local - rows)
    local = jnp.where(place % 2 == 0, shifted, local).astype(jnp.int16)
    places = lax.broadcasted_iota(jnp.int16, (window, edge), 0)
    for j in range(leaf_count):
        out_ref[:, j * edge : (j + 1) * edge] = jnp.where(
            local[j : j + 1, :] == places, jnp.bfloat16(1), jnp.bfloat16(0)
        )


def lift_matrix_kernel(group, inverse_hbm, boundary_hbm, after_ref, out_ref, inverse_ref, boundary_ref, sems):
    leaf_count = out_ref.shape[0]
    copies = []
    for step in range(leaf_count // group):
        leaves = pl.ds(step * group, group)
        parts = (
            (inverse_hbm.at[leaves], inverse_ref.at[leaves]),
            (boundary_hbm.at[leaves], boundary_ref.at[leaves]),
        )
        copies.append(
            [pltpu.make_async_copy(a, b, sems.at[step, i]) for i, (a, b) in enumerate(parts)]
        )
        for copy in copies[-1]:
            copy.start()
    for step in range(leaf_count // group):
        for copy in copies[step]:
            copy.wait()
        for j in range(step * group, (step + 1) * group):
            out_ref[j] = rows_dot(boundary_ref[j], inverse_ref[j]).astype(BF16)


def near_kernel(state_ref, pick_ref, out_ref):
    out_ref[...] = jnp.dot(
        state_ref[...], pick_ref[: state_ref.shape[1], :], preferred_element_type=F32
    ).astype(BF16)


def leaf_kernel(
    group, beside_ref, picked_ref, pick_ref, matrix_ref, interior_ref, out_hbm, out_ref, sems
):
    leaf_count, edge, leaf_size = matrix_ref.shape
    rows = beside_ref.shape[1]
    beside = beside_ref[...]
    copies = []
    for step in range(leaf_count // group):
        first = step * group
        span = slice(first * edge, (first + group) * edge)
        picked = jnp.dot(beside, pick_ref[2 * rows :, span], preferred_element_type=F32)
        picked = (picked + picked_ref[:, span].astype(F32)).astype(BF16)
        for g in range(group):
            lanes = slice((first + g) * leaf_size, (first + g + 1) * leaf_size)
            lifted = jnp.dot(
                picked[:, g * edge : (g + 1) * edge],
                matrix_ref[first + g],
                preferred_element_type=F32,
            )
            out_ref[:, lanes] = (interior_ref[:, lanes].astype(F32) - lifted).astype(BF16)
        lanes = pl.ds(first * leaf_size, group * leaf_size)
        copies.append(
            pltpu.make_async_copy(out_ref.at[:, lanes], out_hbm.at[:, lanes], sems.at[step])
        )
        copies[-1].start()
    for copy in copies:
        copy.wait()


def half_copies(parity, inverse_hbm, to_ref, sems):
    pairs = sems.shape[0]
    span = to_ref.shape[1] // pairs
    copies = []
    for q in range(pairs):
        start = pl.multiple_of((2 * q + parity) * span, span)
        copies.append(
            pltpu.make_async_copy(
                inverse_hbm.at[:, pl.ds(start, span)],
                to_ref.at[:, pl.ds(q * span, span)],
                sems.at[q],
            )
        )
        copies[-1].start()
    return copies


def half_kernel(inverse_hbm, after_ref, out_ref, sems):
    chip, core = own_place()
    for copy in half_copies((chip + core + 1) % 2, inverse_hbm, out_ref, sems):
        copy.wait()


def turn_kernel(inverse_hbm, taken_ref, out_ref, kept_ref, sems):
    columns, rows = out_ref.shape[0], taken_ref.shape[0]
    chip, core = own_place()
    copies = half_copies((chip + core) % 2, inverse_hbm, kept_ref, sems)
    span = columns // len(copies)
    piece = min(span, 256)
    for q, copy in enumerate(copies):
        copy.wait()
        for k in range(q * span, (q + 1) * span, piece):
            kept = jnp.transpose(kept_ref[:, k : k + piece])
            taken = jnp.transpose(taken_ref[:, k : k + piece])

            @pl.when(core == 0)
            def _():
                out_ref[k : k + piece, :rows] = kept
                out_ref[k : k + piece, rows:] = taken

            @pl.when(core != 0)
            def _():
                out_ref[k : k + piece, :rows] = taken
                out_ref[k : k + piece, rows:] = kept


def fold_kernel(turn, blocks, inverse_ref, *refs):
    base_refs = refs[:blocks]
    in_refs = refs[blocks : 2 * blocks] if turn else ()
    out_ref = refs[-1]
    wave_rows, rows = out_ref.shape
    forward, _, wave, fed = own_turn(turn)
    chip = own_place()[0]
    here = pl.ds(pl.multiple_of(wave * wave_rows, wave_rows), wave_rows)
    total = jnp.zeros((wave_rows, rows), F32)
    for i in range(blocks):
        if turn:
            base = jnp.where(forward, base_refs[i][here, :].astype(F32), 0.0)
            vectors = (jnp.where(fed, in_refs[i][...].astype(F32), 0.0) + base).astype(BF16)
        else:
            vectors = base_refs[i][here, :]
        place = pl.ds(pl.multiple_of(((chip // 2) ^ i) * rows, rows), rows)
        total += jnp.dot(vectors, inverse_ref[place, :], preferred_element_type=F32)
    out_ref[...] = total.astype(BF16)


def join_kernel(turn, mine_ref, other_ref, state_ref, scale_ref, next_ref, out_ref):
    wave_rows = mine_ref.shape[0]
    forward, backward, wave, _ = own_turn(turn)
    here = pl.ds(pl.multiple_of(wave * wave_rows, wave_rows), wave_rows)
    solved = (mine_ref[...].astype(F32) + other_ref[...].astype(F32)).astype(BF16).astype(F32)
    older = state_ref[here, :].astype(F32)
    field = (solved + jnp.where(backward, older, 0.0)).astype(BF16)
    scale = jnp.where(backward, scale_ref[1:2, :], scale_ref[0:1, :])
    out_ref[...] = (scale * field.astype(F32)).astype(BF16)

    @pl.when(forward | backward)
    def _():
        next_ref[here, :] = field


def turn_routes(turn, panels, waves):
    at = [s if s < panels else 2 * (panels - 1) - s for s in range(2 * panels - 1)]
    pairs = []
    for wave in range(waves):
        step = turn - wave
        if 0 <= step < 2 * (panels - 1):
            pairs.append((at[step], at[step + 1]))
    sources = [a for a, _ in pairs]
    targets = [b for _, b in pairs]
    for panel in range(panels):
        if panel not in sources and panel not in targets:
            pairs.append((panel, panel))
    spare = [p for p in targets if p not in sources]
    unfed = [p for p in sources if p not in targets]
    return pairs + list(zip(spare, unfed))


def spread(values, panel_pairs, chips):
    received = []
    for i in range(chips // 2):
        route = []
        for start, end in panel_pairs:
            for chip in range(chips):
                for core in range(2):
                    there = chip ^ (2 * i + core)
                    route.append(
                        (2 * (start * chips + chip) + core, 2 * (end * chips + there) + core)
                    )
        received.append(lax.ppermute(values, ("panel", "front"), route))
    return received


def body(top_source, leaf_source, top_inverse, leaf_inverse, boundary, touch_rows, coupling):
    sources = top_source.shape[1]
    rows = top_source.shape[2]
    width = top_inverse.shape[2]
    leaf_count, leaf_size = leaf_inverse.shape[1:3]
    edge = boundary.shape[2]
    panels = lax.axis_size("panel")
    front = lax.axis_size("front")
    chips, half = front // 2, front // 4
    chip_rows = 2 * rows
    panel = lax.axis_index("panel")
    core = lax.axis_index("front") % 2
    wave_rows = sources // WAVES
    group = group_of(leaf_count, 6)
    steps = leaf_count // group
    all_lanes = leaf_count * leaf_size

    swap_core = [(i, i ^ 1) for i in range(front)]
    swap_chip = [(i, i + 1) for i in range(1, front - 1, 2)]
    swap_chip = swap_chip + [(j, i) for i, j in swap_chip]

    outward, partial, interior = pl.pallas_call(
        functools.partial(push_kernel, group),
        out_shape=(
            pltpu.VMEM((sources, rows), BF16),
            pltpu.VMEM((sources, chip_rows), F32),
            pltpu.VMEM((sources, all_lanes), BF16),
        ),
        in_specs=[VMEM, VMEM, ANY, ANY, ANY],
        out_specs=(VMEM, VMEM, VMEM),
        scratch_shapes=[
            pltpu.VMEM((sources, all_lanes), BF16),
            pltpu.VMEM((leaf_count, leaf_size, leaf_size), BF16),
            pltpu.VMEM((leaf_count, edge, leaf_size), BF16),
            pltpu.VMEM((2, group * edge, 3 * rows), BF16),
            pltpu.VMEM((sources, 3 * rows), F32),
            pltpu.SemaphoreType.DMA((steps, 3)),
        ],
        compiler_params=params(20),
    )(
        touch_rows[0],
        top_source[0],
        in_hbm(leaf_source[0]),
        in_hbm(leaf_inverse[0]),
        in_hbm(boundary[0]),
    )
    inward = lax.ppermute(outward, "front", swap_chip)
    blank = jnp.zeros_like(partial[:, :rows])
    whole_inward = jnp.where(
        core == 0,
        jnp.concatenate([inward.astype(F32), blank], axis=1),
        jnp.concatenate([blank, inward.astype(F32)], axis=1),
    )
    partial = (partial - whole_inward).astype(BF16)
    partner = lax.ppermute(partial, "front", swap_core)
    known = (partial.astype(F32) + partner.astype(F32)).astype(BF16)
    base = [in_vmem(b) for b in spread(known, [(p, p) for p in range(panels)], chips)]

    given = pl.pallas_call(
        half_kernel,
        out_shape=jax.ShapeDtypeStruct((rows, width // 2), BF16),
        in_specs=[ANY, ANY],
        out_specs=VMEM,
        scratch_shapes=[pltpu.SemaphoreType.DMA((half,))],
        compiler_params=params(4),
    )(in_hbm(top_inverse[0]), outward)
    taken = lax.ppermute(given, "front", swap_core)
    inverse = pl.pallas_call(
        turn_kernel,
        out_shape=pltpu.VMEM((width // 2, chip_rows), BF16),
        in_specs=[ANY, VMEM],
        out_specs=VMEM,
        scratch_shapes=[
            pltpu.VMEM((rows, width // 2), BF16),
            pltpu.SemaphoreType.DMA((half,)),
        ],
        compiler_params=params(8),
    )(in_hbm(top_inverse[0]), taken)
    inverse = in_vmem(inverse)

    coupling, _ = lax.optimization_barrier((coupling, outward))
    later = lax.ppermute(coupling, "panel", [((p + 1) % panels, p) for p in range(panels)])
    forward_scale = jnp.where(panel == panels - 1, coupling, later)
    scales = jnp.concatenate([forward_scale, coupling], axis=0)
    partner_scales = lax.ppermute(scales, "front", swap_core)
    scales = jnp.where(
        core == 0,
        jnp.concatenate([scales, partner_scales], axis=1),
        jnp.concatenate([partner_scales, scales], axis=1),
    )
    scales = in_vmem(scales)
    state = jnp.zeros((sources, chip_rows), BF16)
    turns = 2 * (panels - 1) + WAVES
    arrived, extra = [], []
    for turn in range(turns):
        share = pl.pallas_call(
            functools.partial(fold_kernel, turn, half),
            out_shape=pltpu.VMEM((wave_rows, chip_rows), BF16),
            in_specs=[VMEM] * (1 + half + len(arrived)) + [ANY] * len(extra),
            out_specs=VMEM,
            compiler_params=params(4),
        )(inverse, *base, *arrived, *extra)
        extra = []
        other = lax.ppermute(share, "front", swap_core)
        state, outgoing = pl.pallas_call(
            functools.partial(join_kernel, turn),
            out_shape=(
                pltpu.VMEM((sources, chip_rows), BF16),
                pltpu.VMEM((wave_rows, chip_rows), BF16),
            ),
            in_specs=[VMEM] * 4,
            out_specs=(VMEM, VMEM),
            input_output_aliases={2: 0},
            compiler_params=params(4),
        )(in_vmem(share), in_vmem(other), in_vmem(state), scales)
        if turn < turns - 1:
            routes = turn_routes(turn, panels, WAVES)
            arrived = [in_vmem(a) for a in spread(outgoing, routes, chips)]
        if turn == 1:
            picks = pl.pallas_call(
                pick_kernel,
                out_shape=pltpu.VMEM((3 * rows, leaf_count * edge), BF16),
                in_specs=[VMEM, ANY],
                out_specs=VMEM,
                compiler_params=params(4),
                cost_estimate=pl.CostEstimate(
                    flops=4 * sources * rows * leaf_count * edge,
                    bytes_accessed=6 * rows * leaf_count * edge,
                    transcendentals=0,
                ),
            )(touch_rows[0], outgoing)
            extra = [in_vmem(picks)]
        if turn == 2:
            matrices = pl.pallas_call(
                functools.partial(lift_matrix_kernel, group),
                out_shape=pltpu.VMEM((leaf_count, edge, leaf_size), BF16),
                in_specs=[ANY, ANY, ANY],
                out_specs=VMEM,
                scratch_shapes=[
                    pltpu.VMEM((leaf_count, leaf_size, leaf_size), BF16),
                    pltpu.VMEM((leaf_count, edge, leaf_size), BF16),
                    pltpu.SemaphoreType.DMA((steps, 2)),
                ],
                compiler_params=params(12),
                cost_estimate=pl.CostEstimate(
                    flops=2 * leaf_count * edge * leaf_size * leaf_size,
                    bytes_accessed=4 * leaf_count * leaf_size * leaf_size,
                    transcendentals=0,
                ),
            )(in_hbm(leaf_inverse[0]), in_hbm(boundary[0]), outgoing)
            extra = [in_vmem(matrices)]

    top_field = jnp.where(core == 0, state[:, :rows], state[:, rows:])
    beside = lax.ppermute(top_field, "front", swap_chip)
    picked = pl.pallas_call(
        near_kernel,
        out_shape=pltpu.VMEM((sources, leaf_count * edge), BF16),
        in_specs=[VMEM] * 2,
        out_specs=VMEM,
        compiler_params=params(8),
        cost_estimate=pl.CostEstimate(
            flops=4 * sources * rows * leaf_count * edge,
            bytes_accessed=4 * rows * leaf_count * edge,
            transcendentals=0,
        ),
    )(in_vmem(state), in_vmem(picks))
    leaf_field = pl.pallas_call(
        functools.partial(leaf_kernel, group),
        out_shape=jax.ShapeDtypeStruct((sources, all_lanes), BF16),
        in_specs=[VMEM] * 5,
        out_specs=ANY,
        scratch_shapes=[
            pltpu.VMEM((sources, all_lanes), BF16),
            pltpu.SemaphoreType.DMA((steps,)),
        ],
        compiler_params=params(8),
    )(in_vmem(beside), in_vmem(picked), in_vmem(picks), in_vmem(matrices), in_vmem(interior))
    return (top_field[None], leaf_field[None])


def solution(mesh):
    placed = (
        P("panel", None, "front"),
        P("panel", None, "front"),
        P("panel", "front", None),
        P("panel", "front", None, None),
        P("panel", "front", None, None),
        P("panel", "front", None),
        P("panel", "front"),
    )
    return jax.shard_map(
        body,
        mesh=mesh,
        in_specs=placed,
        out_specs=(P("panel", None, "front"), P("panel", None, "front")),
        check_vma=False,
    )
```

time: 156 us -> 143 us (0.917)
  Pallas kernels: 42.3 us -> 31.4 us
  waiting for transfers between devices: 56.4 us -> 46.6 us
  starting transfers between devices: 51.9 us -> 60.8 us
    ppermute x16, waiting for transfers between devices: 39.8 us -> 30.3 us  [spread(): received.append(lax.ppermute(values, ('panel', 'front'), route))]
    ppermute x8, starting transfers between devices: 0.57 us -> 9.3 us  [body(): other = lax.ppermute(share, 'front', swap_core)]
    pallas_call x8, Pallas kernels: 6.76 us -> 1.32 us  [body(): pl.pallas_call(functools.partial(join_kernel, turn), out_shape=(pltpu.VME...]
    pallas_call x8, Pallas kernels: 12.2 us -> 6.76 us  [body(): pl.pallas_call(functools.partial(fold_kernel, turn, half), out_shape=pltp...]
    pallas_call x2 -> x3, Pallas kernels: 5.29 us -> 8.01 us  [the longest x1 3.71 us: body(): pl.pallas_call(functools.partial(lift_matrix_kernel, group), out_shape=pl...]
  transfers between devices with their start and end apart: 30 -> 30, of which waited for: 26 -> 25; matrix products, arithmetic and copies ran while one was open for 1% -> 1% of each run, Pallas kernels for 10% -> 8%
where the time goes in v3:
time: 143 us; the launch traced here: 142 us
  starting transfers between devices  60.8 us (43%)
  waiting for transfers between devices  46.6 us (33%)
  Pallas kernels  31.4 us (22%)
  local copies, waits for them, and re-layouts  1.66 us (1%)
    ppermute x16, starting transfers between devices, spread(): received.append(lax.ppermute(values, ('panel', 'front'), route))  42.5 us
    ppermute x16, waiting for transfers between devices, spread(): received.append(lax.ppermute(values, ('panel', 'front'), route))  30.3 us
    ppermute x8, starting transfers between devices, body(): other = lax.ppermute(share, 'front', swap_core)  9.3 us
    ppermute x8, waiting for transfers between devices, body(): other = lax.ppermute(share, 'front', swap_core)  7.95 us
    pallas_call x8, Pallas kernels, body(): pl.pallas_call(functools.partial(fold_kernel, turn, half), out_shape=pltp...  6.76 us
    pallas_call x1, Pallas kernels, body(): pl.pallas_call(functools.partial(push_kernel, group), out_shape=(pltpu.VM...  5.99 us
    pallas_call x1, Pallas kernels, body(): pl.pallas_call(turn_kernel, out_shape=pltpu.VMEM((width // 2, chip_rows),...  4.64 us
    ppermute x1, starting transfers between devices, body(): inward = lax.ppermute(outward, 'front', swap_chip)  4.55 us
  transfers between devices with their start and end apart: 30, of which 25 were waited for; matrix products, arithmetic and copies ran while one was open for 1% of the time, Pallas kernels for 8%

profile of v3, /device:TPU:1, one launch (start us, length us, event | category | flops | bytes accessed | tf_op | source)
XLA Modules:
  0.0 142.4 jit_solution(13080048350490484163)
XLA Ops:
  2.3 6.0 %shard_map.86 = (bf16[128,512]{1,0:T(8,128)(2,1)S(1)}, f32[128,1024]{1,0:T(8,128)S(1)}, bf16[128,9216]{1,0:T(8,128)(2,1)S(1)}) custom-call(s32[36,128]{1,0:T(8,128)S(1)} %bitcast.11, bf16[128,512]{1,0:T(8,128)(2,1)S(1)} %bitcast.13, bf16[128,9216]{1,0:T(8,128)(2,1)} %bitcast.20, bf16[36,256,256]{2,1,0:T(8,128)(2,1)} %bitcast.14, bf16[36,128,256]{2,1,0:T(8,128)(2,1)} %bitcast.18), custom_call_target="tpu_custom_call" | custom-call | tf_op jit(solution)/shard_map/pallas_call | solution.py:338
  8.3 2.9 %shard_map.87 = bf16[512,2048]{1,0:T(8,128)(2,1)} custom-call(bf16[512,4096]{1,0:T(8,128)(2,1)} %bitcast.16, bf16[128,512]{1,0:T(8,128)(2,1)S(1)} %get-tuple-element.21.after_ref), custom_call_target="tpu_custom_call" | custom-call | tf_op jit(solution)/shard_map/pallas_call | solution.py:375
  11.3 4.6 %collective-permute-start.1 = (bf16[128,512]{1,0:T(8,128)(2,1)S(1)}, bf16[128,512]{1,0:T(8,128)(2,1)S(1)}, u32[]{:S(2)}, u32[]{:S(2)}) collective-permute-start(bf16[128,512]{1,0:T(8,128)(2,1)S(1)} %get-tuple-element.21.after_ref), channel_id=1, source_target_pairs={{1,2},{3,4},{5,6},{2,1},{4,3},{6,5},{9,10},{11,12},{13,14},{10,9},... | collective-permute-start | bytes 393224 | tf_op jit(solution)/shard_map/ppermute | solution.py:363
  15.9 2.6 %collective-permute-done.1 = bf16[128,512]{1,0:T(8,128)(2,1)S(1)} collective-permute-done((bf16[128,512]{1,0:T(8,128)(2,1)S(1)}, bf16[128,512]{1,0:T(8,128)(2,1)S(1)}, u32[]{:S(2)}, u32[]{:S(2)}) %collective-permute-start.1) | collective-permute-done | bytes 131104 | tf_op jit(solution)/shard_map/ppermute | solution.py:363
  20.2 3.6 %collective-permute-start.4 = (bf16[128,1024]{1,0:T(8,128)(2,1)S(1)}, bf16[128,1024]{1,0:T(8,128)(2,1)S(1)}, u32[]{:S(2)}, u32[]{:S(2)}) collective-permute-start(bf16[128,1024]{1,0:T(8,128)(2,1)S(1)} %add_convert_fusion), channel_id=1, source_target_pairs={{0,4},{1,7},{2,6},{3,5},{4,0},{5,3},{6,2},{7,1},{8,12},{9,15},{10,... | collective-permute-start | bytes 786440 | tf_op jit(solution)/shard_map/ppermute | solution.py:313
  23.8 1.9 %collective-permute-start.3 = (bf16[128,1024]{1,0:T(8,128)(2,1)S(1)}, bf16[128,1024]{1,0:T(8,128)(2,1)S(1)}, u32[]{:S(2)}, u32[]{:S(2)}) collective-permute-start(bf16[128,1024]{1,0:T(8,128)(2,1)S(1)} %add_convert_fusion), channel_id=1, source_target_pairs={{0,0},{1,3},{2,2},{3,1},{4,4},{5,7},{6,6},{7,5},{8,8},{9,11},{10,1... | collective-permute-start | bytes 786440 | tf_op jit(solution)/shard_map/ppermute | solution.py:313
  25.7 2.2 %collective-permute-start.6 = (f32[1,512]{1,0:T(1,128)S(1)}, f32[1,512]{1,0:T(1,128)S(1)}, u32[]{:S(2)}, u32[]{:S(2)}) collective-permute-start(f32[1,512]{1,0:T(1,128)S(1)} %copy-done.1), channel_id=1, source_target_pairs={{8,0},{16,8},{24,16},{0,24},{9,1},{17,9},{25,17},{1,25},{10,2},{18... | collective-permute-start | bytes 6152 | tf_op jit(solution)/shard_map/ppermute | solution.py:398
  28.7 4.6 %shard_map.88.inverse_ref = bf16[2048,1024]{1,0:T(8,128)(2,1)S(1)} custom-call(bf16[512,4096]{1,0:T(8,128)(2,1)} %bitcast.17, bf16[512,2048]{1,0:T(8,128)(2,1)} %collective-permute-done.taken_ref), custom_call_target="tpu_custom_call" | custom-call | tf_op jit(solution)/shard_map/pallas_call | solution.py:384
  34.2 2.9 %collective-permute-start.5 = (bf16[64,1024]{1,0:T(8,128)(2,1)S(1)}, bf16[64,1024]{1,0:T(8,128)(2,1)S(1)}, u32[]{:S(2)}, u32[]{:S(2)}) collective-permute-start(bf16[64,1024]{1,0:T(8,128)(2,1)S(1)} %shard_map.89.mine_ref), channel_id=1, source_target_pairs={{0,1},{1,0},{2,3},{3,2},{4,5},{5,4},{6,7},{7,6},{8,9},{9,8},{10,11... | collective-permute-start | bytes 393224 | tf_op jit(solution)/shard_map/ppermute | solution.py:420
  38.5 3.2 %collective-permute-start.9 = (bf16[64,1024]{1,0:T(8,128)(2,1)S(1)}, bf16[64,1024]{1,0:T(8,128)(2,1)S(1)}, u32[]{:S(2)}, u32[]{:S(2)}) collective-permute-start(bf16[64,1024]{1,0:T(8,128)(2,1)S(1)} %get-tuple-element.24), channel_id=1, source_target_pairs={{0,12},{1,15},{2,14},{3,13},{4,8},{5,11},{6,10},{7,9},{16,20},{17,... | collective-permute-start | bytes 393224 | tf_op jit(solution)/shard_map/ppermute | solution.py:313
  41.6 1.9 %collective-permute-start.8 = (bf16[64,1024]{1,0:T(8,128)(2,1)S(1)}, bf16[64,1024]{1,0:T(8,128)(2,1)S(1)}, u32[]{:S(2)}, u32[]{:S(2)}) collective-permute-start(bf16[64,1024]{1,0:T(8,128)(2,1)S(1)} %get-tuple-element.24), channel_id=1, source_target_pairs={{0,8},{1,11},{2,10},{3,9},{4,12},{5,15},{6,14},{7,13},{16,16},{17,... | collective-permute-start | bytes 393224 | tf_op jit(solution)/shard_map/ppermute | solution.py:313
  43.6 2.3 %collective-permute-done.9.refs_3_ = bf16[64,1024]{1,0:T(8,128)(2,1)S(1)} collective-permute-done((bf16[64,1024]{1,0:T(8,128)(2,1)S(1)}, bf16[64,1024]{1,0:T(8,128)(2,1)S(1)}, u32[]{:S(2)}, u32[]{:S(2)}) %collective-permute-start.9) | collective-permute-done | bytes 131104 | tf_op jit(solution)/shard_map/ppermute | solution.py:313
  45.9 2.7 %collective-permute-done.8.refs_2_ = bf16[64,1024]{1,0:T(8,128)(2,1)S(1)} collective-permute-done((bf16[64,1024]{1,0:T(8,128)(2,1)S(1)}, bf16[64,1024]{1,0:T(8,128)(2,1)S(1)}, u32[]{:S(2)}, u32[]{:S(2)}) %collective-permute-start.8) | collective-permute-done | bytes 131104 | tf_op jit(solution)/shard_map/ppermute | solution.py:313
  52.1 2.8 %collective-permute-start.12 = (bf16[64,1024]{1,0:T(8,128)(2,1)S(1)}, bf16[64,1024]{1,0:T(8,128)(2,1)S(1)}, u32[]{:S(2)}, u32[]{:S(2)}) collective-permute-start(bf16[64,1024]{1,0:T(8,128)(2,1)S(1)} %get-tuple-element.26.after_ref), channel_id=1, source_target_pairs={{8,20},{9,23},{10,22},{11,21},{12,16},{13,19},{14,18},{15,17},{0,1... | collective-permute-start | bytes 393224 | tf_op jit(solution)/shard_map/ppermute | solution.py:313
  54.8 1.9 %collective-permute-start.11 = (bf16[64,1024]{1,0:T(8,128)(2,1)S(1)}, bf16[64,1024]{1,0:T(8,128)(2,1)S(1)}, u32[]{:S(2)}, u32[]{:S(2)}) collective-permute-start(bf16[64,1024]{1,0:T(8,128)(2,1)S(1)} %get-tuple-element.26.after_ref), channel_id=1, source_target_pairs={{8,16},{9,19},{10,18},{11,17},{12,20},{13,23},{14,22},{15,21},{0,8... | collective-permute-start | bytes 393224 | tf_op jit(solution)/shard_map/ppermute | solution.py:313
  56.7 2.1 %shard_map.93.refs_4_.pick_ref = bf16[1536,4608]{1,0:T(8,128)(2,1)S(1)} custom-call(s32[36,128]{1,0:T(8,128)S(1)} %bitcast.12, bf16[64,1024]{1,0:T(8,128)(2,1)S(1)} %get-tuple-element.26.after_ref), custom_call_target="tpu_custom_call" | custom-call | flops 1207959552 | bytes 14155776 | tf_op jit(solution)/shard_map/pallas_call | solution.py:436
  59.2 2.7 %collective-permute-done.11.refs_2_ = bf16[64,1024]{1,0:T(8,128)(2,1)S(1)} collective-permute-done((bf16[64,1024]{1,0:T(8,128)(2,1)S(1)}, bf16[64,1024]{1,0:T(8,128)(2,1)S(1)}, u32[]{:S(2)}, u32[]{:S(2)}) %collective-permute-start.11) | collective-permute-done | bytes 131104 | tf_op jit(solution)/shard_map/ppermute | solution.py:313
  62.7 2.0 %collective-permute-start.13 = (bf16[64,1024]{1,0:T(8,128)(2,1)S(1)}, bf16[64,1024]{1,0:T(8,128)(2,1)S(1)}, u32[]{:S(2)}, u32[]{:S(2)}) collective-permute-start(bf16[64,1024]{1,0:T(8,128)(2,1)S(1)} %shard_map.94.mine_ref), channel_id=1, source_target_pairs={{0,1},{1,0},{2,3},{3,2},{4,5},{5,4},{6,7},{7,6},{8,9},{9,8},{10,11... | collective-permute-start | bytes 393224 | tf_op jit(solution)/shard_map/ppermute | solution.py:420
  67.3 2.1 %collective-permute-start.14 = (bf16[64,1024]{1,0:T(8,128)(2,1)S(1)}, bf16[64,1024]{1,0:T(8,128)(2,1)S(1)}, u32[]{:S(2)}, u32[]{:S(2)}) collective-permute-start(bf16[64,1024]{1,0:T(8,128)(2,1)S(1)} %get-tuple-element.28.after_ref), channel_id=1, source_target_pairs={{16,24},{17,27},{18,26},{19,25},{20,28},{21,31},{22,30},{23,29},{8... | collective-permute-start | bytes 393224 | tf_op jit(solution)/shard_map/ppermute | solution.py:313
  69.4 3.7 %shard_map.96.refs_4_.matrix_ref = bf16[36,128,256]{2,1,0:T(8,128)(2,1)S(1)} custom-call(bf16[36,256,256]{2,1,0:T(8,128)(2,1)} %bitcast.15, bf16[36,128,256]{2,1,0:T(8,128)(2,1)} %bitcast.19, bf16[64,1024]{1,0:T(8,128)(2,1)S(1)} %get-tuple-element.28.after_ref), custom_call_target="tpu_custom_call" | custom-call | flops 603979776 | bytes 9437184 | tf_op jit(solution)/shard_map/pallas_call | solution.py:450
  80.5 3.1 %collective-permute-done.18.refs_3_ = bf16[64,1024]{1,0:T(8,128)(2,1)S(1)} collective-permute-done((bf16[64,1024]{1,0:T(8,128)(2,1)S(1)}, bf16[64,1024]{1,0:T(8,128)(2,1)S(1)}, u32[]{:S(2)}, u32[]{:S(2)}) %collective-permute-start.18) | collective-permute-done | bytes 131104 | tf_op jit(solution)/shard_map/ppermute | solution.py:313
  83.6 2.4 %collective-permute-done.17.refs_2_ = bf16[64,1024]{1,0:T(8,128)(2,1)S(1)} collective-permute-done((bf16[64,1024]{1,0:T(8,128)(2,1)S(1)}, bf16[64,1024]{1,0:T(8,128)(2,1)S(1)}, u32[]{:S(2)}, u32[]{:S(2)}) %collective-permute-start.17) | collective-permute-done | bytes 131104 | tf_op jit(solution)/shard_map/ppermute | solution.py:313
  92.0 2.6 %collective-permute-done.21.refs_3_ = bf16[64,1024]{1,0:T(8,128)(2,1)S(1)} collective-permute-done((bf16[64,1024]{1,0:T(8,128)(2,1)S(1)}, bf16[64,1024]{1,0:T(8,128)(2,1)S(1)}, u32[]{:S(2)}, u32[]{:S(2)}) %collective-permute-start.21) | collective-permute-done | bytes 131104 | tf_op jit(solution)/shard_map/ppermute | solution.py:313
  94.6 2.7 %collective-permute-done.20.refs_2_ = bf16[64,1024]{1,0:T(8,128)(2,1)S(1)} collective-permute-done((bf16[64,1024]{1,0:T(8,128)(2,1)S(1)}, bf16[64,1024]{1,0:T(8,128)(2,1)S(1)}, u32[]{:S(2)}, u32[]{:S(2)}) %collective-permute-start.20) | collective-permute-done | bytes 131104 | tf_op jit(solution)/shard_map/ppermute | solution.py:313
  99.7 9.0 %collective-permute-start.24 = (bf16[64,1024]{1,0:T(8,128)(2,1)S(1)}, bf16[64,1024]{1,0:T(8,128)(2,1)S(1)}, u32[]{:S(2)}, u32[]{:S(2)}) collective-permute-start(bf16[64,1024]{1,0:T(8,128)(2,1)S(1)} %get-tuple-element.34), channel_id=1, source_target_pairs={{8,4},{9,7},{10,6},{11,5},{12,0},{13,3},{14,2},{15,1},{16,12},{17,... | collective-permute-start | bytes 393224 | tf_op jit(solution)/shard_map/ppermute | solution.py:313
  111.0 4.3 %collective-permute-done.23.refs_2_ = bf16[64,1024]{1,0:T(8,128)(2,1)S(1)} collective-permute-done((bf16[64,1024]{1,0:T(8,128)(2,1)S(1)}, bf16[64,1024]{1,0:T(8,128)(2,1)S(1)}, u32[]{:S(2)}, u32[]{:S(2)}) %collective-permute-start.23) | collective-permute-done | bytes 131104 | tf_op jit(solution)/shard_map/ppermute | solution.py:313
  118.5 3.6 %collective-permute-start.27 = (bf16[64,1024]{1,0:T(8,128)(2,1)S(1)}, bf16[64,1024]{1,0:T(8,128)(2,1)S(1)}, u32[]{:S(2)}, u32[]{:S(2)}) collective-permute-start(bf16[64,1024]{1,0:T(8,128)(2,1)S(1)} %get-tuple-element.36), channel_id=1, source_target_pairs={{8,4},{9,7},{10,6},{11,5},{12,0},{13,3},{14,2},{15,1},{16,20},{17,... | collective-permute-start | bytes 393224 | tf_op jit(solution)/shard_map/ppermute | solution.py:313
  124.0 2.6 %collective-permute-done.27.refs_3_ = bf16[64,1024]{1,0:T(8,128)(2,1)S(1)} collective-permute-done((bf16[64,1024]{1,0:T(8,128)(2,1)S(1)}, bf16[64,1024]{1,0:T(8,128)(2,1)S(1)}, u32[]{:S(2)}, u32[]{:S(2)}) %collective-permute-start.27) | collective-permute-done | bytes 131104 | tf_op jit(solution)/shard_map/ppermute | solution.py:313
  126.5 2.7 %collective-permute-done.26.refs_2_ = bf16[64,1024]{1,0:T(8,128)(2,1)S(1)} collective-permute-done((bf16[64,1024]{1,0:T(8,128)(2,1)S(1)}, bf16[64,1024]{1,0:T(8,128)(2,1)S(1)}, u32[]{:S(2)}, u32[]{:S(2)}) %collective-permute-start.26) | collective-permute-done | bytes 131104 | tf_op jit(solution)/shard_map/ppermute | solution.py:313
  133.4 1.9 %collective-permute-start.29 = (bf16[128,512]{1,0:T(8,128)(2,1)S(1)}, bf16[128,512]{1,0:T(8,128)(2,1)S(1)}, u32[]{:S(2)}, u32[]{:S(2)}) collective-permute-start(bf16[128,512]{1,0:T(8,128)(2,1)S(1)} %slice_select_fusion), channel_id=1, source_target_pairs={{1,2},{3,4},{5,6},{2,1},{4,3},{6,5},{9,10},{11,12},{13,14},{10,9},... | collective-permute-start | bytes 393224 | tf_op jit(solution)/shard_map/ppermute | solution.py:470
  137.4 2.3 %collective-permute-done.29.beside_ref = bf16[128,512]{1,0:T(8,128)(2,1)S(1)} collective-permute-done((bf16[128,512]{1,0:T(8,128)(2,1)S(1)}, bf16[128,512]{1,0:T(8,128)(2,1)S(1)}, u32[]{:S(2)}, u32[]{:S(2)}) %collective-permute-start.29) | collective-permute-done | bytes 131104 | tf_op jit(solution)/shard_map/ppermute | solution.py:470
  139.7 2.6 %shard_map.108 = bf16[128,9216]{1,0:T(8,128)(2,1)} custom-call(bf16[128,512]{1,0:T(8,128)(2,1)S(1)} %collective-permute-done.29.beside_ref, bf16[128,4608]{1,0:T(8,128)(2,1)S(1)} %shard_map.107.picked_ref, bf16[1536,4608]{1,0:T(8,128)(2,1)S(1)} %shard_map.93.refs_4_.pick_ref, bf16[36,128,256]{2,1,0:T(8,128)(2,1)S(1)} %shard_map.96.refs_4_.matrix_ref, ...), custom_call_target="tpu_custom_call" | custom-call | tf_op jit(solution)/shard_map/pallas_call | solution.py:483
  (65 shorter events, 42.9 us)
Async XLA Ops:
  1.4 0.9 copy-start
  8.3 17.5 %copy-start.1 = (f32[1,512]{1,0:T(1,128)S(1)}, f32[1,512]{1,0:T(1,128)}, u32[]{:S(2)}) copy-start(f32[1,512]{1,0:T(1,128)} %param.13) | copy-start | bytes 6148
  11.2 17.5 %collective-permute-start = (bf16[512,2048]{1,0:T(8,128)(2,1)}, bf16[512,2048]{1,0:T(8,128)(2,1)}, u32[]{:S(2)}, u32[]{:S(2)}) collective-permute-start(bf16[512,2048]{1,0:T(8,128)(2,1)} %shard_map.87), channel_id=1, source_target_pairs={{0,1},{1,0},{2,3},{3,2},{4,5},{5,4},{6,7},{7,6},{8,9},{9,8},{10,11... | collective-permute-start | bytes 6291464 | tf_op jit(solution)/shard_map/ppermute | solution.py:383
  11.3 7.2 %collective-permute-start.1 = (bf16[128,512]{1,0:T(8,128)(2,1)S(1)}, bf16[128,512]{1,0:T(8,128)(2,1)S(1)}, u32[]{:S(2)}, u32[]{:S(2)}) collective-permute-start(bf16[128,512]{1,0:T(8,128)(2,1)S(1)} %get-tuple-element.21.after_ref), channel_id=1, source_target_pairs={{1,2},{3,4},{5,6},{2,1},{4,3},{6,5},{9,10},{11,12},{13,14},{10,9},... | collective-permute-start | bytes 393224 | tf_op jit(solution)/shard_map/ppermute | solution.py:363
  18.6 1.6 %collective-permute-start.2 = (bf16[128,1024]{1,0:T(8,128)(2,1)S(1)}, bf16[128,1024]{1,0:T(8,128)(2,1)S(1)}, u32[]{:S(2)}, u32[]{:S(2)}) collective-permute-start(bf16[128,1024]{1,0:T(8,128)(2,1)S(1)} %subtract_convert_fusion), channel_id=1, source_target_pairs={{0,1},{1,0},{2,3},{3,2},{4,5},{5,4},{6,7},{7,6},{8,9},{9,8},{10,11... | collective-permute-start | bytes 786440 | tf_op jit(solution)/shard_map/ppermute | solution.py:371
  20.2 13.1 %collective-permute-start.4 = (bf16[128,1024]{1,0:T(8,128)(2,1)S(1)}, bf16[128,1024]{1,0:T(8,128)(2,1)S(1)}, u32[]{:S(2)}, u32[]{:S(2)}) collective-permute-start(bf16[128,1024]{1,0:T(8,128)(2,1)S(1)} %add_convert_fusion), channel_id=1, source_target_pairs={{0,4},{1,7},{2,6},{3,5},{4,0},{5,3},{6,2},{7,1},{8,12},{9,15},{10,... | collective-permute-start | bytes 786440 | tf_op jit(solution)/shard_map/ppermute | solution.py:313
  23.8 9.5 %collective-permute-start.3 = (bf16[128,1024]{1,0:T(8,128)(2,1)S(1)}, bf16[128,1024]{1,0:T(8,128)(2,1)S(1)}, u32[]{:S(2)}, u32[]{:S(2)}) collective-permute-start(bf16[128,1024]{1,0:T(8,128)(2,1)S(1)} %add_convert_fusion), channel_id=1, source_target_pairs={{0,0},{1,3},{2,2},{3,1},{4,4},{5,7},{6,6},{7,5},{8,8},{9,11},{10,1... | collective-permute-start | bytes 786440 | tf_op jit(solution)/shard_map/ppermute | solution.py:313
  25.7 3.0 %collective-permute-start.6 = (f32[1,512]{1,0:T(1,128)S(1)}, f32[1,512]{1,0:T(1,128)S(1)}, u32[]{:S(2)}, u32[]{:S(2)}) collective-permute-start(f32[1,512]{1,0:T(1,128)S(1)} %copy-done.1), channel_id=1, source_target_pairs={{8,0},{16,8},{24,16},{0,24},{9,1},{17,9},{25,17},{1,25},{10,2},{18... | collective-permute-start | bytes 6152 | tf_op jit(solution)/shard_map/ppermute | solution.py:398
  34.2 4.1 %collective-permute-start.5 = (bf16[64,1024]{1,0:T(8,128)(2,1)S(1)}, bf16[64,1024]{1,0:T(8,128)(2,1)S(1)}, u32[]{:S(2)}, u32[]{:S(2)}) collective-permute-start(bf16[64,1024]{1,0:T(8,128)(2,1)S(1)} %shard_map.89.mine_ref), channel_id=1, source_target_pairs={{0,1},{1,0},{2,3},{3,2},{4,5},{5,4},{6,7},{7,6},{8,9},{9,8},{10,11... | collective-permute-start | bytes 393224 | tf_op jit(solution)/shard_map/ppermute | solution.py:420
  37.1 1.2 collective-permute-start.7
  38.5 7.4 %collective-permute-start.9 = (bf16[64,1024]{1,0:T(8,128)(2,1)S(1)}, bf16[64,1024]{1,0:T(8,128)(2,1)S(1)}, u32[]{:S(2)}, u32[]{:S(2)}) collective-permute-start(bf16[64,1024]{1,0:T(8,128)(2,1)S(1)} %get-tuple-element.24), channel_id=1, source_target_pairs={{0,12},{1,15},{2,14},{3,13},{4,8},{5,11},{6,10},{7,9},{16,20},{17,... | collective-permute-start | bytes 393224 | tf_op jit(solution)/shard_map/ppermute | solution.py:313
  41.6 7.0 %collective-permute-start.8 = (bf16[64,1024]{1,0:T(8,128)(2,1)S(1)}, bf16[64,1024]{1,0:T(8,128)(2,1)S(1)}, u32[]{:S(2)}, u32[]{:S(2)}) collective-permute-start(bf16[64,1024]{1,0:T(8,128)(2,1)S(1)} %get-tuple-element.24), channel_id=1, source_target_pairs={{0,8},{1,11},{2,10},{3,9},{4,12},{5,15},{6,14},{7,13},{16,16},{17,... | collective-permute-start | bytes 393224 | tf_op jit(solution)/shard_map/ppermute | solution.py:313
  49.5 2.5 %collective-permute-start.10 = (bf16[64,1024]{1,0:T(8,128)(2,1)S(1)}, bf16[64,1024]{1,0:T(8,128)(2,1)S(1)}, u32[]{:S(2)}, u32[]{:S(2)}) collective-permute-start(bf16[64,1024]{1,0:T(8,128)(2,1)S(1)} %shard_map.91.mine_ref), channel_id=1, source_target_pairs={{0,1},{1,0},{2,3},{3,2},{4,5},{5,4},{6,7},{7,6},{8,9},{9,8},{10,11... | collective-permute-start | bytes 393224 | tf_op jit(solution)/shard_map/ppermute | solution.py:420
  52.1 7.1 %collective-permute-start.12 = (bf16[64,1024]{1,0:T(8,128)(2,1)S(1)}, bf16[64,1024]{1,0:T(8,128)(2,1)S(1)}, u32[]{:S(2)}, u32[]{:S(2)}) collective-permute-start(bf16[64,1024]{1,0:T(8,128)(2,1)S(1)} %get-tuple-element.26.after_ref), channel_id=1, source_target_pairs={{8,20},{9,23},{10,22},{11,21},{12,16},{13,19},{14,18},{15,17},{0,1... | collective-permute-start | bytes 393224 | tf_op jit(solution)/shard_map/ppermute | solution.py:313
  54.8 7.1 %collective-permute-start.11 = (bf16[64,1024]{1,0:T(8,128)(2,1)S(1)}, bf16[64,1024]{1,0:T(8,128)(2,1)S(1)}, u32[]{:S(2)}, u32[]{:S(2)}) collective-permute-start(bf16[64,1024]{1,0:T(8,128)(2,1)S(1)} %get-tuple-element.26.after_ref), channel_id=1, source_target_pairs={{8,16},{9,19},{10,18},{11,17},{12,20},{13,23},{14,22},{15,21},{0,8... | collective-permute-start | bytes 393224 | tf_op jit(solution)/shard_map/ppermute | solution.py:313
  62.7 2.9 %collective-permute-start.13 = (bf16[64,1024]{1,0:T(8,128)(2,1)S(1)}, bf16[64,1024]{1,0:T(8,128)(2,1)S(1)}, u32[]{:S(2)}, u32[]{:S(2)}) collective-permute-start(bf16[64,1024]{1,0:T(8,128)(2,1)S(1)} %shard_map.94.mine_ref), channel_id=1, source_target_pairs={{0,1},{1,0},{2,3},{3,2},{4,5},{5,4},{6,7},{7,6},{8,9},{9,8},{10,11... | collective-permute-start | bytes 393224 | tf_op jit(solution)/shard_map/ppermute | solution.py:420
  65.7 7.3 %collective-permute-start.15 = (bf16[64,1024]{1,0:T(8,128)(2,1)S(1)}, bf16[64,1024]{1,0:T(8,128)(2,1)S(1)}, u32[]{:S(2)}, u32[]{:S(2)}) collective-permute-start(bf16[64,1024]{1,0:T(8,128)(2,1)S(1)} %get-tuple-element.28.after_ref), channel_id=1, source_target_pairs={{16,28},{17,31},{18,30},{19,29},{20,24},{21,27},{22,26},{23,25},{8... | collective-permute-start | bytes 393224 | tf_op jit(solution)/shard_map/ppermute | solution.py:313
  67.3 7.1 %collective-permute-start.14 = (bf16[64,1024]{1,0:T(8,128)(2,1)S(1)}, bf16[64,1024]{1,0:T(8,128)(2,1)S(1)}, u32[]{:S(2)}, u32[]{:S(2)}) collective-permute-start(bf16[64,1024]{1,0:T(8,128)(2,1)S(1)} %get-tuple-element.28.after_ref), channel_id=1, source_target_pairs={{16,24},{17,27},{18,26},{19,25},{20,28},{21,31},{22,30},{23,29},{8... | collective-permute-start | bytes 393224 | tf_op jit(solution)/shard_map/ppermute | solution.py:313
  75.2 1.4 collective-permute-start.16
  76.7 6.9 %collective-permute-start.18 = (bf16[64,1024]{1,0:T(8,128)(2,1)S(1)}, bf16[64,1024]{1,0:T(8,128)(2,1)S(1)}, u32[]{:S(2)}, u32[]{:S(2)}) collective-permute-start(bf16[64,1024]{1,0:T(8,128)(2,1)S(1)} %get-tuple-element.30), channel_id=1, source_target_pairs={{24,20},{25,23},{26,22},{27,21},{28,16},{29,19},{30,18},{31,17},{1... | collective-permute-start | bytes 393224 | tf_op jit(solution)/shard_map/ppermute | solution.py:313
  78.6 7.5 %collective-permute-start.17 = (bf16[64,1024]{1,0:T(8,128)(2,1)S(1)}, bf16[64,1024]{1,0:T(8,128)(2,1)S(1)}, u32[]{:S(2)}, u32[]{:S(2)}) collective-permute-start(bf16[64,1024]{1,0:T(8,128)(2,1)S(1)} %get-tuple-element.30), channel_id=1, source_target_pairs={{24,16},{25,19},{26,18},{27,17},{28,20},{29,23},{30,22},{31,21},{1... | collective-permute-start | bytes 393224 | tf_op jit(solution)/shard_map/ppermute | solution.py:313
  86.9 1.4 collective-permute-start.19
  88.4 6.2 %collective-permute-start.21 = (bf16[64,1024]{1,0:T(8,128)(2,1)S(1)}, bf16[64,1024]{1,0:T(8,128)(2,1)S(1)}, u32[]{:S(2)}, u32[]{:S(2)}) collective-permute-start(bf16[64,1024]{1,0:T(8,128)(2,1)S(1)} %get-tuple-element.32), channel_id=1, source_target_pairs={{16,12},{17,15},{18,14},{19,13},{20,8},{21,11},{22,10},{23,9},{24,... | collective-permute-start | bytes 393224 | tf_op jit(solution)/shard_map/ppermute | solution.py:313
  90.1 7.2 %collective-permute-start.20 = (bf16[64,1024]{1,0:T(8,128)(2,1)S(1)}, bf16[64,1024]{1,0:T(8,128)(2,1)S(1)}, u32[]{:S(2)}, u32[]{:S(2)}) collective-permute-start(bf16[64,1024]{1,0:T(8,128)(2,1)S(1)} %get-tuple-element.32), channel_id=1, source_target_pairs={{16,8},{17,11},{18,10},{19,9},{20,12},{21,15},{22,14},{23,13},{24,... | collective-permute-start | bytes 393224 | tf_op jit(solution)/shard_map/ppermute | solution.py:313
  98.2 1.4 collective-permute-start.22
  99.7 11.4 %collective-permute-start.24 = (bf16[64,1024]{1,0:T(8,128)(2,1)S(1)}, bf16[64,1024]{1,0:T(8,128)(2,1)S(1)}, u32[]{:S(2)}, u32[]{:S(2)}) collective-permute-start(bf16[64,1024]{1,0:T(8,128)(2,1)S(1)} %get-tuple-element.34), channel_id=1, source_target_pairs={{8,4},{9,7},{10,6},{11,5},{12,0},{13,3},{14,2},{15,1},{16,12},{17,... | collective-permute-start | bytes 393224 | tf_op jit(solution)/shard_map/ppermute | solution.py:313
  108.6 6.7 %collective-permute-start.23 = (bf16[64,1024]{1,0:T(8,128)(2,1)S(1)}, bf16[64,1024]{1,0:T(8,128)(2,1)S(1)}, u32[]{:S(2)}, u32[]{:S(2)}) collective-permute-start(bf16[64,1024]{1,0:T(8,128)(2,1)S(1)} %get-tuple-element.34), channel_id=1, source_target_pairs={{8,0},{9,3},{10,2},{11,1},{12,4},{13,7},{14,6},{15,5},{16,8},{17,1... | collective-permute-start | bytes 393224 | tf_op jit(solution)/shard_map/ppermute | solution.py:313
  116.2 2.2 %collective-permute-start.25 = (bf16[64,1024]{1,0:T(8,128)(2,1)S(1)}, bf16[64,1024]{1,0:T(8,128)(2,1)S(1)}, u32[]{:S(2)}, u32[]{:S(2)}) collective-permute-start(bf16[64,1024]{1,0:T(8,128)(2,1)S(1)} %shard_map.103.mine_ref), channel_id=1, source_target_pairs={{0,1},{1,0},{2,3},{3,2},{4,5},{5,4},{6,7},{7,6},{8,9},{9,8},{10,11... | collective-permute-start | bytes 393224 | tf_op jit(solution)/shard_map/ppermute | solution.py:420
  118.5 8.1 %collective-permute-start.27 = (bf16[64,1024]{1,0:T(8,128)(2,1)S(1)}, bf16[64,1024]{1,0:T(8,128)(2,1)S(1)}, u32[]{:S(2)}, u32[]{:S(2)}) collective-permute-start(bf16[64,1024]{1,0:T(8,128)(2,1)S(1)} %get-tuple-element.36), channel_id=1, source_target_pairs={{8,4},{9,7},{10,6},{11,5},{12,0},{13,3},{14,2},{15,1},{16,20},{17,... | collective-permute-start | bytes 393224 | tf_op jit(solution)/shard_map/ppermute | solution.py:313
  122.0 7.2 %collective-permute-start.26 = (bf16[64,1024]{1,0:T(8,128)(2,1)S(1)}, bf16[64,1024]{1,0:T(8,128)(2,1)S(1)}, u32[]{:S(2)}, u32[]{:S(2)}) collective-permute-start(bf16[64,1024]{1,0:T(8,128)(2,1)S(1)} %get-tuple-element.36), channel_id=1, source_target_pairs={{8,0},{9,3},{10,2},{11,1},{12,4},{13,7},{14,6},{15,5},{16,16},{17,... | collective-permute-start | bytes 393224 | tf_op jit(solution)/shard_map/ppermute | solution.py:313
  130.1 2.5 %collective-permute-start.28 = (bf16[64,1024]{1,0:T(8,128)(2,1)S(1)}, bf16[64,1024]{1,0:T(8,128)(2,1)S(1)}, u32[]{:S(2)}, u32[]{:S(2)}) collective-permute-start(bf16[64,1024]{1,0:T(8,128)(2,1)S(1)} %shard_map.105.mine_ref), channel_id=1, source_target_pairs={{0,1},{1,0},{2,3},{3,2},{4,5},{5,4},{6,7},{7,6},{8,9},{9,8},{10,11... | collective-permute-start | bytes 393224 | tf_op jit(solution)/shard_map/ppermute | solution.py:420
  133.4 6.3 %collective-permute-start.29 = (bf16[128,512]{1,0:T(8,128)(2,1)S(1)}, bf16[128,512]{1,0:T(8,128)(2,1)S(1)}, u32[]{:S(2)}, u32[]{:S(2)}) collective-permute-start(bf16[128,512]{1,0:T(8,128)(2,1)S(1)} %slice_select_fusion), channel_id=1, source_target_pairs={{1,2},{3,4},{5,6},{2,1},{4,3},{6,5},{9,10},{11,12},{13,14},{10,9},... | collective-permute-start | bytes 393224 | tf_op jit(solution)/shard_map/ppermute | solution.py:470

commit v4 on v3

--- a/solution.py
+++ b/solution.py
@@ -47,7 +47,7 @@
     up = (up_wave >= 0) & (up_wave < WAVES)
     down = (down_wave >= 0) & (down_wave < WAVES) & (panel < panels - 1)
     wave = jnp.where(up, up_wave, jnp.where(down, down_wave, 0))
-    return up, down, wave, (panel > 0) | down
+    return up, down, wave
 
 
 def push_kernel(
@@ -57,20 +57,24 @@
     source_hbm,
     inverse_hbm,
     boundary_hbm,
+    solver_hbm,
     outward_ref,
     partial_ref,
     interior_ref,
+    given_ref,
     source_ref,
     inverse_ref,
     boundary_ref,
     pick_ref,
     total_ref,
+    half_sems,
     sems,
 ):
     leaf_count, leaf_size = inverse_ref.shape[:2]
     edge = boundary_ref.shape[1]
-    rows = top_ref.shape[1]
+    rows = top_ref.shape[2]
     window = 3 * rows
+    chip, core = own_place()
     copies = []
     for step in range(leaf_count // group):
         leaves = pl.ds(step * group, group)
@@ -85,20 +89,12 @@
         )
         for copy in copies[-1]:
             copy.start()
-    local = rows_ref[...] - (lax.axis_index("front") - 1) * rows
-    spare = -leaf_count % 8
-    if spare:
-        local = jnp.concatenate([local, jnp.zeros((spare, edge), jnp.int32)], axis=0)
-    columns = jnp.transpose(local).astype(jnp.int16)
+    staged = sum(half_copies((chip + core + 1) % 2, solver_hbm, given_ref, half_sems), [])
     places = lax.broadcasted_iota(jnp.int16, (edge, window), 1)
     for step in range(leaf_count // group):
         for copy in copies[step]:
             copy.wait()
         first = step * group
-        for g in range(group):
-            pick_ref[step % 2, g * edge : (g + 1) * edge, :] = jnp.where(
-                columns[:, first + g : first + g + 1] == places, jnp.bfloat16(1), jnp.bfloat16(0)
-            )
         interior = []
         for j in range(first, first + group):
             lanes = slice(j * leaf_size, (j + 1) * leaf_size)
@@ -107,6 +103,16 @@
         pushed = [
             rows_dot(interior[g], boundary_ref[first + g]).astype(BF16) for g in range(group)
         ]
+        if step == 0:
+            lines = [rows_ref[i] for i in range(rows_ref.shape[0])]
+            if leaf_count % 8:
+                lines.append(jnp.zeros((-leaf_count % 8, edge), jnp.int32))
+            local = jnp.concatenate(lines, axis=0) - (lax.axis_index("front") - 1) * rows
+            columns = jnp.transpose(local).astype(jnp.int16)
+        for g in range(group):
+            pick_ref[step % 2, g * edge : (g + 1) * edge, :] = jnp.where(
+                columns[:, first + g : first + g + 1] == places, jnp.bfloat16(1), jnp.bfloat16(0)
+            )
         total = jnp.dot(
             jnp.concatenate(pushed, axis=1), pick_ref[step % 2], preferred_element_type=F32
         )
@@ -114,8 +120,9 @@
             total_ref[...] = total
         else:
             total_ref[...] += total
-    core = own_place()[1]
-    top = top_ref[...].astype(F32)
+    for copy in staged:
+        copy.wait()
+    top = top_ref[0].astype(F32)
 
     @pl.when(core == 0)
     def _():
@@ -131,17 +138,20 @@
 
 
 def pick_kernel(rows_ref, after_ref, out_ref):
-    leaf_count, edge = rows_ref.shape
+    tile, edge = rows_ref.shape[1:]
+    leaf_count = rows_ref.shape[0] * tile
     window = out_ref.shape[0]
     rows = window // 3
     place = lax.axis_index("front")
     local = rows_ref[...] - (place - 1) * rows
     shifted = jnp.where(local < rows, local + 2 * rows, local - rows)
-    local = jnp.where(place % 2 == 0, shifted, local).astype(jnp.int16)
+    local = jnp.where(place % 2 == 0, shifted, local)
     places = lax.broadcasted_iota(jnp.int16, (window, edge), 0)
     for j in range(leaf_count):
         out_ref[:, j * edge : (j + 1) * edge] = jnp.where(
-            local[j : j + 1, :] == places, jnp.bfloat16(1), jnp.bfloat16(0)
+            local[j // tile, j % tile : j % tile + 1, :].astype(jnp.int16) == places,
+            jnp.bfloat16(1),
+            jnp.bfloat16(0),
         )
 
 
@@ -173,12 +183,24 @@
 
 
 def leaf_kernel(
-    group, beside_ref, picked_ref, pick_ref, matrix_ref, interior_ref, out_hbm, out_ref, sems
+    group,
+    beside_ref,
+    picked_ref,
+    pick_ref,
+    matrix_ref,
+    interior_ref,
+    top_ref,
+    out_hbm,
+    top_hbm,
+    out_ref,
+    top_sem,
+    sems,
 ):
     leaf_count, edge, leaf_size = matrix_ref.shape
     rows = beside_ref.shape[1]
     beside = beside_ref[...]
-    copies = []
+    copies = [pltpu.make_async_copy(top_ref, top_hbm, top_sem)]
+    copies[0].start()
     for step in range(leaf_count // group):
         first = step * group
         span = slice(first * edge, (first + group) * edge)
@@ -202,36 +224,43 @@
 
 
 def half_copies(parity, inverse_hbm, to_ref, sems):
-    pairs = sems.shape[0]
+    pairs, pieces = sems.shape
     span = to_ref.shape[1] // pairs
+    tall = to_ref.shape[0] // pieces
     copies = []
     for q in range(pairs):
         start = pl.multiple_of((2 * q + parity) * span, span)
-        copies.append(
-            pltpu.make_async_copy(
-                inverse_hbm.at[:, pl.ds(start, span)],
-                to_ref.at[:, pl.ds(q * span, span)],
-                sems.at[q],
+        copies.append([])
+        for r in range(pieces):
+            here = pl.ds(r * tall, tall)
+            copies[-1].append(
+                pltpu.make_async_copy(
+                    inverse_hbm.at[here, pl.ds(start, span)],
+                    to_ref.at[here, pl.ds(q * span, span)],
+                    sems.at[q, r],
+                )
             )
-        )
-        copies[-1].start()
+            copies[-1][-1].start()
     return copies
 
 
-def half_kernel(inverse_hbm, after_ref, out_ref, sems):
+def turn_kernel(inverse_hbm, taken_hbm, out_ref, kept_ref, taken_ref, kept_sems, taken_sems):
     chip, core = own_place()
-    for copy in half_copies((chip + core + 1) % 2, inverse_hbm, out_ref, sems):
-        copy.wait()
-
-
-def turn_kernel(inverse_hbm, taken_ref, out_ref, kept_ref, sems):
-    columns, rows = out_ref.shape[0], taken_ref.shape[0]
-    chip, core = own_place()
-    copies = half_copies((chip + core) % 2, inverse_hbm, kept_ref, sems)
-    span = columns // len(copies)
+    rows = taken_ref.shape[0]
+    span = kept_ref.shape[1] // kept_sems.shape[0]
+    taken_copies = []
+    for q in range(taken_sems.shape[0]):
+        lanes = pl.ds(q * span, span)
+        taken_copies.append(
+            pltpu.make_async_copy(taken_hbm.at[:, lanes], taken_ref.at[:, lanes], taken_sems.at[q])
+        )
+        taken_copies[-1].start()
+    kept_copies = half_copies((chip + core) % 2, inverse_hbm, kept_ref, kept_sems)
     piece = min(span, 256)
-    for q, copy in enumerate(copies):
-        copy.wait()
+    for q in range(len(kept_copies)):
+        taken_copies[q].wait()
+        for copy in kept_copies[q]:
+            copy.wait()
         for k in range(q * span, (q + 1) * span, piece):
             kept = jnp.transpose(kept_ref[:, k : k + piece])
             taken = jnp.transpose(taken_ref[:, k : k + piece])
@@ -247,35 +276,36 @@
                 out_ref[k : k + piece, rows:] = kept
 
 
-def fold_kernel(turn, blocks, inverse_ref, *refs):
-    base_refs = refs[:blocks]
-    in_refs = refs[blocks : 2 * blocks] if turn else ()
+def fold_kernel(blocks, more, skipped, inverse_ref, *refs):
+    refs = refs[skipped:]
     out_ref = refs[-1]
     wave_rows, rows = out_ref.shape
-    forward, _, wave, fed = own_turn(turn)
     chip = own_place()[0]
-    here = pl.ds(pl.multiple_of(wave * wave_rows, wave_rows), wave_rows)
-    total = jnp.zeros((wave_rows, rows), F32)
-    for i in range(blocks):
-        if turn:
-            base = jnp.where(forward, base_refs[i][here, :].astype(F32), 0.0)
-            vectors = (jnp.where(fed, in_refs[i][...].astype(F32), 0.0) + base).astype(BF16)
-        else:
-            vectors = base_refs[i][here, :]
+    total = refs[-2][...] if more else jnp.zeros((wave_rows, rows), F32)
+    for n, i in enumerate(blocks):
         place = pl.ds(pl.multiple_of(((chip // 2) ^ i) * rows, rows), rows)
-        total += jnp.dot(vectors, inverse_ref[place, :], preferred_element_type=F32)
-    out_ref[...] = total.astype(BF16)
-
-
-def join_kernel(turn, mine_ref, other_ref, state_ref, scale_ref, next_ref, out_ref):
+        total += jnp.dot(refs[n][...], inverse_ref[place, :], preferred_element_type=F32)
+    out_ref[...] = total.astype(out_ref.dtype)
+
+
+def join_kernel(
+    turn, mine_ref, other_ref, state_ref, scale_ref, later_ref, next_ref, out_ref
+):
     wave_rows = mine_ref.shape[0]
-    forward, backward, wave, _ = own_turn(turn)
+    last = lax.axis_index("panel") == lax.axis_size("panel") - 1
+    forward, backward, wave = own_turn(turn)
     here = pl.ds(pl.multiple_of(wave * wave_rows, wave_rows), wave_rows)
     solved = (mine_ref[...].astype(F32) + other_ref[...].astype(F32)).astype(BF16).astype(F32)
     older = state_ref[here, :].astype(F32)
     field = (solved + jnp.where(backward, older, 0.0)).astype(BF16)
     scale = jnp.where(backward, scale_ref[1:2, :], scale_ref[0:1, :])
-    out_ref[...] = (scale * field.astype(F32)).astype(BF16)
+    ahead = jnp.where(forward & ~last, later_ref[here, :].astype(F32), 0.0)
+    out_ref[...] = (scale * field.astype(F32) + ahead).astype(BF16)
+    if turn == 0:
+
+        @pl.when(last)
+        def _():
+            out_ref[...] = later_ref[wave_rows : 2 * wave_rows, :]
 
     @pl.when(forward | backward)
     def _():
@@ -283,6 +313,8 @@
 
 
 def turn_routes(turn, panels, waves):
+    if turn == 0:
+        return [(p, (p + 1) % panels) for p in range(panels)]
     at = [s if s < panels else 2 * (panels - 1) - s for s in range(2 * panels - 1)]
     pairs = []
     for wave in range(waves):
@@ -335,32 +367,45 @@
     swap_chip = [(i, i + 1) for i in range(1, front - 1, 2)]
     swap_chip = swap_chip + [(j, i) for i, j in swap_chip]
 
-    outward, partial, interior = pl.pallas_call(
+    tile = group_of(leaf_count, 8 if leaf_count % 8 == 0 else 4)
+    touch_rows = touch_rows.reshape(leaf_count // tile, tile, edge)
+    pieces = group_of(rows // 16, 8)
+    outward, partial, interior, given = pl.pallas_call(
         functools.partial(push_kernel, group),
         out_shape=(
             pltpu.VMEM((sources, rows), BF16),
             pltpu.VMEM((sources, chip_rows), F32),
             pltpu.VMEM((sources, all_lanes), BF16),
+            pltpu.VMEM((rows, width // 2), BF16),
         ),
-        in_specs=[VMEM, VMEM, ANY, ANY, ANY],
-        out_specs=(VMEM, VMEM, VMEM),
+        in_specs=[VMEM] * 2 + [ANY] * 4,
+        out_specs=(VMEM, VMEM, VMEM, VMEM),
         scratch_shapes=[
             pltpu.VMEM((sources, all_lanes), BF16),
             pltpu.VMEM((leaf_count, leaf_size, leaf_size), BF16),
             pltpu.VMEM((leaf_count, edge, leaf_size), BF16),
             pltpu.VMEM((2, group * edge, 3 * rows), BF16),
             pltpu.VMEM((sources, 3 * rows), F32),
+            pltpu.SemaphoreType.DMA((half, pieces)),
             pltpu.SemaphoreType.DMA((steps, 3)),
         ],
-        compiler_params=params(20),
+        compiler_params=params(24),
     )(
-        touch_rows[0],
-        top_source[0],
+        touch_rows,
+        top_source,
         in_hbm(leaf_source[0]),
         in_hbm(leaf_inverse[0]),
         in_hbm(boundary[0]),
+        in_hbm(top_inverse[0]),
     )
+    coupling, given, outward = lax.optimization_barrier((coupling, given, outward))
+    taken = lax.ppermute(given, "front", swap_core)
     inward = lax.ppermute(outward, "front", swap_chip)
+    ring = [((p + 1) % panels, p) for p in range(panels)]
+    later = lax.ppermute(coupling, "panel", ring)
+    inward, later = lax.optimization_barrier((inward, later))
+    forward_scale = jnp.where(panel == panels - 1, coupling, later)
+    scales = jnp.concatenate([forward_scale, coupling], axis=0)
     blank = jnp.zeros_like(partial[:, :rows])
     whole_inward = jnp.where(
         core == 0,
@@ -369,54 +414,55 @@
     )
     partial = (partial - whole_inward).astype(BF16)
     partner = lax.ppermute(partial, "front", swap_core)
+    partner_scales = lax.ppermute(scales, "front", swap_core)
     known = (partial.astype(F32) + partner.astype(F32)).astype(BF16)
-    base = [in_vmem(b) for b in spread(known, [(p, p) for p in range(panels)], chips)]
-
-    given = pl.pallas_call(
-        half_kernel,
-        out_shape=jax.ShapeDtypeStruct((rows, width // 2), BF16),
-        in_specs=[ANY, ANY],
-        out_specs=VMEM,
-        scratch_shapes=[pltpu.SemaphoreType.DMA((half,))],
-        compiler_params=params(4),
-    )(in_hbm(top_inverse[0]), outward)
-    taken = lax.ppermute(given, "front", swap_core)
-    inverse = pl.pallas_call(
-        turn_kernel,
-        out_shape=pltpu.VMEM((width // 2, chip_rows), BF16),
-        in_specs=[ANY, VMEM],
-        out_specs=VMEM,
-        scratch_shapes=[
-            pltpu.VMEM((rows, width // 2), BF16),
-            pltpu.SemaphoreType.DMA((half,)),
-        ],
-        compiler_params=params(8),
-    )(in_hbm(top_inverse[0]), taken)
-    inverse = in_vmem(inverse)
-
-    coupling, _ = lax.optimization_barrier((coupling, outward))
-    later = lax.ppermute(coupling, "panel", [((p + 1) % panels, p) for p in range(panels)])
-    forward_scale = jnp.where(panel == panels - 1, coupling, later)
-    scales = jnp.concatenate([forward_scale, coupling], axis=0)
-    partner_scales = lax.ppermute(scales, "front", swap_core)
     scales = jnp.where(
         core == 0,
         jnp.concatenate([scales, partner_scales], axis=1),
         jnp.concatenate([partner_scales, scales], axis=1),
     )
     scales = in_vmem(scales)
+    arrived = [in_vmem(a) for a in spread(known[:wave_rows], [(0, 0)], chips)]
+    later_known = in_vmem(lax.ppermute(known, "panel", ring))
+
+    inverse = pl.pallas_call(
+        turn_kernel,
+        out_shape=pltpu.VMEM((width // 2, chip_rows), BF16),
+        in_specs=[ANY, ANY],
+        out_specs=VMEM,
+        scratch_shapes=[
+            pltpu.VMEM((rows, width // 2), BF16),
+            pltpu.VMEM((rows, width // 2), BF16),
+            pltpu.SemaphoreType.DMA((half, pieces)),
+            pltpu.SemaphoreType.DMA((half,)),
+        ],
+        compiler_params=params(8),
+        cost_estimate=pl.CostEstimate(
+            flops=2 * sources * width * rows, bytes_accessed=4 * width * rows, transcendentals=0
+        ),
+    )(in_hbm(top_inverse[0]), taken)
+    inverse = in_vmem(inverse)
+
     state = jnp.zeros((sources, chip_rows), BF16)
     turns = 2 * (panels - 1) + WAVES
-    arrived, extra = [], []
+    extra = []
     for turn in range(turns):
-        share = pl.pallas_call(
-            functools.partial(fold_kernel, turn, half),
-            out_shape=pltpu.VMEM((wave_rows, chip_rows), BF16),
-            in_specs=[VMEM] * (1 + half + len(arrived)) + [ANY] * len(extra),
-            out_specs=VMEM,
-            compiler_params=params(4),
-        )(inverse, *base, *arrived, *extra)
-        extra = []
+        share = ()
+        halves = (range(half // 2, half), range(half // 2)) if turn else (range(half),)
+        for blocks in halves:
+            last = blocks is halves[-1]
+            behind = extra if last else []
+            operands = [arrived[i] for i in blocks] + [in_vmem(v) for v in share]
+            share = (
+                pl.pallas_call(
+                    functools.partial(fold_kernel, blocks, bool(share), len(behind)),
+                    out_shape=pltpu.VMEM((wave_rows, chip_rows), BF16 if last else F32),
+                    in_specs=[VMEM] + [ANY] * len(behind) + [VMEM] * len(operands),
+                    out_specs=VMEM,
+                    compiler_params=params(4),
+                )(inverse, *behind, *operands),
+            )
+        share, extra = share[0], []
         other = lax.ppermute(share, "front", swap_core)
         state, outgoing = pl.pallas_call(
             functools.partial(join_kernel, turn),
@@ -424,11 +470,11 @@
                 pltpu.VMEM((sources, chip_rows), BF16),
                 pltpu.VMEM((wave_rows, chip_rows), BF16),
             ),
-            in_specs=[VMEM] * 4,
+            in_specs=[VMEM] * 5,
             out_specs=(VMEM, VMEM),
             input_output_aliases={2: 0},
             compiler_params=params(4),
-        )(in_vmem(share), in_vmem(other), in_vmem(state), scales)
+        )(in_vmem(share), in_vmem(other), in_vmem(state), scales, later_known)
         if turn < turns - 1:
             routes = turn_routes(turn, panels, WAVES)
             arrived = [in_vmem(a) for a in spread(outgoing, routes, chips)]
@@ -444,7 +490,7 @@
                     bytes_accessed=6 * rows * leaf_count * edge,
                     transcendentals=0,
                 ),
-            )(touch_rows[0], outgoing)
+            )(touch_rows, outgoing)
             extra = [in_vmem(picks)]
         if turn == 2:
             matrices = pl.pallas_call(
@@ -480,17 +526,21 @@
             transcendentals=0,
         ),
     )(in_vmem(state), in_vmem(picks))
-    leaf_field = pl.pallas_call(
+    leaf_field, top_field = pl.pallas_call(
         functools.partial(leaf_kernel, group),
-        out_shape=jax.ShapeDtypeStruct((sources, all_lanes), BF16),
-        in_specs=[VMEM] * 5,
-        out_specs=ANY,
+        out_shape=(
+            jax.ShapeDtypeStruct((sources, all_lanes), BF16),
+            jax.ShapeDtypeStruct((sources, rows), BF16),
+        ),
+        in_specs=[VMEM] * 6,
+        out_specs=(ANY, ANY),
         scratch_shapes=[
             pltpu.VMEM((sources, all_lanes), BF16),
+            pltpu.SemaphoreType.DMA,
             pltpu.SemaphoreType.DMA((steps,)),
         ],
         compiler_params=params(8),
-    )(in_vmem(beside), in_vmem(picked), in_vmem(picks), in_vmem(matrices), in_vmem(interior))
+    )(in_vmem(beside), in_vmem(picked), in_vmem(picks), in_vmem(matrices), in_vmem(interior), in_vmem(top_field))
     return (top_field[None], leaf_field[None])
 
 

time: 143 us -> 136 us (0.951)
  starting transfers between devices: 60.8 us -> 56.3 us
    ppermute x16, starting transfers between devices: 42.5 us -> 39 us  [spread(): received.append(lax.ppermute(values, ('panel', 'front'), route))]
    ppermute x1, waiting for transfers between devices: 2.62 us -> 0.01 us  [body(): inward = lax.ppermute(outward, 'front', swap_chip)]
    ppermute x16, waiting for transfers between devices: 30.3 us -> 32.5 us  [spread(): received.append(lax.ppermute(values, ('panel', 'front'), route))]
    pallas_call x10 -> x16, Pallas kernels: 12.2 us -> 10.2 us  [the longest x15 7.57 us: body(): pl.pallas_call(functools.partial(fold_kernel, blocks, bool(share), len(be...]
    pallas_call x1, Pallas kernels: 5.99 us -> 7.48 us  [body(): pl.pallas_call(functools.partial(push_kernel, group), out_shape=(pltpu.VM...]
    ppermute x8, starting transfers between devices: 9.3 us -> 7.85 us  [body(): other = lax.ppermute(share, 'front', swap_core)]
  transfers between devices with their start and end apart: 30 -> 31, of which waited for: 25 -> 24; matrix products, arithmetic and copies ran while one was open for 1% -> 0% of each run, Pallas kernels for 8% -> 11%
where the time goes in v4:
time: 136 us
  starting transfers between devices  56.3 us (41%)
  waiting for transfers between devices  46.1 us (34%)
  Pallas kernels  30.2 us (22%)
  local copies, waits for them, and re-layouts  1.66 us (1%)
    ppermute x16, starting transfers between devices, spread(): received.append(lax.ppermute(values, ('panel', 'front'), route))  39 us
    ppermute x16, waiting for transfers between devices, spread(): received.append(lax.ppermute(values, ('panel', 'front'), route))  32.5 us
    ppermute x8, starting transfers between devices, body(): other = lax.ppermute(share, 'front', swap_core)  7.85 us
    ppermute x8, waiting for transfers between devices, body(): other = lax.ppermute(share, 'front', swap_core)  7.6 us
    pallas_call x15, Pallas kernels, body(): pl.pallas_call(functools.partial(fold_kernel, blocks, bool(share), len(be...  7.57 us
    pallas_call x1, Pallas kernels, body(): pl.pallas_call(functools.partial(push_kernel, group), out_shape=(pltpu.VM...  7.48 us
    ppermute x1, starting transfers between devices, body(): inward = lax.ppermute(outward, 'front', swap_chip)  4.55 us
    pallas_call x1, Pallas kernels, body(): pl.pallas_call(turn_kernel, out_shape=pltpu.VMEM((width // 2, chip_rows),...  3.9 us
  transfers between devices with their start and end apart: 31, of which 24 were waited for; matrix products, arithmetic and copies ran while one was open for 0% of the time, Pallas kernels for 11%

profile of v4, /device:TPU:1, one launch (start us, length us, event | category | flops | bytes accessed | tf_op | source)
XLA Modules:
  0.0 135.7 jit_solution(8229941791702279681)
XLA Ops:
  2.3 7.5 %shard_map.86 = (bf16[128,512]{1,0:T(8,128)(2,1)S(1)}, f32[128,1024]{1,0:T(8,128)S(1)}, bf16[128,9216]{1,0:T(8,128)(2,1)S(1)}, bf16[512,2048]{1,0:T(8,128)(2,1)}) custom-call(s32[9,4,128]{2,1,0:T(4,128)S(1)} %bitcast.7, bf16[1,128,512]{2,1,0:T(8,128)(2,1)S(1)} %copy-done, bf16[128,9216]{1,0:T(8,128)(2,1)} %bitcast.15, bf16[36,256,256]{2,1,0:T(8,128)(2,1)} %bitcast.9, ...), custom_call_target="tpu_custom_call" | custom-call | tf_op jit(solution)/shard_map/pallas_call | solution.py:373
  9.9 4.6 %collective-permute-start.1 = (bf16[128,512]{1,0:T(8,128)(2,1)S(1)}, bf16[128,512]{1,0:T(8,128)(2,1)S(1)}, u32[]{:S(2)}, u32[]{:S(2)}) collective-permute-start(bf16[128,512]{1,0:T(8,128)(2,1)S(1)} %get-tuple-element.32), channel_id=1, source_target_pairs={{1,2},{3,4},{5,6},{2,1},{4,3},{6,5},{9,10},{11,12},{13,14},{10,9},... | collective-permute-start | bytes 393224 | tf_op jit(solution)/shard_map/ppermute | solution.py:403
  14.4 2.2 %collective-permute-start.2 = (f32[1,512]{1,0:T(1,128)S(1)}, f32[1,512]{1,0:T(1,128)S(1)}, u32[]{:S(2)}, u32[]{:S(2)}) collective-permute-start(f32[1,512]{1,0:T(1,128)S(1)} %copy-done.3), channel_id=1, source_target_pairs={{8,0},{16,8},{24,16},{0,24},{9,1},{17,9},{25,17},{1,25},{10,2},{18... | collective-permute-start | bytes 6152 | tf_op jit(solution)/shard_map/ppermute | solution.py:405
  17.6 1.5 %collective-permute-done.3 = bf16[128,1024]{1,0:T(8,128)(2,1)S(1)} collective-permute-done((bf16[128,1024]{1,0:T(8,128)(2,1)S(1)}, bf16[128,1024]{1,0:T(8,128)(2,1)S(1)}, u32[]{:S(2)}, u32[]{:S(2)}) %collective-permute-start.3) | collective-permute-done | bytes 262176 | tf_op jit(solution)/shard_map/ppermute | solution.py:416
  19.2 5.1 %collective-permute-start.5 = (bf16[64,1024]{1,0:T(8,128)(2,1)S(1)}, bf16[64,1024]{1,0:T(8,128)(2,1)S(1)}, u32[]{:S(2)}, u32[]{:S(2)}) collective-permute-start(bf16[64,1024]{1,0:T(8,128)(2,1)S(1)} %slice.12), channel_id=1, source_target_pairs={{0,4},{1,7},{2,6},{3,5},{4,0},{5,3},{6,2},{7,1}} | collective-permute-start | bytes 393224 | tf_op jit(solution)/shard_map/ppermute | solution.py:345
  24.3 1.9 %collective-permute-start.4 = (bf16[64,1024]{1,0:T(8,128)(2,1)S(1)}, bf16[64,1024]{1,0:T(8,128)(2,1)S(1)}, u32[]{:S(2)}, u32[]{:S(2)}) collective-permute-start(bf16[64,1024]{1,0:T(8,128)(2,1)S(1)} %slice.12), channel_id=1, source_target_pairs={{0,0},{1,3},{2,2},{3,1},{4,4},{5,7},{6,6},{7,5}} | collective-permute-start | bytes 393224 | tf_op jit(solution)/shard_map/ppermute | solution.py:345
  26.3 3.9 %shard_map.87.inverse_ref = bf16[2048,1024]{1,0:T(8,128)(2,1)S(1)} custom-call(bf16[512,4096]{1,0:T(8,128)(2,1)} %bitcast.12, bf16[512,2048]{1,0:T(8,128)(2,1)} %collective-permute-done.taken_hbm), custom_call_target="tpu_custom_call" | custom-call | flops 536870912 | bytes 8388608 | tf_op jit(solution)/shard_map/pallas_call | solution.py:428
  35.4 7.3 %collective-permute-done.10.refs_0_ = bf16[64,1024]{1,0:T(8,128)(2,1)S(1)} collective-permute-done((bf16[64,1024]{1,0:T(8,128)(2,1)S(1)}, bf16[64,1024]{1,0:T(8,128)(2,1)S(1)}, u32[]{:S(2)}, u32[]{:S(2)}) %collective-permute-start.10) | collective-permute-done | bytes 131104 | tf_op jit(solution)/shard_map/ppermute | solution.py:345
  43.7 2.2 %collective-permute-start.11 = (bf16[64,1024]{1,0:T(8,128)(2,1)S(1)}, bf16[64,1024]{1,0:T(8,128)(2,1)S(1)}, u32[]{:S(2)}, u32[]{:S(2)}) collective-permute-start(bf16[64,1024]{1,0:T(8,128)(2,1)S(1)} %shard_map.91.mine_ref), channel_id=1, source_target_pairs={{0,1},{1,0},{2,3},{3,2},{4,5},{5,4},{6,7},{7,6},{8,9},{9,8},{10,11... | collective-permute-start | bytes 393224 | tf_op jit(solution)/shard_map/ppermute | solution.py:466
  47.6 2.3 %collective-permute-start.12 = (bf16[64,1024]{1,0:T(8,128)(2,1)S(1)}, bf16[64,1024]{1,0:T(8,128)(2,1)S(1)}, u32[]{:S(2)}, u32[]{:S(2)}) collective-permute-start(bf16[64,1024]{1,0:T(8,128)(2,1)S(1)} %get-tuple-element.38.after_ref), channel_id=1, source_target_pairs={{8,16},{9,19},{10,18},{11,17},{12,20},{13,23},{14,22},{15,21},{0,8... | collective-permute-start | bytes 393224 | tf_op jit(solution)/shard_map/ppermute | solution.py:345
  49.9 2.1 %shard_map.93.refs_0_.pick_ref = bf16[1536,4608]{1,0:T(8,128)(2,1)S(1)} custom-call(s32[9,4,128]{2,1,0:T(4,128)S(1)} %bitcast.8, bf16[64,1024]{1,0:T(8,128)(2,1)S(1)} %get-tuple-element.38.after_ref), custom_call_target="tpu_custom_call" | custom-call | flops 1207959552 | bytes 14155776 | tf_op jit(solution)/shard_map/pallas_call | solution.py:482
  52.0 2.6 %collective-permute-done.13.refs_0_ = bf16[64,1024]{1,0:T(8,128)(2,1)S(1)} collective-permute-done((bf16[64,1024]{1,0:T(8,128)(2,1)S(1)}, bf16[64,1024]{1,0:T(8,128)(2,1)S(1)}, u32[]{:S(2)}, u32[]{:S(2)}) %collective-permute-start.13) | collective-permute-done | bytes 131104 | tf_op jit(solution)/shard_map/ppermute | solution.py:345
  55.0 1.7 %collective-permute-done.12.refs_1_ = bf16[64,1024]{1,0:T(8,128)(2,1)S(1)} collective-permute-done((bf16[64,1024]{1,0:T(8,128)(2,1)S(1)}, bf16[64,1024]{1,0:T(8,128)(2,1)S(1)}, u32[]{:S(2)}, u32[]{:S(2)}) %collective-permute-start.12) | collective-permute-done | bytes 131104 | tf_op jit(solution)/shard_map/ppermute | solution.py:345
  57.2 1.9 %collective-permute-start.14 = (bf16[64,1024]{1,0:T(8,128)(2,1)S(1)}, bf16[64,1024]{1,0:T(8,128)(2,1)S(1)}, u32[]{:S(2)}, u32[]{:S(2)}) collective-permute-start(bf16[64,1024]{1,0:T(8,128)(2,1)S(1)} %shard_map.95.mine_ref), channel_id=1, source_target_pairs={{0,1},{1,0},{2,3},{3,2},{4,5},{5,4},{6,7},{7,6},{8,9},{9,8},{10,11... | collective-permute-start | bytes 393224 | tf_op jit(solution)/shard_map/ppermute | solution.py:466
  60.1 2.3 %collective-permute-start.16 = (bf16[64,1024]{1,0:T(8,128)(2,1)S(1)}, bf16[64,1024]{1,0:T(8,128)(2,1)S(1)}, u32[]{:S(2)}, u32[]{:S(2)}) collective-permute-start(bf16[64,1024]{1,0:T(8,128)(2,1)S(1)} %get-tuple-element.40.after_ref), channel_id=1, source_target_pairs={{16,28},{17,31},{18,30},{19,29},{20,24},{21,27},{22,26},{23,25},{8... | collective-permute-start | bytes 393224 | tf_op jit(solution)/shard_map/ppermute | solution.py:345
  62.4 2.1 %collective-permute-start.15 = (bf16[64,1024]{1,0:T(8,128)(2,1)S(1)}, bf16[64,1024]{1,0:T(8,128)(2,1)S(1)}, u32[]{:S(2)}, u32[]{:S(2)}) collective-permute-start(bf16[64,1024]{1,0:T(8,128)(2,1)S(1)} %get-tuple-element.40.after_ref), channel_id=1, source_target_pairs={{16,24},{17,27},{18,26},{19,25},{20,28},{21,31},{22,30},{23,29},{8... | collective-permute-start | bytes 393224 | tf_op jit(solution)/shard_map/ppermute | solution.py:345
  64.5 3.7 %shard_map.97.refs_0_.matrix_ref = bf16[36,128,256]{2,1,0:T(8,128)(2,1)S(1)} custom-call(bf16[36,256,256]{2,1,0:T(8,128)(2,1)} %bitcast.10, bf16[36,128,256]{2,1,0:T(8,128)(2,1)} %bitcast.14, bf16[64,1024]{1,0:T(8,128)(2,1)S(1)} %get-tuple-element.40.after_ref), custom_call_target="tpu_custom_call" | custom-call | flops 603979776 | bytes 9437184 | tf_op jit(solution)/shard_map/pallas_call | solution.py:496
  72.8 1.9 %collective-permute-start.18 = (bf16[64,1024]{1,0:T(8,128)(2,1)S(1)}, bf16[64,1024]{1,0:T(8,128)(2,1)S(1)}, u32[]{:S(2)}, u32[]{:S(2)}) collective-permute-start(bf16[64,1024]{1,0:T(8,128)(2,1)S(1)} %get-tuple-element.42), channel_id=1, source_target_pairs={{24,16},{25,19},{26,18},{27,17},{28,20},{29,23},{30,22},{31,21},{1... | collective-permute-start | bytes 393224 | tf_op jit(solution)/shard_map/ppermute | solution.py:345
  74.8 3.8 %collective-permute-done.19.refs_0_ = bf16[64,1024]{1,0:T(8,128)(2,1)S(1)} collective-permute-done((bf16[64,1024]{1,0:T(8,128)(2,1)S(1)}, bf16[64,1024]{1,0:T(8,128)(2,1)S(1)}, u32[]{:S(2)}, u32[]{:S(2)}) %collective-permute-start.19) | collective-permute-done | bytes 131104 | tf_op jit(solution)/shard_map/ppermute | solution.py:345
  84.2 1.9 %collective-permute-start.21 = (bf16[64,1024]{1,0:T(8,128)(2,1)S(1)}, bf16[64,1024]{1,0:T(8,128)(2,1)S(1)}, u32[]{:S(2)}, u32[]{:S(2)}) collective-permute-start(bf16[64,1024]{1,0:T(8,128)(2,1)S(1)} %get-tuple-element.44), channel_id=1, source_target_pairs={{16,8},{17,11},{18,10},{19,9},{20,12},{21,15},{22,14},{23,13},{24,... | collective-permute-start | bytes 393224 | tf_op jit(solution)/shard_map/ppermute | solution.py:345
  86.2 2.6 %collective-permute-done.22.refs_0_ = bf16[64,1024]{1,0:T(8,128)(2,1)S(1)} collective-permute-done((bf16[64,1024]{1,0:T(8,128)(2,1)S(1)}, bf16[64,1024]{1,0:T(8,128)(2,1)S(1)}, u32[]{:S(2)}, u32[]{:S(2)}) %collective-permute-start.22) | collective-permute-done | bytes 131104 | tf_op jit(solution)/shard_map/ppermute | solution.py:345
  89.3 2.2 %collective-permute-done.21.refs_0_ = bf16[64,1024]{1,0:T(8,128)(2,1)S(1)} collective-permute-done((bf16[64,1024]{1,0:T(8,128)(2,1)S(1)}, bf16[64,1024]{1,0:T(8,128)(2,1)S(1)}, u32[]{:S(2)}, u32[]{:S(2)}) %collective-permute-start.21) | collective-permute-done | bytes 131104 | tf_op jit(solution)/shard_map/ppermute | solution.py:345
  93.5 9.5 %collective-permute-start.25 = (bf16[64,1024]{1,0:T(8,128)(2,1)S(1)}, bf16[64,1024]{1,0:T(8,128)(2,1)S(1)}, u32[]{:S(2)}, u32[]{:S(2)}) collective-permute-start(bf16[64,1024]{1,0:T(8,128)(2,1)S(1)} %get-tuple-element.46), channel_id=1, source_target_pairs={{8,4},{9,7},{10,6},{11,5},{12,0},{13,3},{14,2},{15,1},{16,12},{17,... | collective-permute-start | bytes 393224 | tf_op jit(solution)/shard_map/ppermute | solution.py:345
  103.0 1.9 %collective-permute-start.24 = (bf16[64,1024]{1,0:T(8,128)(2,1)S(1)}, bf16[64,1024]{1,0:T(8,128)(2,1)S(1)}, u32[]{:S(2)}, u32[]{:S(2)}) collective-permute-start(bf16[64,1024]{1,0:T(8,128)(2,1)S(1)} %get-tuple-element.46), channel_id=1, source_target_pairs={{8,0},{9,3},{10,2},{11,1},{12,4},{13,7},{14,6},{15,5},{16,8},{17,1... | collective-permute-start | bytes 393224 | tf_op jit(solution)/shard_map/ppermute | solution.py:345
  105.7 4.0 %collective-permute-done.24.refs_0_ = bf16[64,1024]{1,0:T(8,128)(2,1)S(1)} collective-permute-done((bf16[64,1024]{1,0:T(8,128)(2,1)S(1)}, bf16[64,1024]{1,0:T(8,128)(2,1)S(1)}, u32[]{:S(2)}, u32[]{:S(2)}) %collective-permute-start.24) | collective-permute-done | bytes 131104 | tf_op jit(solution)/shard_map/ppermute | solution.py:345
  112.4 3.4 %collective-permute-start.28 = (bf16[64,1024]{1,0:T(8,128)(2,1)S(1)}, bf16[64,1024]{1,0:T(8,128)(2,1)S(1)}, u32[]{:S(2)}, u32[]{:S(2)}) collective-permute-start(bf16[64,1024]{1,0:T(8,128)(2,1)S(1)} %get-tuple-element.48), channel_id=1, source_target_pairs={{8,4},{9,7},{10,6},{11,5},{12,0},{13,3},{14,2},{15,1},{16,20},{17,... | collective-permute-start | bytes 393224 | tf_op jit(solution)/shard_map/ppermute | solution.py:345
  115.8 1.9 %collective-permute-start.27 = (bf16[64,1024]{1,0:T(8,128)(2,1)S(1)}, bf16[64,1024]{1,0:T(8,128)(2,1)S(1)}, u32[]{:S(2)}, u32[]{:S(2)}) collective-permute-start(bf16[64,1024]{1,0:T(8,128)(2,1)S(1)} %get-tuple-element.48), channel_id=1, source_target_pairs={{8,0},{9,3},{10,2},{11,1},{12,4},{13,7},{14,6},{15,5},{16,16},{17,... | collective-permute-start | bytes 393224 | tf_op jit(solution)/shard_map/ppermute | solution.py:345
  117.7 2.6 %collective-permute-done.28.refs_0_ = bf16[64,1024]{1,0:T(8,128)(2,1)S(1)} collective-permute-done((bf16[64,1024]{1,0:T(8,128)(2,1)S(1)}, bf16[64,1024]{1,0:T(8,128)(2,1)S(1)}, u32[]{:S(2)}, u32[]{:S(2)}) %collective-permute-start.28) | collective-permute-done | bytes 131104 | tf_op jit(solution)/shard_map/ppermute | solution.py:345
  120.8 2.2 %collective-permute-done.27.refs_0_ = bf16[64,1024]{1,0:T(8,128)(2,1)S(1)} collective-permute-done((bf16[64,1024]{1,0:T(8,128)(2,1)S(1)}, bf16[64,1024]{1,0:T(8,128)(2,1)S(1)}, u32[]{:S(2)}, u32[]{:S(2)}) %collective-permute-start.27) | collective-permute-done | bytes 131104 | tf_op jit(solution)/shard_map/ppermute | solution.py:345
  126.7 1.9 %collective-permute-start.30 = (bf16[128,512]{1,0:T(8,128)(2,1)S(1)}, bf16[128,512]{1,0:T(8,128)(2,1)S(1)}, u32[]{:S(2)}, u32[]{:S(2)}) collective-permute-start(bf16[128,512]{1,0:T(8,128)(2,1)S(1)} %slice_select_fusion.top_ref), channel_id=1, source_target_pairs={{1,2},{3,4},{5,6},{2,1},{4,3},{6,5},{9,10},{11,12},{13,14},{10,9},... | collective-permute-start | bytes 393224 | tf_op jit(solution)/shard_map/ppermute | solution.py:516
  130.0 2.9 %collective-permute-done.30.beside_ref = bf16[128,512]{1,0:T(8,128)(2,1)S(1)} collective-permute-done((bf16[128,512]{1,0:T(8,128)(2,1)S(1)}, bf16[128,512]{1,0:T(8,128)(2,1)S(1)}, u32[]{:S(2)}, u32[]{:S(2)}) %collective-permute-start.30) | collective-permute-done | bytes 131104 | tf_op jit(solution)/shard_map/ppermute | solution.py:516
  133.0 2.6 %shard_map.114 = (bf16[128,9216]{1,0:T(8,128)(2,1)}, bf16[128,512]{1,0:T(8,128)(2,1)}) custom-call(bf16[128,512]{1,0:T(8,128)(2,1)S(1)} %collective-permute-done.30.beside_ref, bf16[128,4608]{1,0:T(8,128)(2,1)S(1)} %shard_map.113.picked_ref, bf16[1536,4608]{1,0:T(8,128)(2,1)S(1)} %shard_map.93.refs_0_.pick_ref, ...), custom_call_target="tpu_custom_call" | custom-call | tf_op jit(solution)/shard_map/pallas_call | solution.py:529
  (76 shorter events, 34.3 us)
Async XLA Ops:
  2.3 12.2 %copy-start.3 = (f32[1,512]{1,0:T(1,128)S(1)}, f32[1,512]{1,0:T(1,128)}, u32[]{:S(2)}) copy-start(f32[1,512]{1,0:T(1,128)} %param.13) | copy-start | bytes 6148
  9.7 16.5 %collective-permute-start = (bf16[512,2048]{1,0:T(8,128)(2,1)}, bf16[512,2048]{1,0:T(8,128)(2,1)}, u32[]{:S(2)}, u32[]{:S(2)}) collective-permute-start(bf16[512,2048]{1,0:T(8,128)(2,1)} %get-tuple-element.30), channel_id=1, source_target_pairs={{0,1},{1,0},{2,3},{3,2},{4,5},{5,4},{6,7},{7,6},{8,9},{9,8},{10,11... | collective-permute-start | bytes 6291464 | tf_op jit(solution)/shard_map/ppermute | solution.py:402
  9.9 7.5 %collective-permute-start.1 = (bf16[128,512]{1,0:T(8,128)(2,1)S(1)}, bf16[128,512]{1,0:T(8,128)(2,1)S(1)}, u32[]{:S(2)}, u32[]{:S(2)}) collective-permute-start(bf16[128,512]{1,0:T(8,128)(2,1)S(1)} %get-tuple-element.32), channel_id=1, source_target_pairs={{1,2},{3,4},{5,6},{2,1},{4,3},{6,5},{9,10},{11,12},{13,14},{10,9},... | collective-permute-start | bytes 393224 | tf_op jit(solution)/shard_map/ppermute | solution.py:403
  14.4 3.0 %collective-permute-start.2 = (f32[1,512]{1,0:T(1,128)S(1)}, f32[1,512]{1,0:T(1,128)S(1)}, u32[]{:S(2)}, u32[]{:S(2)}) collective-permute-start(f32[1,512]{1,0:T(1,128)S(1)} %copy-done.3), channel_id=1, source_target_pairs={{8,0},{16,8},{24,16},{0,24},{9,1},{17,9},{25,17},{1,25},{10,2},{18... | collective-permute-start | bytes 6152 | tf_op jit(solution)/shard_map/ppermute | solution.py:405
  17.5 1.6 %collective-permute-start.3 = (bf16[128,1024]{1,0:T(8,128)(2,1)S(1)}, bf16[128,1024]{1,0:T(8,128)(2,1)S(1)}, u32[]{:S(2)}, u32[]{:S(2)}) collective-permute-start(bf16[128,1024]{1,0:T(8,128)(2,1)S(1)} %subtract_convert_fusion), channel_id=1, source_target_pairs={{0,1},{1,0},{2,3},{3,2},{4,5},{5,4},{6,7},{7,6},{8,9},{9,8},{10,11... | collective-permute-start | bytes 786440 | tf_op jit(solution)/shard_map/ppermute | solution.py:416
  19.2 11.0 %collective-permute-start.5 = (bf16[64,1024]{1,0:T(8,128)(2,1)S(1)}, bf16[64,1024]{1,0:T(8,128)(2,1)S(1)}, u32[]{:S(2)}, u32[]{:S(2)}) collective-permute-start(bf16[64,1024]{1,0:T(8,128)(2,1)S(1)} %slice.12), channel_id=1, source_target_pairs={{0,4},{1,7},{2,6},{3,5},{4,0},{5,3},{6,2},{7,1}} | collective-permute-start | bytes 393224 | tf_op jit(solution)/shard_map/ppermute | solution.py:345
  24.3 7.0 %collective-permute-start.4 = (bf16[64,1024]{1,0:T(8,128)(2,1)S(1)}, bf16[64,1024]{1,0:T(8,128)(2,1)S(1)}, u32[]{:S(2)}, u32[]{:S(2)}) collective-permute-start(bf16[64,1024]{1,0:T(8,128)(2,1)S(1)} %slice.12), channel_id=1, source_target_pairs={{0,0},{1,3},{2,2},{3,1},{4,4},{5,7},{6,6},{7,5}} | collective-permute-start | bytes 393224 | tf_op jit(solution)/shard_map/ppermute | solution.py:345
  26.2 7.4 %collective-permute-start.8 = (bf16[128,1024]{1,0:T(8,128)(2,1)S(1)}, bf16[128,1024]{1,0:T(8,128)(2,1)S(1)}, u32[]{:S(2)}, u32[]{:S(2)}) collective-permute-start(bf16[128,1024]{1,0:T(8,128)(2,1)S(1)} %add_convert_fusion), channel_id=1, source_target_pairs={{8,0},{16,8},{24,16},{0,24},{9,1},{17,9},{25,17},{1,25},{10,2},{18... | collective-permute-start | bytes 786440 | tf_op jit(solution)/shard_map/ppermute | solution.py:426
  32.1 1.5 %collective-permute-start.6 = (bf16[64,1024]{1,0:T(8,128)(2,1)S(1)}, bf16[64,1024]{1,0:T(8,128)(2,1)S(1)}, u32[]{:S(2)}, u32[]{:S(2)}) collective-permute-start(bf16[64,1024]{1,0:T(8,128)(2,1)S(1)} %shard_map.88.mine_ref), channel_id=1, source_target_pairs={{0,1},{1,0},{2,3},{3,2},{4,5},{5,4},{6,7},{7,6},{8,9},{9,8},{10,11... | collective-permute-start | bytes 393224 | tf_op jit(solution)/shard_map/ppermute | solution.py:466
  32.2 1.4 %collective-permute-start.7 = (f32[2,512]{1,0:T(2,128)S(1)}, f32[2,512]{1,0:T(2,128)S(1)}, u32[]{:S(2)}, u32[]{:S(2)}) collective-permute-start(f32[2,512]{1,0:T(2,128)S(1)} %pad_maximum_fusion), channel_id=1, source_target_pairs={{0,1},{1,0},{2,3},{3,2},{4,5},{5,4},{6,7},{7,6},{8,9},{9,8},{10,11... | collective-permute-start | bytes 12296 | tf_op jit(solution)/shard_map/ppermute | solution.py:417
  33.8 8.9 %collective-permute-start.10 = (bf16[64,1024]{1,0:T(8,128)(2,1)S(1)}, bf16[64,1024]{1,0:T(8,128)(2,1)S(1)}, u32[]{:S(2)}, u32[]{:S(2)}) collective-permute-start(bf16[64,1024]{1,0:T(8,128)(2,1)S(1)} %get-tuple-element.36), channel_id=1, source_target_pairs={{0,12},{1,15},{2,14},{3,13},{4,8},{5,11},{6,10},{7,9},{8,20},{9,23... | collective-permute-start | bytes 393224 | tf_op jit(solution)/shard_map/ppermute | solution.py:345
  34.6 8.6 %collective-permute-start.9 = (bf16[64,1024]{1,0:T(8,128)(2,1)S(1)}, bf16[64,1024]{1,0:T(8,128)(2,1)S(1)}, u32[]{:S(2)}, u32[]{:S(2)}) collective-permute-start(bf16[64,1024]{1,0:T(8,128)(2,1)S(1)} %get-tuple-element.36), channel_id=1, source_target_pairs={{0,8},{1,11},{2,10},{3,9},{4,12},{5,15},{6,14},{7,13},{8,16},{9,19... | collective-permute-start | bytes 393224 | tf_op jit(solution)/shard_map/ppermute | solution.py:345
  43.7 3.2 %collective-permute-start.11 = (bf16[64,1024]{1,0:T(8,128)(2,1)S(1)}, bf16[64,1024]{1,0:T(8,128)(2,1)S(1)}, u32[]{:S(2)}, u32[]{:S(2)}) collective-permute-start(bf16[64,1024]{1,0:T(8,128)(2,1)S(1)} %shard_map.91.mine_ref), channel_id=1, source_target_pairs={{0,1},{1,0},{2,3},{3,2},{4,5},{5,4},{6,7},{7,6},{8,9},{9,8},{10,11... | collective-permute-start | bytes 393224 | tf_op jit(solution)/shard_map/ppermute | solution.py:466
  47.0 7.5 %collective-permute-start.13 = (bf16[64,1024]{1,0:T(8,128)(2,1)S(1)}, bf16[64,1024]{1,0:T(8,128)(2,1)S(1)}, u32[]{:S(2)}, u32[]{:S(2)}) collective-permute-start(bf16[64,1024]{1,0:T(8,128)(2,1)S(1)} %get-tuple-element.38.after_ref), channel_id=1, source_target_pairs={{8,20},{9,23},{10,22},{11,21},{12,16},{13,19},{14,18},{15,17},{0,1... | collective-permute-start | bytes 393224 | tf_op jit(solution)/shard_map/ppermute | solution.py:345
  47.6 9.1 %collective-permute-start.12 = (bf16[64,1024]{1,0:T(8,128)(2,1)S(1)}, bf16[64,1024]{1,0:T(8,128)(2,1)S(1)}, u32[]{:S(2)}, u32[]{:S(2)}) collective-permute-start(bf16[64,1024]{1,0:T(8,128)(2,1)S(1)} %get-tuple-element.38.after_ref), channel_id=1, source_target_pairs={{8,16},{9,19},{10,18},{11,17},{12,20},{13,23},{14,22},{15,21},{0,8... | collective-permute-start | bytes 393224 | tf_op jit(solution)/shard_map/ppermute | solution.py:345
  57.2 2.9 %collective-permute-start.14 = (bf16[64,1024]{1,0:T(8,128)(2,1)S(1)}, bf16[64,1024]{1,0:T(8,128)(2,1)S(1)}, u32[]{:S(2)}, u32[]{:S(2)}) collective-permute-start(bf16[64,1024]{1,0:T(8,128)(2,1)S(1)} %shard_map.95.mine_ref), channel_id=1, source_target_pairs={{0,1},{1,0},{2,3},{3,2},{4,5},{5,4},{6,7},{7,6},{8,9},{9,8},{10,11... | collective-permute-start | bytes 393224 | tf_op jit(solution)/shard_map/ppermute | solution.py:466
  60.1 8.1 %collective-permute-start.16 = (bf16[64,1024]{1,0:T(8,128)(2,1)S(1)}, bf16[64,1024]{1,0:T(8,128)(2,1)S(1)}, u32[]{:S(2)}, u32[]{:S(2)}) collective-permute-start(bf16[64,1024]{1,0:T(8,128)(2,1)S(1)} %get-tuple-element.40.after_ref), channel_id=1, source_target_pairs={{16,28},{17,31},{18,30},{19,29},{20,24},{21,27},{22,26},{23,25},{8... | collective-permute-start | bytes 393224 | tf_op jit(solution)/shard_map/ppermute | solution.py:345
  62.4 7.1 %collective-permute-start.15 = (bf16[64,1024]{1,0:T(8,128)(2,1)S(1)}, bf16[64,1024]{1,0:T(8,128)(2,1)S(1)}, u32[]{:S(2)}, u32[]{:S(2)}) collective-permute-start(bf16[64,1024]{1,0:T(8,128)(2,1)S(1)} %get-tuple-element.40.after_ref), channel_id=1, source_target_pairs={{16,24},{17,27},{18,26},{19,25},{20,28},{21,31},{22,30},{23,29},{8... | collective-permute-start | bytes 393224 | tf_op jit(solution)/shard_map/ppermute | solution.py:345
  70.0 1.4 %collective-permute-start.17 = (bf16[64,1024]{1,0:T(8,128)(2,1)S(1)}, bf16[64,1024]{1,0:T(8,128)(2,1)S(1)}, u32[]{:S(2)}, u32[]{:S(2)}) collective-permute-start(bf16[64,1024]{1,0:T(8,128)(2,1)S(1)} %shard_map.99.mine_ref), channel_id=1, source_target_pairs={{0,1},{1,0},{2,3},{3,2},{4,5},{5,4},{6,7},{7,6},{8,9},{9,8},{10,11... | collective-permute-start | bytes 393224 | tf_op jit(solution)/shard_map/ppermute | solution.py:466
  71.5 7.1 %collective-permute-start.19 = (bf16[64,1024]{1,0:T(8,128)(2,1)S(1)}, bf16[64,1024]{1,0:T(8,128)(2,1)S(1)}, u32[]{:S(2)}, u32[]{:S(2)}) collective-permute-start(bf16[64,1024]{1,0:T(8,128)(2,1)S(1)} %get-tuple-element.42), channel_id=1, source_target_pairs={{24,20},{25,23},{26,22},{27,21},{28,16},{29,19},{30,18},{31,17},{1... | collective-permute-start | bytes 393224 | tf_op jit(solution)/shard_map/ppermute | solution.py:345
  72.8 7.6 %collective-permute-start.18 = (bf16[64,1024]{1,0:T(8,128)(2,1)S(1)}, bf16[64,1024]{1,0:T(8,128)(2,1)S(1)}, u32[]{:S(2)}, u32[]{:S(2)}) collective-permute-start(bf16[64,1024]{1,0:T(8,128)(2,1)S(1)} %get-tuple-element.42), channel_id=1, source_target_pairs={{24,16},{25,19},{26,18},{27,17},{28,20},{29,23},{30,22},{31,21},{1... | collective-permute-start | bytes 393224 | tf_op jit(solution)/shard_map/ppermute | solution.py:345
  81.0 1.9 %collective-permute-start.20 = (bf16[64,1024]{1,0:T(8,128)(2,1)S(1)}, bf16[64,1024]{1,0:T(8,128)(2,1)S(1)}, u32[]{:S(2)}, u32[]{:S(2)}) collective-permute-start(bf16[64,1024]{1,0:T(8,128)(2,1)S(1)} %shard_map.102.mine_ref), channel_id=1, source_target_pairs={{0,1},{1,0},{2,3},{3,2},{4,5},{5,4},{6,7},{7,6},{8,9},{9,8},{10,11... | collective-permute-start | bytes 393224 | tf_op jit(solution)/shard_map/ppermute | solution.py:466
  83.0 5.8 %collective-permute-start.22 = (bf16[64,1024]{1,0:T(8,128)(2,1)S(1)}, bf16[64,1024]{1,0:T(8,128)(2,1)S(1)}, u32[]{:S(2)}, u32[]{:S(2)}) collective-permute-start(bf16[64,1024]{1,0:T(8,128)(2,1)S(1)} %get-tuple-element.44), channel_id=1, source_target_pairs={{16,12},{17,15},{18,14},{19,13},{20,8},{21,11},{22,10},{23,9},{24,... | collective-permute-start | bytes 393224 | tf_op jit(solution)/shard_map/ppermute | solution.py:345
  84.2 7.2 %collective-permute-start.21 = (bf16[64,1024]{1,0:T(8,128)(2,1)S(1)}, bf16[64,1024]{1,0:T(8,128)(2,1)S(1)}, u32[]{:S(2)}, u32[]{:S(2)}) collective-permute-start(bf16[64,1024]{1,0:T(8,128)(2,1)S(1)} %get-tuple-element.44), channel_id=1, source_target_pairs={{16,8},{17,11},{18,10},{19,9},{20,12},{21,15},{22,14},{23,13},{24,... | collective-permute-start | bytes 393224 | tf_op jit(solution)/shard_map/ppermute | solution.py:345
  92.0 1.4 %collective-permute-start.23 = (bf16[64,1024]{1,0:T(8,128)(2,1)S(1)}, bf16[64,1024]{1,0:T(8,128)(2,1)S(1)}, u32[]{:S(2)}, u32[]{:S(2)}) collective-permute-start(bf16[64,1024]{1,0:T(8,128)(2,1)S(1)} %shard_map.105.mine_ref), channel_id=1, source_target_pairs={{0,1},{1,0},{2,3},{3,2},{4,5},{5,4},{6,7},{7,6},{8,9},{9,8},{10,11... | collective-permute-start | bytes 393224 | tf_op jit(solution)/shard_map/ppermute | solution.py:466
  93.5 11.7 %collective-permute-start.25 = (bf16[64,1024]{1,0:T(8,128)(2,1)S(1)}, bf16[64,1024]{1,0:T(8,128)(2,1)S(1)}, u32[]{:S(2)}, u32[]{:S(2)}) collective-permute-start(bf16[64,1024]{1,0:T(8,128)(2,1)S(1)} %get-tuple-element.46), channel_id=1, source_target_pairs={{8,4},{9,7},{10,6},{11,5},{12,0},{13,3},{14,2},{15,1},{16,12},{17,... | collective-permute-start | bytes 393224 | tf_op jit(solution)/shard_map/ppermute | solution.py:345
  103.0 6.6 %collective-permute-start.24 = (bf16[64,1024]{1,0:T(8,128)(2,1)S(1)}, bf16[64,1024]{1,0:T(8,128)(2,1)S(1)}, u32[]{:S(2)}, u32[]{:S(2)}) collective-permute-start(bf16[64,1024]{1,0:T(8,128)(2,1)S(1)} %get-tuple-element.46), channel_id=1, source_target_pairs={{8,0},{9,3},{10,2},{11,1},{12,4},{13,7},{14,6},{15,5},{16,8},{17,1... | collective-permute-start | bytes 393224 | tf_op jit(solution)/shard_map/ppermute | solution.py:345
  110.1 2.2 %collective-permute-start.26 = (bf16[64,1024]{1,0:T(8,128)(2,1)S(1)}, bf16[64,1024]{1,0:T(8,128)(2,1)S(1)}, u32[]{:S(2)}, u32[]{:S(2)}) collective-permute-start(bf16[64,1024]{1,0:T(8,128)(2,1)S(1)} %shard_map.108.mine_ref), channel_id=1, source_target_pairs={{0,1},{1,0},{2,3},{3,2},{4,5},{5,4},{6,7},{7,6},{8,9},{9,8},{10,11... | collective-permute-start | bytes 393224 | tf_op jit(solution)/shard_map/ppermute | solution.py:466
  112.4 7.9 %collective-permute-start.28 = (bf16[64,1024]{1,0:T(8,128)(2,1)S(1)}, bf16[64,1024]{1,0:T(8,128)(2,1)S(1)}, u32[]{:S(2)}, u32[]{:S(2)}) collective-permute-start(bf16[64,1024]{1,0:T(8,128)(2,1)S(1)} %get-tuple-element.48), channel_id=1, source_target_pairs={{8,4},{9,7},{10,6},{11,5},{12,0},{13,3},{14,2},{15,1},{16,20},{17,... | collective-permute-start | bytes 393224 | tf_op jit(solution)/shard_map/ppermute | solution.py:345
  115.8 7.2 %collective-permute-start.27 = (bf16[64,1024]{1,0:T(8,128)(2,1)S(1)}, bf16[64,1024]{1,0:T(8,128)(2,1)S(1)}, u32[]{:S(2)}, u32[]{:S(2)}) collective-permute-start(bf16[64,1024]{1,0:T(8,128)(2,1)S(1)} %get-tuple-element.48), channel_id=1, source_target_pairs={{8,0},{9,3},{10,2},{11,1},{12,4},{13,7},{14,6},{15,5},{16,16},{17,... | collective-permute-start | bytes 393224 | tf_op jit(solution)/shard_map/ppermute | solution.py:345
  123.5 2.4 %collective-permute-start.29 = (bf16[64,1024]{1,0:T(8,128)(2,1)S(1)}, bf16[64,1024]{1,0:T(8,128)(2,1)S(1)}, u32[]{:S(2)}, u32[]{:S(2)}) collective-permute-start(bf16[64,1024]{1,0:T(8,128)(2,1)S(1)} %shard_map.111.mine_ref), channel_id=1, source_target_pairs={{0,1},{1,0},{2,3},{3,2},{4,5},{5,4},{6,7},{7,6},{8,9},{9,8},{10,11... | collective-permute-start | bytes 393224 | tf_op jit(solution)/shard_map/ppermute | solution.py:466
  126.7 6.3 %collective-permute-start.30 = (bf16[128,512]{1,0:T(8,128)(2,1)S(1)}, bf16[128,512]{1,0:T(8,128)(2,1)S(1)}, u32[]{:S(2)}, u32[]{:S(2)}) collective-permute-start(bf16[128,512]{1,0:T(8,128)(2,1)S(1)} %slice_select_fusion.top_ref), channel_id=1, source_target_pairs={{1,2},{3,4},{5,6},{2,1},{4,3},{6,5},{9,10},{11,12},{13,14},{10,9},... | collective-permute-start | bytes 393224 | tf_op jit(solution)/shard_map/ppermute | solution.py:516
  (3 other events, 8.3 us)

commit v5 on v4

--- a/solution.py
+++ b/solution.py
@@ -37,6 +37,11 @@
 def own_place():
     place = lax.axis_index("front")
     return place // 2, place % 2
+
+
+def own_half():
+    chip, core = own_place()
+    return (chip // (lax.axis_size("front") // 4)) ^ core
 
 
 def own_turn(turn):
@@ -74,7 +79,7 @@
     edge = boundary_ref.shape[1]
     rows = top_ref.shape[2]
     window = 3 * rows
-    chip, core = own_place()
+    core = own_place()[1]
     copies = []
     for step in range(leaf_count // group):
         leaves = pl.ds(step * group, group)
@@ -89,7 +94,7 @@
         )
         for copy in copies[-1]:
             copy.start()
-    staged = sum(half_copies((chip + core + 1) % 2, solver_hbm, given_ref, half_sems), [])
+    staged = sum(half_copies(1 - own_half(), solver_hbm, given_ref, half_sems), [])
     places = lax.broadcasted_iota(jnp.int16, (edge, window), 1)
     for step in range(leaf_count // group):
         for copy in copies[step]:
@@ -223,13 +228,13 @@
         copy.wait()
 
 
-def half_copies(parity, inverse_hbm, to_ref, sems):
+def half_copies(which, inverse_hbm, to_ref, sems):
     pairs, pieces = sems.shape
     span = to_ref.shape[1] // pairs
     tall = to_ref.shape[0] // pieces
     copies = []
     for q in range(pairs):
-        start = pl.multiple_of((2 * q + parity) * span, span)
+        start = pl.multiple_of((pairs * which + q) * span, span)
         copies.append([])
         for r in range(pieces):
             here = pl.ds(r * tall, tall)
@@ -245,7 +250,7 @@
 
 
 def turn_kernel(inverse_hbm, taken_hbm, out_ref, kept_ref, taken_ref, kept_sems, taken_sems):
-    chip, core = own_place()
+    core = own_place()[1]
     rows = taken_ref.shape[0]
     span = kept_ref.shape[1] // kept_sems.shape[0]
     taken_copies = []
@@ -255,7 +260,7 @@
             pltpu.make_async_copy(taken_hbm.at[:, lanes], taken_ref.at[:, lanes], taken_sems.at[q])
         )
         taken_copies[-1].start()
-    kept_copies = half_copies((chip + core) % 2, inverse_hbm, kept_ref, kept_sems)
+    kept_copies = half_copies(own_half(), inverse_hbm, kept_ref, kept_sems)
     piece = min(span, 256)
     for q in range(len(kept_copies)):
         taken_copies[q].wait()
@@ -281,9 +286,10 @@
     out_ref = refs[-1]
     wave_rows, rows = out_ref.shape
     chip = own_place()[0]
+    half = inverse_ref.shape[0] // rows
     total = refs[-2][...] if more else jnp.zeros((wave_rows, rows), F32)
     for n, i in enumerate(blocks):
-        place = pl.ds(pl.multiple_of(((chip // 2) ^ i) * rows, rows), rows)
+        place = pl.ds(pl.multiple_of(((chip % half) ^ i) * rows, rows), rows)
         total += jnp.dot(refs[n][...], inverse_ref[place, :], preferred_element_type=F32)
     out_ref[...] = total.astype(out_ref.dtype)
 
@@ -332,18 +338,19 @@
 
 
 def spread(values, panel_pairs, chips):
+    half = chips // 2
     received = []
-    for i in range(chips // 2):
+    for i in reversed(range(half)):
         route = []
         for start, end in panel_pairs:
             for chip in range(chips):
                 for core in range(2):
-                    there = chip ^ (2 * i + core)
+                    there = chip ^ (half * core + i)
                     route.append(
                         (2 * (start * chips + chip) + core, 2 * (end * chips + there) + core)
                     )
         received.append(lax.ppermute(values, ("panel", "front"), route))
-    return received
+    return received[::-1]
 
 
 def body(top_source, leaf_source, top_inverse, leaf_inverse, boundary, touch_rows, coupling):

time: 136 us -> 132 us (0.971)
  starting transfers between devices: 56.3 us -> 50.5 us
  waiting for transfers between devices: 46.1 us -> 47.9 us
    ppermute x8, starting transfers between devices: 7.85 us -> 0.57 us  [body(): other = lax.ppermute(share, 'front', swap_core)]
    ppermute x8, waiting for transfers between devices: 7.6 us -> 9.35 us  [body(): other = lax.ppermute(share, 'front', swap_core)]
  transfers between devices with their start and end apart: 31 -> 31, of which waited for: 24 -> 25; matrix products, arithmetic and copies ran while one was open for 0% -> 0% of each run, Pallas kernels for 11% -> 12%
where the time goes in v5:
time: 132 us
  starting transfers between devices  50.5 us (38%)
  waiting for transfers between devices  47.9 us (36%)
  Pallas kernels  30.2 us (23%)
  local copies, waits for them, and re-layouts  1.66 us (1%)
    ppermute x16, starting transfers between devices, spread(): received.append(lax.ppermute(values, ('panel', 'front'), route))  39.9 us
    ppermute x16, waiting for transfers between devices, spread(): received.append(lax.ppermute(values, ('panel', 'front'), route))  33.1 us
    ppermute x8, waiting for transfers between devices, body(): other = lax.ppermute(share, 'front', swap_core)  9.35 us
    pallas_call x15, Pallas kernels, body(): pl.pallas_call(functools.partial(fold_kernel, blocks, bool(share), len(be...  7.55 us
    pallas_call x1, Pallas kernels, body(): pl.pallas_call(functools.partial(push_kernel, group), out_shape=(pltpu.VM...  7.48 us
    ppermute x1, starting transfers between devices, body(): inward = lax.ppermute(outward, 'front', swap_chip)  4.55 us
    pallas_call x1, Pallas kernels, body(): pl.pallas_call(turn_kernel, out_shape=pltpu.VMEM((width // 2, chip_rows),...  3.91 us
    pallas_call x1, Pallas kernels, body(): pl.pallas_call(functools.partial(lift_matrix_kernel, group), out_shape=pl...  3.72 us
  transfers between devices with their start and end apart: 31, of which 25 were waited for; matrix products, arithmetic and copies ran while one was open for 0% of the time, Pallas kernels for 12%

profile of v5, /device:TPU:1, one launch (start us, length us, event | category | flops | bytes accessed | tf_op | source)
XLA Modules:
  0.0 131.7 jit_solution(11481316117749608076)
XLA Ops:
  2.3 7.5 %shard_map.86 = (bf16[128,512]{1,0:T(8,128)(2,1)S(1)}, f32[128,1024]{1,0:T(8,128)S(1)}, bf16[128,9216]{1,0:T(8,128)(2,1)S(1)}, bf16[512,2048]{1,0:T(8,128)(2,1)}) custom-call(s32[9,4,128]{2,1,0:T(4,128)S(1)} %bitcast.7, bf16[1,128,512]{2,1,0:T(8,128)(2,1)S(1)} %copy-done, bf16[128,9216]{1,0:T(8,128)(2,1)} %bitcast.15, bf16[36,256,256]{2,1,0:T(8,128)(2,1)} %bitcast.9, ...), custom_call_target="tpu_custom_call" | custom-call | tf_op jit(solution)/shard_map/pallas_call | solution.py:380
  9.9 4.6 %collective-permute-start.1 = (bf16[128,512]{1,0:T(8,128)(2,1)S(1)}, bf16[128,512]{1,0:T(8,128)(2,1)S(1)}, u32[]{:S(2)}, u32[]{:S(2)}) collective-permute-start(bf16[128,512]{1,0:T(8,128)(2,1)S(1)} %get-tuple-element.32), channel_id=1, source_target_pairs={{1,2},{3,4},{5,6},{2,1},{4,3},{6,5},{9,10},{11,12},{13,14},{10,9},... | collective-permute-start | bytes 393224 | tf_op jit(solution)/shard_map/ppermute | solution.py:410
  14.4 2.2 %collective-permute-start.2 = (f32[1,512]{1,0:T(1,128)S(1)}, f32[1,512]{1,0:T(1,128)S(1)}, u32[]{:S(2)}, u32[]{:S(2)}) collective-permute-start(f32[1,512]{1,0:T(1,128)S(1)} %copy-done.3), channel_id=1, source_target_pairs={{8,0},{16,8},{24,16},{0,24},{9,1},{17,9},{25,17},{1,25},{10,2},{18... | collective-permute-start | bytes 6152 | tf_op jit(solution)/shard_map/ppermute | solution.py:412
  19.2 5.1 %collective-permute-start.5 = (bf16[64,1024]{1,0:T(8,128)(2,1)S(1)}, bf16[64,1024]{1,0:T(8,128)(2,1)S(1)}, u32[]{:S(2)}, u32[]{:S(2)}) collective-permute-start(bf16[64,1024]{1,0:T(8,128)(2,1)S(1)} %slice.12), channel_id=1, source_target_pairs={{0,2},{1,7},{2,0},{3,5},{4,6},{5,3},{6,4},{7,1}} | collective-permute-start | bytes 393224 | tf_op jit(solution)/shard_map/ppermute | solution.py:352
  24.3 1.9 %collective-permute-start.4 = (bf16[64,1024]{1,0:T(8,128)(2,1)S(1)}, bf16[64,1024]{1,0:T(8,128)(2,1)S(1)}, u32[]{:S(2)}, u32[]{:S(2)}) collective-permute-start(bf16[64,1024]{1,0:T(8,128)(2,1)S(1)} %slice.12), channel_id=1, source_target_pairs={{0,0},{1,5},{2,2},{3,7},{4,4},{5,1},{6,6},{7,3}} | collective-permute-start | bytes 393224 | tf_op jit(solution)/shard_map/ppermute | solution.py:352
  26.3 3.9 %shard_map.87.inverse_ref = bf16[2048,1024]{1,0:T(8,128)(2,1)S(1)} custom-call(bf16[512,4096]{1,0:T(8,128)(2,1)} %bitcast.12, bf16[512,2048]{1,0:T(8,128)(2,1)} %collective-permute-done.taken_hbm), custom_call_target="tpu_custom_call" | custom-call | flops 536870912 | bytes 8388608 | tf_op jit(solution)/shard_map/pallas_call | solution.py:435
  36.3 6.5 %collective-permute-done.10.refs_0_ = bf16[64,1024]{1,0:T(8,128)(2,1)S(1)} collective-permute-done((bf16[64,1024]{1,0:T(8,128)(2,1)S(1)}, bf16[64,1024]{1,0:T(8,128)(2,1)S(1)}, u32[]{:S(2)}, u32[]{:S(2)}) %collective-permute-start.10) | collective-permute-done | bytes 131104 | tf_op jit(solution)/shard_map/ppermute | solution.py:352
  46.6 1.8 %collective-permute-start.13 = (bf16[64,1024]{1,0:T(8,128)(2,1)S(1)}, bf16[64,1024]{1,0:T(8,128)(2,1)S(1)}, u32[]{:S(2)}, u32[]{:S(2)}) collective-permute-start(bf16[64,1024]{1,0:T(8,128)(2,1)S(1)} %get-tuple-element.38.after_ref), channel_id=1, source_target_pairs={{8,18},{9,23},{10,16},{11,21},{12,22},{13,19},{14,20},{15,17},{0,1... | collective-permute-start | bytes 393224 | tf_op jit(solution)/shard_map/ppermute | solution.py:352
  48.5 1.9 %collective-permute-start.12 = (bf16[64,1024]{1,0:T(8,128)(2,1)S(1)}, bf16[64,1024]{1,0:T(8,128)(2,1)S(1)}, u32[]{:S(2)}, u32[]{:S(2)}) collective-permute-start(bf16[64,1024]{1,0:T(8,128)(2,1)S(1)} %get-tuple-element.38.after_ref), channel_id=1, source_target_pairs={{8,16},{9,21},{10,18},{11,23},{12,20},{13,17},{14,22},{15,19},{0,8... | collective-permute-start | bytes 393224 | tf_op jit(solution)/shard_map/ppermute | solution.py:352
  50.4 2.1 %shard_map.93.refs_0_.pick_ref = bf16[1536,4608]{1,0:T(8,128)(2,1)S(1)} custom-call(s32[9,4,128]{2,1,0:T(4,128)S(1)} %bitcast.8, bf16[64,1024]{1,0:T(8,128)(2,1)S(1)} %get-tuple-element.38.after_ref), custom_call_target="tpu_custom_call" | custom-call | flops 1207959552 | bytes 14155776 | tf_op jit(solution)/shard_map/pallas_call | solution.py:489
  54.5 2.3 %collective-permute-done.12.refs_1_ = bf16[64,1024]{1,0:T(8,128)(2,1)S(1)} collective-permute-done((bf16[64,1024]{1,0:T(8,128)(2,1)S(1)}, bf16[64,1024]{1,0:T(8,128)(2,1)S(1)}, u32[]{:S(2)}, u32[]{:S(2)}) %collective-permute-start.12) | collective-permute-done | bytes 131104 | tf_op jit(solution)/shard_map/ppermute | solution.py:352
  58.8 1.9 %collective-permute-start.16 = (bf16[64,1024]{1,0:T(8,128)(2,1)S(1)}, bf16[64,1024]{1,0:T(8,128)(2,1)S(1)}, u32[]{:S(2)}, u32[]{:S(2)}) collective-permute-start(bf16[64,1024]{1,0:T(8,128)(2,1)S(1)} %get-tuple-element.40.after_ref), channel_id=1, source_target_pairs={{16,26},{17,31},{18,24},{19,29},{20,30},{21,27},{22,28},{23,25},{8... | collective-permute-start | bytes 393224 | tf_op jit(solution)/shard_map/ppermute | solution.py:352
  60.7 2.1 %collective-permute-start.15 = (bf16[64,1024]{1,0:T(8,128)(2,1)S(1)}, bf16[64,1024]{1,0:T(8,128)(2,1)S(1)}, u32[]{:S(2)}, u32[]{:S(2)}) collective-permute-start(bf16[64,1024]{1,0:T(8,128)(2,1)S(1)} %get-tuple-element.40.after_ref), channel_id=1, source_target_pairs={{16,24},{17,29},{18,26},{19,31},{20,28},{21,25},{22,30},{23,27},{8... | collective-permute-start | bytes 393224 | tf_op jit(solution)/shard_map/ppermute | solution.py:352
  62.8 3.7 %shard_map.97.refs_0_.matrix_ref = bf16[36,128,256]{2,1,0:T(8,128)(2,1)S(1)} custom-call(bf16[36,256,256]{2,1,0:T(8,128)(2,1)} %bitcast.10, bf16[36,128,256]{2,1,0:T(8,128)(2,1)} %bitcast.14, bf16[64,1024]{1,0:T(8,128)(2,1)S(1)} %get-tuple-element.40.after_ref), custom_call_target="tpu_custom_call" | custom-call | flops 603979776 | bytes 9437184 | tf_op jit(solution)/shard_map/pallas_call | solution.py:503
  69.8 1.9 %collective-permute-start.19 = (bf16[64,1024]{1,0:T(8,128)(2,1)S(1)}, bf16[64,1024]{1,0:T(8,128)(2,1)S(1)}, u32[]{:S(2)}, u32[]{:S(2)}) collective-permute-start(bf16[64,1024]{1,0:T(8,128)(2,1)S(1)} %get-tuple-element.42), channel_id=1, source_target_pairs={{24,18},{25,23},{26,16},{27,21},{28,22},{29,19},{30,20},{31,17},{1... | collective-permute-start | bytes 393224 | tf_op jit(solution)/shard_map/ppermute | solution.py:352
  71.7 2.2 %collective-permute-start.18 = (bf16[64,1024]{1,0:T(8,128)(2,1)S(1)}, bf16[64,1024]{1,0:T(8,128)(2,1)S(1)}, u32[]{:S(2)}, u32[]{:S(2)}) collective-permute-start(bf16[64,1024]{1,0:T(8,128)(2,1)S(1)} %get-tuple-element.42), channel_id=1, source_target_pairs={{24,16},{25,21},{26,18},{27,23},{28,20},{29,17},{30,22},{31,19},{1... | collective-permute-start | bytes 393224 | tf_op jit(solution)/shard_map/ppermute | solution.py:352
  73.9 2.9 %collective-permute-done.19.refs_0_ = bf16[64,1024]{1,0:T(8,128)(2,1)S(1)} collective-permute-done((bf16[64,1024]{1,0:T(8,128)(2,1)S(1)}, bf16[64,1024]{1,0:T(8,128)(2,1)S(1)}, u32[]{:S(2)}, u32[]{:S(2)}) %collective-permute-start.19) | collective-permute-done | bytes 131104 | tf_op jit(solution)/shard_map/ppermute | solution.py:352
  77.3 2.4 %collective-permute-done.18.refs_0_ = bf16[64,1024]{1,0:T(8,128)(2,1)S(1)} collective-permute-done((bf16[64,1024]{1,0:T(8,128)(2,1)S(1)}, bf16[64,1024]{1,0:T(8,128)(2,1)S(1)}, u32[]{:S(2)}, u32[]{:S(2)}) %collective-permute-start.18) | collective-permute-done | bytes 131104 | tf_op jit(solution)/shard_map/ppermute | solution.py:352
  81.7 1.7 %collective-permute-start.22 = (bf16[64,1024]{1,0:T(8,128)(2,1)S(1)}, bf16[64,1024]{1,0:T(8,128)(2,1)S(1)}, u32[]{:S(2)}, u32[]{:S(2)}) collective-permute-start(bf16[64,1024]{1,0:T(8,128)(2,1)S(1)} %get-tuple-element.44), channel_id=1, source_target_pairs={{16,10},{17,15},{18,8},{19,13},{20,14},{21,11},{22,12},{23,9},{24,... | collective-permute-start | bytes 393224 | tf_op jit(solution)/shard_map/ppermute | solution.py:352
  83.3 1.9 %collective-permute-start.21 = (bf16[64,1024]{1,0:T(8,128)(2,1)S(1)}, bf16[64,1024]{1,0:T(8,128)(2,1)S(1)}, u32[]{:S(2)}, u32[]{:S(2)}) collective-permute-start(bf16[64,1024]{1,0:T(8,128)(2,1)S(1)} %get-tuple-element.44), channel_id=1, source_target_pairs={{16,8},{17,13},{18,10},{19,15},{20,12},{21,9},{22,14},{23,11},{24,... | collective-permute-start | bytes 393224 | tf_op jit(solution)/shard_map/ppermute | solution.py:352
  85.3 2.3 %collective-permute-done.22.refs_0_ = bf16[64,1024]{1,0:T(8,128)(2,1)S(1)} collective-permute-done((bf16[64,1024]{1,0:T(8,128)(2,1)S(1)}, bf16[64,1024]{1,0:T(8,128)(2,1)S(1)}, u32[]{:S(2)}, u32[]{:S(2)}) %collective-permute-start.22) | collective-permute-done | bytes 131104 | tf_op jit(solution)/shard_map/ppermute | solution.py:352
  88.0 2.6 %collective-permute-done.21.refs_0_ = bf16[64,1024]{1,0:T(8,128)(2,1)S(1)} collective-permute-done((bf16[64,1024]{1,0:T(8,128)(2,1)S(1)}, bf16[64,1024]{1,0:T(8,128)(2,1)S(1)}, u32[]{:S(2)}, u32[]{:S(2)}) %collective-permute-start.21) | collective-permute-done | bytes 131104 | tf_op jit(solution)/shard_map/ppermute | solution.py:352
  92.7 5.6 %collective-permute-start.25 = (bf16[64,1024]{1,0:T(8,128)(2,1)S(1)}, bf16[64,1024]{1,0:T(8,128)(2,1)S(1)}, u32[]{:S(2)}, u32[]{:S(2)}) collective-permute-start(bf16[64,1024]{1,0:T(8,128)(2,1)S(1)} %get-tuple-element.46), channel_id=1, source_target_pairs={{8,2},{9,7},{10,0},{11,5},{12,6},{13,3},{14,4},{15,1},{16,10},{17,... | collective-permute-start | bytes 393224 | tf_op jit(solution)/shard_map/ppermute | solution.py:352
  98.3 3.6 %collective-permute-start.24 = (bf16[64,1024]{1,0:T(8,128)(2,1)S(1)}, bf16[64,1024]{1,0:T(8,128)(2,1)S(1)}, u32[]{:S(2)}, u32[]{:S(2)}) collective-permute-start(bf16[64,1024]{1,0:T(8,128)(2,1)S(1)} %get-tuple-element.46), channel_id=1, source_target_pairs={{8,0},{9,5},{10,2},{11,7},{12,4},{13,1},{14,6},{15,3},{16,8},{17,1... | collective-permute-start | bytes 393224 | tf_op jit(solution)/shard_map/ppermute | solution.py:352
  103.7 2.7 %collective-permute-done.24.refs_0_ = bf16[64,1024]{1,0:T(8,128)(2,1)S(1)} collective-permute-done((bf16[64,1024]{1,0:T(8,128)(2,1)S(1)}, bf16[64,1024]{1,0:T(8,128)(2,1)S(1)}, u32[]{:S(2)}, u32[]{:S(2)}) %collective-permute-start.24) | collective-permute-done | bytes 131104 | tf_op jit(solution)/shard_map/ppermute | solution.py:352
  108.4 4.1 %collective-permute-start.28 = (bf16[64,1024]{1,0:T(8,128)(2,1)S(1)}, bf16[64,1024]{1,0:T(8,128)(2,1)S(1)}, u32[]{:S(2)}, u32[]{:S(2)}) collective-permute-start(bf16[64,1024]{1,0:T(8,128)(2,1)S(1)} %get-tuple-element.48), channel_id=1, source_target_pairs={{8,2},{9,7},{10,0},{11,5},{12,6},{13,3},{14,4},{15,1},{16,18},{17,... | collective-permute-start | bytes 393224 | tf_op jit(solution)/shard_map/ppermute | solution.py:352
  112.5 1.9 %collective-permute-start.27 = (bf16[64,1024]{1,0:T(8,128)(2,1)S(1)}, bf16[64,1024]{1,0:T(8,128)(2,1)S(1)}, u32[]{:S(2)}, u32[]{:S(2)}) collective-permute-start(bf16[64,1024]{1,0:T(8,128)(2,1)S(1)} %get-tuple-element.48), channel_id=1, source_target_pairs={{8,0},{9,5},{10,2},{11,7},{12,4},{13,1},{14,6},{15,3},{16,16},{17,... | collective-permute-start | bytes 393224 | tf_op jit(solution)/shard_map/ppermute | solution.py:352
  114.4 1.8 %collective-permute-done.28.refs_0_ = bf16[64,1024]{1,0:T(8,128)(2,1)S(1)} collective-permute-done((bf16[64,1024]{1,0:T(8,128)(2,1)S(1)}, bf16[64,1024]{1,0:T(8,128)(2,1)S(1)}, u32[]{:S(2)}, u32[]{:S(2)}) %collective-permute-start.28) | collective-permute-done | bytes 131104 | tf_op jit(solution)/shard_map/ppermute | solution.py:352
  116.7 3.3 %collective-permute-done.27.refs_0_ = bf16[64,1024]{1,0:T(8,128)(2,1)S(1)} collective-permute-done((bf16[64,1024]{1,0:T(8,128)(2,1)S(1)}, bf16[64,1024]{1,0:T(8,128)(2,1)S(1)}, u32[]{:S(2)}, u32[]{:S(2)}) %collective-permute-start.27) | collective-permute-done | bytes 131104 | tf_op jit(solution)/shard_map/ppermute | solution.py:352
  122.7 2.5 %collective-permute-start.30 = (bf16[128,512]{1,0:T(8,128)(2,1)S(1)}, bf16[128,512]{1,0:T(8,128)(2,1)S(1)}, u32[]{:S(2)}, u32[]{:S(2)}) collective-permute-start(bf16[128,512]{1,0:T(8,128)(2,1)S(1)} %slice_select_fusion.top_ref), channel_id=1, source_target_pairs={{1,2},{3,4},{5,6},{2,1},{4,3},{6,5},{9,10},{11,12},{13,14},{10,9},... | collective-permute-start | bytes 393224 | tf_op jit(solution)/shard_map/ppermute | solution.py:523
  126.6 2.4 %collective-permute-done.30.beside_ref = bf16[128,512]{1,0:T(8,128)(2,1)S(1)} collective-permute-done((bf16[128,512]{1,0:T(8,128)(2,1)S(1)}, bf16[128,512]{1,0:T(8,128)(2,1)S(1)}, u32[]{:S(2)}, u32[]{:S(2)}) %collective-permute-start.30) | collective-permute-done | bytes 131104 | tf_op jit(solution)/shard_map/ppermute | solution.py:523
  129.0 2.6 %shard_map.114 = (bf16[128,9216]{1,0:T(8,128)(2,1)}, bf16[128,512]{1,0:T(8,128)(2,1)}) custom-call(bf16[128,512]{1,0:T(8,128)(2,1)S(1)} %collective-permute-done.30.beside_ref, bf16[128,4608]{1,0:T(8,128)(2,1)S(1)} %shard_map.113.picked_ref, bf16[1536,4608]{1,0:T(8,128)(2,1)S(1)} %shard_map.93.refs_0_.pick_ref, ...), custom_call_target="tpu_custom_call" | custom-call | tf_op jit(solution)/shard_map/pallas_call | solution.py:536
  (76 shorter events, 34.7 us)
Async XLA Ops:
  2.3 12.2 %copy-start.3 = (f32[1,512]{1,0:T(1,128)S(1)}, f32[1,512]{1,0:T(1,128)}, u32[]{:S(2)}) copy-start(f32[1,512]{1,0:T(1,128)} %param.13) | copy-start | bytes 6148
  9.7 16.5 %collective-permute-start = (bf16[512,2048]{1,0:T(8,128)(2,1)}, bf16[512,2048]{1,0:T(8,128)(2,1)}, u32[]{:S(2)}, u32[]{:S(2)}) collective-permute-start(bf16[512,2048]{1,0:T(8,128)(2,1)} %get-tuple-element.30), channel_id=1, source_target_pairs={{0,1},{1,0},{2,3},{3,2},{4,5},{5,4},{6,7},{7,6},{8,9},{9,8},{10,11... | collective-permute-start | bytes 6291464 | tf_op jit(solution)/shard_map/ppermute | solution.py:409
  9.9 7.5 %collective-permute-start.1 = (bf16[128,512]{1,0:T(8,128)(2,1)S(1)}, bf16[128,512]{1,0:T(8,128)(2,1)S(1)}, u32[]{:S(2)}, u32[]{:S(2)}) collective-permute-start(bf16[128,512]{1,0:T(8,128)(2,1)S(1)} %get-tuple-element.32), channel_id=1, source_target_pairs={{1,2},{3,4},{5,6},{2,1},{4,3},{6,5},{9,10},{11,12},{13,14},{10,9},... | collective-permute-start | bytes 393224 | tf_op jit(solution)/shard_map/ppermute | solution.py:410
  14.4 3.0 %collective-permute-start.2 = (f32[1,512]{1,0:T(1,128)S(1)}, f32[1,512]{1,0:T(1,128)S(1)}, u32[]{:S(2)}, u32[]{:S(2)}) collective-permute-start(f32[1,512]{1,0:T(1,128)S(1)} %copy-done.3), channel_id=1, source_target_pairs={{8,0},{16,8},{24,16},{0,24},{9,1},{17,9},{25,17},{1,25},{10,2},{18... | collective-permute-start | bytes 6152 | tf_op jit(solution)/shard_map/ppermute | solution.py:412
  17.5 1.6 %collective-permute-start.3 = (bf16[128,1024]{1,0:T(8,128)(2,1)S(1)}, bf16[128,1024]{1,0:T(8,128)(2,1)S(1)}, u32[]{:S(2)}, u32[]{:S(2)}) collective-permute-start(bf16[128,1024]{1,0:T(8,128)(2,1)S(1)} %subtract_convert_fusion), channel_id=1, source_target_pairs={{0,1},{1,0},{2,3},{3,2},{4,5},{5,4},{6,7},{7,6},{8,9},{9,8},{10,11... | collective-permute-start | bytes 786440 | tf_op jit(solution)/shard_map/ppermute | solution.py:423
  19.2 11.0 %collective-permute-start.5 = (bf16[64,1024]{1,0:T(8,128)(2,1)S(1)}, bf16[64,1024]{1,0:T(8,128)(2,1)S(1)}, u32[]{:S(2)}, u32[]{:S(2)}) collective-permute-start(bf16[64,1024]{1,0:T(8,128)(2,1)S(1)} %slice.12), channel_id=1, source_target_pairs={{0,2},{1,7},{2,0},{3,5},{4,6},{5,3},{6,4},{7,1}} | collective-permute-start | bytes 393224 | tf_op jit(solution)/shard_map/ppermute | solution.py:352
  24.3 7.3 %collective-permute-start.4 = (bf16[64,1024]{1,0:T(8,128)(2,1)S(1)}, bf16[64,1024]{1,0:T(8,128)(2,1)S(1)}, u32[]{:S(2)}, u32[]{:S(2)}) collective-permute-start(bf16[64,1024]{1,0:T(8,128)(2,1)S(1)} %slice.12), channel_id=1, source_target_pairs={{0,0},{1,5},{2,2},{3,7},{4,4},{5,1},{6,6},{7,3}} | collective-permute-start | bytes 393224 | tf_op jit(solution)/shard_map/ppermute | solution.py:352
  26.2 7.7 %collective-permute-start.8 = (bf16[128,1024]{1,0:T(8,128)(2,1)S(1)}, bf16[128,1024]{1,0:T(8,128)(2,1)S(1)}, u32[]{:S(2)}, u32[]{:S(2)}) collective-permute-start(bf16[128,1024]{1,0:T(8,128)(2,1)S(1)} %add_convert_fusion), channel_id=1, source_target_pairs={{8,0},{16,8},{24,16},{0,24},{9,1},{17,9},{25,17},{1,25},{10,2},{18... | collective-permute-start | bytes 786440 | tf_op jit(solution)/shard_map/ppermute | solution.py:433
  32.5 1.5 %collective-permute-start.6 = (bf16[64,1024]{1,0:T(8,128)(2,1)S(1)}, bf16[64,1024]{1,0:T(8,128)(2,1)S(1)}, u32[]{:S(2)}, u32[]{:S(2)}) collective-permute-start(bf16[64,1024]{1,0:T(8,128)(2,1)S(1)} %shard_map.88.mine_ref), channel_id=1, source_target_pairs={{0,1},{1,0},{2,3},{3,2},{4,5},{5,4},{6,7},{7,6},{8,9},{9,8},{10,11... | collective-permute-start | bytes 393224 | tf_op jit(solution)/shard_map/ppermute | solution.py:473
  32.6 1.4 %collective-permute-start.7 = (f32[2,512]{1,0:T(2,128)S(1)}, f32[2,512]{1,0:T(2,128)S(1)}, u32[]{:S(2)}, u32[]{:S(2)}) collective-permute-start(f32[2,512]{1,0:T(2,128)S(1)} %pad_maximum_fusion), channel_id=1, source_target_pairs={{0,1},{1,0},{2,3},{3,2},{4,5},{5,4},{6,7},{7,6},{8,9},{9,8},{10,11... | collective-permute-start | bytes 12296 | tf_op jit(solution)/shard_map/ppermute | solution.py:424
  34.1 8.7 %collective-permute-start.10 = (bf16[64,1024]{1,0:T(8,128)(2,1)S(1)}, bf16[64,1024]{1,0:T(8,128)(2,1)S(1)}, u32[]{:S(2)}, u32[]{:S(2)}) collective-permute-start(bf16[64,1024]{1,0:T(8,128)(2,1)S(1)} %get-tuple-element.36), channel_id=1, source_target_pairs={{0,10},{1,15},{2,8},{3,13},{4,14},{5,11},{6,12},{7,9},{8,18},{9,23... | collective-permute-start | bytes 393224 | tf_op jit(solution)/shard_map/ppermute | solution.py:352
  35.6 9.1 %collective-permute-start.9 = (bf16[64,1024]{1,0:T(8,128)(2,1)S(1)}, bf16[64,1024]{1,0:T(8,128)(2,1)S(1)}, u32[]{:S(2)}, u32[]{:S(2)}) collective-permute-start(bf16[64,1024]{1,0:T(8,128)(2,1)S(1)} %get-tuple-element.36), channel_id=1, source_target_pairs={{0,8},{1,13},{2,10},{3,15},{4,12},{5,9},{6,14},{7,11},{8,16},{9,21... | collective-permute-start | bytes 393224 | tf_op jit(solution)/shard_map/ppermute | solution.py:352
  45.1 1.4 %collective-permute-start.11 = (bf16[64,1024]{1,0:T(8,128)(2,1)S(1)}, bf16[64,1024]{1,0:T(8,128)(2,1)S(1)}, u32[]{:S(2)}, u32[]{:S(2)}) collective-permute-start(bf16[64,1024]{1,0:T(8,128)(2,1)S(1)} %shard_map.91.mine_ref), channel_id=1, source_target_pairs={{0,1},{1,0},{2,3},{3,2},{4,5},{5,4},{6,7},{7,6},{8,9},{9,8},{10,11... | collective-permute-start | bytes 393224 | tf_op jit(solution)/shard_map/ppermute | solution.py:473
  46.6 7.4 %collective-permute-start.13 = (bf16[64,1024]{1,0:T(8,128)(2,1)S(1)}, bf16[64,1024]{1,0:T(8,128)(2,1)S(1)}, u32[]{:S(2)}, u32[]{:S(2)}) collective-permute-start(bf16[64,1024]{1,0:T(8,128)(2,1)S(1)} %get-tuple-element.38.after_ref), channel_id=1, source_target_pairs={{8,18},{9,23},{10,16},{11,21},{12,22},{13,19},{14,20},{15,17},{0,1... | collective-permute-start | bytes 393224 | tf_op jit(solution)/shard_map/ppermute | solution.py:352
  48.5 8.4 %collective-permute-start.12 = (bf16[64,1024]{1,0:T(8,128)(2,1)S(1)}, bf16[64,1024]{1,0:T(8,128)(2,1)S(1)}, u32[]{:S(2)}, u32[]{:S(2)}) collective-permute-start(bf16[64,1024]{1,0:T(8,128)(2,1)S(1)} %get-tuple-element.38.after_ref), channel_id=1, source_target_pairs={{8,16},{9,21},{10,18},{11,23},{12,20},{13,17},{14,22},{15,19},{0,8... | collective-permute-start | bytes 393224 | tf_op jit(solution)/shard_map/ppermute | solution.py:352
  57.3 1.4 %collective-permute-start.14 = (bf16[64,1024]{1,0:T(8,128)(2,1)S(1)}, bf16[64,1024]{1,0:T(8,128)(2,1)S(1)}, u32[]{:S(2)}, u32[]{:S(2)}) collective-permute-start(bf16[64,1024]{1,0:T(8,128)(2,1)S(1)} %shard_map.95.mine_ref), channel_id=1, source_target_pairs={{0,1},{1,0},{2,3},{3,2},{4,5},{5,4},{6,7},{7,6},{8,9},{9,8},{10,11... | collective-permute-start | bytes 393224 | tf_op jit(solution)/shard_map/ppermute | solution.py:473
  58.8 7.7 %collective-permute-start.16 = (bf16[64,1024]{1,0:T(8,128)(2,1)S(1)}, bf16[64,1024]{1,0:T(8,128)(2,1)S(1)}, u32[]{:S(2)}, u32[]{:S(2)}) collective-permute-start(bf16[64,1024]{1,0:T(8,128)(2,1)S(1)} %get-tuple-element.40.after_ref), channel_id=1, source_target_pairs={{16,26},{17,31},{18,24},{19,29},{20,30},{21,27},{22,28},{23,25},{8... | collective-permute-start | bytes 393224 | tf_op jit(solution)/shard_map/ppermute | solution.py:352
  60.7 7.1 %collective-permute-start.15 = (bf16[64,1024]{1,0:T(8,128)(2,1)S(1)}, bf16[64,1024]{1,0:T(8,128)(2,1)S(1)}, u32[]{:S(2)}, u32[]{:S(2)}) collective-permute-start(bf16[64,1024]{1,0:T(8,128)(2,1)S(1)} %get-tuple-element.40.after_ref), channel_id=1, source_target_pairs={{16,24},{17,29},{18,26},{19,31},{20,28},{21,25},{22,30},{23,27},{8... | collective-permute-start | bytes 393224 | tf_op jit(solution)/shard_map/ppermute | solution.py:352
  68.3 1.4 %collective-permute-start.17 = (bf16[64,1024]{1,0:T(8,128)(2,1)S(1)}, bf16[64,1024]{1,0:T(8,128)(2,1)S(1)}, u32[]{:S(2)}, u32[]{:S(2)}) collective-permute-start(bf16[64,1024]{1,0:T(8,128)(2,1)S(1)} %shard_map.99.mine_ref), channel_id=1, source_target_pairs={{0,1},{1,0},{2,3},{3,2},{4,5},{5,4},{6,7},{7,6},{8,9},{9,8},{10,11... | collective-permute-start | bytes 393224 | tf_op jit(solution)/shard_map/ppermute | solution.py:473
  69.8 7.0 %collective-permute-start.19 = (bf16[64,1024]{1,0:T(8,128)(2,1)S(1)}, bf16[64,1024]{1,0:T(8,128)(2,1)S(1)}, u32[]{:S(2)}, u32[]{:S(2)}) collective-permute-start(bf16[64,1024]{1,0:T(8,128)(2,1)S(1)} %get-tuple-element.42), channel_id=1, source_target_pairs={{24,18},{25,23},{26,16},{27,21},{28,22},{29,19},{30,20},{31,17},{1... | collective-permute-start | bytes 393224 | tf_op jit(solution)/shard_map/ppermute | solution.py:352
  71.7 8.0 %collective-permute-start.18 = (bf16[64,1024]{1,0:T(8,128)(2,1)S(1)}, bf16[64,1024]{1,0:T(8,128)(2,1)S(1)}, u32[]{:S(2)}, u32[]{:S(2)}) collective-permute-start(bf16[64,1024]{1,0:T(8,128)(2,1)S(1)} %get-tuple-element.42), channel_id=1, source_target_pairs={{24,16},{25,21},{26,18},{27,23},{28,20},{29,17},{30,22},{31,19},{1... | collective-permute-start | bytes 393224 | tf_op jit(solution)/shard_map/ppermute | solution.py:352
  80.2 1.4 %collective-permute-start.20 = (bf16[64,1024]{1,0:T(8,128)(2,1)S(1)}, bf16[64,1024]{1,0:T(8,128)(2,1)S(1)}, u32[]{:S(2)}, u32[]{:S(2)}) collective-permute-start(bf16[64,1024]{1,0:T(8,128)(2,1)S(1)} %shard_map.102.mine_ref), channel_id=1, source_target_pairs={{0,1},{1,0},{2,3},{3,2},{4,5},{5,4},{6,7},{7,6},{8,9},{9,8},{10,11... | collective-permute-start | bytes 393224 | tf_op jit(solution)/shard_map/ppermute | solution.py:473
  81.7 5.8 %collective-permute-start.22 = (bf16[64,1024]{1,0:T(8,128)(2,1)S(1)}, bf16[64,1024]{1,0:T(8,128)(2,1)S(1)}, u32[]{:S(2)}, u32[]{:S(2)}) collective-permute-start(bf16[64,1024]{1,0:T(8,128)(2,1)S(1)} %get-tuple-element.44), channel_id=1, source_target_pairs={{16,10},{17,15},{18,8},{19,13},{20,14},{21,11},{22,12},{23,9},{24,... | collective-permute-start | bytes 393224 | tf_op jit(solution)/shard_map/ppermute | solution.py:352
  83.3 7.3 %collective-permute-start.21 = (bf16[64,1024]{1,0:T(8,128)(2,1)S(1)}, bf16[64,1024]{1,0:T(8,128)(2,1)S(1)}, u32[]{:S(2)}, u32[]{:S(2)}) collective-permute-start(bf16[64,1024]{1,0:T(8,128)(2,1)S(1)} %get-tuple-element.44), channel_id=1, source_target_pairs={{16,8},{17,13},{18,10},{19,15},{20,12},{21,9},{22,14},{23,11},{24,... | collective-permute-start | bytes 393224 | tf_op jit(solution)/shard_map/ppermute | solution.py:352
  91.1 1.4 %collective-permute-start.23 = (bf16[64,1024]{1,0:T(8,128)(2,1)S(1)}, bf16[64,1024]{1,0:T(8,128)(2,1)S(1)}, u32[]{:S(2)}, u32[]{:S(2)}) collective-permute-start(bf16[64,1024]{1,0:T(8,128)(2,1)S(1)} %shard_map.105.mine_ref), channel_id=1, source_target_pairs={{0,1},{1,0},{2,3},{3,2},{4,5},{5,4},{6,7},{7,6},{8,9},{9,8},{10,11... | collective-permute-start | bytes 393224 | tf_op jit(solution)/shard_map/ppermute | solution.py:473
  92.7 10.6 %collective-permute-start.25 = (bf16[64,1024]{1,0:T(8,128)(2,1)S(1)}, bf16[64,1024]{1,0:T(8,128)(2,1)S(1)}, u32[]{:S(2)}, u32[]{:S(2)}) collective-permute-start(bf16[64,1024]{1,0:T(8,128)(2,1)S(1)} %get-tuple-element.46), channel_id=1, source_target_pairs={{8,2},{9,7},{10,0},{11,5},{12,6},{13,3},{14,4},{15,1},{16,10},{17,... | collective-permute-start | bytes 393224 | tf_op jit(solution)/shard_map/ppermute | solution.py:352
  98.3 8.1 %collective-permute-start.24 = (bf16[64,1024]{1,0:T(8,128)(2,1)S(1)}, bf16[64,1024]{1,0:T(8,128)(2,1)S(1)}, u32[]{:S(2)}, u32[]{:S(2)}) collective-permute-start(bf16[64,1024]{1,0:T(8,128)(2,1)S(1)} %get-tuple-element.46), channel_id=1, source_target_pairs={{8,0},{9,5},{10,2},{11,7},{12,4},{13,1},{14,6},{15,3},{16,8},{17,1... | collective-permute-start | bytes 393224 | tf_op jit(solution)/shard_map/ppermute | solution.py:352
  106.9 1.4 %collective-permute-start.26 = (bf16[64,1024]{1,0:T(8,128)(2,1)S(1)}, bf16[64,1024]{1,0:T(8,128)(2,1)S(1)}, u32[]{:S(2)}, u32[]{:S(2)}) collective-permute-start(bf16[64,1024]{1,0:T(8,128)(2,1)S(1)} %shard_map.108.mine_ref), channel_id=1, source_target_pairs={{0,1},{1,0},{2,3},{3,2},{4,5},{5,4},{6,7},{7,6},{8,9},{9,8},{10,11... | collective-permute-start | bytes 393224 | tf_op jit(solution)/shard_map/ppermute | solution.py:473
  108.4 7.8 %collective-permute-start.28 = (bf16[64,1024]{1,0:T(8,128)(2,1)S(1)}, bf16[64,1024]{1,0:T(8,128)(2,1)S(1)}, u32[]{:S(2)}, u32[]{:S(2)}) collective-permute-start(bf16[64,1024]{1,0:T(8,128)(2,1)S(1)} %get-tuple-element.48), channel_id=1, source_target_pairs={{8,2},{9,7},{10,0},{11,5},{12,6},{13,3},{14,4},{15,1},{16,18},{17,... | collective-permute-start | bytes 393224 | tf_op jit(solution)/shard_map/ppermute | solution.py:352
  112.5 7.5 %collective-permute-start.27 = (bf16[64,1024]{1,0:T(8,128)(2,1)S(1)}, bf16[64,1024]{1,0:T(8,128)(2,1)S(1)}, u32[]{:S(2)}, u32[]{:S(2)}) collective-permute-start(bf16[64,1024]{1,0:T(8,128)(2,1)S(1)} %get-tuple-element.48), channel_id=1, source_target_pairs={{8,0},{9,5},{10,2},{11,7},{12,4},{13,1},{14,6},{15,3},{16,16},{17,... | collective-permute-start | bytes 393224 | tf_op jit(solution)/shard_map/ppermute | solution.py:352
  120.5 1.4 %collective-permute-start.29 = (bf16[64,1024]{1,0:T(8,128)(2,1)S(1)}, bf16[64,1024]{1,0:T(8,128)(2,1)S(1)}, u32[]{:S(2)}, u32[]{:S(2)}) collective-permute-start(bf16[64,1024]{1,0:T(8,128)(2,1)S(1)} %shard_map.111.mine_ref), channel_id=1, source_target_pairs={{0,1},{1,0},{2,3},{3,2},{4,5},{5,4},{6,7},{7,6},{8,9},{9,8},{10,11... | collective-permute-start | bytes 393224 | tf_op jit(solution)/shard_map/ppermute | solution.py:473
  122.7 6.3 %collective-permute-start.30 = (bf16[128,512]{1,0:T(8,128)(2,1)S(1)}, bf16[128,512]{1,0:T(8,128)(2,1)S(1)}, u32[]{:S(2)}, u32[]{:S(2)}) collective-permute-start(bf16[128,512]{1,0:T(8,128)(2,1)S(1)} %slice_select_fusion.top_ref), channel_id=1, source_target_pairs={{1,2},{3,4},{5,6},{2,1},{4,3},{6,5},{9,10},{11,12},{13,14},{10,9},... | collective-permute-start | bytes 393224 | tf_op jit(solution)/shard_map/ppermute | solution.py:523
  (3 other events, 8.7 us)

commit v6 on v5

--- a/solution.py
+++ b/solution.py
@@ -58,7 +58,6 @@
 def push_kernel(
     group,
     rows_ref,
-    top_ref,
     source_hbm,
     inverse_hbm,
     boundary_hbm,
@@ -77,7 +76,7 @@
 ):
     leaf_count, leaf_size = inverse_ref.shape[:2]
     edge = boundary_ref.shape[1]
-    rows = top_ref.shape[2]
+    rows = outward_ref.shape[1]
     window = 3 * rows
     core = own_place()[1]
     copies = []
@@ -127,58 +126,60 @@
             total_ref[...] += total
     for copy in staged:
         copy.wait()
-    top = top_ref[0].astype(F32)
-
     @pl.when(core == 0)
     def _():
         outward_ref[...] = total_ref[:, :rows].astype(BF16)
-        partial_ref[:, :rows] = top - total_ref[:, rows : 2 * rows]
-        partial_ref[:, rows:] = -total_ref[:, 2 * rows :]
+        partial_ref[...] = total_ref[:, rows:]
 
     @pl.when(core != 0)
     def _():
         outward_ref[...] = total_ref[:, 2 * rows :].astype(BF16)
-        partial_ref[:, :rows] = -total_ref[:, :rows]
-        partial_ref[:, rows:] = top - total_ref[:, rows : 2 * rows]
-
-
-def pick_kernel(rows_ref, after_ref, out_ref):
+        partial_ref[...] = total_ref[:, : 2 * rows]
+
+
+def prepare_kernel(
+    group, panels, given, rows_ref, inverse_hbm, boundary_hbm, after_ref, *refs
+):
+    picks_ref, matrix_ref, inverse_ref, boundary_ref, sems = refs[given:]
     tile, edge = rows_ref.shape[1:]
     leaf_count = rows_ref.shape[0] * tile
-    window = out_ref.shape[0]
+    window = picks_ref.shape[0]
     rows = window // 3
+    panel = lax.axis_index("panel")
     place = lax.axis_index("front")
-    local = rows_ref[...] - (place - 1) * rows
-    shifted = jnp.where(local < rows, local + 2 * rows, local - rows)
-    local = jnp.where(place % 2 == 0, shifted, local)
-    places = lax.broadcasted_iota(jnp.int16, (window, edge), 0)
-    for j in range(leaf_count):
-        out_ref[:, j * edge : (j + 1) * edge] = jnp.where(
-            local[j // tile, j % tile : j % tile + 1, :].astype(jnp.int16) == places,
-            jnp.bfloat16(1),
-            jnp.bfloat16(0),
-        )
-
-
-def lift_matrix_kernel(group, inverse_hbm, boundary_hbm, after_ref, out_ref, inverse_ref, boundary_ref, sems):
-    leaf_count = out_ref.shape[0]
-    copies = []
-    for step in range(leaf_count // group):
-        leaves = pl.ds(step * group, group)
-        parts = (
-            (inverse_hbm.at[leaves], inverse_ref.at[leaves]),
-            (boundary_hbm.at[leaves], boundary_ref.at[leaves]),
-        )
-        copies.append(
-            [pltpu.make_async_copy(a, b, sems.at[step, i]) for i, (a, b) in enumerate(parts)]
-        )
-        for copy in copies[-1]:
-            copy.start()
-    for step in range(leaf_count // group):
-        for copy in copies[step]:
-            copy.wait()
-        for j in range(step * group, (step + 1) * group):
-            out_ref[j] = rows_dot(boundary_ref[j], inverse_ref[j]).astype(BF16)
+    chosen = panel == panels[0]
+    for other in panels[1:]:
+        chosen = chosen | (panel == other)
+
+    @pl.when(chosen)
+    def _():
+        copies = []
+        for step in range(leaf_count // group):
+            leaves = pl.ds(step * group, group)
+            parts = (
+                (inverse_hbm.at[leaves], inverse_ref.at[leaves]),
+                (boundary_hbm.at[leaves], boundary_ref.at[leaves]),
+            )
+            copies.append(
+                [pltpu.make_async_copy(a, b, sems.at[step, i]) for i, (a, b) in enumerate(parts)]
+            )
+            for copy in copies[-1]:
+                copy.start()
+        local = rows_ref[...] - (place - 1) * rows
+        shifted = jnp.where(local < rows, local + 2 * rows, local - rows)
+        local = jnp.where(place % 2 == 0, shifted, local)
+        places = lax.broadcasted_iota(jnp.int16, (window, edge), 0)
+        for j in range(leaf_count):
+            picks_ref[:, j * edge : (j + 1) * edge] = jnp.where(
+                local[j // tile, j % tile : j % tile + 1, :].astype(jnp.int16) == places,
+                jnp.bfloat16(1),
+                jnp.bfloat16(0),
+            )
+        for step in range(leaf_count // group):
+            for copy in copies[step]:
+                copy.wait()
+            for j in range(step * group, (step + 1) * group):
+                matrix_ref[j] = rows_dot(boundary_ref[j], inverse_ref[j]).astype(BF16)
 
 
 def near_kernel(state_ref, pick_ref, out_ref):
@@ -318,6 +319,27 @@
         next_ref[here, :] = field
 
 
+def last_join_kernel(turn, mine_ref, other_ref, state_ref, next_ref, top_ref):
+    wave_rows = mine_ref.shape[0]
+    rows = top_ref.shape[1]
+    forward, backward, wave = own_turn(turn)
+    here = pl.ds(pl.multiple_of(wave * wave_rows, wave_rows), wave_rows)
+    solved = (mine_ref[...].astype(F32) + other_ref[...].astype(F32)).astype(BF16).astype(F32)
+    older = state_ref[here, :].astype(F32)
+
+    @pl.when(forward | backward)
+    def _():
+        next_ref[here, :] = (solved + jnp.where(backward, older, 0.0)).astype(BF16)
+
+    @pl.when(own_place()[1] == 0)
+    def _():
+        top_ref[...] = next_ref[:, :rows]
+
+    @pl.when(own_place()[1] != 0)
+    def _():
+        top_ref[...] = next_ref[:, rows:]
+
+
 def turn_routes(turn, panels, waves):
     if turn == 0:
         return [(p, (p + 1) % panels) for p in range(panels)]
@@ -337,6 +359,19 @@
     return pairs + list(zip(spare, unfed))
 
 
+def preparing_turns(panels):
+    turns = range(1, 2 * (panels - 1) + WAVES - 1)
+    alone = {t: [p for p, q in turn_routes(t, panels, WAVES) if p == q] for t in turns}
+    chosen = {}
+    left = list(range(panels))
+    while left:
+        turn = max(turns, key=lambda t: sum(p in left for p in alone[t]))
+        found = [p for p in left if p in alone[turn]] or left
+        chosen[turn] = chosen.get(turn, []) + found
+        left = [p for p in left if p not in found]
+    return chosen
+
+
 def spread(values, panel_pairs, chips):
     half = chips // 2
     received = []
@@ -385,7 +420,7 @@
             pltpu.VMEM((sources, all_lanes), BF16),
             pltpu.VMEM((rows, width // 2), BF16),
         ),
-        in_specs=[VMEM] * 2 + [ANY] * 4,
+        in_specs=[VMEM] + [ANY] * 4,
         out_specs=(VMEM, VMEM, VMEM, VMEM),
         scratch_shapes=[
             pltpu.VMEM((sources, all_lanes), BF16),
@@ -399,7 +434,6 @@
         compiler_params=params(24),
     )(
         touch_rows,
-        top_source,
         in_hbm(leaf_source[0]),
         in_hbm(leaf_inverse[0]),
         in_hbm(boundary[0]),
@@ -413,13 +447,14 @@
     inward, later = lax.optimization_barrier((inward, later))
     forward_scale = jnp.where(panel == panels - 1, coupling, later)
     scales = jnp.concatenate([forward_scale, coupling], axis=0)
-    blank = jnp.zeros_like(partial[:, :rows])
-    whole_inward = jnp.where(
+    own_part = top_source[0].astype(F32) - inward.astype(F32)
+    blank = jnp.zeros_like(own_part)
+    own_part = jnp.where(
         core == 0,
-        jnp.concatenate([inward.astype(F32), blank], axis=1),
-        jnp.concatenate([blank, inward.astype(F32)], axis=1),
+        jnp.concatenate([own_part, blank], axis=1),
+        jnp.concatenate([blank, own_part], axis=1),
     )
-    partial = (partial - whole_inward).astype(BF16)
+    partial = (own_part - partial).astype(BF16)
     partner = lax.ppermute(partial, "front", swap_core)
     partner_scales = lax.ppermute(scales, "front", swap_core)
     known = (partial.astype(F32) + partner.astype(F32)).astype(BF16)
@@ -452,7 +487,8 @@
 
     state = jnp.zeros((sources, chip_rows), BF16)
     turns = 2 * (panels - 1) + WAVES
-    extra = []
+    extra, made = [], []
+    preparing = preparing_turns(panels)
     for turn in range(turns):
         share = ()
         halves = (range(half // 2, half), range(half // 2)) if turn else (range(half),)
@@ -471,6 +507,19 @@
             )
         share, extra = share[0], []
         other = lax.ppermute(share, "front", swap_core)
+        if turn == turns - 1:
+            state, top_field = pl.pallas_call(
+                functools.partial(last_join_kernel, turn),
+                out_shape=(
+                    pltpu.VMEM((sources, chip_rows), BF16),
+                    pltpu.VMEM((sources, rows), BF16),
+                ),
+                in_specs=[VMEM] * 3,
+                out_specs=(VMEM, VMEM),
+                input_output_aliases={2: 0},
+                compiler_params=params(4),
+            )(in_vmem(share), in_vmem(other), in_vmem(state))
+            break
         state, outgoing = pl.pallas_call(
             functools.partial(join_kernel, turn),
             out_shape=(
@@ -482,29 +531,18 @@
             input_output_aliases={2: 0},
             compiler_params=params(4),
         )(in_vmem(share), in_vmem(other), in_vmem(state), scales, later_known)
-        if turn < turns - 1:
-            routes = turn_routes(turn, panels, WAVES)
-            arrived = [in_vmem(a) for a in spread(outgoing, routes, chips)]
-        if turn == 1:
-            picks = pl.pallas_call(
-                pick_kernel,
-                out_shape=pltpu.VMEM((3 * rows, leaf_count * edge), BF16),
-                in_specs=[VMEM, ANY],
-                out_specs=VMEM,
-                compiler_params=params(4),
-                cost_estimate=pl.CostEstimate(
-                    flops=4 * sources * rows * leaf_count * edge,
-                    bytes_accessed=6 * rows * leaf_count * edge,
-                    transcendentals=0,
+        routes = turn_routes(turn, panels, WAVES)
+        arrived = [in_vmem(a) for a in spread(outgoing, routes, chips)]
+        if turn in preparing:
+            made = pl.pallas_call(
+                functools.partial(prepare_kernel, group, preparing[turn], len(made)),
+                out_shape=(
+                    pltpu.VMEM((3 * rows, leaf_count * edge), BF16),
+                    pltpu.VMEM((leaf_count, edge, leaf_size), BF16),
                 ),
-            )(touch_rows, outgoing)
-            extra = [in_vmem(picks)]
-        if turn == 2:
-            matrices = pl.pallas_call(
-                functools.partial(lift_matrix_kernel, group),
-                out_shape=pltpu.VMEM((leaf_count, edge, leaf_size), BF16),
-                in_specs=[ANY, ANY, ANY],
-                out_specs=VMEM,
+                in_specs=[VMEM] + [ANY] * (3 + len(made)),
+                out_specs=(VMEM, VMEM),
+                input_output_aliases={4 + i: i for i in range(len(made))},
                 scratch_shapes=[
                     pltpu.VMEM((leaf_count, leaf_size, leaf_size), BF16),
                     pltpu.VMEM((leaf_count, edge, leaf_size), BF16),
@@ -512,14 +550,15 @@
                 ],
                 compiler_params=params(12),
                 cost_estimate=pl.CostEstimate(
-                    flops=2 * leaf_count * edge * leaf_size * leaf_size,
-                    bytes_accessed=4 * leaf_count * leaf_size * leaf_size,
+                    flops=8 * sources * rows * leaf_count * edge,
+                    bytes_accessed=6 * rows * leaf_count * edge,
                     transcendentals=0,
                 ),
-            )(in_hbm(leaf_inverse[0]), in_hbm(boundary[0]), outgoing)
-            extra = [in_vmem(matrices)]
-
-    top_field = jnp.where(core == 0, state[:, :rows], state[:, rows:])
+            )(touch_rows, in_hbm(leaf_inverse[0]), in_hbm(boundary[0]), outgoing, *made)
+            made = [in_vmem(m) for m in made]
+            extra = made
+    picks, matrices = made
+
     beside = lax.ppermute(top_field, "front", swap_chip)
     picked = pl.pallas_call(
         near_kernel,

time: 132 us -> 130 us (0.985)
  Pallas kernels: 30.2 us -> 28.8 us
    pallas_call x2 -> x3, Pallas kernels: 5.82 us -> 5 us  [the longest x2 4.9 us: body(): pl.pallas_call(functools.partial(prepare_kernel, group, preparing[turn],...]
  transfers between devices with their start and end apart: 31 -> 31, of which waited for: 25 -> 24; matrix products, arithmetic and copies ran while one was open for 0% -> 0% of each run, Pallas kernels for 12% -> 11%
where the time goes in v6:
time: 130 us
  starting transfers between devices  51.8 us (40%)
  waiting for transfers between devices  47.1 us (36%)
  Pallas kernels  28.8 us (22%)
  between operations  1.32 us (1%)
    ppermute x16, starting transfers between devices, spread(): received.append(lax.ppermute(values, ('panel', 'front'), route))  40.8 us
    ppermute x16, waiting for transfers between devices, spread(): received.append(lax.ppermute(values, ('panel', 'front'), route))  32.7 us
    ppermute x8, waiting for transfers between devices, body(): other = lax.ppermute(share, 'front', swap_core)  9.35 us
    pallas_call x15, Pallas kernels, body(): pl.pallas_call(functools.partial(fold_kernel, blocks, bool(share), len(be...  7.6 us
    pallas_call x1, Pallas kernels, body(): pl.pallas_call(functools.partial(push_kernel, group), out_shape=(pltpu.VM...  7.5 us
    pallas_call x2, Pallas kernels, body(): pl.pallas_call(functools.partial(prepare_kernel, group, preparing[turn],...  4.9 us
    ppermute x1, starting transfers between devices, body(): inward = lax.ppermute(outward, 'front', swap_chip)  4.55 us
    pallas_call x1, Pallas kernels, body(): pl.pallas_call(turn_kernel, out_shape=pltpu.VMEM((width // 2, chip_rows),...  3.91 us
  transfers between devices with their start and end apart: 31, of which 24 were waited for; matrix products, arithmetic and copies ran while one was open for 0% of the time, Pallas kernels for 11%

profile of v6, /device:TPU:1, one launch (start us, length us, event | category | flops | bytes accessed | tf_op | source)
XLA Modules:
  0.0 129.9 jit_solution(10314851247123210073)
XLA Ops:
  1.4 7.5 %shard_map.86 = (bf16[128,512]{1,0:T(8,128)(2,1)S(1)}, f32[128,1024]{1,0:T(8,128)S(1)}, bf16[128,9216]{1,0:T(8,128)(2,1)S(1)}, bf16[512,2048]{1,0:T(8,128)(2,1)}) custom-call(s32[9,4,128]{2,1,0:T(4,128)S(1)} %bitcast.10, bf16[128,9216]{1,0:T(8,128)(2,1)} %bitcast.21, bf16[36,256,256]{2,1,0:T(8,128)(2,1)} %bitcast.13, bf16[36,128,256]{2,1,0:T(8,128)(2,1)} %bitcast.18, ...), custom_call_target="tpu_custom_call" | custom-call | tf_op jit(solution)/shard_map/pallas_call | solution.py:415
  9.0 4.6 %collective-permute-start.1 = (bf16[128,512]{1,0:T(8,128)(2,1)S(1)}, bf16[128,512]{1,0:T(8,128)(2,1)S(1)}, u32[]{:S(2)}, u32[]{:S(2)}) collective-permute-start(bf16[128,512]{1,0:T(8,128)(2,1)S(1)} %get-tuple-element.36), channel_id=1, source_target_pairs={{1,2},{3,4},{5,6},{2,1},{4,3},{6,5},{9,10},{11,12},{13,14},{10,9},... | collective-permute-start | bytes 393224 | tf_op jit(solution)/shard_map/ppermute | solution.py:444
  13.6 2.2 %collective-permute-start.2 = (f32[1,512]{1,0:T(1,128)S(1)}, f32[1,512]{1,0:T(1,128)S(1)}, u32[]{:S(2)}, u32[]{:S(2)}) collective-permute-start(f32[1,512]{1,0:T(1,128)S(1)} %copy-done.3), channel_id=1, source_target_pairs={{8,0},{16,8},{24,16},{0,24},{9,1},{17,9},{25,17},{1,25},{10,2},{18... | collective-permute-start | bytes 6152 | tf_op jit(solution)/shard_map/ppermute | solution.py:446
  16.7 1.5 %collective-permute-done.3 = bf16[128,1024]{1,0:T(8,128)(2,1)S(1)} collective-permute-done((bf16[128,1024]{1,0:T(8,128)(2,1)S(1)}, bf16[128,1024]{1,0:T(8,128)(2,1)S(1)}, u32[]{:S(2)}, u32[]{:S(2)}) %collective-permute-start.3) | collective-permute-done | bytes 262176 | tf_op jit(solution)/shard_map/ppermute | solution.py:458
  18.3 5.1 %collective-permute-start.5 = (bf16[64,1024]{1,0:T(8,128)(2,1)S(1)}, bf16[64,1024]{1,0:T(8,128)(2,1)S(1)}, u32[]{:S(2)}, u32[]{:S(2)}) collective-permute-start(bf16[64,1024]{1,0:T(8,128)(2,1)S(1)} %slice.4), channel_id=1, source_target_pairs={{0,2},{1,7},{2,0},{3,5},{4,6},{5,3},{6,4},{7,1}} | collective-permute-start | bytes 393224 | tf_op jit(solution)/shard_map/ppermute | solution.py:387
  23.4 1.9 %collective-permute-start.4 = (bf16[64,1024]{1,0:T(8,128)(2,1)S(1)}, bf16[64,1024]{1,0:T(8,128)(2,1)S(1)}, u32[]{:S(2)}, u32[]{:S(2)}) collective-permute-start(bf16[64,1024]{1,0:T(8,128)(2,1)S(1)} %slice.4), channel_id=1, source_target_pairs={{0,0},{1,5},{2,2},{3,7},{4,4},{5,1},{6,6},{7,3}} | collective-permute-start | bytes 393224 | tf_op jit(solution)/shard_map/ppermute | solution.py:387
  25.4 3.9 %shard_map.87.inverse_ref = bf16[2048,1024]{1,0:T(8,128)(2,1)S(1)} custom-call(bf16[512,4096]{1,0:T(8,128)(2,1)} %bitcast.17, bf16[512,2048]{1,0:T(8,128)(2,1)} %collective-permute-done.taken_hbm), custom_call_target="tpu_custom_call" | custom-call | flops 536870912 | bytes 8388608 | tf_op jit(solution)/shard_map/pallas_call | solution.py:470
  35.5 6.5 %collective-permute-done.10.refs_0_ = bf16[64,1024]{1,0:T(8,128)(2,1)S(1)} collective-permute-done((bf16[64,1024]{1,0:T(8,128)(2,1)S(1)}, bf16[64,1024]{1,0:T(8,128)(2,1)S(1)}, u32[]{:S(2)}, u32[]{:S(2)}) %collective-permute-start.10) | collective-permute-done | bytes 131104 | tf_op jit(solution)/shard_map/ppermute | solution.py:387
  45.8 1.8 %collective-permute-start.13 = (bf16[64,1024]{1,0:T(8,128)(2,1)S(1)}, bf16[64,1024]{1,0:T(8,128)(2,1)S(1)}, u32[]{:S(2)}, u32[]{:S(2)}) collective-permute-start(bf16[64,1024]{1,0:T(8,128)(2,1)S(1)} %get-tuple-element.43), channel_id=1, source_target_pairs={{8,18},{9,23},{10,16},{11,21},{12,22},{13,19},{14,20},{15,17},{0,1... | collective-permute-start | bytes 393224 | tf_op jit(solution)/shard_map/ppermute | solution.py:387
  47.6 1.9 %collective-permute-start.12 = (bf16[64,1024]{1,0:T(8,128)(2,1)S(1)}, bf16[64,1024]{1,0:T(8,128)(2,1)S(1)}, u32[]{:S(2)}, u32[]{:S(2)}) collective-permute-start(bf16[64,1024]{1,0:T(8,128)(2,1)S(1)} %get-tuple-element.43), channel_id=1, source_target_pairs={{8,16},{9,21},{10,18},{11,23},{12,20},{13,17},{14,22},{15,19},{0,8... | collective-permute-start | bytes 393224 | tf_op jit(solution)/shard_map/ppermute | solution.py:387
  49.5 3.7 %collective-permute-done.13.refs_0_ = bf16[64,1024]{1,0:T(8,128)(2,1)S(1)} collective-permute-done((bf16[64,1024]{1,0:T(8,128)(2,1)S(1)}, bf16[64,1024]{1,0:T(8,128)(2,1)S(1)}, u32[]{:S(2)}, u32[]{:S(2)}) %collective-permute-start.13) | collective-permute-done | bytes 131104 | tf_op jit(solution)/shard_map/ppermute | solution.py:387
  53.7 2.3 %collective-permute-done.12.refs_0_ = bf16[64,1024]{1,0:T(8,128)(2,1)S(1)} collective-permute-done((bf16[64,1024]{1,0:T(8,128)(2,1)S(1)}, bf16[64,1024]{1,0:T(8,128)(2,1)S(1)}, u32[]{:S(2)}, u32[]{:S(2)}) %collective-permute-start.12) | collective-permute-done | bytes 131104 | tf_op jit(solution)/shard_map/ppermute | solution.py:387
  57.9 1.9 %collective-permute-start.16 = (bf16[64,1024]{1,0:T(8,128)(2,1)S(1)}, bf16[64,1024]{1,0:T(8,128)(2,1)S(1)}, u32[]{:S(2)}, u32[]{:S(2)}) collective-permute-start(bf16[64,1024]{1,0:T(8,128)(2,1)S(1)} %get-tuple-element.45), channel_id=1, source_target_pairs={{16,26},{17,31},{18,24},{19,29},{20,30},{21,27},{22,28},{23,25},{8... | collective-permute-start | bytes 393224 | tf_op jit(solution)/shard_map/ppermute | solution.py:387
  59.9 1.9 %collective-permute-start.15 = (bf16[64,1024]{1,0:T(8,128)(2,1)S(1)}, bf16[64,1024]{1,0:T(8,128)(2,1)S(1)}, u32[]{:S(2)}, u32[]{:S(2)}) collective-permute-start(bf16[64,1024]{1,0:T(8,128)(2,1)S(1)} %get-tuple-element.45), channel_id=1, source_target_pairs={{16,24},{17,29},{18,26},{19,31},{20,28},{21,25},{22,30},{23,27},{8... | collective-permute-start | bytes 393224 | tf_op jit(solution)/shard_map/ppermute | solution.py:387
  61.8 2.4 %collective-permute-done.16.refs_0_ = bf16[64,1024]{1,0:T(8,128)(2,1)S(1)} collective-permute-done((bf16[64,1024]{1,0:T(8,128)(2,1)S(1)}, bf16[64,1024]{1,0:T(8,128)(2,1)S(1)}, u32[]{:S(2)}, u32[]{:S(2)}) %collective-permute-start.16) | collective-permute-done | bytes 131104 | tf_op jit(solution)/shard_map/ppermute | solution.py:387
  64.7 2.3 %collective-permute-done.15.refs_0_ = bf16[64,1024]{1,0:T(8,128)(2,1)S(1)} collective-permute-done((bf16[64,1024]{1,0:T(8,128)(2,1)S(1)}, bf16[64,1024]{1,0:T(8,128)(2,1)S(1)}, u32[]{:S(2)}, u32[]{:S(2)}) %collective-permute-start.15) | collective-permute-done | bytes 131104 | tf_op jit(solution)/shard_map/ppermute | solution.py:387
  69.0 1.9 %collective-permute-start.19 = (bf16[64,1024]{1,0:T(8,128)(2,1)S(1)}, bf16[64,1024]{1,0:T(8,128)(2,1)S(1)}, u32[]{:S(2)}, u32[]{:S(2)}) collective-permute-start(bf16[64,1024]{1,0:T(8,128)(2,1)S(1)} %get-tuple-element.47.after_ref), channel_id=1, source_target_pairs={{24,18},{25,23},{26,16},{27,21},{28,22},{29,19},{30,20},{31,17},{1... | collective-permute-start | bytes 393224 | tf_op jit(solution)/shard_map/ppermute | solution.py:387
  70.9 1.9 %collective-permute-start.18 = (bf16[64,1024]{1,0:T(8,128)(2,1)S(1)}, bf16[64,1024]{1,0:T(8,128)(2,1)S(1)}, u32[]{:S(2)}, u32[]{:S(2)}) collective-permute-start(bf16[64,1024]{1,0:T(8,128)(2,1)S(1)} %get-tuple-element.47.after_ref), channel_id=1, source_target_pairs={{24,16},{25,21},{26,18},{27,23},{28,20},{29,17},{30,22},{31,19},{1... | collective-permute-start | bytes 393224 | tf_op jit(solution)/shard_map/ppermute | solution.py:387
  72.8 4.8 %shard_map.99 = (bf16[1536,4608]{1,0:T(8,128)(2,1)S(1)}, bf16[36,128,256]{2,1,0:T(8,128)(2,1)S(1)}) custom-call(s32[9,4,128]{2,1,0:T(4,128)S(1)} %bitcast.11, bf16[36,256,256]{2,1,0:T(8,128)(2,1)} %bitcast.14, bf16[36,128,256]{2,1,0:T(8,128)(2,1)} %bitcast.19, bf16[64,1024]{1,0:T(8,128)(2,1)S(1)} %get-tuple-element.47.after_ref), custom_call_target="tpu_custom_call" | custom-call | flops 2415919104 | bytes 14155776 | tf_op jit(solution)/shard_map/pallas_call | solution.py:537
  80.1 1.7 %collective-permute-start.22 = (bf16[64,1024]{1,0:T(8,128)(2,1)S(1)}, bf16[64,1024]{1,0:T(8,128)(2,1)S(1)}, u32[]{:S(2)}, u32[]{:S(2)}) collective-permute-start(bf16[64,1024]{1,0:T(8,128)(2,1)S(1)} %get-tuple-element.51), channel_id=1, source_target_pairs={{16,10},{17,15},{18,8},{19,13},{20,14},{21,11},{22,12},{23,9},{24,... | collective-permute-start | bytes 393224 | tf_op jit(solution)/shard_map/ppermute | solution.py:387
  81.9 3.1 %collective-permute-start.21 = (bf16[64,1024]{1,0:T(8,128)(2,1)S(1)}, bf16[64,1024]{1,0:T(8,128)(2,1)S(1)}, u32[]{:S(2)}, u32[]{:S(2)}) collective-permute-start(bf16[64,1024]{1,0:T(8,128)(2,1)S(1)} %get-tuple-element.51), channel_id=1, source_target_pairs={{16,8},{17,13},{18,10},{19,15},{20,12},{21,9},{22,14},{23,11},{24,... | collective-permute-start | bytes 393224 | tf_op jit(solution)/shard_map/ppermute | solution.py:387
  86.8 3.0 %collective-permute-done.21.refs_0_ = bf16[64,1024]{1,0:T(8,128)(2,1)S(1)} collective-permute-done((bf16[64,1024]{1,0:T(8,128)(2,1)S(1)}, bf16[64,1024]{1,0:T(8,128)(2,1)S(1)}, u32[]{:S(2)}, u32[]{:S(2)}) %collective-permute-start.21) | collective-permute-done | bytes 131104 | tf_op jit(solution)/shard_map/ppermute | solution.py:387
  91.9 6.1 %collective-permute-start.25 = (bf16[64,1024]{1,0:T(8,128)(2,1)S(1)}, bf16[64,1024]{1,0:T(8,128)(2,1)S(1)}, u32[]{:S(2)}, u32[]{:S(2)}) collective-permute-start(bf16[64,1024]{1,0:T(8,128)(2,1)S(1)} %get-tuple-element.53), channel_id=1, source_target_pairs={{8,2},{9,7},{10,0},{11,5},{12,6},{13,3},{14,4},{15,1},{16,10},{17,... | collective-permute-start | bytes 393224 | tf_op jit(solution)/shard_map/ppermute | solution.py:387
  97.9 3.5 %collective-permute-start.24 = (bf16[64,1024]{1,0:T(8,128)(2,1)S(1)}, bf16[64,1024]{1,0:T(8,128)(2,1)S(1)}, u32[]{:S(2)}, u32[]{:S(2)}) collective-permute-start(bf16[64,1024]{1,0:T(8,128)(2,1)S(1)} %get-tuple-element.53), channel_id=1, source_target_pairs={{8,0},{9,5},{10,2},{11,7},{12,4},{13,1},{14,6},{15,3},{16,8},{17,1... | collective-permute-start | bytes 393224 | tf_op jit(solution)/shard_map/ppermute | solution.py:387
  102.4 3.0 %collective-permute-done.24.refs_0_ = bf16[64,1024]{1,0:T(8,128)(2,1)S(1)} collective-permute-done((bf16[64,1024]{1,0:T(8,128)(2,1)S(1)}, bf16[64,1024]{1,0:T(8,128)(2,1)S(1)}, u32[]{:S(2)}, u32[]{:S(2)}) %collective-permute-start.24) | collective-permute-done | bytes 131104 | tf_op jit(solution)/shard_map/ppermute | solution.py:387
  107.4 3.8 %collective-permute-start.28 = (bf16[64,1024]{1,0:T(8,128)(2,1)S(1)}, bf16[64,1024]{1,0:T(8,128)(2,1)S(1)}, u32[]{:S(2)}, u32[]{:S(2)}) collective-permute-start(bf16[64,1024]{1,0:T(8,128)(2,1)S(1)} %get-tuple-element.55.after_ref), channel_id=1, source_target_pairs={{8,2},{9,7},{10,0},{11,5},{12,6},{13,3},{14,4},{15,1},{16,18},{17,... | collective-permute-start | bytes 393224 | tf_op jit(solution)/shard_map/ppermute | solution.py:387
  111.3 1.9 %collective-permute-start.27 = (bf16[64,1024]{1,0:T(8,128)(2,1)S(1)}, bf16[64,1024]{1,0:T(8,128)(2,1)S(1)}, u32[]{:S(2)}, u32[]{:S(2)}) collective-permute-start(bf16[64,1024]{1,0:T(8,128)(2,1)S(1)} %get-tuple-element.55.after_ref), channel_id=1, source_target_pairs={{8,0},{9,5},{10,2},{11,7},{12,4},{13,1},{14,6},{15,3},{16,16},{17,... | collective-permute-start | bytes 393224 | tf_op jit(solution)/shard_map/ppermute | solution.py:387
  113.3 2.1 %collective-permute-done.28.refs_0_ = bf16[64,1024]{1,0:T(8,128)(2,1)S(1)} collective-permute-done((bf16[64,1024]{1,0:T(8,128)(2,1)S(1)}, bf16[64,1024]{1,0:T(8,128)(2,1)S(1)}, u32[]{:S(2)}, u32[]{:S(2)}) %collective-permute-start.28) | collective-permute-done | bytes 131104 | tf_op jit(solution)/shard_map/ppermute | solution.py:387
  116.0 2.8 %collective-permute-done.27.refs_2_ = bf16[64,1024]{1,0:T(8,128)(2,1)S(1)} collective-permute-done((bf16[64,1024]{1,0:T(8,128)(2,1)S(1)}, bf16[64,1024]{1,0:T(8,128)(2,1)S(1)}, u32[]{:S(2)}, u32[]{:S(2)}) %collective-permute-start.27) | collective-permute-done | bytes 131104 | tf_op jit(solution)/shard_map/ppermute | solution.py:387
  120.8 2.9 %collective-permute-start.30 = (bf16[128,512]{1,0:T(8,128)(2,1)S(1)}, bf16[128,512]{1,0:T(8,128)(2,1)S(1)}, u32[]{:S(2)}, u32[]{:S(2)}) collective-permute-start(bf16[128,512]{1,0:T(8,128)(2,1)S(1)} %get-tuple-element.59.top_ref), channel_id=1, source_target_pairs={{1,2},{3,4},{5,6},{2,1},{4,3},{6,5},{9,10},{11,12},{13,14},{10,9},... | collective-permute-start | bytes 393224 | tf_op jit(solution)/shard_map/ppermute | solution.py:562
  125.1 2.0 %collective-permute-done.30.beside_ref = bf16[128,512]{1,0:T(8,128)(2,1)S(1)} collective-permute-done((bf16[128,512]{1,0:T(8,128)(2,1)S(1)}, bf16[128,512]{1,0:T(8,128)(2,1)S(1)}, u32[]{:S(2)}, u32[]{:S(2)}) %collective-permute-start.30) | collective-permute-done | bytes 131104 | tf_op jit(solution)/shard_map/ppermute | solution.py:562
  127.1 2.7 %shard_map.114 = (bf16[128,9216]{1,0:T(8,128)(2,1)}, bf16[128,512]{1,0:T(8,128)(2,1)}) custom-call(bf16[128,512]{1,0:T(8,128)(2,1)S(1)} %collective-permute-done.30.beside_ref, bf16[128,4608]{1,0:T(8,128)(2,1)S(1)} %shard_map.113.picked_ref, bf16[1536,4608]{1,0:T(8,128)(2,1)S(1)} %get-tuple-element.56.refs_0_.pick_ref, ...), custom_call_target="tpu_custom_call" | custom-call | tf_op jit(solution)/shard_map/pallas_call | solution.py:575
  (75 shorter events, 29.9 us)
Async XLA Ops:
  1.4 15.2 %copy-start.2 = (bf16[1,128,512]{2,1,0:T(8,128)(2,1)S(1)}, bf16[1,128,512]{2,1,0:T(8,128)(2,1)}, u32[]{:S(2)}) copy-start(bf16[1,128,512]{2,1,0:T(8,128)(2,1)} %param.7) | copy-start | bytes 393220
  8.9 16.5 %collective-permute-start = (bf16[512,2048]{1,0:T(8,128)(2,1)}, bf16[512,2048]{1,0:T(8,128)(2,1)}, u32[]{:S(2)}, u32[]{:S(2)}) collective-permute-start(bf16[512,2048]{1,0:T(8,128)(2,1)} %get-tuple-element.35), channel_id=1, source_target_pairs={{0,1},{1,0},{2,3},{3,2},{4,5},{5,4},{6,7},{7,6},{8,9},{9,8},{10,11... | collective-permute-start | bytes 6291464 | tf_op jit(solution)/shard_map/ppermute | solution.py:443
  9.0 7.5 %collective-permute-start.1 = (bf16[128,512]{1,0:T(8,128)(2,1)S(1)}, bf16[128,512]{1,0:T(8,128)(2,1)S(1)}, u32[]{:S(2)}, u32[]{:S(2)}) collective-permute-start(bf16[128,512]{1,0:T(8,128)(2,1)S(1)} %get-tuple-element.36), channel_id=1, source_target_pairs={{1,2},{3,4},{5,6},{2,1},{4,3},{6,5},{9,10},{11,12},{13,14},{10,9},... | collective-permute-start | bytes 393224 | tf_op jit(solution)/shard_map/ppermute | solution.py:444
  13.6 3.0 %collective-permute-start.2 = (f32[1,512]{1,0:T(1,128)S(1)}, f32[1,512]{1,0:T(1,128)S(1)}, u32[]{:S(2)}, u32[]{:S(2)}) collective-permute-start(f32[1,512]{1,0:T(1,128)S(1)} %copy-done.3), channel_id=1, source_target_pairs={{8,0},{16,8},{24,16},{0,24},{9,1},{17,9},{25,17},{1,25},{10,2},{18... | collective-permute-start | bytes 6152 | tf_op jit(solution)/shard_map/ppermute | solution.py:446
  16.6 1.6 %collective-permute-start.3 = (bf16[128,1024]{1,0:T(8,128)(2,1)S(1)}, bf16[128,1024]{1,0:T(8,128)(2,1)S(1)}, u32[]{:S(2)}, u32[]{:S(2)}) collective-permute-start(bf16[128,1024]{1,0:T(8,128)(2,1)S(1)} %subtract_convert_fusion), channel_id=1, source_target_pairs={{0,1},{1,0},{2,3},{3,2},{4,5},{5,4},{6,7},{7,6},{8,9},{9,8},{10,11... | collective-permute-start | bytes 786440 | tf_op jit(solution)/shard_map/ppermute | solution.py:458
  18.3 11.0 %collective-permute-start.5 = (bf16[64,1024]{1,0:T(8,128)(2,1)S(1)}, bf16[64,1024]{1,0:T(8,128)(2,1)S(1)}, u32[]{:S(2)}, u32[]{:S(2)}) collective-permute-start(bf16[64,1024]{1,0:T(8,128)(2,1)S(1)} %slice.4), channel_id=1, source_target_pairs={{0,2},{1,7},{2,0},{3,5},{4,6},{5,3},{6,4},{7,1}} | collective-permute-start | bytes 393224 | tf_op jit(solution)/shard_map/ppermute | solution.py:387
  23.4 7.3 %collective-permute-start.4 = (bf16[64,1024]{1,0:T(8,128)(2,1)S(1)}, bf16[64,1024]{1,0:T(8,128)(2,1)S(1)}, u32[]{:S(2)}, u32[]{:S(2)}) collective-permute-start(bf16[64,1024]{1,0:T(8,128)(2,1)S(1)} %slice.4), channel_id=1, source_target_pairs={{0,0},{1,5},{2,2},{3,7},{4,4},{5,1},{6,6},{7,3}} | collective-permute-start | bytes 393224 | tf_op jit(solution)/shard_map/ppermute | solution.py:387
  25.3 7.7 %collective-permute-start.8 = (bf16[128,1024]{1,0:T(8,128)(2,1)S(1)}, bf16[128,1024]{1,0:T(8,128)(2,1)S(1)}, u32[]{:S(2)}, u32[]{:S(2)}) collective-permute-start(bf16[128,1024]{1,0:T(8,128)(2,1)S(1)} %add_convert_fusion), channel_id=1, source_target_pairs={{8,0},{16,8},{24,16},{0,24},{9,1},{17,9},{25,17},{1,25},{10,2},{18... | collective-permute-start | bytes 786440 | tf_op jit(solution)/shard_map/ppermute | solution.py:468
  31.6 1.5 %collective-permute-start.6 = (bf16[64,1024]{1,0:T(8,128)(2,1)S(1)}, bf16[64,1024]{1,0:T(8,128)(2,1)S(1)}, u32[]{:S(2)}, u32[]{:S(2)}) collective-permute-start(bf16[64,1024]{1,0:T(8,128)(2,1)S(1)} %shard_map.88.mine_ref), channel_id=1, source_target_pairs={{0,1},{1,0},{2,3},{3,2},{4,5},{5,4},{6,7},{7,6},{8,9},{9,8},{10,11... | collective-permute-start | bytes 393224 | tf_op jit(solution)/shard_map/ppermute | solution.py:509
  31.7 1.4 %collective-permute-start.7 = (f32[2,512]{1,0:T(2,128)S(1)}, f32[2,512]{1,0:T(2,128)S(1)}, u32[]{:S(2)}, u32[]{:S(2)}) collective-permute-start(f32[2,512]{1,0:T(2,128)S(1)} %pad_maximum_fusion), channel_id=1, source_target_pairs={{0,1},{1,0},{2,3},{3,2},{4,5},{5,4},{6,7},{7,6},{8,9},{9,8},{10,11... | collective-permute-start | bytes 12296 | tf_op jit(solution)/shard_map/ppermute | solution.py:459
  33.2 8.7 %collective-permute-start.10 = (bf16[64,1024]{1,0:T(8,128)(2,1)S(1)}, bf16[64,1024]{1,0:T(8,128)(2,1)S(1)}, u32[]{:S(2)}, u32[]{:S(2)}) collective-permute-start(bf16[64,1024]{1,0:T(8,128)(2,1)S(1)} %get-tuple-element.41), channel_id=1, source_target_pairs={{0,10},{1,15},{2,8},{3,13},{4,14},{5,11},{6,12},{7,9},{8,18},{9,23... | collective-permute-start | bytes 393224 | tf_op jit(solution)/shard_map/ppermute | solution.py:387
  34.7 9.1 %collective-permute-start.9 = (bf16[64,1024]{1,0:T(8,128)(2,1)S(1)}, bf16[64,1024]{1,0:T(8,128)(2,1)S(1)}, u32[]{:S(2)}, u32[]{:S(2)}) collective-permute-start(bf16[64,1024]{1,0:T(8,128)(2,1)S(1)} %get-tuple-element.41), channel_id=1, source_target_pairs={{0,8},{1,13},{2,10},{3,15},{4,12},{5,9},{6,14},{7,11},{8,16},{9,21... | collective-permute-start | bytes 393224 | tf_op jit(solution)/shard_map/ppermute | solution.py:387
  44.3 1.4 %collective-permute-start.11 = (bf16[64,1024]{1,0:T(8,128)(2,1)S(1)}, bf16[64,1024]{1,0:T(8,128)(2,1)S(1)}, u32[]{:S(2)}, u32[]{:S(2)}) collective-permute-start(bf16[64,1024]{1,0:T(8,128)(2,1)S(1)} %shard_map.91.mine_ref), channel_id=1, source_target_pairs={{0,1},{1,0},{2,3},{3,2},{4,5},{5,4},{6,7},{7,6},{8,9},{9,8},{10,11... | collective-permute-start | bytes 393224 | tf_op jit(solution)/shard_map/ppermute | solution.py:509
  45.8 7.4 %collective-permute-start.13 = (bf16[64,1024]{1,0:T(8,128)(2,1)S(1)}, bf16[64,1024]{1,0:T(8,128)(2,1)S(1)}, u32[]{:S(2)}, u32[]{:S(2)}) collective-permute-start(bf16[64,1024]{1,0:T(8,128)(2,1)S(1)} %get-tuple-element.43), channel_id=1, source_target_pairs={{8,18},{9,23},{10,16},{11,21},{12,22},{13,19},{14,20},{15,17},{0,1... | collective-permute-start | bytes 393224 | tf_op jit(solution)/shard_map/ppermute | solution.py:387
  47.6 8.3 %collective-permute-start.12 = (bf16[64,1024]{1,0:T(8,128)(2,1)S(1)}, bf16[64,1024]{1,0:T(8,128)(2,1)S(1)}, u32[]{:S(2)}, u32[]{:S(2)}) collective-permute-start(bf16[64,1024]{1,0:T(8,128)(2,1)S(1)} %get-tuple-element.43), channel_id=1, source_target_pairs={{8,16},{9,21},{10,18},{11,23},{12,20},{13,17},{14,22},{15,19},{0,8... | collective-permute-start | bytes 393224 | tf_op jit(solution)/shard_map/ppermute | solution.py:387
  56.4 1.4 %collective-permute-start.14 = (bf16[64,1024]{1,0:T(8,128)(2,1)S(1)}, bf16[64,1024]{1,0:T(8,128)(2,1)S(1)}, u32[]{:S(2)}, u32[]{:S(2)}) collective-permute-start(bf16[64,1024]{1,0:T(8,128)(2,1)S(1)} %shard_map.94.mine_ref), channel_id=1, source_target_pairs={{0,1},{1,0},{2,3},{3,2},{4,5},{5,4},{6,7},{7,6},{8,9},{9,8},{10,11... | collective-permute-start | bytes 393224 | tf_op jit(solution)/shard_map/ppermute | solution.py:509
  57.9 6.2 %collective-permute-start.16 = (bf16[64,1024]{1,0:T(8,128)(2,1)S(1)}, bf16[64,1024]{1,0:T(8,128)(2,1)S(1)}, u32[]{:S(2)}, u32[]{:S(2)}) collective-permute-start(bf16[64,1024]{1,0:T(8,128)(2,1)S(1)} %get-tuple-element.45), channel_id=1, source_target_pairs={{16,26},{17,31},{18,24},{19,29},{20,30},{21,27},{22,28},{23,25},{8... | collective-permute-start | bytes 393224 | tf_op jit(solution)/shard_map/ppermute | solution.py:387
  59.9 7.1 %collective-permute-start.15 = (bf16[64,1024]{1,0:T(8,128)(2,1)S(1)}, bf16[64,1024]{1,0:T(8,128)(2,1)S(1)}, u32[]{:S(2)}, u32[]{:S(2)}) collective-permute-start(bf16[64,1024]{1,0:T(8,128)(2,1)S(1)} %get-tuple-element.45), channel_id=1, source_target_pairs={{16,24},{17,29},{18,26},{19,31},{20,28},{21,25},{22,30},{23,27},{8... | collective-permute-start | bytes 393224 | tf_op jit(solution)/shard_map/ppermute | solution.py:387
  67.5 1.4 %collective-permute-start.17 = (bf16[64,1024]{1,0:T(8,128)(2,1)S(1)}, bf16[64,1024]{1,0:T(8,128)(2,1)S(1)}, u32[]{:S(2)}, u32[]{:S(2)}) collective-permute-start(bf16[64,1024]{1,0:T(8,128)(2,1)S(1)} %shard_map.97.mine_ref), channel_id=1, source_target_pairs={{0,1},{1,0},{2,3},{3,2},{4,5},{5,4},{6,7},{7,6},{8,9},{9,8},{10,11... | collective-permute-start | bytes 393224 | tf_op jit(solution)/shard_map/ppermute | solution.py:509
  69.0 8.6 %collective-permute-start.19 = (bf16[64,1024]{1,0:T(8,128)(2,1)S(1)}, bf16[64,1024]{1,0:T(8,128)(2,1)S(1)}, u32[]{:S(2)}, u32[]{:S(2)}) collective-permute-start(bf16[64,1024]{1,0:T(8,128)(2,1)S(1)} %get-tuple-element.47.after_ref), channel_id=1, source_target_pairs={{24,18},{25,23},{26,16},{27,21},{28,22},{29,19},{30,20},{31,17},{1... | collective-permute-start | bytes 393224 | tf_op jit(solution)/shard_map/ppermute | solution.py:387
  70.9 7.2 %collective-permute-start.18 = (bf16[64,1024]{1,0:T(8,128)(2,1)S(1)}, bf16[64,1024]{1,0:T(8,128)(2,1)S(1)}, u32[]{:S(2)}, u32[]{:S(2)}) collective-permute-start(bf16[64,1024]{1,0:T(8,128)(2,1)S(1)} %get-tuple-element.47.after_ref), channel_id=1, source_target_pairs={{24,16},{25,21},{26,18},{27,23},{28,20},{29,17},{30,22},{31,19},{1... | collective-permute-start | bytes 393224 | tf_op jit(solution)/shard_map/ppermute | solution.py:387
  78.6 1.4 %collective-permute-start.20 = (bf16[64,1024]{1,0:T(8,128)(2,1)S(1)}, bf16[64,1024]{1,0:T(8,128)(2,1)S(1)}, u32[]{:S(2)}, u32[]{:S(2)}) collective-permute-start(bf16[64,1024]{1,0:T(8,128)(2,1)S(1)} %shard_map.101.mine_ref), channel_id=1, source_target_pairs={{0,1},{1,0},{2,3},{3,2},{4,5},{5,4},{6,7},{7,6},{8,9},{9,8},{10,11... | collective-permute-start | bytes 393224 | tf_op jit(solution)/shard_map/ppermute | solution.py:509
  80.1 6.2 %collective-permute-start.22 = (bf16[64,1024]{1,0:T(8,128)(2,1)S(1)}, bf16[64,1024]{1,0:T(8,128)(2,1)S(1)}, u32[]{:S(2)}, u32[]{:S(2)}) collective-permute-start(bf16[64,1024]{1,0:T(8,128)(2,1)S(1)} %get-tuple-element.51), channel_id=1, source_target_pairs={{16,10},{17,15},{18,8},{19,13},{20,14},{21,11},{22,12},{23,9},{24,... | collective-permute-start | bytes 393224 | tf_op jit(solution)/shard_map/ppermute | solution.py:387
  81.9 8.0 %collective-permute-start.21 = (bf16[64,1024]{1,0:T(8,128)(2,1)S(1)}, bf16[64,1024]{1,0:T(8,128)(2,1)S(1)}, u32[]{:S(2)}, u32[]{:S(2)}) collective-permute-start(bf16[64,1024]{1,0:T(8,128)(2,1)S(1)} %get-tuple-element.51), channel_id=1, source_target_pairs={{16,8},{17,13},{18,10},{19,15},{20,12},{21,9},{22,14},{23,11},{24,... | collective-permute-start | bytes 393224 | tf_op jit(solution)/shard_map/ppermute | solution.py:387
  90.3 1.4 %collective-permute-start.23 = (bf16[64,1024]{1,0:T(8,128)(2,1)S(1)}, bf16[64,1024]{1,0:T(8,128)(2,1)S(1)}, u32[]{:S(2)}, u32[]{:S(2)}) collective-permute-start(bf16[64,1024]{1,0:T(8,128)(2,1)S(1)} %shard_map.104.mine_ref), channel_id=1, source_target_pairs={{0,1},{1,0},{2,3},{3,2},{4,5},{5,4},{6,7},{7,6},{8,9},{9,8},{10,11... | collective-permute-start | bytes 393224 | tf_op jit(solution)/shard_map/ppermute | solution.py:509
  91.9 10.1 %collective-permute-start.25 = (bf16[64,1024]{1,0:T(8,128)(2,1)S(1)}, bf16[64,1024]{1,0:T(8,128)(2,1)S(1)}, u32[]{:S(2)}, u32[]{:S(2)}) collective-permute-start(bf16[64,1024]{1,0:T(8,128)(2,1)S(1)} %get-tuple-element.53), channel_id=1, source_target_pairs={{8,2},{9,7},{10,0},{11,5},{12,6},{13,3},{14,4},{15,1},{16,10},{17,... | collective-permute-start | bytes 393224 | tf_op jit(solution)/shard_map/ppermute | solution.py:387
  97.9 7.5 %collective-permute-start.24 = (bf16[64,1024]{1,0:T(8,128)(2,1)S(1)}, bf16[64,1024]{1,0:T(8,128)(2,1)S(1)}, u32[]{:S(2)}, u32[]{:S(2)}) collective-permute-start(bf16[64,1024]{1,0:T(8,128)(2,1)S(1)} %get-tuple-element.53), channel_id=1, source_target_pairs={{8,0},{9,5},{10,2},{11,7},{12,4},{13,1},{14,6},{15,3},{16,8},{17,1... | collective-permute-start | bytes 393224 | tf_op jit(solution)/shard_map/ppermute | solution.py:387
  105.9 1.4 %collective-permute-start.26 = (bf16[64,1024]{1,0:T(8,128)(2,1)S(1)}, bf16[64,1024]{1,0:T(8,128)(2,1)S(1)}, u32[]{:S(2)}, u32[]{:S(2)}) collective-permute-start(bf16[64,1024]{1,0:T(8,128)(2,1)S(1)} %shard_map.107.mine_ref), channel_id=1, source_target_pairs={{0,1},{1,0},{2,3},{3,2},{4,5},{5,4},{6,7},{7,6},{8,9},{9,8},{10,11... | collective-permute-start | bytes 393224 | tf_op jit(solution)/shard_map/ppermute | solution.py:509
  107.4 8.0 %collective-permute-start.28 = (bf16[64,1024]{1,0:T(8,128)(2,1)S(1)}, bf16[64,1024]{1,0:T(8,128)(2,1)S(1)}, u32[]{:S(2)}, u32[]{:S(2)}) collective-permute-start(bf16[64,1024]{1,0:T(8,128)(2,1)S(1)} %get-tuple-element.55.after_ref), channel_id=1, source_target_pairs={{8,2},{9,7},{10,0},{11,5},{12,6},{13,3},{14,4},{15,1},{16,18},{17,... | collective-permute-start | bytes 393224 | tf_op jit(solution)/shard_map/ppermute | solution.py:387
  111.3 7.5 %collective-permute-start.27 = (bf16[64,1024]{1,0:T(8,128)(2,1)S(1)}, bf16[64,1024]{1,0:T(8,128)(2,1)S(1)}, u32[]{:S(2)}, u32[]{:S(2)}) collective-permute-start(bf16[64,1024]{1,0:T(8,128)(2,1)S(1)} %get-tuple-element.55.after_ref), channel_id=1, source_target_pairs={{8,0},{9,5},{10,2},{11,7},{12,4},{13,1},{14,6},{15,3},{16,16},{17,... | collective-permute-start | bytes 393224 | tf_op jit(solution)/shard_map/ppermute | solution.py:387
  119.3 1.4 %collective-permute-start.29 = (bf16[64,1024]{1,0:T(8,128)(2,1)S(1)}, bf16[64,1024]{1,0:T(8,128)(2,1)S(1)}, u32[]{:S(2)}, u32[]{:S(2)}) collective-permute-start(bf16[64,1024]{1,0:T(8,128)(2,1)S(1)} %shard_map.111.mine_ref), channel_id=1, source_target_pairs={{0,1},{1,0},{2,3},{3,2},{4,5},{5,4},{6,7},{7,6},{8,9},{9,8},{10,11... | collective-permute-start | bytes 393224 | tf_op jit(solution)/shard_map/ppermute | solution.py:509
  120.8 6.3 %collective-permute-start.30 = (bf16[128,512]{1,0:T(8,128)(2,1)S(1)}, bf16[128,512]{1,0:T(8,128)(2,1)S(1)}, u32[]{:S(2)}, u32[]{:S(2)}) collective-permute-start(bf16[128,512]{1,0:T(8,128)(2,1)S(1)} %get-tuple-element.59.top_ref), channel_id=1, source_target_pairs={{1,2},{3,4},{5,6},{2,1},{4,3},{6,5},{9,10},{11,12},{13,14},{10,9},... | collective-permute-start | bytes 393224 | tf_op jit(solution)/shard_map/ppermute | solution.py:562
  (3 other events, 21.1 us)

commit v7 on v6

--- a/solution.py
+++ b/solution.py
@@ -198,25 +198,24 @@
     top_ref,
     out_hbm,
     top_hbm,
+    all_ref,
     out_ref,
     top_sem,
     sems,
 ):
     leaf_count, edge, leaf_size = matrix_ref.shape
     rows = beside_ref.shape[1]
-    beside = beside_ref[...]
     copies = [pltpu.make_async_copy(top_ref, top_hbm, top_sem)]
     copies[0].start()
+    picked = jnp.dot(beside_ref[...], pick_ref[2 * rows :, :], preferred_element_type=F32)
+    all_ref[...] = (picked + picked_ref[...].astype(F32)).astype(BF16)
     for step in range(leaf_count // group):
         first = step * group
-        span = slice(first * edge, (first + group) * edge)
-        picked = jnp.dot(beside, pick_ref[2 * rows :, span], preferred_element_type=F32)
-        picked = (picked + picked_ref[:, span].astype(F32)).astype(BF16)
-        for g in range(group):
-            lanes = slice((first + g) * leaf_size, (first + g + 1) * leaf_size)
+        for j in range(first, first + group):
+            lanes = slice(j * leaf_size, (j + 1) * leaf_size)
             lifted = jnp.dot(
-                picked[:, g * edge : (g + 1) * edge],
-                matrix_ref[first + g],
+                all_ref[:, j * edge : (j + 1) * edge],
+                matrix_ref[j],
                 preferred_element_type=F32,
             )
             out_ref[:, lanes] = (interior_ref[:, lanes].astype(F32) - lifted).astype(BF16)
@@ -491,7 +490,7 @@
     preparing = preparing_turns(panels)
     for turn in range(turns):
         share = ()
-        halves = (range(half // 2, half), range(half // 2)) if turn else (range(half),)
+        halves = (range(half // 2, half), range(half // 2))
         for blocks in halves:
             last = blocks is halves[-1]
             behind = extra if last else []
@@ -581,6 +580,7 @@
         in_specs=[VMEM] * 6,
         out_specs=(ANY, ANY),
         scratch_shapes=[
+            pltpu.VMEM((sources, leaf_count * edge), BF16),
             pltpu.VMEM((sources, all_lanes), BF16),
             pltpu.SemaphoreType.DMA,
             pltpu.SemaphoreType.DMA((steps,)),

time: 130 us -> 130 us (level)
    pallas_call x15 -> x16, Pallas kernels: 7.6 us -> 7.72 us  [body(): pl.pallas_call(functools.partial(fold_kernel, blocks, bool(share), len(be...]
  transfers between devices with their start and end apart: 31 -> 31, of which waited for: 24 -> 25; matrix products, arithmetic and copies ran while one was open for 0% -> 0% of each run, Pallas kernels for 11% -> 11%
where the time goes in v7:
time: 130 us
  starting transfers between devices  51.7 us (40%)
  waiting for transfers between devices  47.2 us (36%)
  Pallas kernels  28.7 us (22%)
  between operations  1.31 us (1%)
    ppermute x16, starting transfers between devices, spread(): received.append(lax.ppermute(values, ('panel', 'front'), route))  40.4 us
    ppermute x16, waiting for transfers between devices, spread(): received.append(lax.ppermute(values, ('panel', 'front'), route))  33 us
    ppermute x8, waiting for transfers between devices, body(): other = lax.ppermute(share, 'front', swap_core)  9.01 us
    pallas_call x16, Pallas kernels, body(): pl.pallas_call(functools.partial(fold_kernel, blocks, bool(share), len(be...  7.72 us
    pallas_call x1, Pallas kernels, body(): pl.pallas_call(functools.partial(push_kernel, group), out_shape=(pltpu.VM...  7.5 us
    pallas_call x2, Pallas kernels, body(): pl.pallas_call(functools.partial(prepare_kernel, group, preparing[turn],...  4.9 us
    ppermute x1, starting transfers between devices, body(): inward = lax.ppermute(outward, 'front', swap_chip)  4.55 us
    pallas_call x1, Pallas kernels, body(): pl.pallas_call(turn_kernel, out_shape=pltpu.VMEM((width // 2, chip_rows),...  3.91 us
  transfers between devices with their start and end apart: 31, of which 25 were waited for; matrix products, arithmetic and copies ran while one was open for 0% of the time, Pallas kernels for 11%

profile of v7, /device:TPU:1, one launch (start us, length us, event | category | flops | bytes accessed | tf_op | source)
XLA Modules:
  0.0 129.8 jit_solution(5616656194708475431)
XLA Ops:
  1.4 7.5 %shard_map.86 = (bf16[128,512]{1,0:T(8,128)(2,1)S(1)}, f32[128,1024]{1,0:T(8,128)S(1)}, bf16[128,9216]{1,0:T(8,128)(2,1)S(1)}, bf16[512,2048]{1,0:T(8,128)(2,1)}) custom-call(s32[9,4,128]{2,1,0:T(4,128)S(1)} %bitcast.10, bf16[128,9216]{1,0:T(8,128)(2,1)} %bitcast.21, bf16[36,256,256]{2,1,0:T(8,128)(2,1)} %bitcast.13, bf16[36,128,256]{2,1,0:T(8,128)(2,1)} %bitcast.18, ...), custom_call_target="tpu_custom_call" | custom-call | tf_op jit(solution)/shard_map/pallas_call | solution.py:414
  9.0 4.6 %collective-permute-start.1 = (bf16[128,512]{1,0:T(8,128)(2,1)S(1)}, bf16[128,512]{1,0:T(8,128)(2,1)S(1)}, u32[]{:S(2)}, u32[]{:S(2)}) collective-permute-start(bf16[128,512]{1,0:T(8,128)(2,1)S(1)} %get-tuple-element.36), channel_id=1, source_target_pairs={{1,2},{3,4},{5,6},{2,1},{4,3},{6,5},{9,10},{11,12},{13,14},{10,9},... | collective-permute-start | bytes 393224 | tf_op jit(solution)/shard_map/ppermute | solution.py:443
  13.6 2.2 %collective-permute-start.2 = (f32[1,512]{1,0:T(1,128)S(1)}, f32[1,512]{1,0:T(1,128)S(1)}, u32[]{:S(2)}, u32[]{:S(2)}) collective-permute-start(f32[1,512]{1,0:T(1,128)S(1)} %copy-done.3), channel_id=1, source_target_pairs={{8,0},{16,8},{24,16},{0,24},{9,1},{17,9},{25,17},{1,25},{10,2},{18... | collective-permute-start | bytes 6152 | tf_op jit(solution)/shard_map/ppermute | solution.py:445
  16.7 1.5 %collective-permute-done.3 = bf16[128,1024]{1,0:T(8,128)(2,1)S(1)} collective-permute-done((bf16[128,1024]{1,0:T(8,128)(2,1)S(1)}, bf16[128,1024]{1,0:T(8,128)(2,1)S(1)}, u32[]{:S(2)}, u32[]{:S(2)}) %collective-permute-start.3) | collective-permute-done | bytes 262176 | tf_op jit(solution)/shard_map/ppermute | solution.py:457
  18.3 5.1 %collective-permute-start.5 = (bf16[64,1024]{1,0:T(8,128)(2,1)S(1)}, bf16[64,1024]{1,0:T(8,128)(2,1)S(1)}, u32[]{:S(2)}, u32[]{:S(2)}) collective-permute-start(bf16[64,1024]{1,0:T(8,128)(2,1)S(1)} %slice.4), channel_id=1, source_target_pairs={{0,2},{1,7},{2,0},{3,5},{4,6},{5,3},{6,4},{7,1}} | collective-permute-start | bytes 393224 | tf_op jit(solution)/shard_map/ppermute | solution.py:386
  23.4 1.9 %collective-permute-start.4 = (bf16[64,1024]{1,0:T(8,128)(2,1)S(1)}, bf16[64,1024]{1,0:T(8,128)(2,1)S(1)}, u32[]{:S(2)}, u32[]{:S(2)}) collective-permute-start(bf16[64,1024]{1,0:T(8,128)(2,1)S(1)} %slice.4), channel_id=1, source_target_pairs={{0,0},{1,5},{2,2},{3,7},{4,4},{5,1},{6,6},{7,3}} | collective-permute-start | bytes 393224 | tf_op jit(solution)/shard_map/ppermute | solution.py:386
  25.4 3.9 %shard_map.87.inverse_ref = bf16[2048,1024]{1,0:T(8,128)(2,1)S(1)} custom-call(bf16[512,4096]{1,0:T(8,128)(2,1)} %bitcast.17, bf16[512,2048]{1,0:T(8,128)(2,1)} %collective-permute-done.taken_hbm), custom_call_target="tpu_custom_call" | custom-call | flops 536870912 | bytes 8388608 | tf_op jit(solution)/shard_map/pallas_call | solution.py:469
  32.9 2.0 %collective-permute-start.10 = (bf16[64,1024]{1,0:T(8,128)(2,1)S(1)}, bf16[64,1024]{1,0:T(8,128)(2,1)S(1)}, u32[]{:S(2)}, u32[]{:S(2)}) collective-permute-start(bf16[64,1024]{1,0:T(8,128)(2,1)S(1)} %get-tuple-element.41), channel_id=1, source_target_pairs={{0,10},{1,15},{2,8},{3,13},{4,14},{5,11},{6,12},{7,9},{8,18},{9,23... | collective-permute-start | bytes 393224 | tf_op jit(solution)/shard_map/ppermute | solution.py:386
  35.6 6.0 %collective-permute-done.10.refs_0_ = bf16[64,1024]{1,0:T(8,128)(2,1)S(1)} collective-permute-done((bf16[64,1024]{1,0:T(8,128)(2,1)S(1)}, bf16[64,1024]{1,0:T(8,128)(2,1)S(1)}, u32[]{:S(2)}, u32[]{:S(2)}) %collective-permute-start.10) | collective-permute-done | bytes 131104 | tf_op jit(solution)/shard_map/ppermute | solution.py:386
  45.6 2.2 %collective-permute-start.13 = (bf16[64,1024]{1,0:T(8,128)(2,1)S(1)}, bf16[64,1024]{1,0:T(8,128)(2,1)S(1)}, u32[]{:S(2)}, u32[]{:S(2)}) collective-permute-start(bf16[64,1024]{1,0:T(8,128)(2,1)S(1)} %get-tuple-element.43), channel_id=1, source_target_pairs={{8,18},{9,23},{10,16},{11,21},{12,22},{13,19},{14,20},{15,17},{0,1... | collective-permute-start | bytes 393224 | tf_op jit(solution)/shard_map/ppermute | solution.py:386
  47.7 1.9 %collective-permute-start.12 = (bf16[64,1024]{1,0:T(8,128)(2,1)S(1)}, bf16[64,1024]{1,0:T(8,128)(2,1)S(1)}, u32[]{:S(2)}, u32[]{:S(2)}) collective-permute-start(bf16[64,1024]{1,0:T(8,128)(2,1)S(1)} %get-tuple-element.43), channel_id=1, source_target_pairs={{8,16},{9,21},{10,18},{11,23},{12,20},{13,17},{14,22},{15,19},{0,8... | collective-permute-start | bytes 393224 | tf_op jit(solution)/shard_map/ppermute | solution.py:386
  49.7 3.7 %collective-permute-done.13.refs_0_ = bf16[64,1024]{1,0:T(8,128)(2,1)S(1)} collective-permute-done((bf16[64,1024]{1,0:T(8,128)(2,1)S(1)}, bf16[64,1024]{1,0:T(8,128)(2,1)S(1)}, u32[]{:S(2)}, u32[]{:S(2)}) %collective-permute-start.13) | collective-permute-done | bytes 131104 | tf_op jit(solution)/shard_map/ppermute | solution.py:386
  53.8 2.3 %collective-permute-done.12.refs_0_ = bf16[64,1024]{1,0:T(8,128)(2,1)S(1)} collective-permute-done((bf16[64,1024]{1,0:T(8,128)(2,1)S(1)}, bf16[64,1024]{1,0:T(8,128)(2,1)S(1)}, u32[]{:S(2)}, u32[]{:S(2)}) %collective-permute-start.12) | collective-permute-done | bytes 131104 | tf_op jit(solution)/shard_map/ppermute | solution.py:386
  59.1 1.9 %collective-permute-start.15 = (bf16[64,1024]{1,0:T(8,128)(2,1)S(1)}, bf16[64,1024]{1,0:T(8,128)(2,1)S(1)}, u32[]{:S(2)}, u32[]{:S(2)}) collective-permute-start(bf16[64,1024]{1,0:T(8,128)(2,1)S(1)} %get-tuple-element.45), channel_id=1, source_target_pairs={{16,24},{17,29},{18,26},{19,31},{20,28},{21,25},{22,30},{23,27},{8... | collective-permute-start | bytes 393224 | tf_op jit(solution)/shard_map/ppermute | solution.py:386
  61.0 3.2 %collective-permute-done.16.refs_0_ = bf16[64,1024]{1,0:T(8,128)(2,1)S(1)} collective-permute-done((bf16[64,1024]{1,0:T(8,128)(2,1)S(1)}, bf16[64,1024]{1,0:T(8,128)(2,1)S(1)}, u32[]{:S(2)}, u32[]{:S(2)}) %collective-permute-start.16) | collective-permute-done | bytes 131104 | tf_op jit(solution)/shard_map/ppermute | solution.py:386
  64.7 2.4 %collective-permute-done.15.refs_0_ = bf16[64,1024]{1,0:T(8,128)(2,1)S(1)} collective-permute-done((bf16[64,1024]{1,0:T(8,128)(2,1)S(1)}, bf16[64,1024]{1,0:T(8,128)(2,1)S(1)}, u32[]{:S(2)}, u32[]{:S(2)}) %collective-permute-start.15) | collective-permute-done | bytes 131104 | tf_op jit(solution)/shard_map/ppermute | solution.py:386
  70.4 1.9 %collective-permute-start.18 = (bf16[64,1024]{1,0:T(8,128)(2,1)S(1)}, bf16[64,1024]{1,0:T(8,128)(2,1)S(1)}, u32[]{:S(2)}, u32[]{:S(2)}) collective-permute-start(bf16[64,1024]{1,0:T(8,128)(2,1)S(1)} %get-tuple-element.47.after_ref), channel_id=1, source_target_pairs={{24,16},{25,21},{26,18},{27,23},{28,20},{29,17},{30,22},{31,19},{1... | collective-permute-start | bytes 393224 | tf_op jit(solution)/shard_map/ppermute | solution.py:386
  72.3 4.8 %shard_map.100 = (bf16[1536,4608]{1,0:T(8,128)(2,1)S(1)}, bf16[36,128,256]{2,1,0:T(8,128)(2,1)S(1)}) custom-call(s32[9,4,128]{2,1,0:T(4,128)S(1)} %bitcast.11, bf16[36,256,256]{2,1,0:T(8,128)(2,1)} %bitcast.14, bf16[36,128,256]{2,1,0:T(8,128)(2,1)} %bitcast.19, bf16[64,1024]{1,0:T(8,128)(2,1)S(1)} %get-tuple-element.47.after_ref), custom_call_target="tpu_custom_call" | custom-call | flops 2415919104 | bytes 14155776 | tf_op jit(solution)/shard_map/pallas_call | solution.py:536
  80.1 1.7 %collective-permute-start.22 = (bf16[64,1024]{1,0:T(8,128)(2,1)S(1)}, bf16[64,1024]{1,0:T(8,128)(2,1)S(1)}, u32[]{:S(2)}, u32[]{:S(2)}) collective-permute-start(bf16[64,1024]{1,0:T(8,128)(2,1)S(1)} %get-tuple-element.51), channel_id=1, source_target_pairs={{16,10},{17,15},{18,8},{19,13},{20,14},{21,11},{22,12},{23,9},{24,... | collective-permute-start | bytes 393224 | tf_op jit(solution)/shard_map/ppermute | solution.py:386
  81.7 3.4 %collective-permute-start.21 = (bf16[64,1024]{1,0:T(8,128)(2,1)S(1)}, bf16[64,1024]{1,0:T(8,128)(2,1)S(1)}, u32[]{:S(2)}, u32[]{:S(2)}) collective-permute-start(bf16[64,1024]{1,0:T(8,128)(2,1)S(1)} %get-tuple-element.51), channel_id=1, source_target_pairs={{16,8},{17,13},{18,10},{19,15},{20,12},{21,9},{22,14},{23,11},{24,... | collective-permute-start | bytes 393224 | tf_op jit(solution)/shard_map/ppermute | solution.py:386
  85.1 1.7 %collective-permute-done.22.refs_0_ = bf16[64,1024]{1,0:T(8,128)(2,1)S(1)} collective-permute-done((bf16[64,1024]{1,0:T(8,128)(2,1)S(1)}, bf16[64,1024]{1,0:T(8,128)(2,1)S(1)}, u32[]{:S(2)}, u32[]{:S(2)}) %collective-permute-start.22) | collective-permute-done | bytes 131104 | tf_op jit(solution)/shard_map/ppermute | solution.py:386
  87.3 2.5 %collective-permute-done.21.refs_0_ = bf16[64,1024]{1,0:T(8,128)(2,1)S(1)} collective-permute-done((bf16[64,1024]{1,0:T(8,128)(2,1)S(1)}, bf16[64,1024]{1,0:T(8,128)(2,1)S(1)}, u32[]{:S(2)}, u32[]{:S(2)}) %collective-permute-start.21) | collective-permute-done | bytes 131104 | tf_op jit(solution)/shard_map/ppermute | solution.py:386
  91.8 6.2 %collective-permute-start.25 = (bf16[64,1024]{1,0:T(8,128)(2,1)S(1)}, bf16[64,1024]{1,0:T(8,128)(2,1)S(1)}, u32[]{:S(2)}, u32[]{:S(2)}) collective-permute-start(bf16[64,1024]{1,0:T(8,128)(2,1)S(1)} %get-tuple-element.53), channel_id=1, source_target_pairs={{8,2},{9,7},{10,0},{11,5},{12,6},{13,3},{14,4},{15,1},{16,10},{17,... | collective-permute-start | bytes 393224 | tf_op jit(solution)/shard_map/ppermute | solution.py:386
  97.9 3.5 %collective-permute-start.24 = (bf16[64,1024]{1,0:T(8,128)(2,1)S(1)}, bf16[64,1024]{1,0:T(8,128)(2,1)S(1)}, u32[]{:S(2)}, u32[]{:S(2)}) collective-permute-start(bf16[64,1024]{1,0:T(8,128)(2,1)S(1)} %get-tuple-element.53), channel_id=1, source_target_pairs={{8,0},{9,5},{10,2},{11,7},{12,4},{13,1},{14,6},{15,3},{16,8},{17,1... | collective-permute-start | bytes 393224 | tf_op jit(solution)/shard_map/ppermute | solution.py:386
  102.5 2.9 %collective-permute-done.24.refs_0_ = bf16[64,1024]{1,0:T(8,128)(2,1)S(1)} collective-permute-done((bf16[64,1024]{1,0:T(8,128)(2,1)S(1)}, bf16[64,1024]{1,0:T(8,128)(2,1)S(1)}, u32[]{:S(2)}, u32[]{:S(2)}) %collective-permute-start.24) | collective-permute-done | bytes 131104 | tf_op jit(solution)/shard_map/ppermute | solution.py:386
  107.5 3.9 %collective-permute-start.28 = (bf16[64,1024]{1,0:T(8,128)(2,1)S(1)}, bf16[64,1024]{1,0:T(8,128)(2,1)S(1)}, u32[]{:S(2)}, u32[]{:S(2)}) collective-permute-start(bf16[64,1024]{1,0:T(8,128)(2,1)S(1)} %get-tuple-element.55.after_ref), channel_id=1, source_target_pairs={{8,2},{9,7},{10,0},{11,5},{12,6},{13,3},{14,4},{15,1},{16,18},{17,... | collective-permute-start | bytes 393224 | tf_op jit(solution)/shard_map/ppermute | solution.py:386
  111.4 1.9 %collective-permute-start.27 = (bf16[64,1024]{1,0:T(8,128)(2,1)S(1)}, bf16[64,1024]{1,0:T(8,128)(2,1)S(1)}, u32[]{:S(2)}, u32[]{:S(2)}) collective-permute-start(bf16[64,1024]{1,0:T(8,128)(2,1)S(1)} %get-tuple-element.55.after_ref), channel_id=1, source_target_pairs={{8,0},{9,5},{10,2},{11,7},{12,4},{13,1},{14,6},{15,3},{16,16},{17,... | collective-permute-start | bytes 393224 | tf_op jit(solution)/shard_map/ppermute | solution.py:386
  113.4 2.0 %collective-permute-done.28.refs_0_ = bf16[64,1024]{1,0:T(8,128)(2,1)S(1)} collective-permute-done((bf16[64,1024]{1,0:T(8,128)(2,1)S(1)}, bf16[64,1024]{1,0:T(8,128)(2,1)S(1)}, u32[]{:S(2)}, u32[]{:S(2)}) %collective-permute-start.28) | collective-permute-done | bytes 131104 | tf_op jit(solution)/shard_map/ppermute | solution.py:386
  115.9 3.0 %collective-permute-done.27.refs_2_ = bf16[64,1024]{1,0:T(8,128)(2,1)S(1)} collective-permute-done((bf16[64,1024]{1,0:T(8,128)(2,1)S(1)}, bf16[64,1024]{1,0:T(8,128)(2,1)S(1)}, u32[]{:S(2)}, u32[]{:S(2)}) %collective-permute-start.27) | collective-permute-done | bytes 131104 | tf_op jit(solution)/shard_map/ppermute | solution.py:386
  120.9 2.8 %collective-permute-start.30 = (bf16[128,512]{1,0:T(8,128)(2,1)S(1)}, bf16[128,512]{1,0:T(8,128)(2,1)S(1)}, u32[]{:S(2)}, u32[]{:S(2)}) collective-permute-start(bf16[128,512]{1,0:T(8,128)(2,1)S(1)} %get-tuple-element.59.top_ref), channel_id=1, source_target_pairs={{1,2},{3,4},{5,6},{2,1},{4,3},{6,5},{9,10},{11,12},{13,14},{10,9},... | collective-permute-start | bytes 393224 | tf_op jit(solution)/shard_map/ppermute | solution.py:561
  125.1 2.1 %collective-permute-done.30.beside_ref = bf16[128,512]{1,0:T(8,128)(2,1)S(1)} collective-permute-done((bf16[128,512]{1,0:T(8,128)(2,1)S(1)}, bf16[128,512]{1,0:T(8,128)(2,1)S(1)}, u32[]{:S(2)}, u32[]{:S(2)}) %collective-permute-start.30) | collective-permute-done | bytes 131104 | tf_op jit(solution)/shard_map/ppermute | solution.py:561
  127.2 2.4 %shard_map.115 = (bf16[128,9216]{1,0:T(8,128)(2,1)}, bf16[128,512]{1,0:T(8,128)(2,1)}) custom-call(bf16[128,512]{1,0:T(8,128)(2,1)S(1)} %collective-permute-done.30.beside_ref, bf16[128,4608]{1,0:T(8,128)(2,1)S(1)} %shard_map.114.picked_ref, bf16[1536,4608]{1,0:T(8,128)(2,1)S(1)} %get-tuple-element.56.refs_0_.pick_ref, ...), custom_call_target="tpu_custom_call" | custom-call | tf_op jit(solution)/shard_map/pallas_call | solution.py:574
  (76 shorter events, 29.8 us)
Async XLA Ops:
  1.4 15.2 %copy-start.2 = (bf16[1,128,512]{2,1,0:T(8,128)(2,1)S(1)}, bf16[1,128,512]{2,1,0:T(8,128)(2,1)}, u32[]{:S(2)}) copy-start(bf16[1,128,512]{2,1,0:T(8,128)(2,1)} %param.7) | copy-start | bytes 393220
  8.9 16.5 %collective-permute-start = (bf16[512,2048]{1,0:T(8,128)(2,1)}, bf16[512,2048]{1,0:T(8,128)(2,1)}, u32[]{:S(2)}, u32[]{:S(2)}) collective-permute-start(bf16[512,2048]{1,0:T(8,128)(2,1)} %get-tuple-element.35), channel_id=1, source_target_pairs={{0,1},{1,0},{2,3},{3,2},{4,5},{5,4},{6,7},{7,6},{8,9},{9,8},{10,11... | collective-permute-start | bytes 6291464 | tf_op jit(solution)/shard_map/ppermute | solution.py:442
  9.0 7.5 %collective-permute-start.1 = (bf16[128,512]{1,0:T(8,128)(2,1)S(1)}, bf16[128,512]{1,0:T(8,128)(2,1)S(1)}, u32[]{:S(2)}, u32[]{:S(2)}) collective-permute-start(bf16[128,512]{1,0:T(8,128)(2,1)S(1)} %get-tuple-element.36), channel_id=1, source_target_pairs={{1,2},{3,4},{5,6},{2,1},{4,3},{6,5},{9,10},{11,12},{13,14},{10,9},... | collective-permute-start | bytes 393224 | tf_op jit(solution)/shard_map/ppermute | solution.py:443
  13.6 3.0 %collective-permute-start.2 = (f32[1,512]{1,0:T(1,128)S(1)}, f32[1,512]{1,0:T(1,128)S(1)}, u32[]{:S(2)}, u32[]{:S(2)}) collective-permute-start(f32[1,512]{1,0:T(1,128)S(1)} %copy-done.3), channel_id=1, source_target_pairs={{8,0},{16,8},{24,16},{0,24},{9,1},{17,9},{25,17},{1,25},{10,2},{18... | collective-permute-start | bytes 6152 | tf_op jit(solution)/shard_map/ppermute | solution.py:445
  16.6 1.6 %collective-permute-start.3 = (bf16[128,1024]{1,0:T(8,128)(2,1)S(1)}, bf16[128,1024]{1,0:T(8,128)(2,1)S(1)}, u32[]{:S(2)}, u32[]{:S(2)}) collective-permute-start(bf16[128,1024]{1,0:T(8,128)(2,1)S(1)} %subtract_convert_fusion), channel_id=1, source_target_pairs={{0,1},{1,0},{2,3},{3,2},{4,5},{5,4},{6,7},{7,6},{8,9},{9,8},{10,11... | collective-permute-start | bytes 786440 | tf_op jit(solution)/shard_map/ppermute | solution.py:457
  18.3 11.0 %collective-permute-start.5 = (bf16[64,1024]{1,0:T(8,128)(2,1)S(1)}, bf16[64,1024]{1,0:T(8,128)(2,1)S(1)}, u32[]{:S(2)}, u32[]{:S(2)}) collective-permute-start(bf16[64,1024]{1,0:T(8,128)(2,1)S(1)} %slice.4), channel_id=1, source_target_pairs={{0,2},{1,7},{2,0},{3,5},{4,6},{5,3},{6,4},{7,1}} | collective-permute-start | bytes 393224 | tf_op jit(solution)/shard_map/ppermute | solution.py:386
  23.4 7.3 %collective-permute-start.4 = (bf16[64,1024]{1,0:T(8,128)(2,1)S(1)}, bf16[64,1024]{1,0:T(8,128)(2,1)S(1)}, u32[]{:S(2)}, u32[]{:S(2)}) collective-permute-start(bf16[64,1024]{1,0:T(8,128)(2,1)S(1)} %slice.4), channel_id=1, source_target_pairs={{0,0},{1,5},{2,2},{3,7},{4,4},{5,1},{6,6},{7,3}} | collective-permute-start | bytes 393224 | tf_op jit(solution)/shard_map/ppermute | solution.py:386
  25.3 7.4 %collective-permute-start.8 = (bf16[128,1024]{1,0:T(8,128)(2,1)S(1)}, bf16[128,1024]{1,0:T(8,128)(2,1)S(1)}, u32[]{:S(2)}, u32[]{:S(2)}) collective-permute-start(bf16[128,1024]{1,0:T(8,128)(2,1)S(1)} %add_convert_fusion), channel_id=1, source_target_pairs={{8,0},{16,8},{24,16},{0,24},{9,1},{17,9},{25,17},{1,25},{10,2},{18... | collective-permute-start | bytes 786440 | tf_op jit(solution)/shard_map/ppermute | solution.py:467
  31.2 1.5 %collective-permute-start.6 = (bf16[64,1024]{1,0:T(8,128)(2,1)S(1)}, bf16[64,1024]{1,0:T(8,128)(2,1)S(1)}, u32[]{:S(2)}, u32[]{:S(2)}) collective-permute-start(bf16[64,1024]{1,0:T(8,128)(2,1)S(1)} %shard_map.89.mine_ref), channel_id=1, source_target_pairs={{0,1},{1,0},{2,3},{3,2},{4,5},{5,4},{6,7},{7,6},{8,9},{9,8},{10,11... | collective-permute-start | bytes 393224 | tf_op jit(solution)/shard_map/ppermute | solution.py:508
  31.3 1.4 %collective-permute-start.7 = (f32[2,512]{1,0:T(2,128)S(1)}, f32[2,512]{1,0:T(2,128)S(1)}, u32[]{:S(2)}, u32[]{:S(2)}) collective-permute-start(f32[2,512]{1,0:T(2,128)S(1)} %pad_maximum_fusion), channel_id=1, source_target_pairs={{0,1},{1,0},{2,3},{3,2},{4,5},{5,4},{6,7},{7,6},{8,9},{9,8},{10,11... | collective-permute-start | bytes 12296 | tf_op jit(solution)/shard_map/ppermute | solution.py:458
  32.9 8.7 %collective-permute-start.10 = (bf16[64,1024]{1,0:T(8,128)(2,1)S(1)}, bf16[64,1024]{1,0:T(8,128)(2,1)S(1)}, u32[]{:S(2)}, u32[]{:S(2)}) collective-permute-start(bf16[64,1024]{1,0:T(8,128)(2,1)S(1)} %get-tuple-element.41), channel_id=1, source_target_pairs={{0,10},{1,15},{2,8},{3,13},{4,14},{5,11},{6,12},{7,9},{8,18},{9,23... | collective-permute-start | bytes 393224 | tf_op jit(solution)/shard_map/ppermute | solution.py:386
  34.9 8.7 %collective-permute-start.9 = (bf16[64,1024]{1,0:T(8,128)(2,1)S(1)}, bf16[64,1024]{1,0:T(8,128)(2,1)S(1)}, u32[]{:S(2)}, u32[]{:S(2)}) collective-permute-start(bf16[64,1024]{1,0:T(8,128)(2,1)S(1)} %get-tuple-element.41), channel_id=1, source_target_pairs={{0,8},{1,13},{2,10},{3,15},{4,12},{5,9},{6,14},{7,11},{8,16},{9,21... | collective-permute-start | bytes 393224 | tf_op jit(solution)/shard_map/ppermute | solution.py:386
  44.1 1.4 %collective-permute-start.11 = (bf16[64,1024]{1,0:T(8,128)(2,1)S(1)}, bf16[64,1024]{1,0:T(8,128)(2,1)S(1)}, u32[]{:S(2)}, u32[]{:S(2)}) collective-permute-start(bf16[64,1024]{1,0:T(8,128)(2,1)S(1)} %shard_map.92.mine_ref), channel_id=1, source_target_pairs={{0,1},{1,0},{2,3},{3,2},{4,5},{5,4},{6,7},{7,6},{8,9},{9,8},{10,11... | collective-permute-start | bytes 393224 | tf_op jit(solution)/shard_map/ppermute | solution.py:508
  45.6 7.7 %collective-permute-start.13 = (bf16[64,1024]{1,0:T(8,128)(2,1)S(1)}, bf16[64,1024]{1,0:T(8,128)(2,1)S(1)}, u32[]{:S(2)}, u32[]{:S(2)}) collective-permute-start(bf16[64,1024]{1,0:T(8,128)(2,1)S(1)} %get-tuple-element.43), channel_id=1, source_target_pairs={{8,18},{9,23},{10,16},{11,21},{12,22},{13,19},{14,20},{15,17},{0,1... | collective-permute-start | bytes 393224 | tf_op jit(solution)/shard_map/ppermute | solution.py:386
  47.7 8.4 %collective-permute-start.12 = (bf16[64,1024]{1,0:T(8,128)(2,1)S(1)}, bf16[64,1024]{1,0:T(8,128)(2,1)S(1)}, u32[]{:S(2)}, u32[]{:S(2)}) collective-permute-start(bf16[64,1024]{1,0:T(8,128)(2,1)S(1)} %get-tuple-element.43), channel_id=1, source_target_pairs={{8,16},{9,21},{10,18},{11,23},{12,20},{13,17},{14,22},{15,19},{0,8... | collective-permute-start | bytes 393224 | tf_op jit(solution)/shard_map/ppermute | solution.py:386
  56.6 1.4 %collective-permute-start.14 = (bf16[64,1024]{1,0:T(8,128)(2,1)S(1)}, bf16[64,1024]{1,0:T(8,128)(2,1)S(1)}, u32[]{:S(2)}, u32[]{:S(2)}) collective-permute-start(bf16[64,1024]{1,0:T(8,128)(2,1)S(1)} %shard_map.95.mine_ref), channel_id=1, source_target_pairs={{0,1},{1,0},{2,3},{3,2},{4,5},{5,4},{6,7},{7,6},{8,9},{9,8},{10,11... | collective-permute-start | bytes 393224 | tf_op jit(solution)/shard_map/ppermute | solution.py:508
  58.1 6.1 %collective-permute-start.16 = (bf16[64,1024]{1,0:T(8,128)(2,1)S(1)}, bf16[64,1024]{1,0:T(8,128)(2,1)S(1)}, u32[]{:S(2)}, u32[]{:S(2)}) collective-permute-start(bf16[64,1024]{1,0:T(8,128)(2,1)S(1)} %get-tuple-element.45), channel_id=1, source_target_pairs={{16,26},{17,31},{18,24},{19,29},{20,30},{21,27},{22,28},{23,25},{8... | collective-permute-start | bytes 393224 | tf_op jit(solution)/shard_map/ppermute | solution.py:386
  59.1 8.0 %collective-permute-start.15 = (bf16[64,1024]{1,0:T(8,128)(2,1)S(1)}, bf16[64,1024]{1,0:T(8,128)(2,1)S(1)}, u32[]{:S(2)}, u32[]{:S(2)}) collective-permute-start(bf16[64,1024]{1,0:T(8,128)(2,1)S(1)} %get-tuple-element.45), channel_id=1, source_target_pairs={{16,24},{17,29},{18,26},{19,31},{20,28},{21,25},{22,30},{23,27},{8... | collective-permute-start | bytes 393224 | tf_op jit(solution)/shard_map/ppermute | solution.py:386
  67.5 1.4 %collective-permute-start.17 = (bf16[64,1024]{1,0:T(8,128)(2,1)S(1)}, bf16[64,1024]{1,0:T(8,128)(2,1)S(1)}, u32[]{:S(2)}, u32[]{:S(2)}) collective-permute-start(bf16[64,1024]{1,0:T(8,128)(2,1)S(1)} %shard_map.98.mine_ref), channel_id=1, source_target_pairs={{0,1},{1,0},{2,3},{3,2},{4,5},{5,4},{6,7},{7,6},{8,9},{9,8},{10,11... | collective-permute-start | bytes 393224 | tf_op jit(solution)/shard_map/ppermute | solution.py:508
  69.1 8.0 %collective-permute-start.19 = (bf16[64,1024]{1,0:T(8,128)(2,1)S(1)}, bf16[64,1024]{1,0:T(8,128)(2,1)S(1)}, u32[]{:S(2)}, u32[]{:S(2)}) collective-permute-start(bf16[64,1024]{1,0:T(8,128)(2,1)S(1)} %get-tuple-element.47.after_ref), channel_id=1, source_target_pairs={{24,18},{25,23},{26,16},{27,21},{28,22},{29,19},{30,20},{31,17},{1... | collective-permute-start | bytes 393224 | tf_op jit(solution)/shard_map/ppermute | solution.py:386
  70.4 7.7 %collective-permute-start.18 = (bf16[64,1024]{1,0:T(8,128)(2,1)S(1)}, bf16[64,1024]{1,0:T(8,128)(2,1)S(1)}, u32[]{:S(2)}, u32[]{:S(2)}) collective-permute-start(bf16[64,1024]{1,0:T(8,128)(2,1)S(1)} %get-tuple-element.47.after_ref), channel_id=1, source_target_pairs={{24,16},{25,21},{26,18},{27,23},{28,20},{29,17},{30,22},{31,19},{1... | collective-permute-start | bytes 393224 | tf_op jit(solution)/shard_map/ppermute | solution.py:386
  78.5 1.4 %collective-permute-start.20 = (bf16[64,1024]{1,0:T(8,128)(2,1)S(1)}, bf16[64,1024]{1,0:T(8,128)(2,1)S(1)}, u32[]{:S(2)}, u32[]{:S(2)}) collective-permute-start(bf16[64,1024]{1,0:T(8,128)(2,1)S(1)} %shard_map.102.mine_ref), channel_id=1, source_target_pairs={{0,1},{1,0},{2,3},{3,2},{4,5},{5,4},{6,7},{7,6},{8,9},{9,8},{10,11... | collective-permute-start | bytes 393224 | tf_op jit(solution)/shard_map/ppermute | solution.py:508
  80.1 6.7 %collective-permute-start.22 = (bf16[64,1024]{1,0:T(8,128)(2,1)S(1)}, bf16[64,1024]{1,0:T(8,128)(2,1)S(1)}, u32[]{:S(2)}, u32[]{:S(2)}) collective-permute-start(bf16[64,1024]{1,0:T(8,128)(2,1)S(1)} %get-tuple-element.51), channel_id=1, source_target_pairs={{16,10},{17,15},{18,8},{19,13},{20,14},{21,11},{22,12},{23,9},{24,... | collective-permute-start | bytes 393224 | tf_op jit(solution)/shard_map/ppermute | solution.py:386
  81.7 8.0 %collective-permute-start.21 = (bf16[64,1024]{1,0:T(8,128)(2,1)S(1)}, bf16[64,1024]{1,0:T(8,128)(2,1)S(1)}, u32[]{:S(2)}, u32[]{:S(2)}) collective-permute-start(bf16[64,1024]{1,0:T(8,128)(2,1)S(1)} %get-tuple-element.51), channel_id=1, source_target_pairs={{16,8},{17,13},{18,10},{19,15},{20,12},{21,9},{22,14},{23,11},{24,... | collective-permute-start | bytes 393224 | tf_op jit(solution)/shard_map/ppermute | solution.py:386
  90.2 1.4 %collective-permute-start.23 = (bf16[64,1024]{1,0:T(8,128)(2,1)S(1)}, bf16[64,1024]{1,0:T(8,128)(2,1)S(1)}, u32[]{:S(2)}, u32[]{:S(2)}) collective-permute-start(bf16[64,1024]{1,0:T(8,128)(2,1)S(1)} %shard_map.105.mine_ref), channel_id=1, source_target_pairs={{0,1},{1,0},{2,3},{3,2},{4,5},{5,4},{6,7},{7,6},{8,9},{9,8},{10,11... | collective-permute-start | bytes 393224 | tf_op jit(solution)/shard_map/ppermute | solution.py:508
  91.8 10.3 %collective-permute-start.25 = (bf16[64,1024]{1,0:T(8,128)(2,1)S(1)}, bf16[64,1024]{1,0:T(8,128)(2,1)S(1)}, u32[]{:S(2)}, u32[]{:S(2)}) collective-permute-start(bf16[64,1024]{1,0:T(8,128)(2,1)S(1)} %get-tuple-element.53), channel_id=1, source_target_pairs={{8,2},{9,7},{10,0},{11,5},{12,6},{13,3},{14,4},{15,1},{16,10},{17,... | collective-permute-start | bytes 393224 | tf_op jit(solution)/shard_map/ppermute | solution.py:386
  97.9 7.5 %collective-permute-start.24 = (bf16[64,1024]{1,0:T(8,128)(2,1)S(1)}, bf16[64,1024]{1,0:T(8,128)(2,1)S(1)}, u32[]{:S(2)}, u32[]{:S(2)}) collective-permute-start(bf16[64,1024]{1,0:T(8,128)(2,1)S(1)} %get-tuple-element.53), channel_id=1, source_target_pairs={{8,0},{9,5},{10,2},{11,7},{12,4},{13,1},{14,6},{15,3},{16,8},{17,1... | collective-permute-start | bytes 393224 | tf_op jit(solution)/shard_map/ppermute | solution.py:386
  105.9 1.4 %collective-permute-start.26 = (bf16[64,1024]{1,0:T(8,128)(2,1)S(1)}, bf16[64,1024]{1,0:T(8,128)(2,1)S(1)}, u32[]{:S(2)}, u32[]{:S(2)}) collective-permute-start(bf16[64,1024]{1,0:T(8,128)(2,1)S(1)} %shard_map.108.mine_ref), channel_id=1, source_target_pairs={{0,1},{1,0},{2,3},{3,2},{4,5},{5,4},{6,7},{7,6},{8,9},{9,8},{10,11... | collective-permute-start | bytes 393224 | tf_op jit(solution)/shard_map/ppermute | solution.py:508
  107.5 8.0 %collective-permute-start.28 = (bf16[64,1024]{1,0:T(8,128)(2,1)S(1)}, bf16[64,1024]{1,0:T(8,128)(2,1)S(1)}, u32[]{:S(2)}, u32[]{:S(2)}) collective-permute-start(bf16[64,1024]{1,0:T(8,128)(2,1)S(1)} %get-tuple-element.55.after_ref), channel_id=1, source_target_pairs={{8,2},{9,7},{10,0},{11,5},{12,6},{13,3},{14,4},{15,1},{16,18},{17,... | collective-permute-start | bytes 393224 | tf_op jit(solution)/shard_map/ppermute | solution.py:386
  111.4 7.5 %collective-permute-start.27 = (bf16[64,1024]{1,0:T(8,128)(2,1)S(1)}, bf16[64,1024]{1,0:T(8,128)(2,1)S(1)}, u32[]{:S(2)}, u32[]{:S(2)}) collective-permute-start(bf16[64,1024]{1,0:T(8,128)(2,1)S(1)} %get-tuple-element.55.after_ref), channel_id=1, source_target_pairs={{8,0},{9,5},{10,2},{11,7},{12,4},{13,1},{14,6},{15,3},{16,16},{17,... | collective-permute-start | bytes 393224 | tf_op jit(solution)/shard_map/ppermute | solution.py:386
  119.4 1.4 %collective-permute-start.29 = (bf16[64,1024]{1,0:T(8,128)(2,1)S(1)}, bf16[64,1024]{1,0:T(8,128)(2,1)S(1)}, u32[]{:S(2)}, u32[]{:S(2)}) collective-permute-start(bf16[64,1024]{1,0:T(8,128)(2,1)S(1)} %shard_map.112.mine_ref), channel_id=1, source_target_pairs={{0,1},{1,0},{2,3},{3,2},{4,5},{5,4},{6,7},{7,6},{8,9},{9,8},{10,11... | collective-permute-start | bytes 393224 | tf_op jit(solution)/shard_map/ppermute | solution.py:508
  120.9 6.3 %collective-permute-start.30 = (bf16[128,512]{1,0:T(8,128)(2,1)S(1)}, bf16[128,512]{1,0:T(8,128)(2,1)S(1)}, u32[]{:S(2)}, u32[]{:S(2)}) collective-permute-start(bf16[128,512]{1,0:T(8,128)(2,1)S(1)} %get-tuple-element.59.top_ref), channel_id=1, source_target_pairs={{1,2},{3,4},{5,6},{2,1},{4,3},{6,5},{9,10},{11,12},{13,14},{10,9},... | collective-permute-start | bytes 393224 | tf_op jit(solution)/shard_map/ppermute | solution.py:561
  (3 other events, 20.6 us)

commit v8 on v7

--- a/solution.py
+++ b/solution.py
@@ -190,7 +190,8 @@
 
 def leaf_kernel(
     group,
-    beside_ref,
+    ready_ref,
+    last_ref,
     picked_ref,
     pick_ref,
     matrix_ref,
@@ -204,10 +205,11 @@
     sems,
 ):
     leaf_count, edge, leaf_size = matrix_ref.shape
-    rows = beside_ref.shape[1]
+    rows = last_ref.shape[1]
     copies = [pltpu.make_async_copy(top_ref, top_hbm, top_sem)]
     copies[0].start()
-    picked = jnp.dot(beside_ref[...], pick_ref[2 * rows :, :], preferred_element_type=F32)
+    beside = jnp.concatenate([ready_ref[...], last_ref[...]], axis=0)
+    picked = jnp.dot(beside, pick_ref[2 * rows :, :], preferred_element_type=F32)
     all_ref[...] = (picked + picked_ref[...].astype(F32)).astype(BF16)
     for step in range(leaf_count // group):
         first = step * group
@@ -530,6 +532,10 @@
             input_output_aliases={2: 0},
             compiler_params=params(4),
         )(in_vmem(share), in_vmem(other), in_vmem(state), scales, later_known)
+        if turn == turns - 2:
+            ready = state[: sources - wave_rows]
+            ready = jnp.where(core == 0, ready[:, :rows], ready[:, rows:])
+            beside_ready = lax.ppermute(ready, "front", swap_chip)
         routes = turn_routes(turn, panels, WAVES)
         arrived = [in_vmem(a) for a in spread(outgoing, routes, chips)]
         if turn in preparing:
@@ -558,7 +564,7 @@
             extra = made
     picks, matrices = made
 
-    beside = lax.ppermute(top_field, "front", swap_chip)
+    beside_last = lax.ppermute(top_field[sources - wave_rows :], "front", swap_chip)
     picked = pl.pallas_call(
         near_kernel,
         out_shape=pltpu.VMEM((sources, leaf_count * edge), BF16),
@@ -577,7 +583,7 @@
             jax.ShapeDtypeStruct((sources, all_lanes), BF16),
             jax.ShapeDtypeStruct((sources, rows), BF16),
         ),
-        in_specs=[VMEM] * 6,
+        in_specs=[VMEM] * 7,
         out_specs=(ANY, ANY),
         scratch_shapes=[
             pltpu.VMEM((sources, leaf_count * edge), BF16),
@@ -586,7 +592,7 @@
             pltpu.SemaphoreType.DMA((steps,)),
         ],
         compiler_params=params(8),
-    )(in_vmem(beside), in_vmem(picked), in_vmem(picks), in_vmem(matrices), in_vmem(interior), in_vmem(top_field))
+    )(in_vmem(beside_ready), in_vmem(beside_last), in_vmem(picked), in_vmem(picks), in_vmem(matrices), in_vmem(interior), in_vmem(top_field))
     return (top_field[None], leaf_field[None])
 
 

time: 130 us -> 131 us (level)
  starting transfers between devices: 51.7 us -> 54.7 us
  waiting for transfers between devices: 47.2 us -> 44.7 us
    ppermute x1 -> x2, starting transfers between devices: 2.76 us -> 5.78 us  [the longest x1 3.25 us: body(): lax.ppermute(top_field[sources - wave_rows:], 'front', swap_chip)]
    ppermute x8, waiting for transfers between devices: 9.01 us -> 7.67 us  [body(): other = lax.ppermute(share, 'front', swap_core)]
  transfers between devices with their start and end apart: 31 -> 32, of which waited for: 25 -> 24; matrix products, arithmetic and copies ran while one was open for 0% -> 0% of each run, Pallas kernels for 11% -> 11%
where the time goes in v8:
time: 131 us; the launch traced here: 130 us
  starting transfers between devices  54.7 us (42%)
  waiting for transfers between devices  44.7 us (34%)
  Pallas kernels  28.6 us (22%)
  between operations  1.35 us (1%)
    ppermute x16, starting transfers between devices, spread(): received.append(lax.ppermute(values, ('panel', 'front'), route))  40.4 us
    ppermute x16, waiting for transfers between devices, spread(): received.append(lax.ppermute(values, ('panel', 'front'), route))  33 us
    pallas_call x16, Pallas kernels, body(): pl.pallas_call(functools.partial(fold_kernel, blocks, bool(share), len(be...  7.72 us
    ppermute x8, waiting for transfers between devices, body(): other = lax.ppermute(share, 'front', swap_core)  7.67 us
    pallas_call x1, Pallas kernels, body(): pl.pallas_call(functools.partial(push_kernel, group), out_shape=(pltpu.VM...  7.5 us
    pallas_call x2, Pallas kernels, body(): pl.pallas_call(functools.partial(prepare_kernel, group, preparing[turn],...  4.9 us
    ppermute x1, starting transfers between devices, body(): inward = lax.ppermute(outward, 'front', swap_chip)  4.55 us
    pallas_call x1, Pallas kernels, body(): pl.pallas_call(turn_kernel, out_shape=pltpu.VMEM((width // 2, chip_rows),...  3.91 us
  transfers between devices with their start and end apart: 32, of which 24 were waited for; matrix products, arithmetic and copies ran while one was open for 0% of the time, Pallas kernels for 11%

profile of v8, /device:TPU:1, one launch (start us, length us, event | category | flops | bytes accessed | tf_op | source)
XLA Modules:
  0.0 130.3 jit_solution(70606272556549305)
XLA Ops:
  1.4 7.5 %shard_map.86 = (bf16[128,512]{1,0:T(8,128)(2,1)S(1)}, f32[128,1024]{1,0:T(8,128)S(1)}, bf16[128,9216]{1,0:T(8,128)(2,1)S(1)}, bf16[512,2048]{1,0:T(8,128)(2,1)}) custom-call(s32[9,4,128]{2,1,0:T(4,128)S(1)} %bitcast.10, bf16[128,9216]{1,0:T(8,128)(2,1)} %bitcast.21, bf16[36,256,256]{2,1,0:T(8,128)(2,1)} %bitcast.13, bf16[36,128,256]{2,1,0:T(8,128)(2,1)} %bitcast.18, ...), custom_call_target="tpu_custom_call" | custom-call | tf_op jit(solution)/shard_map/pallas_call | solution.py:416
  9.0 4.6 %collective-permute-start.1 = (bf16[128,512]{1,0:T(8,128)(2,1)S(1)}, bf16[128,512]{1,0:T(8,128)(2,1)S(1)}, u32[]{:S(2)}, u32[]{:S(2)}) collective-permute-start(bf16[128,512]{1,0:T(8,128)(2,1)S(1)} %get-tuple-element.36), channel_id=1, source_target_pairs={{1,2},{3,4},{5,6},{2,1},{4,3},{6,5},{9,10},{11,12},{13,14},{10,9},... | collective-permute-start | bytes 393224 | tf_op jit(solution)/shard_map/ppermute | solution.py:445
  13.6 2.2 %collective-permute-start.2 = (f32[1,512]{1,0:T(1,128)S(1)}, f32[1,512]{1,0:T(1,128)S(1)}, u32[]{:S(2)}, u32[]{:S(2)}) collective-permute-start(f32[1,512]{1,0:T(1,128)S(1)} %copy-done.3), channel_id=1, source_target_pairs={{8,0},{16,8},{24,16},{0,24},{9,1},{17,9},{25,17},{1,25},{10,2},{18... | collective-permute-start | bytes 6152 | tf_op jit(solution)/shard_map/ppermute | solution.py:447
  16.7 1.5 %collective-permute-done.3 = bf16[128,1024]{1,0:T(8,128)(2,1)S(1)} collective-permute-done((bf16[128,1024]{1,0:T(8,128)(2,1)S(1)}, bf16[128,1024]{1,0:T(8,128)(2,1)S(1)}, u32[]{:S(2)}, u32[]{:S(2)}) %collective-permute-start.3) | collective-permute-done | bytes 262176 | tf_op jit(solution)/shard_map/ppermute | solution.py:459
  18.3 5.1 %collective-permute-start.5 = (bf16[64,1024]{1,0:T(8,128)(2,1)S(1)}, bf16[64,1024]{1,0:T(8,128)(2,1)S(1)}, u32[]{:S(2)}, u32[]{:S(2)}) collective-permute-start(bf16[64,1024]{1,0:T(8,128)(2,1)S(1)} %slice.19), channel_id=1, source_target_pairs={{0,2},{1,7},{2,0},{3,5},{4,6},{5,3},{6,4},{7,1}} | collective-permute-start | bytes 393224 | tf_op jit(solution)/shard_map/ppermute | solution.py:388
  23.4 1.9 %collective-permute-start.4 = (bf16[64,1024]{1,0:T(8,128)(2,1)S(1)}, bf16[64,1024]{1,0:T(8,128)(2,1)S(1)}, u32[]{:S(2)}, u32[]{:S(2)}) collective-permute-start(bf16[64,1024]{1,0:T(8,128)(2,1)S(1)} %slice.19), channel_id=1, source_target_pairs={{0,0},{1,5},{2,2},{3,7},{4,4},{5,1},{6,6},{7,3}} | collective-permute-start | bytes 393224 | tf_op jit(solution)/shard_map/ppermute | solution.py:388
  25.4 3.9 %shard_map.87.inverse_ref = bf16[2048,1024]{1,0:T(8,128)(2,1)S(1)} custom-call(bf16[512,4096]{1,0:T(8,128)(2,1)} %bitcast.17, bf16[512,2048]{1,0:T(8,128)(2,1)} %collective-permute-done.taken_hbm), custom_call_target="tpu_custom_call" | custom-call | flops 536870912 | bytes 8388608 | tf_op jit(solution)/shard_map/pallas_call | solution.py:471
  32.9 2.0 %collective-permute-start.10 = (bf16[64,1024]{1,0:T(8,128)(2,1)S(1)}, bf16[64,1024]{1,0:T(8,128)(2,1)S(1)}, u32[]{:S(2)}, u32[]{:S(2)}) collective-permute-start(bf16[64,1024]{1,0:T(8,128)(2,1)S(1)} %get-tuple-element.41), channel_id=1, source_target_pairs={{0,10},{1,15},{2,8},{3,13},{4,14},{5,11},{6,12},{7,9},{8,18},{9,23... | collective-permute-start | bytes 393224 | tf_op jit(solution)/shard_map/ppermute | solution.py:388
  35.6 6.0 %collective-permute-done.10.refs_0_ = bf16[64,1024]{1,0:T(8,128)(2,1)S(1)} collective-permute-done((bf16[64,1024]{1,0:T(8,128)(2,1)S(1)}, bf16[64,1024]{1,0:T(8,128)(2,1)S(1)}, u32[]{:S(2)}, u32[]{:S(2)}) %collective-permute-start.10) | collective-permute-done | bytes 131104 | tf_op jit(solution)/shard_map/ppermute | solution.py:388
  45.6 2.2 %collective-permute-start.13 = (bf16[64,1024]{1,0:T(8,128)(2,1)S(1)}, bf16[64,1024]{1,0:T(8,128)(2,1)S(1)}, u32[]{:S(2)}, u32[]{:S(2)}) collective-permute-start(bf16[64,1024]{1,0:T(8,128)(2,1)S(1)} %get-tuple-element.43), channel_id=1, source_target_pairs={{8,18},{9,23},{10,16},{11,21},{12,22},{13,19},{14,20},{15,17},{0,1... | collective-permute-start | bytes 393224 | tf_op jit(solution)/shard_map/ppermute | solution.py:388
  47.7 1.9 %collective-permute-start.12 = (bf16[64,1024]{1,0:T(8,128)(2,1)S(1)}, bf16[64,1024]{1,0:T(8,128)(2,1)S(1)}, u32[]{:S(2)}, u32[]{:S(2)}) collective-permute-start(bf16[64,1024]{1,0:T(8,128)(2,1)S(1)} %get-tuple-element.43), channel_id=1, source_target_pairs={{8,16},{9,21},{10,18},{11,23},{12,20},{13,17},{14,22},{15,19},{0,8... | collective-permute-start | bytes 393224 | tf_op jit(solution)/shard_map/ppermute | solution.py:388
  49.7 3.7 %collective-permute-done.13.refs_0_ = bf16[64,1024]{1,0:T(8,128)(2,1)S(1)} collective-permute-done((bf16[64,1024]{1,0:T(8,128)(2,1)S(1)}, bf16[64,1024]{1,0:T(8,128)(2,1)S(1)}, u32[]{:S(2)}, u32[]{:S(2)}) %collective-permute-start.13) | collective-permute-done | bytes 131104 | tf_op jit(solution)/shard_map/ppermute | solution.py:388
  53.8 2.3 %collective-permute-done.12.refs_0_ = bf16[64,1024]{1,0:T(8,128)(2,1)S(1)} collective-permute-done((bf16[64,1024]{1,0:T(8,128)(2,1)S(1)}, bf16[64,1024]{1,0:T(8,128)(2,1)S(1)}, u32[]{:S(2)}, u32[]{:S(2)}) %collective-permute-start.12) | collective-permute-done | bytes 131104 | tf_op jit(solution)/shard_map/ppermute | solution.py:388
  59.1 1.9 %collective-permute-start.15 = (bf16[64,1024]{1,0:T(8,128)(2,1)S(1)}, bf16[64,1024]{1,0:T(8,128)(2,1)S(1)}, u32[]{:S(2)}, u32[]{:S(2)}) collective-permute-start(bf16[64,1024]{1,0:T(8,128)(2,1)S(1)} %get-tuple-element.45), channel_id=1, source_target_pairs={{16,24},{17,29},{18,26},{19,31},{20,28},{21,25},{22,30},{23,27},{8... | collective-permute-start | bytes 393224 | tf_op jit(solution)/shard_map/ppermute | solution.py:388
  61.0 3.2 %collective-permute-done.16.refs_0_ = bf16[64,1024]{1,0:T(8,128)(2,1)S(1)} collective-permute-done((bf16[64,1024]{1,0:T(8,128)(2,1)S(1)}, bf16[64,1024]{1,0:T(8,128)(2,1)S(1)}, u32[]{:S(2)}, u32[]{:S(2)}) %collective-permute-start.16) | collective-permute-done | bytes 131104 | tf_op jit(solution)/shard_map/ppermute | solution.py:388
  64.7 2.4 %collective-permute-done.15.refs_0_ = bf16[64,1024]{1,0:T(8,128)(2,1)S(1)} collective-permute-done((bf16[64,1024]{1,0:T(8,128)(2,1)S(1)}, bf16[64,1024]{1,0:T(8,128)(2,1)S(1)}, u32[]{:S(2)}, u32[]{:S(2)}) %collective-permute-start.15) | collective-permute-done | bytes 131104 | tf_op jit(solution)/shard_map/ppermute | solution.py:388
  70.4 1.9 %collective-permute-start.18 = (bf16[64,1024]{1,0:T(8,128)(2,1)S(1)}, bf16[64,1024]{1,0:T(8,128)(2,1)S(1)}, u32[]{:S(2)}, u32[]{:S(2)}) collective-permute-start(bf16[64,1024]{1,0:T(8,128)(2,1)S(1)} %get-tuple-element.47.after_ref), channel_id=1, source_target_pairs={{24,16},{25,21},{26,18},{27,23},{28,20},{29,17},{30,22},{31,19},{1... | collective-permute-start | bytes 393224 | tf_op jit(solution)/shard_map/ppermute | solution.py:388
  72.3 4.8 %shard_map.100 = (bf16[1536,4608]{1,0:T(8,128)(2,1)S(1)}, bf16[36,128,256]{2,1,0:T(8,128)(2,1)S(1)}) custom-call(s32[9,4,128]{2,1,0:T(4,128)S(1)} %bitcast.11, bf16[36,256,256]{2,1,0:T(8,128)(2,1)} %bitcast.14, bf16[36,128,256]{2,1,0:T(8,128)(2,1)} %bitcast.19, bf16[64,1024]{1,0:T(8,128)(2,1)S(1)} %get-tuple-element.47.after_ref), custom_call_target="tpu_custom_call" | custom-call | flops 2415919104 | bytes 14155776 | tf_op jit(solution)/shard_map/pallas_call | solution.py:542
  80.1 1.7 %collective-permute-start.22 = (bf16[64,1024]{1,0:T(8,128)(2,1)S(1)}, bf16[64,1024]{1,0:T(8,128)(2,1)S(1)}, u32[]{:S(2)}, u32[]{:S(2)}) collective-permute-start(bf16[64,1024]{1,0:T(8,128)(2,1)S(1)} %get-tuple-element.51), channel_id=1, source_target_pairs={{16,10},{17,15},{18,8},{19,13},{20,14},{21,11},{22,12},{23,9},{24,... | collective-permute-start | bytes 393224 | tf_op jit(solution)/shard_map/ppermute | solution.py:388
  81.7 3.4 %collective-permute-start.21 = (bf16[64,1024]{1,0:T(8,128)(2,1)S(1)}, bf16[64,1024]{1,0:T(8,128)(2,1)S(1)}, u32[]{:S(2)}, u32[]{:S(2)}) collective-permute-start(bf16[64,1024]{1,0:T(8,128)(2,1)S(1)} %get-tuple-element.51), channel_id=1, source_target_pairs={{16,8},{17,13},{18,10},{19,15},{20,12},{21,9},{22,14},{23,11},{24,... | collective-permute-start | bytes 393224 | tf_op jit(solution)/shard_map/ppermute | solution.py:388
  85.1 1.7 %collective-permute-done.22.refs_0_ = bf16[64,1024]{1,0:T(8,128)(2,1)S(1)} collective-permute-done((bf16[64,1024]{1,0:T(8,128)(2,1)S(1)}, bf16[64,1024]{1,0:T(8,128)(2,1)S(1)}, u32[]{:S(2)}, u32[]{:S(2)}) %collective-permute-start.22) | collective-permute-done | bytes 131104 | tf_op jit(solution)/shard_map/ppermute | solution.py:388
  87.3 2.5 %collective-permute-done.21.refs_0_ = bf16[64,1024]{1,0:T(8,128)(2,1)S(1)} collective-permute-done((bf16[64,1024]{1,0:T(8,128)(2,1)S(1)}, bf16[64,1024]{1,0:T(8,128)(2,1)S(1)}, u32[]{:S(2)}, u32[]{:S(2)}) %collective-permute-start.21) | collective-permute-done | bytes 131104 | tf_op jit(solution)/shard_map/ppermute | solution.py:388
  91.8 6.2 %collective-permute-start.25 = (bf16[64,1024]{1,0:T(8,128)(2,1)S(1)}, bf16[64,1024]{1,0:T(8,128)(2,1)S(1)}, u32[]{:S(2)}, u32[]{:S(2)}) collective-permute-start(bf16[64,1024]{1,0:T(8,128)(2,1)S(1)} %get-tuple-element.53), channel_id=1, source_target_pairs={{8,2},{9,7},{10,0},{11,5},{12,6},{13,3},{14,4},{15,1},{16,10},{17,... | collective-permute-start | bytes 393224 | tf_op jit(solution)/shard_map/ppermute | solution.py:388
  97.9 3.5 %collective-permute-start.24 = (bf16[64,1024]{1,0:T(8,128)(2,1)S(1)}, bf16[64,1024]{1,0:T(8,128)(2,1)S(1)}, u32[]{:S(2)}, u32[]{:S(2)}) collective-permute-start(bf16[64,1024]{1,0:T(8,128)(2,1)S(1)} %get-tuple-element.53), channel_id=1, source_target_pairs={{8,0},{9,5},{10,2},{11,7},{12,4},{13,1},{14,6},{15,3},{16,8},{17,1... | collective-permute-start | bytes 393224 | tf_op jit(solution)/shard_map/ppermute | solution.py:388
  102.5 2.9 %collective-permute-done.24.refs_0_ = bf16[64,1024]{1,0:T(8,128)(2,1)S(1)} collective-permute-done((bf16[64,1024]{1,0:T(8,128)(2,1)S(1)}, bf16[64,1024]{1,0:T(8,128)(2,1)S(1)}, u32[]{:S(2)}, u32[]{:S(2)}) %collective-permute-start.24) | collective-permute-done | bytes 131104 | tf_op jit(solution)/shard_map/ppermute | solution.py:388
  107.5 3.9 %collective-permute-start.29 = (bf16[64,1024]{1,0:T(8,128)(2,1)S(1)}, bf16[64,1024]{1,0:T(8,128)(2,1)S(1)}, u32[]{:S(2)}, u32[]{:S(2)}) collective-permute-start(bf16[64,1024]{1,0:T(8,128)(2,1)S(1)} %get-tuple-element.56.after_ref), channel_id=1, source_target_pairs={{8,2},{9,7},{10,0},{11,5},{12,6},{13,3},{14,4},{15,1},{16,18},{17,... | collective-permute-start | bytes 393224 | tf_op jit(solution)/shard_map/ppermute | solution.py:388
  111.4 1.9 %collective-permute-start.28 = (bf16[64,1024]{1,0:T(8,128)(2,1)S(1)}, bf16[64,1024]{1,0:T(8,128)(2,1)S(1)}, u32[]{:S(2)}, u32[]{:S(2)}) collective-permute-start(bf16[64,1024]{1,0:T(8,128)(2,1)S(1)} %get-tuple-element.56.after_ref), channel_id=1, source_target_pairs={{8,0},{9,5},{10,2},{11,7},{12,4},{13,1},{14,6},{15,3},{16,16},{17,... | collective-permute-start | bytes 393224 | tf_op jit(solution)/shard_map/ppermute | solution.py:388
  113.4 2.0 %collective-permute-done.29.refs_0_ = bf16[64,1024]{1,0:T(8,128)(2,1)S(1)} collective-permute-done((bf16[64,1024]{1,0:T(8,128)(2,1)S(1)}, bf16[64,1024]{1,0:T(8,128)(2,1)S(1)}, u32[]{:S(2)}, u32[]{:S(2)}) %collective-permute-start.29) | collective-permute-done | bytes 131104 | tf_op jit(solution)/shard_map/ppermute | solution.py:388
  115.9 3.0 %collective-permute-done.28.refs_2_ = bf16[64,1024]{1,0:T(8,128)(2,1)S(1)} collective-permute-done((bf16[64,1024]{1,0:T(8,128)(2,1)S(1)}, bf16[64,1024]{1,0:T(8,128)(2,1)S(1)}, u32[]{:S(2)}, u32[]{:S(2)}) %collective-permute-start.28) | collective-permute-done | bytes 131104 | tf_op jit(solution)/shard_map/ppermute | solution.py:388
  119.5 2.5 %collective-permute-start.27 = (bf16[64,512]{1,0:T(8,128)(2,1)S(1)}, bf16[64,512]{1,0:T(8,128)(2,1)S(1)}, u32[]{:S(2)}, u32[]{:S(2)}) collective-permute-start(bf16[64,512]{1,0:T(8,128)(2,1)S(1)} %slice_select_fusion), channel_id=1, source_target_pairs={{1,2},{3,4},{5,6},{2,1},{4,3},{6,5},{9,10},{11,12},{13,14},{10,9},... | collective-permute-start | bytes 196616 | tf_op jit(solution)/shard_map/ppermute | solution.py:538
  122.1 3.2 %collective-permute-start.31 = (bf16[64,512]{1,0:T(8,128)(2,1)S(1)}, bf16[64,512]{1,0:T(8,128)(2,1)S(1)}, u32[]{:S(2)}, u32[]{:S(2)}) collective-permute-start(bf16[64,512]{1,0:T(8,128)(2,1)S(1)} %slice.18), channel_id=1, source_target_pairs={{1,2},{3,4},{5,6},{2,1},{4,3},{6,5},{9,10},{11,12},{13,14},{10,9},... | collective-permute-start | bytes 196616 | tf_op jit(solution)/shard_map/ppermute | solution.py:567
  127.7 2.4 %shard_map.115 = (bf16[128,9216]{1,0:T(8,128)(2,1)}, bf16[128,512]{1,0:T(8,128)(2,1)}) custom-call(bf16[64,512]{1,0:T(8,128)(2,1)S(1)} %collective-permute-done.27.ready_ref, bf16[64,512]{1,0:T(8,128)(2,1)S(1)} %collective-permute-done.31.last_ref, bf16[128,4608]{1,0:T(8,128)(2,1)S(1)} %shard_map.114.picked_ref, ...), custom_call_target="tpu_custom_call" | custom-call | tf_op jit(solution)/shard_map/pallas_call | solution.py:580
  (80 shorter events, 29.4 us)
Async XLA Ops:
  8.9 16.5 %collective-permute-start = (bf16[512,2048]{1,0:T(8,128)(2,1)}, bf16[512,2048]{1,0:T(8,128)(2,1)}, u32[]{:S(2)}, u32[]{:S(2)}) collective-permute-start(bf16[512,2048]{1,0:T(8,128)(2,1)} %get-tuple-element.35), channel_id=1, source_target_pairs={{0,1},{1,0},{2,3},{3,2},{4,5},{5,4},{6,7},{7,6},{8,9},{9,8},{10,11... | collective-permute-start | bytes 6291464 | tf_op jit(solution)/shard_map/ppermute | solution.py:444
  9.0 7.5 %collective-permute-start.1 = (bf16[128,512]{1,0:T(8,128)(2,1)S(1)}, bf16[128,512]{1,0:T(8,128)(2,1)S(1)}, u32[]{:S(2)}, u32[]{:S(2)}) collective-permute-start(bf16[128,512]{1,0:T(8,128)(2,1)S(1)} %get-tuple-element.36), channel_id=1, source_target_pairs={{1,2},{3,4},{5,6},{2,1},{4,3},{6,5},{9,10},{11,12},{13,14},{10,9},... | collective-permute-start | bytes 393224 | tf_op jit(solution)/shard_map/ppermute | solution.py:445
  13.6 3.0 %collective-permute-start.2 = (f32[1,512]{1,0:T(1,128)S(1)}, f32[1,512]{1,0:T(1,128)S(1)}, u32[]{:S(2)}, u32[]{:S(2)}) collective-permute-start(f32[1,512]{1,0:T(1,128)S(1)} %copy-done.3), channel_id=1, source_target_pairs={{8,0},{16,8},{24,16},{0,24},{9,1},{17,9},{25,17},{1,25},{10,2},{18... | collective-permute-start | bytes 6152 | tf_op jit(solution)/shard_map/ppermute | solution.py:447
  16.6 1.6 %collective-permute-start.3 = (bf16[128,1024]{1,0:T(8,128)(2,1)S(1)}, bf16[128,1024]{1,0:T(8,128)(2,1)S(1)}, u32[]{:S(2)}, u32[]{:S(2)}) collective-permute-start(bf16[128,1024]{1,0:T(8,128)(2,1)S(1)} %subtract_convert_fusion), channel_id=1, source_target_pairs={{0,1},{1,0},{2,3},{3,2},{4,5},{5,4},{6,7},{7,6},{8,9},{9,8},{10,11... | collective-permute-start | bytes 786440 | tf_op jit(solution)/shard_map/ppermute | solution.py:459
  18.3 11.0 %collective-permute-start.5 = (bf16[64,1024]{1,0:T(8,128)(2,1)S(1)}, bf16[64,1024]{1,0:T(8,128)(2,1)S(1)}, u32[]{:S(2)}, u32[]{:S(2)}) collective-permute-start(bf16[64,1024]{1,0:T(8,128)(2,1)S(1)} %slice.19), channel_id=1, source_target_pairs={{0,2},{1,7},{2,0},{3,5},{4,6},{5,3},{6,4},{7,1}} | collective-permute-start | bytes 393224 | tf_op jit(solution)/shard_map/ppermute | solution.py:388
  23.4 7.3 %collective-permute-start.4 = (bf16[64,1024]{1,0:T(8,128)(2,1)S(1)}, bf16[64,1024]{1,0:T(8,128)(2,1)S(1)}, u32[]{:S(2)}, u32[]{:S(2)}) collective-permute-start(bf16[64,1024]{1,0:T(8,128)(2,1)S(1)} %slice.19), channel_id=1, source_target_pairs={{0,0},{1,5},{2,2},{3,7},{4,4},{5,1},{6,6},{7,3}} | collective-permute-start | bytes 393224 | tf_op jit(solution)/shard_map/ppermute | solution.py:388
  25.3 7.4 %collective-permute-start.8 = (bf16[128,1024]{1,0:T(8,128)(2,1)S(1)}, bf16[128,1024]{1,0:T(8,128)(2,1)S(1)}, u32[]{:S(2)}, u32[]{:S(2)}) collective-permute-start(bf16[128,1024]{1,0:T(8,128)(2,1)S(1)} %add_convert_fusion), channel_id=1, source_target_pairs={{8,0},{16,8},{24,16},{0,24},{9,1},{17,9},{25,17},{1,25},{10,2},{18... | collective-permute-start | bytes 786440 | tf_op jit(solution)/shard_map/ppermute | solution.py:469
  31.2 1.5 %collective-permute-start.6 = (bf16[64,1024]{1,0:T(8,128)(2,1)S(1)}, bf16[64,1024]{1,0:T(8,128)(2,1)S(1)}, u32[]{:S(2)}, u32[]{:S(2)}) collective-permute-start(bf16[64,1024]{1,0:T(8,128)(2,1)S(1)} %shard_map.89.mine_ref), channel_id=1, source_target_pairs={{0,1},{1,0},{2,3},{3,2},{4,5},{5,4},{6,7},{7,6},{8,9},{9,8},{10,11... | collective-permute-start | bytes 393224 | tf_op jit(solution)/shard_map/ppermute | solution.py:510
  31.3 1.4 %collective-permute-start.7 = (f32[2,512]{1,0:T(2,128)S(1)}, f32[2,512]{1,0:T(2,128)S(1)}, u32[]{:S(2)}, u32[]{:S(2)}) collective-permute-start(f32[2,512]{1,0:T(2,128)S(1)} %pad_maximum_fusion), channel_id=1, source_target_pairs={{0,1},{1,0},{2,3},{3,2},{4,5},{5,4},{6,7},{7,6},{8,9},{9,8},{10,11... | collective-permute-start | bytes 12296 | tf_op jit(solution)/shard_map/ppermute | solution.py:460
  32.9 8.7 %collective-permute-start.10 = (bf16[64,1024]{1,0:T(8,128)(2,1)S(1)}, bf16[64,1024]{1,0:T(8,128)(2,1)S(1)}, u32[]{:S(2)}, u32[]{:S(2)}) collective-permute-start(bf16[64,1024]{1,0:T(8,128)(2,1)S(1)} %get-tuple-element.41), channel_id=1, source_target_pairs={{0,10},{1,15},{2,8},{3,13},{4,14},{5,11},{6,12},{7,9},{8,18},{9,23... | collective-permute-start | bytes 393224 | tf_op jit(solution)/shard_map/ppermute | solution.py:388
  34.9 8.7 %collective-permute-start.9 = (bf16[64,1024]{1,0:T(8,128)(2,1)S(1)}, bf16[64,1024]{1,0:T(8,128)(2,1)S(1)}, u32[]{:S(2)}, u32[]{:S(2)}) collective-permute-start(bf16[64,1024]{1,0:T(8,128)(2,1)S(1)} %get-tuple-element.41), channel_id=1, source_target_pairs={{0,8},{1,13},{2,10},{3,15},{4,12},{5,9},{6,14},{7,11},{8,16},{9,21... | collective-permute-start | bytes 393224 | tf_op jit(solution)/shard_map/ppermute | solution.py:388
  44.1 1.4 %collective-permute-start.11 = (bf16[64,1024]{1,0:T(8,128)(2,1)S(1)}, bf16[64,1024]{1,0:T(8,128)(2,1)S(1)}, u32[]{:S(2)}, u32[]{:S(2)}) collective-permute-start(bf16[64,1024]{1,0:T(8,128)(2,1)S(1)} %shard_map.92.mine_ref), channel_id=1, source_target_pairs={{0,1},{1,0},{2,3},{3,2},{4,5},{5,4},{6,7},{7,6},{8,9},{9,8},{10,11... | collective-permute-start | bytes 393224 | tf_op jit(solution)/shard_map/ppermute | solution.py:510
  45.6 7.7 %collective-permute-start.13 = (bf16[64,1024]{1,0:T(8,128)(2,1)S(1)}, bf16[64,1024]{1,0:T(8,128)(2,1)S(1)}, u32[]{:S(2)}, u32[]{:S(2)}) collective-permute-start(bf16[64,1024]{1,0:T(8,128)(2,1)S(1)} %get-tuple-element.43), channel_id=1, source_target_pairs={{8,18},{9,23},{10,16},{11,21},{12,22},{13,19},{14,20},{15,17},{0,1... | collective-permute-start | bytes 393224 | tf_op jit(solution)/shard_map/ppermute | solution.py:388
  47.7 8.4 %collective-permute-start.12 = (bf16[64,1024]{1,0:T(8,128)(2,1)S(1)}, bf16[64,1024]{1,0:T(8,128)(2,1)S(1)}, u32[]{:S(2)}, u32[]{:S(2)}) collective-permute-start(bf16[64,1024]{1,0:T(8,128)(2,1)S(1)} %get-tuple-element.43), channel_id=1, source_target_pairs={{8,16},{9,21},{10,18},{11,23},{12,20},{13,17},{14,22},{15,19},{0,8... | collective-permute-start | bytes 393224 | tf_op jit(solution)/shard_map/ppermute | solution.py:388
  56.6 1.4 %collective-permute-start.14 = (bf16[64,1024]{1,0:T(8,128)(2,1)S(1)}, bf16[64,1024]{1,0:T(8,128)(2,1)S(1)}, u32[]{:S(2)}, u32[]{:S(2)}) collective-permute-start(bf16[64,1024]{1,0:T(8,128)(2,1)S(1)} %shard_map.95.mine_ref), channel_id=1, source_target_pairs={{0,1},{1,0},{2,3},{3,2},{4,5},{5,4},{6,7},{7,6},{8,9},{9,8},{10,11... | collective-permute-start | bytes 393224 | tf_op jit(solution)/shard_map/ppermute | solution.py:510
  58.1 6.1 %collective-permute-start.16 = (bf16[64,1024]{1,0:T(8,128)(2,1)S(1)}, bf16[64,1024]{1,0:T(8,128)(2,1)S(1)}, u32[]{:S(2)}, u32[]{:S(2)}) collective-permute-start(bf16[64,1024]{1,0:T(8,128)(2,1)S(1)} %get-tuple-element.45), channel_id=1, source_target_pairs={{16,26},{17,31},{18,24},{19,29},{20,30},{21,27},{22,28},{23,25},{8... | collective-permute-start | bytes 393224 | tf_op jit(solution)/shard_map/ppermute | solution.py:388
  59.1 8.0 %collective-permute-start.15 = (bf16[64,1024]{1,0:T(8,128)(2,1)S(1)}, bf16[64,1024]{1,0:T(8,128)(2,1)S(1)}, u32[]{:S(2)}, u32[]{:S(2)}) collective-permute-start(bf16[64,1024]{1,0:T(8,128)(2,1)S(1)} %get-tuple-element.45), channel_id=1, source_target_pairs={{16,24},{17,29},{18,26},{19,31},{20,28},{21,25},{22,30},{23,27},{8... | collective-permute-start | bytes 393224 | tf_op jit(solution)/shard_map/ppermute | solution.py:388
  67.5 1.4 %collective-permute-start.17 = (bf16[64,1024]{1,0:T(8,128)(2,1)S(1)}, bf16[64,1024]{1,0:T(8,128)(2,1)S(1)}, u32[]{:S(2)}, u32[]{:S(2)}) collective-permute-start(bf16[64,1024]{1,0:T(8,128)(2,1)S(1)} %shard_map.98.mine_ref), channel_id=1, source_target_pairs={{0,1},{1,0},{2,3},{3,2},{4,5},{5,4},{6,7},{7,6},{8,9},{9,8},{10,11... | collective-permute-start | bytes 393224 | tf_op jit(solution)/shard_map/ppermute | solution.py:510
  69.1 8.0 %collective-permute-start.19 = (bf16[64,1024]{1,0:T(8,128)(2,1)S(1)}, bf16[64,1024]{1,0:T(8,128)(2,1)S(1)}, u32[]{:S(2)}, u32[]{:S(2)}) collective-permute-start(bf16[64,1024]{1,0:T(8,128)(2,1)S(1)} %get-tuple-element.47.after_ref), channel_id=1, source_target_pairs={{24,18},{25,23},{26,16},{27,21},{28,22},{29,19},{30,20},{31,17},{1... | collective-permute-start | bytes 393224 | tf_op jit(solution)/shard_map/ppermute | solution.py:388
  70.4 7.7 %collective-permute-start.18 = (bf16[64,1024]{1,0:T(8,128)(2,1)S(1)}, bf16[64,1024]{1,0:T(8,128)(2,1)S(1)}, u32[]{:S(2)}, u32[]{:S(2)}) collective-permute-start(bf16[64,1024]{1,0:T(8,128)(2,1)S(1)} %get-tuple-element.47.after_ref), channel_id=1, source_target_pairs={{24,16},{25,21},{26,18},{27,23},{28,20},{29,17},{30,22},{31,19},{1... | collective-permute-start | bytes 393224 | tf_op jit(solution)/shard_map/ppermute | solution.py:388
  78.5 1.4 %collective-permute-start.20 = (bf16[64,1024]{1,0:T(8,128)(2,1)S(1)}, bf16[64,1024]{1,0:T(8,128)(2,1)S(1)}, u32[]{:S(2)}, u32[]{:S(2)}) collective-permute-start(bf16[64,1024]{1,0:T(8,128)(2,1)S(1)} %shard_map.102.mine_ref), channel_id=1, source_target_pairs={{0,1},{1,0},{2,3},{3,2},{4,5},{5,4},{6,7},{7,6},{8,9},{9,8},{10,11... | collective-permute-start | bytes 393224 | tf_op jit(solution)/shard_map/ppermute | solution.py:510
  80.1 6.7 %collective-permute-start.22 = (bf16[64,1024]{1,0:T(8,128)(2,1)S(1)}, bf16[64,1024]{1,0:T(8,128)(2,1)S(1)}, u32[]{:S(2)}, u32[]{:S(2)}) collective-permute-start(bf16[64,1024]{1,0:T(8,128)(2,1)S(1)} %get-tuple-element.51), channel_id=1, source_target_pairs={{16,10},{17,15},{18,8},{19,13},{20,14},{21,11},{22,12},{23,9},{24,... | collective-permute-start | bytes 393224 | tf_op jit(solution)/shard_map/ppermute | solution.py:388
  81.7 8.0 %collective-permute-start.21 = (bf16[64,1024]{1,0:T(8,128)(2,1)S(1)}, bf16[64,1024]{1,0:T(8,128)(2,1)S(1)}, u32[]{:S(2)}, u32[]{:S(2)}) collective-permute-start(bf16[64,1024]{1,0:T(8,128)(2,1)S(1)} %get-tuple-element.51), channel_id=1, source_target_pairs={{16,8},{17,13},{18,10},{19,15},{20,12},{21,9},{22,14},{23,11},{24,... | collective-permute-start | bytes 393224 | tf_op jit(solution)/shard_map/ppermute | solution.py:388
  90.2 1.4 %collective-permute-start.23 = (bf16[64,1024]{1,0:T(8,128)(2,1)S(1)}, bf16[64,1024]{1,0:T(8,128)(2,1)S(1)}, u32[]{:S(2)}, u32[]{:S(2)}) collective-permute-start(bf16[64,1024]{1,0:T(8,128)(2,1)S(1)} %shard_map.105.mine_ref), channel_id=1, source_target_pairs={{0,1},{1,0},{2,3},{3,2},{4,5},{5,4},{6,7},{7,6},{8,9},{9,8},{10,11... | collective-permute-start | bytes 393224 | tf_op jit(solution)/shard_map/ppermute | solution.py:510
  91.8 10.3 %collective-permute-start.25 = (bf16[64,1024]{1,0:T(8,128)(2,1)S(1)}, bf16[64,1024]{1,0:T(8,128)(2,1)S(1)}, u32[]{:S(2)}, u32[]{:S(2)}) collective-permute-start(bf16[64,1024]{1,0:T(8,128)(2,1)S(1)} %get-tuple-element.53), channel_id=1, source_target_pairs={{8,2},{9,7},{10,0},{11,5},{12,6},{13,3},{14,4},{15,1},{16,10},{17,... | collective-permute-start | bytes 393224 | tf_op jit(solution)/shard_map/ppermute | solution.py:388
  97.9 7.5 %collective-permute-start.24 = (bf16[64,1024]{1,0:T(8,128)(2,1)S(1)}, bf16[64,1024]{1,0:T(8,128)(2,1)S(1)}, u32[]{:S(2)}, u32[]{:S(2)}) collective-permute-start(bf16[64,1024]{1,0:T(8,128)(2,1)S(1)} %get-tuple-element.53), channel_id=1, source_target_pairs={{8,0},{9,5},{10,2},{11,7},{12,4},{13,1},{14,6},{15,3},{16,8},{17,1... | collective-permute-start | bytes 393224 | tf_op jit(solution)/shard_map/ppermute | solution.py:388
  105.9 1.4 %collective-permute-start.26 = (bf16[64,1024]{1,0:T(8,128)(2,1)S(1)}, bf16[64,1024]{1,0:T(8,128)(2,1)S(1)}, u32[]{:S(2)}, u32[]{:S(2)}) collective-permute-start(bf16[64,1024]{1,0:T(8,128)(2,1)S(1)} %shard_map.108.mine_ref), channel_id=1, source_target_pairs={{0,1},{1,0},{2,3},{3,2},{4,5},{5,4},{6,7},{7,6},{8,9},{9,8},{10,11... | collective-permute-start | bytes 393224 | tf_op jit(solution)/shard_map/ppermute | solution.py:510
  107.5 8.0 %collective-permute-start.29 = (bf16[64,1024]{1,0:T(8,128)(2,1)S(1)}, bf16[64,1024]{1,0:T(8,128)(2,1)S(1)}, u32[]{:S(2)}, u32[]{:S(2)}) collective-permute-start(bf16[64,1024]{1,0:T(8,128)(2,1)S(1)} %get-tuple-element.56.after_ref), channel_id=1, source_target_pairs={{8,2},{9,7},{10,0},{11,5},{12,6},{13,3},{14,4},{15,1},{16,18},{17,... | collective-permute-start | bytes 393224 | tf_op jit(solution)/shard_map/ppermute | solution.py:388
  111.4 7.5 %collective-permute-start.28 = (bf16[64,1024]{1,0:T(8,128)(2,1)S(1)}, bf16[64,1024]{1,0:T(8,128)(2,1)S(1)}, u32[]{:S(2)}, u32[]{:S(2)}) collective-permute-start(bf16[64,1024]{1,0:T(8,128)(2,1)S(1)} %get-tuple-element.56.after_ref), channel_id=1, source_target_pairs={{8,0},{9,5},{10,2},{11,7},{12,4},{13,1},{14,6},{15,3},{16,16},{17,... | collective-permute-start | bytes 393224 | tf_op jit(solution)/shard_map/ppermute | solution.py:388
  119.4 2.6 %collective-permute-start.30 = (bf16[64,1024]{1,0:T(8,128)(2,1)S(1)}, bf16[64,1024]{1,0:T(8,128)(2,1)S(1)}, u32[]{:S(2)}, u32[]{:S(2)}) collective-permute-start(bf16[64,1024]{1,0:T(8,128)(2,1)S(1)} %shard_map.112.mine_ref), channel_id=1, source_target_pairs={{0,1},{1,0},{2,3},{3,2},{4,5},{5,4},{6,7},{7,6},{8,9},{9,8},{10,11... | collective-permute-start | bytes 393224 | tf_op jit(solution)/shard_map/ppermute | solution.py:510
  119.5 7.3 %collective-permute-start.27 = (bf16[64,512]{1,0:T(8,128)(2,1)S(1)}, bf16[64,512]{1,0:T(8,128)(2,1)S(1)}, u32[]{:S(2)}, u32[]{:S(2)}) collective-permute-start(bf16[64,512]{1,0:T(8,128)(2,1)S(1)} %slice_select_fusion), channel_id=1, source_target_pairs={{1,2},{3,4},{5,6},{2,1},{4,3},{6,5},{9,10},{11,12},{13,14},{10,9},... | collective-permute-start | bytes 196616 | tf_op jit(solution)/shard_map/ppermute | solution.py:538
  122.1 5.6 %collective-permute-start.31 = (bf16[64,512]{1,0:T(8,128)(2,1)S(1)}, bf16[64,512]{1,0:T(8,128)(2,1)S(1)}, u32[]{:S(2)}, u32[]{:S(2)}) collective-permute-start(bf16[64,512]{1,0:T(8,128)(2,1)S(1)} %slice.18), channel_id=1, source_target_pairs={{1,2},{3,4},{5,6},{2,1},{4,3},{6,5},{9,10},{11,12},{13,14},{10,9},... | collective-permute-start | bytes 196616 | tf_op jit(solution)/shard_map/ppermute | solution.py:567
  (4 other events, 35.7 us)
